TPU v7x, 32 devices: a whole 2x2x4 slice. The times are simulated.
32 devices in a mesh: band: 4 (over y, core), tg: 8 (over z, x).
Axes of the slice: x: 2, y: 2, z: 4, core: 2. Of those that a mesh axis runs over, the one named last changes fastest.
Arguments:
- coefficients: float32 [4, 1536, 2, 128], P('band', 'tg'), may hold values from -6 to 6
- stick_col: int32 [1536], replicated, may hold values from 0 to 191, as said below
- stick_row: int32 [1536], replicated, may hold values from 0 to 191, as said below
- stick_length: int32 [1536], replicated, may hold values from 1 to 97, as said below
- plane_of_slot: int32 [192], replicated, may hold values from 0 to 191, each once
- potential: float32 [192, 192, 192], P('tg'), may hold values from -8 to 8
Outputs:
- applied: float32 [4, 1536, 2, 128], P('band', 'tg')
- subspace: float32 [2, 4, 4], P(None, 'band')
Inputs may be any that keep to these rules, and one draw needn't show every extreme that they name: With signed values g(v) = v if v <= 48 else v - 192, every stick has g(stick_col)^2 + g(stick_row)^2 <= 48^2; no two sticks share a column and a row; stick 0 lies at column 0, row 0. stick_row is the grid row of each stick; the conditions stated for stick_col hold for the pairs (stick_col, stick_row). stick_length is odd; with h = (stick_length - 1) / 2: h^2 + g(stick_col)^2 + g(stick_row)^2 <= 48^2. `plane_of_slot`: each plane once.
All inputs are finite; a program needn't handle non-finite values.
Results may differ from a plain program's by a relative error of at most 0.00005.
Values sent between devices are 32-bit elements; how exact they have to be, the bound alone decides.
No kernel may reach another device: no remote copies, remote signals or barrier semaphores. Data moves between devices by JAX's collectives and lax.ppermute only.
A program may use at most 128 MiB of HBM per device.

v0:
```python
import math

import jax
import jax.numpy as jnp
from jax import lax
from jax.sharding import PartitionSpec as P

RADIUS = 48


def contract(form, left, right):
    return jnp.einsum(
        form, left, right, precision=lax.Precision.HIGHEST, preferred_element_type=jnp.float32
    )


def rotation(first, second, extent):
    angle = (first[:, None] * second[None, :] % extent).astype(jnp.float32) * (
        2.0 * math.pi / extent
    )
    return (jnp.cos(angle), jnp.sin(angle))


def block_table(cos_table, sin_table, sign):
    upper = jnp.stack([cos_table, sign * sin_table], axis=1)
    lower = jnp.stack([-sign * sin_table, cos_table], axis=1)
    return jnp.stack([upper, lower], axis=0)


def shards(coefficients, stick_col, stick_row, stick_length, plane_of_slot, potential):
    extent = plane_of_slot.shape[0]
    sticks = coefficients.shape[1]
    padded = coefficients.shape[3]
    total_sticks = stick_col.shape[0]
    offset = lax.axis_index("tg") * sticks
    local_col = lax.dynamic_slice_in_dim(stick_col, offset, sticks)
    local_row = lax.dynamic_slice_in_dim(stick_row, offset, sticks)
    local_length = lax.dynamic_slice_in_dim(stick_length, offset, sticks)
    middle = (local_length - 1) // 2
    positions = jnp.arange(padded, dtype=jnp.int32)
    kept_mask = (positions[None, :] < local_length[:, None]).astype(jnp.float32)
    masked = coefficients * kept_mask[None, :, None, :]
    wave_real = masked[:, :, 0, :]
    wave_imag = masked[:, :, 1, :]
    wave_cos, wave_sin = rotation(positions, plane_of_slot, extent)
    shift_cos, shift_sin = rotation(plane_of_slot, middle, extent)
    columns_raw = contract("bsck,ckdz->bzds", masked, block_table(wave_cos, wave_sin, 1.0))
    col_real = columns_raw[:, :, 0, :]
    col_imag = columns_raw[:, :, 1, :]
    along_real = col_real * shift_cos + col_imag * shift_sin
    along_imag = col_imag * shift_cos - col_real * shift_sin
    columns = jnp.stack([along_real, along_imag], axis=2)
    frequency = jnp.arange(extent, dtype=jnp.int32)
    space_index = jnp.arange(extent, dtype=jnp.int32)
    grid_cos, grid_sin = rotation(frequency, space_index, extent)
    table_plus = block_table(grid_cos, grid_sin, 1.0)
    table_minus = block_table(grid_cos, grid_sin, -1.0)
    received = lax.all_to_all(columns, "tg", split_axis=1, concat_axis=3, tiled=True)
    item_count = received.shape[0]
    plane_count = received.shape[1]
    blank_grid = jnp.zeros((item_count, plane_count, 2, extent, extent), jnp.float32)
    spectrum = blank_grid.at[:, :, :, stick_row, stick_col].set(received)
    half = contract("npcyx,cxdr->npdyr", spectrum, table_plus)
    field = contract("npcyr,cydq->npdqr", half, table_plus)
    weighted = potential[None, :, None] * field
    back = contract("npcqr,cydq->npdyr", weighted, table_minus)
    freq = contract("npcyr,cxdr->npdyx", back, table_minus)
    picked = freq[:, :, :, stick_row, stick_col]
    returned = lax.all_to_all(picked, "tg", split_axis=3, concat_axis=1, tiled=True)
    ret_real = returned[:, :, 0, :]
    ret_imag = returned[:, :, 1, :]
    reverted_real = ret_real * shift_cos - ret_imag * shift_sin
    reverted_imag = ret_real * shift_sin + ret_imag * shift_cos
    reverted = jnp.stack([reverted_real, reverted_imag], axis=2)
    volume = 1.0 / (extent * extent * extent)
    local_both = contract("bzcs,ckdz->bsdk", reverted, block_table(wave_cos, wave_sin, -1.0))
    signed_col = jnp.where(local_col <= RADIUS, local_col, local_col - extent)
    signed_row = jnp.where(local_row <= RADIUS, local_row, local_row - extent)
    offsets = positions[None, :] - middle[:, None]
    squares = (signed_col * signed_col + signed_row * signed_row)[:, None] + offsets * offsets
    kinetic = squares.astype(jnp.float32) / (RADIUS * RADIUS)
    applied = kept_mask[None, :, None, :] * (
        kinetic[None, :, None, :] * masked + local_both * volume
    )
    gathered_piece = lax.all_gather(applied, "band", axis=0, tiled=True)
    piece_real = gathered_piece[:, :, 0, :]
    piece_imag = gathered_piece[:, :, 1, :]
    real_sum = contract("isk,jsk->ij", wave_real, piece_real) + contract(
        "isk,jsk->ij", wave_imag, piece_imag
    )
    imag_sum = contract("isk,jsk->ij", wave_real, piece_imag) - contract(
        "isk,jsk->ij", wave_imag, piece_real
    )
    partial_sum = jnp.stack([real_sum, imag_sum], axis=0)
    subspace = lax.psum(partial_sum, "tg") / (total_sticks * padded)
    return (applied, subspace)


def solution(mesh):
    in_specs = (P("band", "tg", None, None), P(), P(), P(), P(), P("tg", None, None))
    out_specs = (P("band", "tg", None, None), P(None, "band", None))
    return jax.shard_map(shards, mesh=mesh, in_specs=in_specs, out_specs=out_specs, check_vma=False)
```

profile of v0, /device:TPU:0, one launch (start us, length us, event | category | flops | bytes accessed | tf_op | source)
XLA Modules:
  0.0 435.6 jit_solution(3929095347770587442)
XLA Ops:
  0.6 1.2 broadcast_multiply_fusion.1
  1.8 0.8 and_select_fusion
  2.7 1.0 copy_multiply_fusion
  5.0 1.6 multiply_add_fusion.1
  6.6 1.1 copy.40
  7.7 7.4 %all-to-all-start = ((f32[1,192,2,192]{3,2,0,1:T(2,128)}), f32[1,192,2,192]{3,2,0,1:T(2,128)S(1)}, u32[]{:S(2)}, u32[]{:S(2)}) async-start(f32[1,192,2,192]{3,2,0,1:T(2,128)} %copy.40), calls=%async_computation | async-start | bytes 786432 | tf_op jit(solution)/shard_map/all_to_all | solution.py:58
  19.1 7.6 %all-to-all-done = f32[1,192,2,192]{3,2,0,1:T(2,128)S(1)} async-done(((f32[1,192,2,192]{3,2,0,1:T(2,128)}), f32[1,192,2,192]{3,2,0,1:T(2,128)S(1)}, u32[]{:S(2)}, u32[]{:S(2)}) %all-to-all-start) | async-done | bytes 294944 | tf_op jit(solution)/shard_map/all_to_all | solution.py:58
  27.5 2.7 copy.41
  30.2 12.4 %broadcast.518 = f32[24,2,36864]{0,1,2:T(2,128)} broadcast(f32[]{:T(128)} %constant.64.clone.1), dimensions={} | broadcast | bytes 7077892
  42.6 140.6 %scatter_fusion = f32[24,2,36864]{0,1,2:T(2,128)} fusion(f32[24,2,36864]{0,1,2:T(2,128)} %broadcast.518, s32[1536]{0:T(1024)S(1)} %broadcast_select_fusion, f32[1536,24,2]{1,2,0:T(2,128)S(1)} %bitcast.188), kind=kCustom, calls=%fused_computation.1 | custom fusion | bytes 890880
  183.2 40.8 %copy.42 = f32[24,2,192,192]{3,2,1,0:T(8,128)} copy(f32[24,2,192,192]{0,1,3,2:T(2,128)} %bitcast.184) | data formatting | bytes 14155776 | tf_op jit(solution)/shard_map/reshape.8
  224.0 18.8 %fusion.7 = f32[2,192,24,192,1]{3,1,4,2,0:T(8,128)S(1)} fusion(f32[24,2,192,192]{3,2,1,0:T(8,128)} %copy.42, f32[1,192,2,192]{1,3,0,2:T(8,128)S(1)} %get-tuple-element.17, f32[1,192,2,192]{1,3,0,2:T(8,128)S(1)} %get-tuple-element.22), kind=kOutput, calls=%fused_computation.10 | convolution fusion | flops 8153874432 | bytes 14745600 | tf_op jit(solution)/shard_map/npcyx,cxdr->npdyr/dot_general | solution.py:12
  242.8 16.3 %fusion = f32[24,2,192,192]{3,2,0,1:T(8,128)S(1)} fusion(f32[24,192,192]{2,1,0:T(8,128)S(1)} %bitcast.186, f32[2,192,24,192,1]{3,1,4,2,0:T(8,128)S(1)} %fusion.7, f32[1,192,2,192]{1,3,0,2:T(8,128)S(1)} %get-tuple-element.17, f32[1,192,2,192]{1,3,0,2:T(8,128)S(1)} %get-tuple-element.22), kind=kOutput, calls=%fused_computation.3 | convolution fusion | flops 8155643904 | bytes 18284544 | tf_op jit(solution)/shard_map/npcyr,cydq->npdqr/dot_general | solution.py:12
  259.1 16.9 %fusion.11 = f32[24,2,192,192]{3,2,0,1:T(8,128)S(1)} fusion(f32[24,2,192,192]{3,2,0,1:T(8,128)S(1)} %fusion, f32[1,192,2,192]{1,3,2,0:T(8,128)S(1)} %get-tuple-element.23, f32[1,192,2,192]{1,3,2,0:T(8,128)S(1)} %get-tuple-element.16), kind=kOutput, calls=%fused_computation.14 | convolution fusion | flops 8153874432 | bytes 14745600 | tf_op jit(solution)/shard_map/npcqr,cydq->npdyr/dot_general | solution.py:12
  276.1 38.9 %fusion.14 = f32[24,2,192,192]{2,3,0,1:T(8,128)} fusion(f32[24,2,192,192]{3,2,0,1:T(8,128)S(1)} %fusion.11, f32[1,192,2,192]{1,3,2,0:T(8,128)S(1)} %get-tuple-element.23, f32[1,192,2,192]{1,3,2,0:T(8,128)S(1)} %get-tuple-element.16), kind=kOutput, calls=%fused_computation.15 | convolution fusion | flops 8153874432 | bytes 14745600 | tf_op jit(solution)/shard_map/npcyr,cxdr->npdyx/dot_general | solution.py:12
  315.0 40.2 %copy.48 = f32[24,2,192,192]{0,1,3,2:T(2,128)} copy(f32[24,2,192,192]{2,3,0,1:T(8,128)} %fusion.14) | data formatting | bytes 14155776 | tf_op jit(solution)/shard_map/npcyr,cxdr->npdyx/transpose | solution.py:12
  355.2 17.1 %gather_fusion = f32[1536,24,2]{1,2,0:T(2,128)S(1)} fusion(f32[24,2,192,192]{0,1,3,2:T(2,128)} %copy.48, s32[1536]{0:T(1024)S(1)} %or_reduce_fusion), kind=kCustom, calls=%fused_computation | custom fusion | bytes 602112 | tf_op jit(solution)/shard_map/gather | solution.py:68
  372.5 3.5 reshape.485
  376.0 3.6 all-to-all-start.1
  379.7 9.3 %all-to-all-done.1 = f32[8,1,9216]{2,1,0:T(1,128)S(1)} async-done(((f32[8,1,9216]{2,1,0:T(1,128)}), f32[8,1,9216]{2,1,0:T(1,128)S(1)}, u32[]{:S(2)}, u32[]{:S(2)}) %all-to-all-start.1) | async-done | bytes 294944 | tf_op jit(solution)/shard_map/all_to_all | solution.py:69
  389.6 1.4 reduce.6
  391.0 2.6 reshape.486
  393.5 1.5 copy.75
  395.1 0.9 multiply_subtract_fusion
  396.0 1.8 fusion.22
  397.8 8.8 %all_gather.3 = f32[4,192,2,128]{3,1,2,0:T(8,128)S(1)} all-gather(f32[1,192,2,128]{3,1,2,0:T(8,128)S(1)} %fusion.22), channel_id=1, replica_groups=mesh['band'=4,'tg'=8] {'band'}, dimensions={0}, use_global_device_ids=true | all-gather | bytes 983040 | tf_op jit(solution)/shard_map/all_gather | solution.py:85
  406.7 1.9 convolution_bitcast_fusion.2
  408.7 1.9 convolution_bitcast_fusion.4
  410.6 1.9 fusion.26
  412.5 2.0 fusion.24
  414.5 0.8 copy.53
  415.4 19.4 %psum.7 = f32[2,1,4]{2,1,0:T(1,128)S(1)} all-reduce(f32[2,1,4]{2,1,0:T(1,128)S(1)} %pad_maximum_fusion.12), channel_id=1, replica_groups=mesh['band'=4,'tg'=8] {'tg'}, use_global_device_ids=true, to_apply=%region_1.2 | all-reduce | flops 8 | bytes 64 | tf_op jit(solution)/shard_map/psum | solution.py:95
  (31 shorter events, 7.5 us)
Async XLA Ops:
  7.7 19.1 %all-to-all-start = ((f32[1,192,2,192]{3,2,0,1:T(2,128)}), f32[1,192,2,192]{3,2,0,1:T(2,128)S(1)}, u32[]{:S(2)}, u32[]{:S(2)}) async-start(f32[1,192,2,192]{3,2,0,1:T(2,128)} %copy.40), calls=%async_computation | async-start | bytes 786432 | tf_op jit(solution)/shard_map/all_to_all | solution.py:58
  26.7 0.8 copy-start
  224.0 18.8 %slice-start = ((s8[4718592]{0:T(1024)(128)(4,1)}), s8[4194304]{0:T(1024)(128)(4,1)S(1)}, s32[]{:S(2)}) async-start(s8[4718592]{0:T(1024)(128)(4,1)} %bitcast.185), calls=%async_computation.2 | async-start | bytes 8388608
  224.0 18.8 %slice-start.1 = ((s8[4718592]{0:T(1024)(128)(4,1)}), s8[524288]{0:T(1024)(128)(4,1)S(1)}, s32[]{:S(2)}) async-start(s8[4718592]{0:T(1024)(128)(4,1)} %bitcast.185), calls=%async_computation.3 | async-start | bytes 1048576
  355.2 39.9 %copy-start.1 = (s32[192]{0:T(256)S(1)}, s32[192]{0:T(256)}, u32[]{:S(2)}) copy-start(s32[192]{0:T(256)} %param.10) | copy-start | bytes 2308
  376.0 13.1 %all-to-all-start.1 = ((f32[8,1,9216]{2,1,0:T(1,128)}), f32[8,1,9216]{2,1,0:T(1,128)S(1)}, u32[]{:S(2)}, u32[]{:S(2)}) async-start(f32[8,1,9216]{2,1,0:T(1,128)} %reshape.485), calls=%async_computation.1 | async-start | bytes 589824 | tf_op jit(solution)/shard_map/all_to_all | solution.py:69
where the time goes:
time: 443 us; the launch traced here: 436 us
  local copies, waits for them, and re-layouts  265 us (60%)
  matrix products  101 us (23%)
  blocking collectives  28.2 us (6%)
  waiting for transfers between devices  17 us (4%)
  other arithmetic  12.3 us (3%)
  starting transfers between devices  11.1 us (3%)
    unnamed x14, local copies, waits for them, and re-layouts  161 us
    dot_general x10, matrix products, contract(): jnp.einsum(form, left, right, precision=lax.Precision.HIGHEST, preferred_...  101 us
    another operation x1, local copies, waits for them, and re-layouts  40.8 us
    transpose x1, local copies, waits for them, and re-layouts, contract(): jnp.einsum(form, left, right, precision=lax.Precision.HIGHEST, preferred_...  40.2 us
    psum x1, blocking collectives, shards(): subspace = lax.psum(partial_sum, 'tg') / (total_sticks * padded)  19.4 us
    gather x1, local copies, waits for them, and re-layouts, shards(): picked = freq[:, :, :, stick_row, stick_col]  17.1 us
    all_to_all x1, waiting for transfers between devices, shards(): lax.all_to_all(picked, 'tg', split_axis=3, concat_axis=1, tiled=True)  9.33 us
  transfers between devices with their start and end apart: 2, of which 2 were waited for; matrix products, arithmetic and copies ran while one was open for 1% of the time, Pallas kernels for 0%

commit v1 on v0

v1 whole, which is shorter than its diff:
```python
import functools
import math

import jax
import jax.numpy as jnp
import ml_dtypes
import numpy as np
from jax import lax
from jax.experimental import pallas as pl
from jax.experimental.pallas import tpu as pltpu
from jax.sharding import PartitionSpec as P

RADIUS = 48
LANES = 128
F32 = jnp.float32
BF16 = jnp.bfloat16
VMEM_LIMIT = 56 * 1024 * 1024


def up8(n):
    return -(-n // 8) * 8


def split(x):
    hi = x.astype(BF16)
    return hi, (x - hi.astype(F32)).astype(BF16)


def dot3(a, b, dims=((1,), (0,))):
    def dot(x, y):
        return lax.dot_general(x, y, (dims, ((), ())), preferred_element_type=F32)

    return dot(a[0], b[0]) + (dot(a[0], b[1]) + dot(a[1], b[0]))


def trig(product, extent):
    n = product - extent * jnp.floor(product * (1.0 / extent) + 0.5)
    quarter = extent / 4.0
    unit = 2.0 * math.pi / extent

    def sine(m):
        u = m * unit
        v = u * u
        s = 1.0 / 6227020800.0
        for term in (-39916800.0, 362880.0, -5040.0, 120.0, -6.0, 1.0):
            s = s * v + 1.0 / term
        return u * s

    folded = jnp.where(
        jnp.abs(n) > quarter, jnp.where(n > 0, 2.0 * quarter, -2.0 * quarter) - n, n
    )
    return sine(quarter - jnp.abs(n)), sine(folded)


def pair(table):
    hi = table.astype(np.float32).astype(ml_dtypes.bfloat16)
    lo = (table - hi.astype(np.float64)).astype(ml_dtypes.bfloat16)
    return hi, lo


@functools.cache
def tables(extent):
    kept = 2 * RADIUS + 1
    rows = up8(kept)
    grid = np.arange(extent)
    freq = np.arange(kept) - RADIUS
    angle = 2.0 * np.pi * ((freq[:, None] * grid[None, :]) % extent) / extent
    cos, sin = np.cos(angle), np.sin(angle)
    pad_q = np.zeros((LANES - kept, extent))
    cq, sq = np.concatenate([cos, pad_q]), np.concatenate([sin, pad_q])
    pad_r = np.zeros((rows - kept, extent))
    cr, sr = np.concatenate([cos, pad_r]), np.concatenate([sin, pad_r])
    x_re = np.concatenate([cq, -sq], axis=0)
    x_im = np.concatenate([sq, cq], axis=0)
    y_fw = np.concatenate(
        [np.concatenate([cr.T, -sr.T], axis=1), np.concatenate([sr.T, cr.T], axis=1)], axis=0
    )
    y_bw = y_fw.T.copy()
    xb_re = x_re.T.copy()
    xb_im = x_im.T.copy()
    out = []
    for table in (x_re, x_im, y_fw, y_bw, xb_re, xb_im):
        out.extend(pair(table))
    return tuple(out)


def params():
    return pltpu.CompilerParams(vmem_limit_bytes=VMEM_LIMIT)


def wave_kernel(extent, planes, aux_ref, plane_ref, coef_ref, out_ref, kc_ref, whi_ref, wlo_ref, sc_ref, ss_ref):
    devices = out_ref.shape[0]
    sticks, _, padded = coef_ref.shape
    padded_planes = plane_ref.shape[1] // devices
    aux = aux_ref[...]
    aux_col = jnp.transpose(jnp.concatenate([aux] * (LANES // 8), axis=0))
    length = aux_col[:sticks, 0:1]
    square = aux_col[:sticks, 1:2]
    middle = (length - 1.0) * 0.5
    position = lax.broadcasted_iota(jnp.int32, (sticks, padded), 1).astype(F32)
    kept = (position < length).astype(F32)
    kinetic = (square + (position - middle) * (position - middle)) * (1.0 / (RADIUS * RADIUS))
    wave = jnp.concatenate([coef_ref[:, 0, :] * kept, coef_ref[:, 1, :] * kept], axis=1)
    kc_ref[...] = wave * jnp.concatenate([kinetic, kinetic], axis=1)

    total = plane_ref.shape[1]
    plane_row = jnp.broadcast_to(plane_ref[...], (LANES, total))
    plane_col = jnp.transpose(plane_row)[:, 0:1]
    slot = lax.broadcasted_iota(jnp.int32, (total, 1), 0)
    real = (plane_col >= 0.0).astype(F32)
    harmonic = lax.broadcasted_iota(jnp.int32, (total, padded), 1).astype(F32)
    cos, sin = trig(jnp.maximum(plane_col, 0.0) * harmonic, extent)
    cos, sin = cos * real, sin * real
    parts = []
    for d in range(devices):
        c = cos[d * padded_planes:(d + 1) * padded_planes]
        s = sin[d * padded_planes:(d + 1) * padded_planes]
        parts.append(jnp.concatenate([c, -s], axis=1))
        parts.append(jnp.concatenate([s, c], axis=1))
    table = split(jnp.concatenate(parts, axis=0))
    whi_ref[...] = table[0]
    wlo_ref[...] = table[1]
    middle_row = (aux[0:1, :sticks] - 1.0) * 0.5
    shift_cos, shift_sin = trig(jnp.maximum(plane_col, 0.0) * middle_row, extent)
    sc_ref[...] = shift_cos
    ss_ref[...] = shift_sin
    raw = dot3(table, split(wave), ((1,), (1,)))
    for d in range(devices):
        at = 2 * d * padded_planes
        re, im = raw[at:at + padded_planes], raw[at + padded_planes:at + 2 * padded_planes]
        c = shift_cos[d * padded_planes:(d + 1) * padded_planes]
        s = shift_sin[d * padded_planes:(d + 1) * padded_planes]
        along_re = re * c + im * s
        along_im = im * c - re * s
        out_ref[d, 0:padded_planes, :] = along_re[:, :LANES]
        out_ref[d, padded_planes:2 * padded_planes, :] = along_im[:, :LANES]
        out_ref[d, 2 * padded_planes:3 * padded_planes, :] = jnp.concatenate(
            [along_re[:, LANES:], along_im[:, LANES:]], axis=1
        )


def map_kernel(row_ref, col_ref, map_ref):
    rows = map_ref.shape[0]
    total = row_ref.shape[1]
    r = lax.broadcasted_iota(jnp.int32, (rows, total), 0)
    q = lax.broadcasted_iota(jnp.int32, (LANES, total), 0)
    place = lax.broadcasted_iota(jnp.int32, (LANES, total), 1) + 1
    in_row = (r == row_ref[...]).astype(F32).astype(BF16)
    in_col = q == col_ref[...]
    upper = jnp.where(in_col, place >> 6, 0).astype(F32).astype(BF16)
    lower = jnp.where(in_col, place & 63, 0).astype(F32).astype(BF16)

    def dot(x, y):
        return lax.dot_general(x, y, (((1,), (1,)), ((), ())), preferred_element_type=F32)

    found = dot(in_row, upper) * 64.0 + dot(in_row, lower)
    map_ref[...] = found.astype(jnp.int32) - 1


def lane_take(x, index):
    return jnp.take_along_axis(x, index, axis=1, mode="promise_in_bounds")


def plane_kernel(
    planes, map_ref, row_ref, col_ref, recv_ref,
    xr_hi, xr_lo, xi_hi, xi_lo, y_hi, y_lo, yb_hi, yb_lo, br_hi, br_lo, bi_hi, bi_lo,
    pot_hbm, out_ref, x_ref, gr_ref, gi_ref, pot_ref, sem,
):
    devices = recv_ref.shape[0]
    padded_planes = recv_ref.shape[1] // 3
    windows = x_ref.shape[0]
    rows = map_ref.shape[0]
    extent = pot_ref.shape[1]
    half = LANES // 2
    fetch = pltpu.make_async_copy(pot_hbm, pot_ref, sem)
    fetch.start()

    low = lax.broadcasted_iota(jnp.int32, (padded_planes, LANES), 1) < half
    for d in range(devices):
        x_ref[d] = recv_ref[d, 0:2 * padded_planes, :]
    for e in range(devices // 2):
        first = recv_ref[2 * e, 2 * padded_planes:3 * padded_planes, :]
        second = recv_ref[2 * e + 1, 2 * padded_planes:3 * padded_planes, :]
        x_ref[devices + e, 0:padded_planes, :] = jnp.where(low, first, pltpu.roll(second, half, 1))
        x_ref[devices + e, padded_planes:2 * padded_planes, :] = jnp.where(
            low, pltpu.roll(first, half, 1), second
        )

    blocks = padded_planes // 8
    grids = (gr_ref, gi_ref)

    @pl.loop(0, rows)
    def _(r):
        code = jnp.broadcast_to(map_ref[pl.ds(r, 1), :], (8, LANES))
        index = code & (LANES - 1)
        window = code >> 7
        for j in range(2 * blocks):
            value = jnp.zeros((8, LANES), F32)
            for w in range(windows):
                value = jnp.where(window == w, lane_take(x_ref[w, 8 * j:8 * j + 8, :], index), value)
            part, at = j // blocks, 8 * (j % blocks)
            grids[part][pl.ds(r + at * rows, 8, stride=rows), :] = value

    fetch.wait()
    table_xr = (xr_hi[...], xr_lo[...])
    table_xi = (xi_hi[...], xi_lo[...])
    table_y = (y_hi[...], y_lo[...])
    table_yb = (yb_hi[...], yb_lo[...])
    table_br = (br_hi[...], br_lo[...])
    table_bi = (bi_hi[...], bi_lo[...])

    @pl.loop(0, planes // 2)
    def _(step):
        base = pl.multiple_of(step * 2 * rows, 8)
        pick = pl.ds(base, 2 * rows)
        spectrum = split(jnp.concatenate([gr_ref[pick, :], gi_ref[pick, :]], axis=1))
        a_re = dot3(spectrum, table_xr)
        a_im = dot3(spectrum, table_xi)
        back_re, back_im = [], []
        for t in range(2):
            mid = jnp.concatenate(
                [a_re[t * rows:(t + 1) * rows], a_im[t * rows:(t + 1) * rows]], axis=0
            )
            field = dot3(table_y, split(mid))
            v = pot_ref[2 * step + t]
            weighted = jnp.concatenate([field[:extent] * v, field[extent:] * v], axis=0)
            back = dot3(table_yb, split(weighted))
            back_re.append(back[:rows])
            back_im.append(back[rows:])
        b_re = split(jnp.concatenate(back_re, axis=0))
        b_im = split(jnp.concatenate(back_im, axis=0))
        back = dot3(b_re, table_br) + dot3(b_im, table_bi)
        gr_ref[pick, :] = back[:, :LANES]
        gi_ref[pick, :] = back[:, LANES:]

    for w in range(windows):
        index = jnp.broadcast_to(col_ref[w:w + 1, :], (8, LANES))
        which = jnp.broadcast_to(row_ref[w:w + 1, :], (8, LANES))

        def body(r, acc):
            hit = which == r
            new = []
            for j in range(2 * blocks):
                part, at = j // blocks, 8 * (j % blocks)
                value = grids[part][pl.ds(r + at * rows, 8, stride=rows), :]
                new.append(jnp.where(hit, lane_take(value, index), acc[j]))
            return tuple(new)

        acc = lax.fori_loop(
            0, 2 * RADIUS + 1, body, tuple(jnp.zeros((8, LANES), F32) for _ in range(2 * blocks))
        )
        full = jnp.concatenate(acc, axis=0)
        if w < devices:
            out_ref[w, 0:2 * padded_planes, :] = full
        else:
            e = w - devices
            re, im = full[:padded_planes], full[padded_planes:]
            out_ref[2 * e, 2 * padded_planes:3 * padded_planes, :] = jnp.where(
                low, re, pltpu.roll(im, half, 1)
            )
            out_ref[2 * e + 1, 2 * padded_planes:3 * padded_planes, :] = jnp.where(
                low, pltpu.roll(re, half, 1), im
            )
    for d in range(devices):
        out_ref[d, 3 * padded_planes:, :] = jnp.zeros((8, LANES), F32)


def inner_kernel(bands, volume, norm, band_ref, *refs):
    kc_ref = refs[0]
    coefs = refs[1:1 + bands]
    fields = refs[1 + bands:1 + 2 * bands]
    in_ref = refs[1 + 2 * bands]
    out_ref = refs[2 + 2 * bands]
    devices = in_ref.shape[0]
    padded_planes = (in_ref.shape[1] - 8) // 3
    half = LANES // 2
    padded = coefs[0].shape[2]
    me = band_ref[0]
    low = lax.broadcasted_iota(jnp.int32, (padded_planes, LANES), 1) < half

    def fold(x):
        rows = x.shape[0]
        total = x[0:8]
        for at in range(8, rows, 8):
            total = total + x[at:at + 8]
        return total

    kc = kc_ref[...]
    kc_re, kc_im = kc[:, :padded], kc[:, padded:]
    sums = []
    for m in range(bands):
        c_re, c_im = coefs[m][:, 0, :], coefs[m][:, 1, :]
        sums.append([fold(c_re * kc_re + c_im * kc_im), fold(c_re * kc_im - c_im * kc_re)])
    local = [[jnp.zeros((8, LANES), F32), jnp.zeros((8, LANES), F32)] for _ in range(bands)]
    for d in range(devices):
        value = in_ref[d, 0:3 * padded_planes, :]
        re, im, rest = value[:padded_planes], value[padded_planes:2 * padded_planes], value[2 * padded_planes:]
        turned = pltpu.roll(rest, half, 1)
        other = jnp.concatenate([im, -re, jnp.where(low, turned, -turned)], axis=0)
        for m in range(bands):
            col = fields[m][d, 0:3 * padded_planes, :]
            local[m][0] = local[m][0] + fold(col * value)
            local[m][1] = local[m][1] + fold(col * other)
    lane = lax.broadcasted_iota(jnp.int32, (8, LANES), 1)
    row = lax.broadcasted_iota(jnp.int32, (8, LANES), 0)
    tile = jnp.zeros((8, LANES), F32)
    for m in range(bands):
        at = lax.rem(me + m, bands)
        for part, sign in ((0, 1.0), (1, -1.0)):
            partial = sums[m][part] + volume * local[m][part]
            scalar = jnp.sum(jnp.sum(partial, axis=1, keepdims=True), axis=0, keepdims=True)
            tile = jnp.where((lane == at) & (row == part), sign * norm * scalar, tile)
    for d in range(devices):
        out_ref[d, 0:3 * padded_planes, :] = in_ref[d, 0:3 * padded_planes, :]
        out_ref[d, 3 * padded_planes:, :] = tile


def final_kernel(volume, aux_ref, ret_ref, kc_ref, whi_ref, wlo_ref, sc_ref, ss_ref, out_ref, sub_ref):
    devices = ret_ref.shape[0]
    padded_planes = (ret_ref.shape[1] - 8) // 3
    sticks, _, padded = out_ref.shape
    half = LANES // 2
    bands = sub_ref.shape[2]
    total = jnp.zeros((8, LANES), F32)
    parts = []
    for d in range(devices):
        value = ret_ref[d]
        total = total + value[3 * padded_planes:]
        rest = value[2 * padded_planes:3 * padded_planes]
        re = jnp.concatenate([value[:padded_planes], rest[:, :half]], axis=1)
        im = jnp.concatenate([value[padded_planes:2 * padded_planes], rest[:, half:]], axis=1)
        c = sc_ref[d * padded_planes:(d + 1) * padded_planes, :]
        s = ss_ref[d * padded_planes:(d + 1) * padded_planes, :]
        parts.append(re * c - im * s)
        parts.append(re * s + im * c)
    stacked = jnp.concatenate(parts, axis=0)
    spare = jnp.zeros((stacked.shape[0], 2 * LANES - sticks), F32)
    turned = jnp.transpose(jnp.concatenate([stacked, spare], axis=1))[:sticks]
    local = dot3(split(turned), (whi_ref[...], wlo_ref[...])) * volume
    aux_col = jnp.transpose(jnp.concatenate([aux_ref[...]] * (LANES // 8), axis=0))
    length = aux_col[:sticks, 0:1]
    position = lax.broadcasted_iota(jnp.int32, (sticks, padded), 1).astype(F32)
    kept = position < length
    kc = kc_ref[...]
    out_ref[:, 0, :] = jnp.where(kept, kc[:, :padded] + local[:, :padded], 0.0)
    out_ref[:, 1, :] = jnp.where(kept, kc[:, padded:] + local[:, padded:], 0.0)
    sub_ref[:, 0, :] = total[0:2, :bands]


def window_order(values, devices):
    blocks = values.reshape(devices, -1)
    return jnp.concatenate(
        [blocks[:, :LANES].reshape(-1, LANES), blocks[:, LANES:].reshape(-1, LANES)], axis=0
    )


def shards(bands, devices, coefficients, stick_col, stick_row, stick_length, plane_of_slot, potential):
    extent = plane_of_slot.shape[0]
    sticks = coefficients.shape[1]
    padded = coefficients.shape[3]
    total_sticks = stick_col.shape[0]
    planes = potential.shape[0]
    padded_planes = up8(planes)
    if sticks != LANES + LANES // 2 or devices % 2 or planes % 2:
        raise ValueError("sizes")
    kept = 2 * RADIUS + 1
    rows = up8(kept)
    volume = 1.0 / (extent * extent * extent)
    me = lax.axis_index("tg")
    coef = coefficients.reshape(sticks, 2, padded)

    signed_col = jnp.where(stick_col <= RADIUS, stick_col, stick_col - extent)
    signed_row = jnp.where(stick_row <= RADIUS, stick_row, stick_row - extent)
    info = jnp.stack([stick_length, signed_col * signed_col + signed_row * signed_row])
    info = lax.dynamic_slice_in_dim(info, me * sticks, sticks, axis=1).astype(F32)
    aux = jnp.pad(info, ((0, 6), (0, 2 * LANES - sticks)), constant_values=1.0)
    slots = jnp.pad(
        plane_of_slot.astype(F32).reshape(devices, planes),
        ((0, 0), (0, padded_planes - planes)),
        constant_values=-1.0,
    ).reshape(1, devices * padded_planes)

    block = 3 * padded_planes
    total_planes = devices * padded_planes
    sent, kc, whi, wlo, shift_cos, shift_sin = pl.pallas_call(
        functools.partial(wave_kernel, extent, planes),
        out_shape=(
            jax.ShapeDtypeStruct((devices, block, LANES), F32),
            jax.ShapeDtypeStruct((sticks, 2 * padded), F32),
            jax.ShapeDtypeStruct((2 * total_planes, 2 * padded), BF16),
            jax.ShapeDtypeStruct((2 * total_planes, 2 * padded), BF16),
            jax.ShapeDtypeStruct((total_planes, sticks), F32),
            jax.ShapeDtypeStruct((total_planes, sticks), F32),
        ),
        compiler_params=params(),
        name="wave_to_planes",
    )(aux, slots, coef)

    received = lax.all_to_all(sent, "tg", split_axis=0, concat_axis=0, tiled=True)

    row_w = window_order(signed_row + RADIUS, devices)
    col_w = window_order(signed_col + RADIUS, devices)
    windows = row_w.shape[0]
    stick_map = pl.pallas_call(
        map_kernel,
        out_shape=jax.ShapeDtypeStruct((rows, LANES), jnp.int32),
        compiler_params=params(),
        name="stick_map",
    )(row_w.reshape(1, -1), col_w.reshape(1, -1))

    vmem = pl.BlockSpec(memory_space=pltpu.VMEM)
    weighted = pl.pallas_call(
        functools.partial(plane_kernel, planes),
        out_shape=jax.ShapeDtypeStruct((devices, block + 8, LANES), F32),
        in_specs=[vmem] * 16 + [pl.BlockSpec(memory_space=pl.ANY)],
        out_specs=vmem,
        scratch_shapes=[
            pltpu.VMEM((windows, 2 * padded_planes, LANES), F32),
            pltpu.VMEM((padded_planes * rows, LANES), F32),
            pltpu.VMEM((padded_planes * rows, LANES), F32),
            pltpu.VMEM(potential.shape, F32),
            pltpu.SemaphoreType.DMA,
        ],
        compiler_params=params(),
        name="planes",
    )(stick_map, row_w, col_w, received, *[jnp.asarray(t) for t in tables(extent)], potential)

    coefs, fields = [coef], [received]
    for shift in range(1, bands):
        ring = [((b + shift) % bands, b) for b in range(bands)]
        coefs.append(lax.ppermute(coef, "band", ring))
        fields.append(lax.ppermute(received, "band", ring))
    band = lax.axis_index("band").astype(jnp.int32).reshape(1)
    norm = 1.0 / (total_sticks * padded)
    outgoing = pl.pallas_call(
        functools.partial(inner_kernel, bands, volume, norm),
        out_shape=jax.ShapeDtypeStruct((devices, block + 8, LANES), F32),
        in_specs=[pl.BlockSpec(memory_space=pltpu.SMEM)] + [vmem] * (2 + 2 * bands),
        out_specs=vmem,
        compiler_params=params(),
        name="inner",
    )(band, kc, *coefs, *fields, weighted)

    returned = lax.all_to_all(outgoing, "tg", split_axis=0, concat_axis=0, tiled=True)
    applied, subspace = pl.pallas_call(
        functools.partial(final_kernel, volume),
        out_shape=(
            jax.ShapeDtypeStruct((sticks, 2, padded), F32),
            jax.ShapeDtypeStruct((2, 1, bands), F32),
        ),
        compiler_params=params(),
        name="planes_to_wave",
    )(aux, returned, kc, whi, wlo, shift_cos, shift_sin)
    return applied.reshape(1, sticks, 2, padded), subspace


def solution(mesh):
    in_specs = (P("band", "tg", None, None), P(), P(), P(), P(), P("tg", None, None))
    out_specs = (P("band", "tg", None, None), P(None, "band", None))
    body = functools.partial(shards, mesh.shape["band"], mesh.shape["tg"])
    return jax.shard_map(body, mesh=mesh, in_specs=in_specs, out_specs=out_specs, check_vma=False)
```

time: 443 us -> 179 us (0.40); the launches traced: 436 us -> 179 us
  local copies, waits for them, and re-layouts: 265 us -> 3.2 us
  Pallas kernels: 0 us -> 139 us
  matrix products: 101 us -> 0 us
  blocking collectives: 28.2 us -> 14.5 us
  waiting for transfers between devices: 17 us -> 5.13 us
  other arithmetic: 12.3 us -> 3.25 us
    unnamed x14, local copies, waits for them, and re-layouts: 161 us -> 0.98 us
    pallas_call x0 -> x5, Pallas kernels: none -> 139 us  [the longest x1 128 us: shards(): pl.pallas_call(functools.partial(plane_kernel, planes), out_shape=jax.Sha...]
    dot_general x10 -> x0, matrix products: 101 us -> none  [contract(): jnp.einsum(form, left, right, precision=lax.Precision.HIGHEST, preferred_...]
    another operation x2, local copies, waits for them, and re-layouts: 41.9 us -> 0.71 us  [shards(): jnp.stack([stick_length, signed_col * signed_col + signed_row * signed_row])]
    transpose x1 -> x0, local copies, waits for them, and re-layouts: 40.2 us -> none  [contract(): jnp.einsum(form, left, right, precision=lax.Precision.HIGHEST, preferred_...]
    psum x1 -> x0, blocking collectives: 19.4 us -> none  [shards(): subspace = lax.psum(partial_sum, 'tg') / (total_sticks * padded)]
    gather x1 -> x0, local copies, waits for them, and re-layouts: 17.1 us -> none  [shards(): picked = freq[:, :, :, stick_row, stick_col]]
    all_to_all x0 -> x1, blocking collectives: none -> 14.5 us  [shards(): lax.all_to_all(outgoing, 'tg', split_axis=0, concat_axis=0, tiled=True)]
  transfers between devices with their start and end apart: 2 -> 7, of which waited for: 2 -> 1; matrix products, arithmetic and copies ran while one was open for 1% -> 1% of each run, Pallas kernels for 0% -> 73%
where the time goes in v1:
time: 179 us
  Pallas kernels  139 us (78%)
  blocking collectives  14.5 us (8%)
  starting transfers between devices  13.2 us (7%)
  waiting for transfers between devices  5.13 us (3%)
  other arithmetic  3.25 us (2%)
  local copies, waits for them, and re-layouts  3.2 us (2%)
    pallas_call x1, Pallas kernels, shards(): pl.pallas_call(functools.partial(plane_kernel, planes), out_shape=jax.Sha...  128 us
    all_to_all x1, blocking collectives, shards(): lax.all_to_all(outgoing, 'tg', split_axis=0, concat_axis=0, tiled=True)  14.5 us
    all_to_all x1, starting transfers between devices, shards(): lax.all_to_all(sent, 'tg', split_axis=0, concat_axis=0, tiled=True)  7.25 us
    all_to_all x1, waiting for transfers between devices, shards(): lax.all_to_all(sent, 'tg', split_axis=0, concat_axis=0, tiled=True)  5.11 us
  transfers between devices with their start and end apart: 7, of which 1 were waited for; matrix products, arithmetic and copies ran while one was open for 1% of the time, Pallas kernels for 73%

profile of v1, /device:TPU:0, one launch (start us, length us, event | category | flops | bytes accessed | tf_op | source)
XLA Modules:
  0.0 178.7 jit_solution(9372840581711297133)
XLA Ops:
  0.6 1.2 convert_element_type.7
  1.9 0.7 stack.9
  2.6 0.7 fusion
  3.3 0.1 fusion.3
  3.4 0.6 pad.4.aux_ref
  4.0 2.7 %wave_to_planes.1 = (f32[8,72,128]{2,1,0:T(8,128)}, f32[192,256]{1,0:T(8,128)}, bf16[384,256]{1,0:T(8,128)(2,1)}, bf16[384,256]{1,0:T(8,128)(2,1)}, f32[192,192]{1,0:T(8,128)}, /*index=5*/f32[192,192]{1,0:T(8,128)}) custom-call(f32[8,256]{1,0:T(8,128)} %pad.4.aux_ref, f32[1,192]{1,0:T(1,128)} %bitcast.19, f32[192,2,128]{2,1,0:T(2,128)} %bitcast.14), custom_call_target="tpu_custom_call" | custom-call | tf_op jit(solution)/shard_map/wave_to_planes/pallas_call | solution.py:385
  6.7 7.3 %all-to-all-start = ((f32[8,72,128]{2,1,0:T(8,128)}), f32[8,72,128]{2,1,0:T(8,128)S(1)}, u32[]{:S(2)}, u32[]{:S(2)}) async-start(f32[8,72,128]{2,1,0:T(8,128)} %get-tuple-element.11), calls=%async_computation | async-start | bytes 589824 | tf_op jit(solution)/shard_map/all_to_all | solution.py:399
  14.0 0.0 collective-permute-start.2
  14.0 1.6 collective-permute-start.1
  15.6 1.4 collective-permute-start
  17.0 0.1 reshape.42
  17.0 0.1 reshape.39
  17.1 0.1 reshape.43
  17.2 0.1 reshape.40
  17.3 0.6 pad_add_fusion
  17.9 0.6 pad_add_fusion.1
  18.5 5.1 %all-to-all-done.recv_ref.refs_5_ = f32[8,72,128]{2,1,0:T(8,128)S(1)} async-done(((f32[8,72,128]{2,1,0:T(8,128)}), f32[8,72,128]{2,1,0:T(8,128)S(1)}, u32[]{:S(2)}, u32[]{:S(2)}) %all-to-all-start) | async-done | bytes 294944 | tf_op jit(solution)/shard_map/all_to_all | solution.py:399
  23.6 0.0 collective-permute-start.5
  23.6 1.6 collective-permute-start.4
  25.1 1.4 collective-permute-start.3
  26.6 0.6 copy_bitcast_fusion
  27.2 1.7 stick_map.1.map_ref
  28.9 128.4 %planes.1.refs_9_ = f32[8,80,128]{2,1,0:T(8,128)} custom-call(s32[104,128]{1,0:T(8,128)} %stick_map.1.map_ref, s32[12,128]{1,0:T(8,128)} %get-tuple-element.23.row_ref, s32[12,128]{1,0:T(8,128)} %get-tuple-element.21.col_ref, f32[8,72,128]{2,1,0:T(8,128)} %copy-done, bf16[256,192]{1,0:T(8,128)(2,1)} %constant.47.clone.xr_hi, ...), custom_call_target="tpu_custom_call" | custom-call | tf_op jit(solution)/shard_map/planes/pallas_call | solution.py:412
  157.3 0.0 copy-start.6
  157.4 0.6 copy-done.5
  158.0 0.1 copy-done.6
  158.0 0.1 copy-done.1
  158.1 0.1 copy-done.2
  158.2 0.1 copy-done.3
  158.3 3.3 %inner.1 = f32[8,80,128]{2,1,0:T(8,128)} custom-call(s32[1]{0:T(128)} %bitcast.band_ref, f32[192,256]{1,0:T(8,128)} %get-tuple-element.10.refs_0_.kc_ref, f32[192,2,128]{2,1,0:T(2,128)} %bitcast.18, f32[192,2,128]{2,1,0:T(2,128)} %copy-done.6, f32[192,2,128]{2,1,0:T(2,128)} %copy-done.5, f32[192,2,128]{2,1,0:T(2,128)} %copy-done.4, f32[8,72,128]{2,1,0:T(8,128)} %copy-done, ...), custom_call_target="tpu_custom_call" | custom-call | tf_op jit(solution)/shard_map/inner/pallas_call | solution.py:435
  161.6 14.5 %all_to_all.10.ret_ref = f32[8,80,128]{2,1,0:T(8,128)} all-to-all(f32[8,80,128]{2,1,0:T(8,128)} %inner.1), channel_id=1, replica_groups=mesh['band'=4,'tg'=8] {'tg'}, dimensions={0} | all-to-all | bytes 655360 | tf_op jit(solution)/shard_map/all_to_all | solution.py:444
  176.1 2.5 %planes_to_wave.1 = (f32[192,2,128]{2,1,0:T(2,128)}, f32[2,1,4]{2,1,0:T(1,128)}) custom-call(f32[8,256]{1,0:T(8,128)} %pad.4.aux_ref, f32[8,80,128]{2,1,0:T(8,128)} %all_to_all.10.ret_ref, f32[192,256]{1,0:T(8,128)} %get-tuple-element.10.refs_0_.kc_ref, bf16[384,256]{1,0:T(8,128)(2,1)} %get-tuple-element.12.whi_ref, ...), custom_call_target="tpu_custom_call" | custom-call | tf_op jit(solution)/shard_map/planes_to_wave/pallas_call | solution.py:445
  (19 shorter events, 0.1 us)
Async XLA Ops:
  6.7 16.9 %all-to-all-start = ((f32[8,72,128]{2,1,0:T(8,128)}), f32[8,72,128]{2,1,0:T(8,128)S(1)}, u32[]{:S(2)}, u32[]{:S(2)}) async-start(f32[8,72,128]{2,1,0:T(8,128)} %get-tuple-element.11), calls=%async_computation | async-start | bytes 589824 | tf_op jit(solution)/shard_map/all_to_all | solution.py:399
  14.0 11.2 %collective-permute-start.2 = (f32[192,2,128]{2,1,0:T(2,128)}, f32[192,2,128]{2,1,0:T(2,128)S(1)}, u32[]{:S(2)}, u32[]{:S(2)}) collective-permute-start(f32[192,2,128]{2,1,0:T(2,128)} %bitcast.15), channel_id=1, source_target_pairs={{24,0},{0,8},{8,16},{16,24},{25,1},{1,9},{9,17},{17,25},{26,2},{2,... | collective-permute-start | bytes 589832 | tf_op jit(solution)/shard_map/ppermute | solution.py:431
  14.0 143.3 %collective-permute-start.1 = (f32[192,2,128]{2,1,0:T(2,128)}, f32[192,2,128]{2,1,0:T(2,128)S(1)}, u32[]{:S(2)}, u32[]{:S(2)}) collective-permute-start(f32[192,2,128]{2,1,0:T(2,128)} %bitcast.16), channel_id=1, source_target_pairs={{16,0},{24,8},{0,16},{8,24},{17,1},{25,9},{1,17},{9,25},{18,2},{26... | collective-permute-start | bytes 589832 | tf_op jit(solution)/shard_map/ppermute | solution.py:431
  15.6 141.7 %collective-permute-start = (f32[192,2,128]{2,1,0:T(2,128)}, f32[192,2,128]{2,1,0:T(2,128)S(1)}, u32[]{:S(2)}, u32[]{:S(2)}) collective-permute-start(f32[192,2,128]{2,1,0:T(2,128)} %bitcast.17), channel_id=1, source_target_pairs={{8,0},{16,8},{24,16},{0,24},{9,1},{17,9},{25,17},{1,25},{10,2},{18... | collective-permute-start | bytes 589832 | tf_op jit(solution)/shard_map/ppermute | solution.py:431
  23.6 5.3 %copy-start = (f32[8,72,128]{2,1,0:T(8,128)}, f32[8,72,128]{2,1,0:T(8,128)S(1)}, u32[]{:S(2)}) copy-start(f32[8,72,128]{2,1,0:T(8,128)S(1)} %all-to-all-done.recv_ref.refs_5_) | copy-start | bytes 884740
  23.6 133.7 %collective-permute-start.5 = (f32[8,72,128]{2,1,0:T(8,128)S(1)}, f32[8,72,128]{2,1,0:T(8,128)S(1)}, u32[]{:S(2)}, u32[]{:S(2)}) collective-permute-start(f32[8,72,128]{2,1,0:T(8,128)S(1)} %all-to-all-done.recv_ref.refs_5_), channel_id=1, source_target_pairs={{24,0},{0,8},{8,16},{16,24},{25,1},{1,9},{9,17},{17,25},{26,2},{2,... | collective-permute-start | bytes 884744 | tf_op jit(solution)/shard_map/ppermute | solution.py:432
  23.6 133.7 %collective-permute-start.4 = (f32[8,72,128]{2,1,0:T(8,128)S(1)}, f32[8,72,128]{2,1,0:T(8,128)S(1)}, u32[]{:S(2)}, u32[]{:S(2)}) collective-permute-start(f32[8,72,128]{2,1,0:T(8,128)S(1)} %all-to-all-done.recv_ref.refs_5_), channel_id=1, source_target_pairs={{16,0},{24,8},{0,16},{8,24},{17,1},{25,9},{1,17},{9,25},{18,2},{26... | collective-permute-start | bytes 884744 | tf_op jit(solution)/shard_map/ppermute | solution.py:432
  25.1 132.2 %copy-start.4 = (f32[192,2,128]{2,1,0:T(2,128)}, f32[192,2,128]{2,1,0:T(2,128)S(1)}, u32[]{:S(2)}) copy-start(f32[192,2,128]{2,1,0:T(2,128)S(1)} %collective-permute-done.2.refs_4_) | copy-start | bytes 589828
  25.1 132.2 %collective-permute-start.3 = (f32[8,72,128]{2,1,0:T(8,128)S(1)}, f32[8,72,128]{2,1,0:T(8,128)S(1)}, u32[]{:S(2)}, u32[]{:S(2)}) collective-permute-start(f32[8,72,128]{2,1,0:T(8,128)S(1)} %all-to-all-done.recv_ref.refs_5_), channel_id=1, source_target_pairs={{8,0},{16,8},{24,16},{0,24},{9,1},{17,9},{25,17},{1,25},{10,2},{18... | collective-permute-start | bytes 884744 | tf_op jit(solution)/shard_map/ppermute | solution.py:432
  157.3 0.7 copy-start.5
  157.3 0.7 copy-start.6
  157.3 0.8 copy-start.1
  157.3 0.9 copy-start.2
  157.3 1.0 copy-start.3

commit v2 on v1

--- a/solution.py
+++ b/solution.py
@@ -189,7 +189,7 @@
     blocks = padded_planes // 8
     grids = (gr_ref, gi_ref)
 
-    @pl.loop(0, rows)
+    @pl.loop(0, rows, unroll=4)
     def _(r):
         code = jnp.broadcast_to(map_ref[pl.ds(r, 1), :], (8, LANES))
         index = code & (LANES - 1)
@@ -247,7 +247,7 @@
             return tuple(new)
 
         acc = lax.fori_loop(
-            0, 2 * RADIUS + 1, body, tuple(jnp.zeros((8, LANES), F32) for _ in range(2 * blocks))
+            0, rows, body, tuple(jnp.zeros((8, LANES), F32) for _ in range(2 * blocks)), unroll=8
         )
         full = jnp.concatenate(acc, axis=0)
         if w < devices:

time: 179 us -> 104 us (0.58)
  Pallas kernels: 139 us -> 63 us
    pallas_call x1, Pallas kernels: 128 us -> 52.8 us  [shards(): pl.pallas_call(functools.partial(plane_kernel, planes), out_shape=jax.Sha...]
  transfers between devices with their start and end apart: 7 -> 7, of which waited for: 1 -> 1; matrix products, arithmetic and copies ran while one was open for 1% -> 2% of each run, Pallas kernels for 73% -> 53%
where the time goes in v2:
time: 104 us; the launch traced here: 103 us
  Pallas kernels  63 us (61%)
  blocking collectives  14.5 us (14%)
  starting transfers between devices  13.2 us (13%)
  waiting for transfers between devices  5.13 us (5%)
  other arithmetic  3.25 us (3%)
  local copies, waits for them, and re-layouts  3.2 us (3%)
    pallas_call x1, Pallas kernels, shards(): pl.pallas_call(functools.partial(plane_kernel, planes), out_shape=jax.Sha...  52.8 us
    all_to_all x1, blocking collectives, shards(): lax.all_to_all(outgoing, 'tg', split_axis=0, concat_axis=0, tiled=True)  14.5 us
    all_to_all x1, starting transfers between devices, shards(): lax.all_to_all(sent, 'tg', split_axis=0, concat_axis=0, tiled=True)  7.25 us
    all_to_all x1, waiting for transfers between devices, shards(): lax.all_to_all(sent, 'tg', split_axis=0, concat_axis=0, tiled=True)  5.11 us
    pallas_call x1, Pallas kernels, shards(): pl.pallas_call(functools.partial(inner_kernel, bands, volume, norm), out_...  3.27 us
    ppermute x3, starting transfers between devices, shards(): fields.append(lax.ppermute(received, 'band', ring))  2.99 us
    ppermute x3, starting transfers between devices, shards(): coefs.append(lax.ppermute(coef, 'band', ring))  2.98 us
    pallas_call x1, Pallas kernels, shards(): pl.pallas_call(functools.partial(wave_kernel, extent, planes), out_shape=...  2.71 us
  transfers between devices with their start and end apart: 7, of which 1 were waited for; matrix products, arithmetic and copies ran while one was open for 2% of the time, Pallas kernels for 53%

profile of v2, /device:TPU:0, one launch (start us, length us, event | category | flops | bytes accessed | tf_op | source)
XLA Modules:
  0.0 103.1 jit_solution(14496481600126132755)
XLA Ops:
  0.6 1.2 %convert_element_type.7 = f32[192]{0:T(256)} convert(s32[192]{0:T(256)} %param.22) | non-fusion elementwise | flops 192 | bytes 1536 | tf_op jit(solution)/shard_map/convert_element_type | solution.py:378
  1.9 0.7 stack.9
  2.6 0.7 fusion
  3.3 0.1 fusion.3
  3.4 0.6 pad.4.aux_ref
  4.0 2.7 %wave_to_planes.1 = (f32[8,72,128]{2,1,0:T(8,128)}, f32[192,256]{1,0:T(8,128)}, bf16[384,256]{1,0:T(8,128)(2,1)}, bf16[384,256]{1,0:T(8,128)(2,1)}, f32[192,192]{1,0:T(8,128)}, /*index=5*/f32[192,192]{1,0:T(8,128)}) custom-call(f32[8,256]{1,0:T(8,128)} %pad.4.aux_ref, f32[1,192]{1,0:T(1,128)} %bitcast.19, f32[192,2,128]{2,1,0:T(2,128)} %bitcast.14), custom_call_target="tpu_custom_call" | custom-call | tf_op jit(solution)/shard_map/wave_to_planes/pallas_call | solution.py:385
  6.7 7.3 %all-to-all-start = ((f32[8,72,128]{2,1,0:T(8,128)}), f32[8,72,128]{2,1,0:T(8,128)S(1)}, u32[]{:S(2)}, u32[]{:S(2)}) async-start(f32[8,72,128]{2,1,0:T(8,128)} %get-tuple-element.11), calls=%async_computation | async-start | bytes 589824 | tf_op jit(solution)/shard_map/all_to_all | solution.py:399
  14.0 0.0 collective-permute-start.2
  14.0 1.6 %collective-permute-start.1 = (f32[192,2,128]{2,1,0:T(2,128)}, f32[192,2,128]{2,1,0:T(2,128)S(1)}, u32[]{:S(2)}, u32[]{:S(2)}) collective-permute-start(f32[192,2,128]{2,1,0:T(2,128)} %bitcast.16), channel_id=1, source_target_pairs={{16,0},{24,8},{0,16},{8,24},{17,1},{25,9},{1,17},{9,25},{18,2},{26... | collective-permute-start | bytes 589832 | tf_op jit(solution)/shard_map/ppermute | solution.py:431
  15.6 1.4 %collective-permute-start = (f32[192,2,128]{2,1,0:T(2,128)}, f32[192,2,128]{2,1,0:T(2,128)S(1)}, u32[]{:S(2)}, u32[]{:S(2)}) collective-permute-start(f32[192,2,128]{2,1,0:T(2,128)} %bitcast.17), channel_id=1, source_target_pairs={{8,0},{16,8},{24,16},{0,24},{9,1},{17,9},{25,17},{1,25},{10,2},{18... | collective-permute-start | bytes 589832 | tf_op jit(solution)/shard_map/ppermute | solution.py:431
  17.0 0.1 reshape.42
  17.0 0.1 reshape.39
  17.1 0.1 reshape.43
  17.2 0.1 reshape.40
  17.3 0.6 pad_add_fusion
  17.9 0.6 pad_add_fusion.1
  18.5 5.1 %all-to-all-done.recv_ref.refs_5_ = f32[8,72,128]{2,1,0:T(8,128)S(1)} async-done(((f32[8,72,128]{2,1,0:T(8,128)}), f32[8,72,128]{2,1,0:T(8,128)S(1)}, u32[]{:S(2)}, u32[]{:S(2)}) %all-to-all-start) | async-done | bytes 294944 | tf_op jit(solution)/shard_map/all_to_all | solution.py:399
  23.6 0.0 collective-permute-start.5
  23.6 1.6 %collective-permute-start.4 = (f32[8,72,128]{2,1,0:T(8,128)S(1)}, f32[8,72,128]{2,1,0:T(8,128)S(1)}, u32[]{:S(2)}, u32[]{:S(2)}) collective-permute-start(f32[8,72,128]{2,1,0:T(8,128)S(1)} %all-to-all-done.recv_ref.refs_5_), channel_id=1, source_target_pairs={{16,0},{24,8},{0,16},{8,24},{17,1},{25,9},{1,17},{9,25},{18,2},{26... | collective-permute-start | bytes 884744 | tf_op jit(solution)/shard_map/ppermute | solution.py:432
  25.1 1.4 %collective-permute-start.3 = (f32[8,72,128]{2,1,0:T(8,128)S(1)}, f32[8,72,128]{2,1,0:T(8,128)S(1)}, u32[]{:S(2)}, u32[]{:S(2)}) collective-permute-start(f32[8,72,128]{2,1,0:T(8,128)S(1)} %all-to-all-done.recv_ref.refs_5_), channel_id=1, source_target_pairs={{8,0},{16,8},{24,16},{0,24},{9,1},{17,9},{25,17},{1,25},{10,2},{18... | collective-permute-start | bytes 884744 | tf_op jit(solution)/shard_map/ppermute | solution.py:432
  26.6 0.6 copy_bitcast_fusion
  27.2 1.7 %stick_map.1.map_ref = s32[104,128]{1,0:T(8,128)} custom-call(s32[1,1536]{1,0:T(1,128)} %get-tuple-element.26.row_ref, s32[1,1536]{1,0:T(1,128)} %get-tuple-element.25.col_ref), custom_call_target="tpu_custom_call" | custom-call | tf_op jit(solution)/shard_map/stick_map/pallas_call | solution.py:404
  28.9 52.8 %planes.1.refs_9_ = f32[8,80,128]{2,1,0:T(8,128)} custom-call(s32[104,128]{1,0:T(8,128)} %stick_map.1.map_ref, s32[12,128]{1,0:T(8,128)} %get-tuple-element.23.row_ref, s32[12,128]{1,0:T(8,128)} %get-tuple-element.21.col_ref, f32[8,72,128]{2,1,0:T(8,128)} %copy-done, bf16[256,192]{1,0:T(8,128)(2,1)} %constant.47.clone.xr_hi, ...), custom_call_target="tpu_custom_call" | custom-call | tf_op jit(solution)/shard_map/planes/pallas_call | solution.py:412
  81.7 0.0 copy-start.6
  81.8 0.6 copy-done.5
  82.4 0.1 copy-done.6
  82.4 0.1 copy-done.1
  82.5 0.1 copy-done.2
  82.6 0.1 copy-done.3
  82.7 3.3 %inner.1 = f32[8,80,128]{2,1,0:T(8,128)} custom-call(s32[1]{0:T(128)} %bitcast.band_ref, f32[192,256]{1,0:T(8,128)} %get-tuple-element.10.refs_0_.kc_ref, f32[192,2,128]{2,1,0:T(2,128)} %bitcast.18, f32[192,2,128]{2,1,0:T(2,128)} %copy-done.6, f32[192,2,128]{2,1,0:T(2,128)} %copy-done.5, f32[192,2,128]{2,1,0:T(2,128)} %copy-done.4, f32[8,72,128]{2,1,0:T(8,128)} %copy-done, ...), custom_call_target="tpu_custom_call" | custom-call | tf_op jit(solution)/shard_map/inner/pallas_call | solution.py:435
  86.0 14.5 %all_to_all.10.ret_ref = f32[8,80,128]{2,1,0:T(8,128)} all-to-all(f32[8,80,128]{2,1,0:T(8,128)} %inner.1), channel_id=1, replica_groups=mesh['band'=4,'tg'=8] {'tg'}, dimensions={0} | all-to-all | bytes 655360 | tf_op jit(solution)/shard_map/all_to_all | solution.py:444
  100.6 2.5 %planes_to_wave.1 = (f32[192,2,128]{2,1,0:T(2,128)}, f32[2,1,4]{2,1,0:T(1,128)}) custom-call(f32[8,256]{1,0:T(8,128)} %pad.4.aux_ref, f32[8,80,128]{2,1,0:T(8,128)} %all_to_all.10.ret_ref, f32[192,256]{1,0:T(8,128)} %get-tuple-element.10.refs_0_.kc_ref, bf16[384,256]{1,0:T(8,128)(2,1)} %get-tuple-element.12.whi_ref, ...), custom_call_target="tpu_custom_call" | custom-call | tf_op jit(solution)/shard_map/planes_to_wave/pallas_call | solution.py:445
  (19 shorter events, 0.1 us)
Async XLA Ops:
  6.7 16.9 %all-to-all-start = ((f32[8,72,128]{2,1,0:T(8,128)}), f32[8,72,128]{2,1,0:T(8,128)S(1)}, u32[]{:S(2)}, u32[]{:S(2)}) async-start(f32[8,72,128]{2,1,0:T(8,128)} %get-tuple-element.11), calls=%async_computation | async-start | bytes 589824 | tf_op jit(solution)/shard_map/all_to_all | solution.py:399
  14.0 11.2 %collective-permute-start.2 = (f32[192,2,128]{2,1,0:T(2,128)}, f32[192,2,128]{2,1,0:T(2,128)S(1)}, u32[]{:S(2)}, u32[]{:S(2)}) collective-permute-start(f32[192,2,128]{2,1,0:T(2,128)} %bitcast.15), channel_id=1, source_target_pairs={{24,0},{0,8},{8,16},{16,24},{25,1},{1,9},{9,17},{17,25},{26,2},{2,... | collective-permute-start | bytes 589832 | tf_op jit(solution)/shard_map/ppermute | solution.py:431
  14.0 67.7 %collective-permute-start.1 = (f32[192,2,128]{2,1,0:T(2,128)}, f32[192,2,128]{2,1,0:T(2,128)S(1)}, u32[]{:S(2)}, u32[]{:S(2)}) collective-permute-start(f32[192,2,128]{2,1,0:T(2,128)} %bitcast.16), channel_id=1, source_target_pairs={{16,0},{24,8},{0,16},{8,24},{17,1},{25,9},{1,17},{9,25},{18,2},{26... | collective-permute-start | bytes 589832 | tf_op jit(solution)/shard_map/ppermute | solution.py:431
  15.6 66.1 %collective-permute-start = (f32[192,2,128]{2,1,0:T(2,128)}, f32[192,2,128]{2,1,0:T(2,128)S(1)}, u32[]{:S(2)}, u32[]{:S(2)}) collective-permute-start(f32[192,2,128]{2,1,0:T(2,128)} %bitcast.17), channel_id=1, source_target_pairs={{8,0},{16,8},{24,16},{0,24},{9,1},{17,9},{25,17},{1,25},{10,2},{18... | collective-permute-start | bytes 589832 | tf_op jit(solution)/shard_map/ppermute | solution.py:431
  23.6 5.3 %copy-start = (f32[8,72,128]{2,1,0:T(8,128)}, f32[8,72,128]{2,1,0:T(8,128)S(1)}, u32[]{:S(2)}) copy-start(f32[8,72,128]{2,1,0:T(8,128)S(1)} %all-to-all-done.recv_ref.refs_5_) | copy-start | bytes 884740
  23.6 58.1 %collective-permute-start.5 = (f32[8,72,128]{2,1,0:T(8,128)S(1)}, f32[8,72,128]{2,1,0:T(8,128)S(1)}, u32[]{:S(2)}, u32[]{:S(2)}) collective-permute-start(f32[8,72,128]{2,1,0:T(8,128)S(1)} %all-to-all-done.recv_ref.refs_5_), channel_id=1, source_target_pairs={{24,0},{0,8},{8,16},{16,24},{25,1},{1,9},{9,17},{17,25},{26,2},{2,... | collective-permute-start | bytes 884744 | tf_op jit(solution)/shard_map/ppermute | solution.py:432
  23.6 58.1 %collective-permute-start.4 = (f32[8,72,128]{2,1,0:T(8,128)S(1)}, f32[8,72,128]{2,1,0:T(8,128)S(1)}, u32[]{:S(2)}, u32[]{:S(2)}) collective-permute-start(f32[8,72,128]{2,1,0:T(8,128)S(1)} %all-to-all-done.recv_ref.refs_5_), channel_id=1, source_target_pairs={{16,0},{24,8},{0,16},{8,24},{17,1},{25,9},{1,17},{9,25},{18,2},{26... | collective-permute-start | bytes 884744 | tf_op jit(solution)/shard_map/ppermute | solution.py:432
  25.1 56.6 %copy-start.4 = (f32[192,2,128]{2,1,0:T(2,128)}, f32[192,2,128]{2,1,0:T(2,128)S(1)}, u32[]{:S(2)}) copy-start(f32[192,2,128]{2,1,0:T(2,128)S(1)} %collective-permute-done.2.refs_4_) | copy-start | bytes 589828
  25.1 56.6 %collective-permute-start.3 = (f32[8,72,128]{2,1,0:T(8,128)S(1)}, f32[8,72,128]{2,1,0:T(8,128)S(1)}, u32[]{:S(2)}, u32[]{:S(2)}) collective-permute-start(f32[8,72,128]{2,1,0:T(8,128)S(1)} %all-to-all-done.recv_ref.refs_5_), channel_id=1, source_target_pairs={{8,0},{16,8},{24,16},{0,24},{9,1},{17,9},{25,17},{1,25},{10,2},{18... | collective-permute-start | bytes 884744 | tf_op jit(solution)/shard_map/ppermute | solution.py:432
  81.7 0.7 copy-start.5
  81.7 0.7 copy-start.6
  81.7 0.8 copy-start.1
  81.7 0.9 copy-start.2
  81.8 1.0 copy-start.3

commit v3 on v2

--- a/solution.py
+++ b/solution.py
@@ -189,7 +189,7 @@
     blocks = padded_planes // 8
     grids = (gr_ref, gi_ref)
 
-    @pl.loop(0, rows, unroll=4)
+    @pl.loop(0, rows, unroll=8)
     def _(r):
         code = jnp.broadcast_to(map_ref[pl.ds(r, 1), :], (8, LANES))
         index = code & (LANES - 1)
@@ -209,7 +209,7 @@
     table_br = (br_hi[...], br_lo[...])
     table_bi = (bi_hi[...], bi_lo[...])
 
-    @pl.loop(0, planes // 2)
+    @pl.loop(0, planes // 2, unroll=3)
     def _(step):
         base = pl.multiple_of(step * 2 * rows, 8)
         pick = pl.ds(base, 2 * rows)
@@ -247,7 +247,7 @@
             return tuple(new)
 
         acc = lax.fori_loop(
-            0, rows, body, tuple(jnp.zeros((8, LANES), F32) for _ in range(2 * blocks)), unroll=8
+            0, rows, body, tuple(jnp.zeros((8, LANES), F32) for _ in range(2 * blocks)), unroll=26
         )
         full = jnp.concatenate(acc, axis=0)
         if w < devices:

time: 104 us -> 93.1 us (0.90)
  Pallas kernels: 63 us -> 52.4 us
    pallas_call x1, Pallas kernels: 52.8 us -> 42.2 us  [shards(): pl.pallas_call(functools.partial(plane_kernel, planes), out_shape=jax.Sha...]
  transfers between devices with their start and end apart: 7 -> 7, of which waited for: 1 -> 1; matrix products, arithmetic and copies ran while one was open for 2% -> 2% of each run, Pallas kernels for 53% -> 47%
where the time goes in v3:
time: 93.1 us; the launch traced here: 92.5 us
  Pallas kernels  52.4 us (56%)
  blocking collectives  14.5 us (16%)
  starting transfers between devices  13.2 us (14%)
  waiting for transfers between devices  5.13 us (6%)
  other arithmetic  3.25 us (3%)
  local copies, waits for them, and re-layouts  3.2 us (3%)
    pallas_call x1, Pallas kernels, shards(): pl.pallas_call(functools.partial(plane_kernel, planes), out_shape=jax.Sha...  42.2 us
    all_to_all x1, blocking collectives, shards(): lax.all_to_all(outgoing, 'tg', split_axis=0, concat_axis=0, tiled=True)  14.5 us
    all_to_all x1, starting transfers between devices, shards(): lax.all_to_all(sent, 'tg', split_axis=0, concat_axis=0, tiled=True)  7.25 us
    all_to_all x1, waiting for transfers between devices, shards(): lax.all_to_all(sent, 'tg', split_axis=0, concat_axis=0, tiled=True)  5.11 us
    pallas_call x1, Pallas kernels, shards(): pl.pallas_call(functools.partial(inner_kernel, bands, volume, norm), out_...  3.27 us
    ppermute x3, starting transfers between devices, shards(): fields.append(lax.ppermute(received, 'band', ring))  2.99 us
    ppermute x3, starting transfers between devices, shards(): coefs.append(lax.ppermute(coef, 'band', ring))  2.98 us
    pallas_call x1, Pallas kernels, shards(): pl.pallas_call(functools.partial(wave_kernel, extent, planes), out_shape=...  2.71 us
  transfers between devices with their start and end apart: 7, of which 1 were waited for; matrix products, arithmetic and copies ran while one was open for 2% of the time, Pallas kernels for 47%

profile of v3, /device:TPU:0, one launch (start us, length us, event | category | flops | bytes accessed | tf_op | source)
XLA Modules:
  0.0 92.5 jit_solution(16508493260079517758)
XLA Ops:
  0.6 1.2 %convert_element_type.7 = f32[192]{0:T(256)} convert(s32[192]{0:T(256)} %param.22) | non-fusion elementwise | flops 192 | bytes 1536 | tf_op jit(solution)/shard_map/convert_element_type | solution.py:378
  1.9 0.7 stack.9
  2.6 0.7 fusion
  3.3 0.1 fusion.3
  3.4 0.6 pad.4.aux_ref
  4.0 2.7 %wave_to_planes.1 = (f32[8,72,128]{2,1,0:T(8,128)}, f32[192,256]{1,0:T(8,128)}, bf16[384,256]{1,0:T(8,128)(2,1)}, bf16[384,256]{1,0:T(8,128)(2,1)}, f32[192,192]{1,0:T(8,128)}, /*index=5*/f32[192,192]{1,0:T(8,128)}) custom-call(f32[8,256]{1,0:T(8,128)} %pad.4.aux_ref, f32[1,192]{1,0:T(1,128)} %bitcast.19, f32[192,2,128]{2,1,0:T(2,128)} %bitcast.14), custom_call_target="tpu_custom_call" | custom-call | tf_op jit(solution)/shard_map/wave_to_planes/pallas_call | solution.py:385
  6.7 7.3 %all-to-all-start = ((f32[8,72,128]{2,1,0:T(8,128)}), f32[8,72,128]{2,1,0:T(8,128)S(1)}, u32[]{:S(2)}, u32[]{:S(2)}) async-start(f32[8,72,128]{2,1,0:T(8,128)} %get-tuple-element.11), calls=%async_computation | async-start | bytes 589824 | tf_op jit(solution)/shard_map/all_to_all | solution.py:399
  14.0 0.0 collective-permute-start.2
  14.0 1.6 %collective-permute-start.1 = (f32[192,2,128]{2,1,0:T(2,128)}, f32[192,2,128]{2,1,0:T(2,128)S(1)}, u32[]{:S(2)}, u32[]{:S(2)}) collective-permute-start(f32[192,2,128]{2,1,0:T(2,128)} %bitcast.16), channel_id=1, source_target_pairs={{16,0},{24,8},{0,16},{8,24},{17,1},{25,9},{1,17},{9,25},{18,2},{26... | collective-permute-start | bytes 589832 | tf_op jit(solution)/shard_map/ppermute | solution.py:431
  15.6 1.4 %collective-permute-start = (f32[192,2,128]{2,1,0:T(2,128)}, f32[192,2,128]{2,1,0:T(2,128)S(1)}, u32[]{:S(2)}, u32[]{:S(2)}) collective-permute-start(f32[192,2,128]{2,1,0:T(2,128)} %bitcast.17), channel_id=1, source_target_pairs={{8,0},{16,8},{24,16},{0,24},{9,1},{17,9},{25,17},{1,25},{10,2},{18... | collective-permute-start | bytes 589832 | tf_op jit(solution)/shard_map/ppermute | solution.py:431
  17.0 0.1 reshape.42
  17.0 0.1 reshape.39
  17.1 0.1 reshape.43
  17.2 0.1 reshape.40
  17.3 0.6 pad_add_fusion
  17.9 0.6 pad_add_fusion.1
  18.5 5.1 %all-to-all-done.recv_ref.refs_5_ = f32[8,72,128]{2,1,0:T(8,128)S(1)} async-done(((f32[8,72,128]{2,1,0:T(8,128)}), f32[8,72,128]{2,1,0:T(8,128)S(1)}, u32[]{:S(2)}, u32[]{:S(2)}) %all-to-all-start) | async-done | bytes 294944 | tf_op jit(solution)/shard_map/all_to_all | solution.py:399
  23.6 0.0 collective-permute-start.5
  23.6 1.6 %collective-permute-start.4 = (f32[8,72,128]{2,1,0:T(8,128)S(1)}, f32[8,72,128]{2,1,0:T(8,128)S(1)}, u32[]{:S(2)}, u32[]{:S(2)}) collective-permute-start(f32[8,72,128]{2,1,0:T(8,128)S(1)} %all-to-all-done.recv_ref.refs_5_), channel_id=1, source_target_pairs={{16,0},{24,8},{0,16},{8,24},{17,1},{25,9},{1,17},{9,25},{18,2},{26... | collective-permute-start | bytes 884744 | tf_op jit(solution)/shard_map/ppermute | solution.py:432
  25.1 1.4 %collective-permute-start.3 = (f32[8,72,128]{2,1,0:T(8,128)S(1)}, f32[8,72,128]{2,1,0:T(8,128)S(1)}, u32[]{:S(2)}, u32[]{:S(2)}) collective-permute-start(f32[8,72,128]{2,1,0:T(8,128)S(1)} %all-to-all-done.recv_ref.refs_5_), channel_id=1, source_target_pairs={{8,0},{16,8},{24,16},{0,24},{9,1},{17,9},{25,17},{1,25},{10,2},{18... | collective-permute-start | bytes 884744 | tf_op jit(solution)/shard_map/ppermute | solution.py:432
  26.6 0.6 copy_bitcast_fusion
  27.2 1.7 %stick_map.1.map_ref = s32[104,128]{1,0:T(8,128)} custom-call(s32[1,1536]{1,0:T(1,128)} %get-tuple-element.26.row_ref, s32[1,1536]{1,0:T(1,128)} %get-tuple-element.25.col_ref), custom_call_target="tpu_custom_call" | custom-call | tf_op jit(solution)/shard_map/stick_map/pallas_call | solution.py:404
  28.9 42.2 %planes.1.refs_9_ = f32[8,80,128]{2,1,0:T(8,128)} custom-call(s32[104,128]{1,0:T(8,128)} %stick_map.1.map_ref, s32[12,128]{1,0:T(8,128)} %get-tuple-element.23.row_ref, s32[12,128]{1,0:T(8,128)} %get-tuple-element.21.col_ref, f32[8,72,128]{2,1,0:T(8,128)} %copy-done, bf16[256,192]{1,0:T(8,128)(2,1)} %constant.47.clone.xr_hi, ...), custom_call_target="tpu_custom_call" | custom-call | tf_op jit(solution)/shard_map/planes/pallas_call | solution.py:412
  71.1 0.0 copy-start.6
  71.2 0.6 copy-done.5
  71.8 0.1 copy-done.6
  71.9 0.1 copy-done.1
  72.0 0.1 copy-done.2
  72.1 0.1 copy-done.3
  72.2 3.3 %inner.1 = f32[8,80,128]{2,1,0:T(8,128)} custom-call(s32[1]{0:T(128)} %bitcast.band_ref, f32[192,256]{1,0:T(8,128)} %get-tuple-element.10.refs_0_.kc_ref, f32[192,2,128]{2,1,0:T(2,128)} %bitcast.18, f32[192,2,128]{2,1,0:T(2,128)} %copy-done.6, f32[192,2,128]{2,1,0:T(2,128)} %copy-done.5, f32[192,2,128]{2,1,0:T(2,128)} %copy-done.4, f32[8,72,128]{2,1,0:T(8,128)} %copy-done, ...), custom_call_target="tpu_custom_call" | custom-call | tf_op jit(solution)/shard_map/inner/pallas_call | solution.py:435
  75.5 14.5 %all_to_all.10.ret_ref = f32[8,80,128]{2,1,0:T(8,128)} all-to-all(f32[8,80,128]{2,1,0:T(8,128)} %inner.1), channel_id=1, replica_groups=mesh['band'=4,'tg'=8] {'tg'}, dimensions={0} | all-to-all | bytes 655360 | tf_op jit(solution)/shard_map/all_to_all | solution.py:444
  90.0 2.5 %planes_to_wave.1 = (f32[192,2,128]{2,1,0:T(2,128)}, f32[2,1,4]{2,1,0:T(1,128)}) custom-call(f32[8,256]{1,0:T(8,128)} %pad.4.aux_ref, f32[8,80,128]{2,1,0:T(8,128)} %all_to_all.10.ret_ref, f32[192,256]{1,0:T(8,128)} %get-tuple-element.10.refs_0_.kc_ref, bf16[384,256]{1,0:T(8,128)(2,1)} %get-tuple-element.12.whi_ref, ...), custom_call_target="tpu_custom_call" | custom-call | tf_op jit(solution)/shard_map/planes_to_wave/pallas_call | solution.py:445
  (19 shorter events, 0.1 us)
Async XLA Ops:
  6.7 16.9 %all-to-all-start = ((f32[8,72,128]{2,1,0:T(8,128)}), f32[8,72,128]{2,1,0:T(8,128)S(1)}, u32[]{:S(2)}, u32[]{:S(2)}) async-start(f32[8,72,128]{2,1,0:T(8,128)} %get-tuple-element.11), calls=%async_computation | async-start | bytes 589824 | tf_op jit(solution)/shard_map/all_to_all | solution.py:399
  14.0 11.2 %collective-permute-start.2 = (f32[192,2,128]{2,1,0:T(2,128)}, f32[192,2,128]{2,1,0:T(2,128)S(1)}, u32[]{:S(2)}, u32[]{:S(2)}) collective-permute-start(f32[192,2,128]{2,1,0:T(2,128)} %bitcast.15), channel_id=1, source_target_pairs={{24,0},{0,8},{8,16},{16,24},{25,1},{1,9},{9,17},{17,25},{26,2},{2,... | collective-permute-start | bytes 589832 | tf_op jit(solution)/shard_map/ppermute | solution.py:431
  14.0 57.1 %collective-permute-start.1 = (f32[192,2,128]{2,1,0:T(2,128)}, f32[192,2,128]{2,1,0:T(2,128)S(1)}, u32[]{:S(2)}, u32[]{:S(2)}) collective-permute-start(f32[192,2,128]{2,1,0:T(2,128)} %bitcast.16), channel_id=1, source_target_pairs={{16,0},{24,8},{0,16},{8,24},{17,1},{25,9},{1,17},{9,25},{18,2},{26... | collective-permute-start | bytes 589832 | tf_op jit(solution)/shard_map/ppermute | solution.py:431
  15.6 55.6 %collective-permute-start = (f32[192,2,128]{2,1,0:T(2,128)}, f32[192,2,128]{2,1,0:T(2,128)S(1)}, u32[]{:S(2)}, u32[]{:S(2)}) collective-permute-start(f32[192,2,128]{2,1,0:T(2,128)} %bitcast.17), channel_id=1, source_target_pairs={{8,0},{16,8},{24,16},{0,24},{9,1},{17,9},{25,17},{1,25},{10,2},{18... | collective-permute-start | bytes 589832 | tf_op jit(solution)/shard_map/ppermute | solution.py:431
  23.6 5.3 %copy-start = (f32[8,72,128]{2,1,0:T(8,128)}, f32[8,72,128]{2,1,0:T(8,128)S(1)}, u32[]{:S(2)}) copy-start(f32[8,72,128]{2,1,0:T(8,128)S(1)} %all-to-all-done.recv_ref.refs_5_) | copy-start | bytes 884740
  23.6 47.6 %collective-permute-start.5 = (f32[8,72,128]{2,1,0:T(8,128)S(1)}, f32[8,72,128]{2,1,0:T(8,128)S(1)}, u32[]{:S(2)}, u32[]{:S(2)}) collective-permute-start(f32[8,72,128]{2,1,0:T(8,128)S(1)} %all-to-all-done.recv_ref.refs_5_), channel_id=1, source_target_pairs={{24,0},{0,8},{8,16},{16,24},{25,1},{1,9},{9,17},{17,25},{26,2},{2,... | collective-permute-start | bytes 884744 | tf_op jit(solution)/shard_map/ppermute | solution.py:432
  23.6 47.6 %collective-permute-start.4 = (f32[8,72,128]{2,1,0:T(8,128)S(1)}, f32[8,72,128]{2,1,0:T(8,128)S(1)}, u32[]{:S(2)}, u32[]{:S(2)}) collective-permute-start(f32[8,72,128]{2,1,0:T(8,128)S(1)} %all-to-all-done.recv_ref.refs_5_), channel_id=1, source_target_pairs={{16,0},{24,8},{0,16},{8,24},{17,1},{25,9},{1,17},{9,25},{18,2},{26... | collective-permute-start | bytes 884744 | tf_op jit(solution)/shard_map/ppermute | solution.py:432
  25.1 46.1 %copy-start.4 = (f32[192,2,128]{2,1,0:T(2,128)}, f32[192,2,128]{2,1,0:T(2,128)S(1)}, u32[]{:S(2)}) copy-start(f32[192,2,128]{2,1,0:T(2,128)S(1)} %collective-permute-done.2.refs_4_) | copy-start | bytes 589828
  25.1 46.1 %collective-permute-start.3 = (f32[8,72,128]{2,1,0:T(8,128)S(1)}, f32[8,72,128]{2,1,0:T(8,128)S(1)}, u32[]{:S(2)}, u32[]{:S(2)}) collective-permute-start(f32[8,72,128]{2,1,0:T(8,128)S(1)} %all-to-all-done.recv_ref.refs_5_), channel_id=1, source_target_pairs={{8,0},{16,8},{24,16},{0,24},{9,1},{17,9},{25,17},{1,25},{10,2},{18... | collective-permute-start | bytes 884744 | tf_op jit(solution)/shard_map/ppermute | solution.py:432
  71.1 0.7 copy-start.5
  71.1 0.7 copy-start.6
  71.2 0.8 copy-start.1
  71.2 0.9 copy-start.2
  71.2 1.0 %copy-start.3 = (f32[8,72,128]{2,1,0:T(8,128)}, f32[8,72,128]{2,1,0:T(8,128)S(1)}, u32[]{:S(2)}) copy-start(f32[8,72,128]{2,1,0:T(8,128)S(1)} %collective-permute-done.3.refs_6_) | copy-start | bytes 884740

commit v4 on v3

--- a/solution.py
+++ b/solution.py
@@ -88,14 +88,29 @@
     return pltpu.CompilerParams(vmem_limit_bytes=VMEM_LIMIT)
 
 
-def wave_kernel(extent, planes, aux_ref, plane_ref, coef_ref, out_ref, kc_ref, whi_ref, wlo_ref, sc_ref, ss_ref):
+def wave_kernel(extent, me_ref, info_ref, plane_ref, coef_ref, out_ref, kc_ref, len_ref, whi_ref, wlo_ref, sc_ref, ss_ref):
     devices = out_ref.shape[0]
     sticks, _, padded = coef_ref.shape
     padded_planes = plane_ref.shape[1] // devices
-    aux = aux_ref[...]
-    aux_col = jnp.transpose(jnp.concatenate([aux] * (LANES // 8), axis=0))
-    length = aux_col[:sticks, 0:1]
-    square = aux_col[:sticks, 1:2]
+    me = me_ref[0]
+    length_row = info_ref[0, pl.ds(me, 1), :].astype(F32)
+    at_row = info_ref[1, pl.ds(me, 1), :]
+    at_col = info_ref[2, pl.ds(me, 1), :]
+    at_row = jnp.where(at_row <= RADIUS, at_row, at_row - extent).astype(F32)
+    at_col = jnp.where(at_col <= RADIUS, at_col, at_col - extent).astype(F32)
+    square_row = at_row * at_row + at_col * at_col
+    spare = jnp.ones((1, 2 * LANES - sticks), F32)
+    aux = jnp.concatenate(
+        [
+            jnp.broadcast_to(jnp.concatenate([length_row, spare], axis=1), (LANES // 2, 2 * LANES)),
+            jnp.broadcast_to(jnp.concatenate([square_row, spare], axis=1), (LANES // 2, 2 * LANES)),
+        ],
+        axis=0,
+    )
+    aux_col = jnp.transpose(aux)[:sticks]
+    len_ref[...] = aux_col
+    length = aux_col[:, 0:1]
+    square = aux_col[:, LANES // 2:LANES // 2 + 1]
     middle = (length - 1.0) * 0.5
     position = lax.broadcasted_iota(jnp.int32, (sticks, padded), 1).astype(F32)
     kept = (position < length).astype(F32)
@@ -104,12 +119,12 @@
     kc_ref[...] = wave * jnp.concatenate([kinetic, kinetic], axis=1)
 
     total = plane_ref.shape[1]
-    plane_row = jnp.broadcast_to(plane_ref[...], (LANES, total))
+    plane_row = jnp.broadcast_to(plane_ref[...].astype(F32), (LANES, total))
     plane_col = jnp.transpose(plane_row)[:, 0:1]
-    slot = lax.broadcasted_iota(jnp.int32, (total, 1), 0)
     real = (plane_col >= 0.0).astype(F32)
+    plane_col = jnp.maximum(plane_col, 0.0)
     harmonic = lax.broadcasted_iota(jnp.int32, (total, padded), 1).astype(F32)
-    cos, sin = trig(jnp.maximum(plane_col, 0.0) * harmonic, extent)
+    cos, sin = trig(plane_col * harmonic, extent)
     cos, sin = cos * real, sin * real
     parts = []
     for d in range(devices):
@@ -120,8 +135,7 @@
     table = split(jnp.concatenate(parts, axis=0))
     whi_ref[...] = table[0]
     wlo_ref[...] = table[1]
-    middle_row = (aux[0:1, :sticks] - 1.0) * 0.5
-    shift_cos, shift_sin = trig(jnp.maximum(plane_col, 0.0) * middle_row, extent)
+    shift_cos, shift_sin = trig(plane_col * ((length_row - 1.0) * 0.5), extent)
     sc_ref[...] = shift_cos
     ss_ref[...] = shift_sin
     raw = dot3(table, split(wave), ((1,), (1,)))
@@ -139,22 +153,74 @@
         )
 
 
-def map_kernel(row_ref, col_ref, map_ref):
-    rows = map_ref.shape[0]
-    total = row_ref.shape[1]
-    r = lax.broadcasted_iota(jnp.int32, (rows, total), 0)
-    q = lax.broadcasted_iota(jnp.int32, (LANES, total), 0)
-    place = lax.broadcasted_iota(jnp.int32, (LANES, total), 1) + 1
-    in_row = (r == row_ref[...]).astype(F32).astype(BF16)
-    in_col = q == col_ref[...]
-    upper = jnp.where(in_col, place >> 6, 0).astype(F32).astype(BF16)
-    lower = jnp.where(in_col, place & 63, 0).astype(F32).astype(BF16)
-
-    def dot(x, y):
-        return lax.dot_general(x, y, (((1,), (1,)), ((), ())), preferred_element_type=F32)
-
-    found = dot(in_row, upper) * 64.0 + dot(in_row, lower)
-    map_ref[...] = found.astype(jnp.int32) - 1
+def window_row(values):
+    devices = values.shape[0]
+    parts = [values[d:d + 1, :LANES] for d in range(devices)]
+    parts += [values[d:d + 1, LANES:] for d in range(devices)]
+    return jnp.concatenate(parts, axis=1)
+
+
+def map_kernel(extent, info_ref, map_ref, first_ref, src_ref, dst_ref, row_ref, col_ref):
+    windows = src_ref.shape[0]
+    total = windows * LANES
+
+    def signed(part):
+        value = info_ref[part]
+        return window_row(jnp.where(value <= RADIUS, value, value - extent) + RADIUS)
+
+    def dot(x, y, dims=((1,), (0,))):
+        return lax.dot_general(x, y, (dims, ((), ())), preferred_element_type=F32)
+
+    def bits(condition):
+        return condition.astype(F32).astype(BF16)
+
+    nt = ((1,), (1,))
+    own_row, own_col = signed(1), signed(2)
+    tall = lax.broadcasted_iota(jnp.int32, (LANES, total), 0)
+    place = lax.broadcasted_iota(jnp.int32, (LANES, total), 1)
+    in_col = tall == own_col
+    row_hot, col_hot = bits(tall == own_row), bits(in_col)
+    down = lax.broadcasted_iota(jnp.int32, (LANES, LANES), 0)
+    across = lax.broadcasted_iota(jnp.int32, (LANES, LANES), 1)
+    before = bits(down < across)
+    after = bits(down > across)
+    upto = bits(down >= across)
+    ones = jnp.ones((LANES, LANES), BF16)
+    taken = dot(row_hot, col_hot, nt)
+    taken_t = dot(col_hot, row_hot, nt)
+    taken_b, taken_tb = taken.astype(BF16), taken_t.astype(BF16)
+    start = dot(dot(after, taken_b).astype(BF16), ones)
+    end = start + dot(taken_b, ones)
+    start_t = dot(ones, dot(taken_tb, before).astype(BF16))
+    limit = windows - 1.0
+    first = jnp.minimum(jnp.floor(start * (1.0 / LANES)), limit)
+    code = jnp.where(taken > 0.5, dot(taken_b, before) + start - LANES * first, -1.0)
+    map_ref[...] = code.astype(jnp.int32)
+    first_ref[...] = jnp.minimum(jnp.floor(start_t[0:8] * (1.0 / LANES)), limit).astype(jnp.int32)
+
+    spot = place.astype(F32)
+    in_range = (spot >= start[:, 0:1]) & (spot < end[:, 0:1])
+    sorted_hot = bits(in_range)
+    sorted_row = jnp.sum(jnp.where(in_range, tall, 0).astype(F32), axis=0, keepdims=True)
+    sorted_rank = spot[0:1] - jnp.sum(jnp.where(in_range, start[:, 0:1], 0.0), axis=0, keepdims=True)
+    counts = dot(dot(upto, taken_tb).astype(BF16), sorted_hot)
+    sorted_col = jnp.sum((counts <= sorted_rank).astype(F32), axis=0, keepdims=True)
+    names = place + 1
+    name_hi = dot(jnp.where(in_col, names >> 6, 0).astype(F32).astype(BF16), row_hot, nt)
+    name_lo = dot(jnp.where(in_col, names & 63, 0).astype(F32).astype(BF16), row_hot, nt)
+    named = dot(name_hi.astype(BF16), sorted_hot) * 64.0 + dot(name_lo.astype(BF16), sorted_hot)
+    source = jnp.sum(jnp.where(tall.astype(F32) == sorted_col, named, 0.0), axis=0, keepdims=True) - 1.0
+    place_t = dot(after, taken_tb) + start_t
+    place_hi = jnp.floor(place_t * (1.0 / 64.0))
+    place_lo = place_t - 64.0 * place_hi
+    placed = dot(place_hi.astype(BF16), row_hot) * 64.0 + dot(place_lo.astype(BF16), row_hot)
+    target = jnp.sum(jnp.where(in_col, placed, 0.0), axis=0, keepdims=True)
+    for values, ref in ((source, src_ref), (target, dst_ref), (sorted_row, row_ref), (sorted_col, col_ref)):
+        values = values.astype(jnp.int32)
+        for w in range(windows):
+            ref[w:w + 1, :] = values[:, w * LANES:(w + 1) * LANES]
+    row_ref[windows:windows + 1, :] = jnp.full((1, LANES), -1, jnp.int32)
+    col_ref[windows:windows + 1, :] = jnp.zeros((1, LANES), jnp.int32)
 
 
 def lane_take(x, index):
@@ -162,14 +228,14 @@
 
 
 def plane_kernel(
-    planes, map_ref, row_ref, col_ref, recv_ref,
+    planes, first_ref, map_ref, src_ref, dst_ref, row_ref, col_ref, recv_ref,
     xr_hi, xr_lo, xi_hi, xi_lo, y_hi, y_lo, yb_hi, yb_lo, br_hi, br_lo, bi_hi, bi_lo,
-    pot_hbm, out_ref, x_ref, gr_ref, gi_ref, pot_ref, sem,
+    pot_hbm, out_ref, x_ref, s_ref, gr_ref, gi_ref, pot_ref, sem,
 ):
     devices = recv_ref.shape[0]
     padded_planes = recv_ref.shape[1] // 3
     windows = x_ref.shape[0]
-    rows = map_ref.shape[0]
+    rows = gr_ref.shape[0] // padded_planes
     extent = pot_ref.shape[1]
     half = LANES // 2
     fetch = pltpu.make_async_copy(pot_hbm, pot_ref, sem)
@@ -189,15 +255,30 @@
     blocks = padded_planes // 8
     grids = (gr_ref, gi_ref)
 
+    def reorder(order_ref, from_ref, to_ref):
+        @pl.loop(0, windows, unroll=4)
+        def _(v):
+            order = jnp.broadcast_to(order_ref[pl.ds(v, 1), :], (8, LANES))
+            index = order & (LANES - 1)
+            window = order >> 7
+            for j in range(2 * blocks):
+                value = jnp.zeros((8, LANES), F32)
+                for w in range(windows):
+                    value = jnp.where(window == w, lane_take(from_ref[w, 8 * j:8 * j + 8, :], index), value)
+                to_ref[v, 8 * j:8 * j + 8, :] = value
+
+    reorder(src_ref, x_ref, s_ref)
+
     @pl.loop(0, rows, unroll=8)
     def _(r):
+        first = first_ref[0, r]
         code = jnp.broadcast_to(map_ref[pl.ds(r, 1), :], (8, LANES))
         index = code & (LANES - 1)
         window = code >> 7
         for j in range(2 * blocks):
-            value = jnp.zeros((8, LANES), F32)
-            for w in range(windows):
-                value = jnp.where(window == w, lane_take(x_ref[w, 8 * j:8 * j + 8, :], index), value)
+            lead = lane_take(s_ref[first, 8 * j:8 * j + 8, :], index)
+            trail = lane_take(s_ref[first + 1, 8 * j:8 * j + 8, :], index)
+            value = jnp.where(window == 0, lead, jnp.where(window == 1, trail, 0.0))
             part, at = j // blocks, 8 * (j % blocks)
             grids[part][pl.ds(r + at * rows, 8, stride=rows), :] = value
 
@@ -233,34 +314,33 @@
         gr_ref[pick, :] = back[:, :LANES]
         gi_ref[pick, :] = back[:, LANES:]
 
-    for w in range(windows):
-        index = jnp.broadcast_to(col_ref[w:w + 1, :], (8, LANES))
-        which = jnp.broadcast_to(row_ref[w:w + 1, :], (8, LANES))
-
-        def body(r, acc):
-            hit = which == r
-            new = []
+    @pl.loop(0, rows, unroll=8)
+    def _(r):
+        first = first_ref[0, r]
+        values = []
+        for j in range(2 * blocks):
+            part, at = j // blocks, 8 * (j % blocks)
+            values.append(grids[part][pl.ds(r + at * rows, 8, stride=rows), :])
+        for t in range(2):
+            index = jnp.broadcast_to(col_ref[pl.ds(first + t, 1), :], (8, LANES))
+            hit = jnp.broadcast_to(row_ref[pl.ds(first + t, 1), :], (8, LANES)) == r
             for j in range(2 * blocks):
-                part, at = j // blocks, 8 * (j % blocks)
-                value = grids[part][pl.ds(r + at * rows, 8, stride=rows), :]
-                new.append(jnp.where(hit, lane_take(value, index), acc[j]))
-            return tuple(new)
-
-        acc = lax.fori_loop(
-            0, rows, body, tuple(jnp.zeros((8, LANES), F32) for _ in range(2 * blocks)), unroll=26
+                pltpu.store(
+                    s_ref.at[first + t, 8 * j:8 * j + 8, :], lane_take(values[j], index), mask=hit
+                )
+
+    reorder(dst_ref, s_ref, x_ref)
+    for w in range(devices):
+        out_ref[w, 0:2 * padded_planes, :] = x_ref[w]
+    for e in range(devices // 2):
+        re = x_ref[devices + e, 0:padded_planes, :]
+        im = x_ref[devices + e, padded_planes:2 * padded_planes, :]
+        out_ref[2 * e, 2 * padded_planes:3 * padded_planes, :] = jnp.where(
+            low, re, pltpu.roll(im, half, 1)
         )
-        full = jnp.concatenate(acc, axis=0)
-        if w < devices:
-            out_ref[w, 0:2 * padded_planes, :] = full
-        else:
-            e = w - devices
-            re, im = full[:padded_planes], full[padded_planes:]
-            out_ref[2 * e, 2 * padded_planes:3 * padded_planes, :] = jnp.where(
-                low, re, pltpu.roll(im, half, 1)
-            )
-            out_ref[2 * e + 1, 2 * padded_planes:3 * padded_planes, :] = jnp.where(
-                low, pltpu.roll(re, half, 1), im
-            )
+        out_ref[2 * e + 1, 2 * padded_planes:3 * padded_planes, :] = jnp.where(
+            low, pltpu.roll(re, half, 1), im
+        )
     for d in range(devices):
         out_ref[d, 3 * padded_planes:, :] = jnp.zeros((8, LANES), F32)
 
@@ -315,7 +395,7 @@
         out_ref[d, 3 * padded_planes:, :] = tile
 
 
-def final_kernel(volume, aux_ref, ret_ref, kc_ref, whi_ref, wlo_ref, sc_ref, ss_ref, out_ref, sub_ref):
+def final_kernel(volume, len_ref, ret_ref, kc_ref, whi_ref, wlo_ref, sc_ref, ss_ref, out_ref, sub_ref):
     devices = ret_ref.shape[0]
     padded_planes = (ret_ref.shape[1] - 8) // 3
     sticks, _, padded = out_ref.shape
@@ -337,21 +417,12 @@
     spare = jnp.zeros((stacked.shape[0], 2 * LANES - sticks), F32)
     turned = jnp.transpose(jnp.concatenate([stacked, spare], axis=1))[:sticks]
     local = dot3(split(turned), (whi_ref[...], wlo_ref[...])) * volume
-    aux_col = jnp.transpose(jnp.concatenate([aux_ref[...]] * (LANES // 8), axis=0))
-    length = aux_col[:sticks, 0:1]
     position = lax.broadcasted_iota(jnp.int32, (sticks, padded), 1).astype(F32)
-    kept = position < length
+    kept = position < len_ref[:, 0:1]
     kc = kc_ref[...]
     out_ref[:, 0, :] = jnp.where(kept, kc[:, :padded] + local[:, :padded], 0.0)
     out_ref[:, 1, :] = jnp.where(kept, kc[:, padded:] + local[:, padded:], 0.0)
     sub_ref[:, 0, :] = total[0:2, :bands]
-
-
-def window_order(values, devices):
-    blocks = values.reshape(devices, -1)
-    return jnp.concatenate(
-        [blocks[:, :LANES].reshape(-1, LANES), blocks[:, LANES:].reshape(-1, LANES)], axis=0
-    )
 
 
 def shards(bands, devices, coefficients, stick_col, stick_row, stick_length, plane_of_slot, potential):
@@ -366,56 +437,62 @@
     kept = 2 * RADIUS + 1
     rows = up8(kept)
     volume = 1.0 / (extent * extent * extent)
-    me = lax.axis_index("tg")
+    me = lax.axis_index("tg").astype(jnp.int32)
     coef = coefficients.reshape(sticks, 2, padded)
 
-    signed_col = jnp.where(stick_col <= RADIUS, stick_col, stick_col - extent)
-    signed_row = jnp.where(stick_row <= RADIUS, stick_row, stick_row - extent)
-    info = jnp.stack([stick_length, signed_col * signed_col + signed_row * signed_row])
-    info = lax.dynamic_slice_in_dim(info, me * sticks, sticks, axis=1).astype(F32)
-    aux = jnp.pad(info, ((0, 6), (0, 2 * LANES - sticks)), constant_values=1.0)
-    slots = jnp.pad(
-        plane_of_slot.astype(F32).reshape(devices, planes),
-        ((0, 0), (0, padded_planes - planes)),
-        constant_values=-1.0,
-    ).reshape(1, devices * padded_planes)
+    info = jnp.stack([stick_length, stick_row, stick_col]).reshape(3, devices, sticks)
+    slots = plane_of_slot.reshape(devices, planes)
+    if padded_planes > planes:
+        slots = jnp.pad(slots, ((0, 0), (0, padded_planes - planes)), constant_values=-1)
+    slots = slots.reshape(1, devices * padded_planes)
+    windows = total_sticks // LANES
+    smem = pl.BlockSpec(memory_space=pltpu.SMEM)
+    vmem = pl.BlockSpec(memory_space=pltpu.VMEM)
 
     block = 3 * padded_planes
     total_planes = devices * padded_planes
-    sent, kc, whi, wlo, shift_cos, shift_sin = pl.pallas_call(
-        functools.partial(wave_kernel, extent, planes),
+    sent, kc, lengths, whi, wlo, shift_cos, shift_sin = pl.pallas_call(
+        functools.partial(wave_kernel, extent),
         out_shape=(
             jax.ShapeDtypeStruct((devices, block, LANES), F32),
             jax.ShapeDtypeStruct((sticks, 2 * padded), F32),
+            jax.ShapeDtypeStruct((sticks, LANES), F32),
             jax.ShapeDtypeStruct((2 * total_planes, 2 * padded), BF16),
             jax.ShapeDtypeStruct((2 * total_planes, 2 * padded), BF16),
             jax.ShapeDtypeStruct((total_planes, sticks), F32),
             jax.ShapeDtypeStruct((total_planes, sticks), F32),
         ),
+        in_specs=[smem] + [vmem] * 3,
         compiler_params=params(),
         name="wave_to_planes",
-    )(aux, slots, coef)
+    )(me.reshape(1), info, slots, coef)
 
     received = lax.all_to_all(sent, "tg", split_axis=0, concat_axis=0, tiled=True)
 
-    row_w = window_order(signed_row + RADIUS, devices)
-    col_w = window_order(signed_col + RADIUS, devices)
-    windows = row_w.shape[0]
-    stick_map = pl.pallas_call(
-        map_kernel,
-        out_shape=jax.ShapeDtypeStruct((rows, LANES), jnp.int32),
+    window_list = jax.ShapeDtypeStruct((windows, LANES), jnp.int32)
+    longer_list = jax.ShapeDtypeStruct((windows + 1, LANES), jnp.int32)
+    stick_map, first, source, target, row_w, col_w = pl.pallas_call(
+        functools.partial(map_kernel, extent),
+        out_shape=(
+            jax.ShapeDtypeStruct((LANES, LANES), jnp.int32),
+            jax.ShapeDtypeStruct((8, LANES), jnp.int32),
+            window_list,
+            window_list,
+            longer_list,
+            longer_list,
+        ),
         compiler_params=params(),
         name="stick_map",
-    )(row_w.reshape(1, -1), col_w.reshape(1, -1))
-
-    vmem = pl.BlockSpec(memory_space=pltpu.VMEM)
+    )(info)
+
     weighted = pl.pallas_call(
         functools.partial(plane_kernel, planes),
         out_shape=jax.ShapeDtypeStruct((devices, block + 8, LANES), F32),
-        in_specs=[vmem] * 16 + [pl.BlockSpec(memory_space=pl.ANY)],
+        in_specs=[smem] + [vmem] * 18 + [pl.BlockSpec(memory_space=pl.ANY)],
         out_specs=vmem,
         scratch_shapes=[
             pltpu.VMEM((windows, 2 * padded_planes, LANES), F32),
+            pltpu.VMEM((windows + 1, 2 * padded_planes, LANES), F32),
             pltpu.VMEM((padded_planes * rows, LANES), F32),
             pltpu.VMEM((padded_planes * rows, LANES), F32),
             pltpu.VMEM(potential.shape, F32),
@@ -423,7 +500,7 @@
         ],
         compiler_params=params(),
         name="planes",
-    )(stick_map, row_w, col_w, received, *[jnp.asarray(t) for t in tables(extent)], potential)
+    )(first, stick_map, source, target, row_w, col_w, received, *[jnp.asarray(t) for t in tables(extent)], potential)
 
     coefs, fields = [coef], [received]
     for shift in range(1, bands):
@@ -450,7 +527,7 @@
         ),
         compiler_params=params(),
         name="planes_to_wave",
-    )(aux, returned, kc, whi, wlo, shift_cos, shift_sin)
+    )(lengths, returned, kc, whi, wlo, shift_cos, shift_sin)
     return applied.reshape(1, sticks, 2, padded), subspace
 
 

time: 93.1 us -> 83 us (0.89)
  Pallas kernels: 52.4 us -> 41.4 us
  waiting for transfers between devices: 5.13 us -> 9.62 us
  other arithmetic: 3.25 us -> 0 us
  starting transfers between devices: 13.2 us -> 10.8 us
  blocking collectives: 14.5 us -> 15.9 us
    pallas_call x1, Pallas kernels: 42.2 us -> 29.5 us  [shards(): pl.pallas_call(functools.partial(plane_kernel, planes), out_shape=jax.Sha...]
    all_to_all x1, waiting for transfers between devices: 5.11 us -> 9.61 us  [shards(): lax.all_to_all(sent, 'tg', split_axis=0, concat_axis=0, tiled=True)]
    ppermute x3, starting transfers between devices: 2.98 us -> 0.51 us  [shards(): coefs.append(lax.ppermute(coef, 'band', ring))]
    pallas_call x2, Pallas kernels: 4.41 us -> 6.12 us  [the longest x1 3.39 us: shards(): pl.pallas_call(functools.partial(map_kernel, extent), out_shape=(jax.Shap...]
    another operation x2 -> x4, local copies, waits for them, and re-layouts: 0.71 us -> 2.31 us  [shards(): jnp.stack([stick_length, stick_row, stick_col]).reshape(3, devices, sticks)]
    all_to_all x1, blocking collectives: 14.5 us -> 15.9 us  [shards(): lax.all_to_all(outgoing, 'tg', split_axis=0, concat_axis=0, tiled=True)]
    convert_element_type x2 -> x0, other arithmetic: 1.33 us -> none  [the longest x1 1.24 us: shards(): plane_of_slot.astype(F32).reshape(devices, planes)]
    concatenate x2 -> x0, other arithmetic: 1.2 us -> none  [window_order(): jnp.concatenate([blocks[:, :LANES].reshape(-1, LANES), blocks[:, LANES:]....]
  transfers between devices with their start and end apart: 7 -> 7, of which waited for: 1 -> 1; matrix products, arithmetic and copies ran while one was open for 2% -> 0% of each run, Pallas kernels for 47% -> 40%
where the time goes in v4:
time: 83 us; the launch traced here: 82.4 us
  Pallas kernels  41.4 us (50%)
  blocking collectives  15.9 us (19%)
  starting transfers between devices  10.8 us (13%)
  waiting for transfers between devices  9.62 us (12%)
  local copies, waits for them, and re-layouts  3.89 us (5%)
    pallas_call x1, Pallas kernels, shards(): pl.pallas_call(functools.partial(plane_kernel, planes), out_shape=jax.Sha...  29.5 us
    all_to_all x1, blocking collectives, shards(): lax.all_to_all(outgoing, 'tg', split_axis=0, concat_axis=0, tiled=True)  15.9 us
    all_to_all x1, waiting for transfers between devices, shards(): lax.all_to_all(sent, 'tg', split_axis=0, concat_axis=0, tiled=True)  9.61 us
    all_to_all x1, starting transfers between devices, shards(): lax.all_to_all(sent, 'tg', split_axis=0, concat_axis=0, tiled=True)  7.26 us
    pallas_call x1, Pallas kernels, shards(): pl.pallas_call(functools.partial(map_kernel, extent), out_shape=(jax.Shap...  3.39 us
    pallas_call x1, Pallas kernels, shards(): pl.pallas_call(functools.partial(inner_kernel, bands, volume, norm), out_...  3.26 us
    ppermute x3, starting transfers between devices, shards(): fields.append(lax.ppermute(received, 'band', ring))  2.98 us
    pallas_call x1, Pallas kernels, shards(): pl.pallas_call(functools.partial(wave_kernel, extent), out_shape=(jax.Sha...  2.73 us
  transfers between devices with their start and end apart: 7, of which 1 were waited for; matrix products, arithmetic and copies ran while one was open for 0% of the time, Pallas kernels for 40%

profile of v4, /device:TPU:0, one launch (start us, length us, event | category | flops | bytes accessed | tf_op | source)
XLA Modules:
  0.0 82.4 jit_solution(10449951003345248904)
XLA Ops:
  0.6 0.8 stack.14
  1.4 0.8 stack.13
  2.2 0.8 stack.12
  2.9 0.6 copy-done.7
  3.6 2.7 %wave_to_planes.1 = (f32[8,72,128]{2,1,0:T(8,128)}, f32[192,256]{1,0:T(8,128)}, f32[192,128]{1,0:T(8,128)}, bf16[384,256]{1,0:T(8,128)(2,1)}, bf16[384,256]{1,0:...) custom-call(s32[1]{0:T(128)} %bitcast.me_ref, s32[3,8,192]{2,1,0:T(8,128)} %copy-done.7, s32[1,192]{1,0:T(1,128)} %bitcast.10, ...), custom_call_target="tpu_custom_call" | custom-call | tf_op jit(solution)/shard_map/wave_to_planes/pallas_call | solution.py:454
  6.3 7.3 %all-to-all-start = ((f32[8,72,128]{2,1,0:T(8,128)}), f32[8,72,128]{2,1,0:T(8,128)S(1)}, u32[]{:S(2)}, u32[]{:S(2)}) async-start(f32[8,72,128]{2,1,0:T(8,128)} %get-tuple-element.19), calls=%async_computation | async-start | bytes 589824 | tf_op jit(solution)/shard_map/all_to_all | solution.py:470
  13.5 0.0 collective-permute-start.2
  13.6 9.6 %all-to-all-done.recv_ref.refs_5_ = f32[8,72,128]{2,1,0:T(8,128)S(1)} async-done(((f32[8,72,128]{2,1,0:T(8,128)}), f32[8,72,128]{2,1,0:T(8,128)S(1)}, u32[]{:S(2)}, u32[]{:S(2)}) %all-to-all-start) | async-done | bytes 294944 | tf_op jit(solution)/shard_map/all_to_all | solution.py:470
  23.2 0.0 collective-permute-start.5
  23.2 1.5 %collective-permute-start.4 = (f32[8,72,128]{2,1,0:T(8,128)S(1)}, f32[8,72,128]{2,1,0:T(8,128)S(1)}, u32[]{:S(2)}, u32[]{:S(2)}) collective-permute-start(f32[8,72,128]{2,1,0:T(8,128)S(1)} %all-to-all-done.recv_ref.refs_5_), channel_id=1, source_target_pairs={{16,0},{24,8},{0,16},{8,24},{17,1},{25,9},{1,17},{9,25},{18,2},{26... | collective-permute-start | bytes 884744 | tf_op jit(solution)/shard_map/ppermute | solution.py:509
  24.7 1.4 %collective-permute-start.3 = (f32[8,72,128]{2,1,0:T(8,128)S(1)}, f32[8,72,128]{2,1,0:T(8,128)S(1)}, u32[]{:S(2)}, u32[]{:S(2)}) collective-permute-start(f32[8,72,128]{2,1,0:T(8,128)S(1)} %all-to-all-done.recv_ref.refs_5_), channel_id=1, source_target_pairs={{8,0},{16,8},{24,16},{0,24},{9,1},{17,9},{25,17},{1,25},{10,2},{18... | collective-permute-start | bytes 884744 | tf_op jit(solution)/shard_map/ppermute | solution.py:509
  26.2 0.5 collective-permute-start.1
  26.7 0.0 collective-permute-done.2.refs_4_
  26.7 0.0 collective-permute-start
  26.7 3.4 %stick_map.1 = (s32[128,128]{1,0:T(8,128)}, s32[8,128]{1,0:T(8,128)}, s32[12,128]{1,0:T(8,128)}, s32[12,128]{1,0:T(8,128)}, s32[13,128]{1,0:T(8,128)}, /*index=5*/s32[13,128]{1,0:T(8,128)}) custom-call(s32[3,8,192]{2,1,0:T(8,128)} %copy-done.7), custom_call_target="tpu_custom_call" | custom-call | tf_op jit(solution)/shard_map/stick_map/pallas_call | solution.py:474
  30.1 0.0 copy-done
  30.1 29.5 %planes.1.refs_9_ = f32[8,80,128]{2,1,0:T(8,128)} custom-call(s32[8,128]{1,0:T(8,128)} %get-tuple-element.20.first_ref, s32[128,128]{1,0:T(8,128)} %get-tuple-element.21.map_ref, s32[12,128]{1,0:T(8,128)} %get-tuple-element.22.src_ref, s32[12,128]{1,0:T(8,128)} %get-tuple-element.23.dst_ref, s32[13,128]{1,0:T(8,128)} %get-tuple-element.24.row_ref, ...), custom_call_target="tpu_custom_call" | custom-call | tf_op jit(solution)/shard_map/planes/pallas_call | solution.py:488
  59.6 0.0 collective-permute-done.1.refs_3_
  59.6 0.0 collective-permute-done.refs_2_
  59.6 0.0 copy-start.6
  59.6 0.0 collective-permute-done.5.refs_8_
  59.7 0.0 collective-permute-done.4.refs_7_
  59.7 0.0 copy-start.2
  59.7 0.0 collective-permute-done.3.refs_6_
  59.7 0.6 copy-done.5
  60.3 0.1 copy-done.6
  60.3 0.1 copy-done.1
  60.4 0.1 copy-done.2
  60.5 0.1 copy-done.3
  60.7 3.3 %inner.1 = f32[8,80,128]{2,1,0:T(8,128)} custom-call(s32[1]{0:T(128)} %bitcast.3.band_ref, f32[192,256]{1,0:T(8,128)} %get-tuple-element.18.refs_0_.kc_ref, f32[192,2,128]{2,1,0:T(2,128)} %bitcast.9, f32[192,2,128]{2,1,0:T(2,128)} %copy-done.6, f32[192,2,128]{2,1,0:T(2,128)} %copy-done.5, f32[192,2,128]{2,1,0:T(2,128)} %copy-done.4, f32[8,72,128]{2,1,0:T(8,128)} %copy-done, ...), custom_call_target="tpu_custom_call" | custom-call | tf_op jit(solution)/shard_map/inner/pallas_call | solution.py:512
  63.9 15.9 %all_to_all.10.ret_ref = f32[8,80,128]{2,1,0:T(8,128)} all-to-all(f32[8,80,128]{2,1,0:T(8,128)} %inner.1), channel_id=1, replica_groups=mesh['band'=4,'tg'=8] {'tg'}, dimensions={0} | all-to-all | bytes 655360 | tf_op jit(solution)/shard_map/all_to_all | solution.py:521
  79.8 2.5 %planes_to_wave.1 = (f32[192,2,128]{2,1,0:T(2,128)}, f32[2,1,4]{2,1,0:T(1,128)}) custom-call(f32[192,128]{1,0:T(8,128)} %get-tuple-element.17.len_ref, f32[8,80,128]{2,1,0:T(8,128)} %all_to_all.10.ret_ref, f32[192,256]{1,0:T(8,128)} %get-tuple-element.18.refs_0_.kc_ref, bf16[384,256]{1,0:T(8,128)(2,1)} %get-tuple-element.26.whi_ref, ...), custom_call_target="tpu_custom_call" | custom-call | tf_op jit(solution)/shard_map/planes_to_wave/pallas_call | solution.py:522
  (10 shorter events, 0.0 us)
Async XLA Ops:
  2.9 0.6 copy-start.7
  6.3 16.9 %all-to-all-start = ((f32[8,72,128]{2,1,0:T(8,128)}), f32[8,72,128]{2,1,0:T(8,128)S(1)}, u32[]{:S(2)}, u32[]{:S(2)}) async-start(f32[8,72,128]{2,1,0:T(8,128)} %get-tuple-element.19), calls=%async_computation | async-start | bytes 589824 | tf_op jit(solution)/shard_map/all_to_all | solution.py:470
  13.5 13.1 %collective-permute-start.2 = (f32[192,2,128]{2,1,0:T(2,128)}, f32[192,2,128]{2,1,0:T(2,128)S(1)}, u32[]{:S(2)}, u32[]{:S(2)}) collective-permute-start(f32[192,2,128]{2,1,0:T(2,128)} %bitcast.6), channel_id=1, source_target_pairs={{24,0},{0,8},{8,16},{16,24},{25,1},{1,9},{9,17},{17,25},{26,2},{2,... | collective-permute-start | bytes 589832 | tf_op jit(solution)/shard_map/ppermute | solution.py:508
  23.2 6.9 %copy-start = (f32[8,72,128]{2,1,0:T(8,128)}, f32[8,72,128]{2,1,0:T(8,128)S(1)}, u32[]{:S(2)}) copy-start(f32[8,72,128]{2,1,0:T(8,128)S(1)} %all-to-all-done.recv_ref.refs_5_) | copy-start | bytes 884740
  23.2 36.5 %collective-permute-start.5 = (f32[8,72,128]{2,1,0:T(8,128)S(1)}, f32[8,72,128]{2,1,0:T(8,128)S(1)}, u32[]{:S(2)}, u32[]{:S(2)}) collective-permute-start(f32[8,72,128]{2,1,0:T(8,128)S(1)} %all-to-all-done.recv_ref.refs_5_), channel_id=1, source_target_pairs={{24,0},{0,8},{8,16},{16,24},{25,1},{1,9},{9,17},{17,25},{26,2},{2,... | collective-permute-start | bytes 884744 | tf_op jit(solution)/shard_map/ppermute | solution.py:509
  23.2 36.5 %collective-permute-start.4 = (f32[8,72,128]{2,1,0:T(8,128)S(1)}, f32[8,72,128]{2,1,0:T(8,128)S(1)}, u32[]{:S(2)}, u32[]{:S(2)}) collective-permute-start(f32[8,72,128]{2,1,0:T(8,128)S(1)} %all-to-all-done.recv_ref.refs_5_), channel_id=1, source_target_pairs={{16,0},{24,8},{0,16},{8,24},{17,1},{25,9},{1,17},{9,25},{18,2},{26... | collective-permute-start | bytes 884744 | tf_op jit(solution)/shard_map/ppermute | solution.py:509
  24.7 35.0 %collective-permute-start.3 = (f32[8,72,128]{2,1,0:T(8,128)S(1)}, f32[8,72,128]{2,1,0:T(8,128)S(1)}, u32[]{:S(2)}, u32[]{:S(2)}) collective-permute-start(f32[8,72,128]{2,1,0:T(8,128)S(1)} %all-to-all-done.recv_ref.refs_5_), channel_id=1, source_target_pairs={{8,0},{16,8},{24,16},{0,24},{9,1},{17,9},{25,17},{1,25},{10,2},{18... | collective-permute-start | bytes 884744 | tf_op jit(solution)/shard_map/ppermute | solution.py:509
  26.2 33.4 %collective-permute-start.1 = (f32[192,2,128]{2,1,0:T(2,128)}, f32[192,2,128]{2,1,0:T(2,128)S(1)}, u32[]{:S(2)}, u32[]{:S(2)}) collective-permute-start(f32[192,2,128]{2,1,0:T(2,128)} %bitcast.7), channel_id=1, source_target_pairs={{16,0},{24,8},{0,16},{8,24},{17,1},{25,9},{1,17},{9,25},{18,2},{26... | collective-permute-start | bytes 589832 | tf_op jit(solution)/shard_map/ppermute | solution.py:508
  26.7 33.0 %copy-start.4 = (f32[192,2,128]{2,1,0:T(2,128)}, f32[192,2,128]{2,1,0:T(2,128)S(1)}, u32[]{:S(2)}) copy-start(f32[192,2,128]{2,1,0:T(2,128)S(1)} %collective-permute-done.2.refs_4_) | copy-start | bytes 589828
  26.7 33.0 %collective-permute-start = (f32[192,2,128]{2,1,0:T(2,128)}, f32[192,2,128]{2,1,0:T(2,128)S(1)}, u32[]{:S(2)}, u32[]{:S(2)}) collective-permute-start(f32[192,2,128]{2,1,0:T(2,128)} %bitcast.8), channel_id=1, source_target_pairs={{8,0},{16,8},{24,16},{0,24},{9,1},{17,9},{25,17},{1,25},{10,2},{18... | collective-permute-start | bytes 589832 | tf_op jit(solution)/shard_map/ppermute | solution.py:508
  59.6 0.7 copy-start.5
  59.6 0.7 copy-start.6
  59.6 0.8 copy-start.1
  59.7 0.9 %copy-start.2 = (f32[8,72,128]{2,1,0:T(8,128)}, f32[8,72,128]{2,1,0:T(8,128)S(1)}, u32[]{:S(2)}) copy-start(f32[8,72,128]{2,1,0:T(8,128)S(1)} %collective-permute-done.4.refs_7_) | copy-start | bytes 884740
  59.7 1.0 %copy-start.3 = (f32[8,72,128]{2,1,0:T(8,128)}, f32[8,72,128]{2,1,0:T(8,128)S(1)}, u32[]{:S(2)}) copy-start(f32[8,72,128]{2,1,0:T(8,128)S(1)} %collective-permute-done.3.refs_6_) | copy-start | bytes 884740

commit v5 on v4

--- a/solution.py
+++ b/solution.py
@@ -58,34 +58,57 @@
     return hi, lo
 
 
+def row_blocks():
+    even = -(-(RADIUS + 1) // 16) * 16
+    odd = -(-RADIUS // 16) * 16
+    return even, odd
+
+
 @functools.cache
 def tables(extent):
     kept = 2 * RADIUS + 1
-    rows = up8(kept)
+    half = extent // 2
     grid = np.arange(extent)
     freq = np.arange(kept) - RADIUS
-    angle = 2.0 * np.pi * ((freq[:, None] * grid[None, :]) % extent) / extent
-    cos, sin = np.cos(angle), np.sin(angle)
-    pad_q = np.zeros((LANES - kept, extent))
-    cq, sq = np.concatenate([cos, pad_q]), np.concatenate([sin, pad_q])
-    pad_r = np.zeros((rows - kept, extent))
-    cr, sr = np.concatenate([cos, pad_r]), np.concatenate([sin, pad_r])
-    x_re = np.concatenate([cq, -sq], axis=0)
-    x_im = np.concatenate([sq, cq], axis=0)
-    y_fw = np.concatenate(
-        [np.concatenate([cr.T, -sr.T], axis=1), np.concatenate([sr.T, cr.T], axis=1)], axis=0
-    )
-    y_bw = y_fw.T.copy()
-    xb_re = x_re.T.copy()
-    xb_im = x_im.T.copy()
-    out = []
-    for table in (x_re, x_im, y_fw, y_bw, xb_re, xb_im):
-        out.extend(pair(table))
-    return tuple(out)
+
+    def angles(f, g):
+        a = 2.0 * np.pi * ((f[:, None] * g[None, :]) % extent) / extent
+        return np.cos(a), np.sin(a)
+
+    cos, sin = angles(freq, grid)
+    wide = 2 * LANES
+    x_table = np.zeros((wide, 2 * wide))
+    x_table[:kept, :extent] = cos
+    x_table[LANES:LANES + kept, :extent] = -sin
+    x_table[:kept, wide:wide + extent] = sin
+    x_table[LANES:LANES + kept, wide:wide + extent] = cos
+    forward, back = [], []
+    for offset, rows in zip((0, 1), row_blocks()):
+        cos, sin = angles(freq[offset::2], grid[:half])
+        count = cos.shape[0]
+        table = np.zeros((2 * half, rows))
+        table[:half, :count] = cos.T
+        table[half:, :count] = sin.T
+        hi, lo = pair(table)
+        forward.append(np.concatenate([hi, hi, lo], axis=1))
+        table = np.zeros((2 * rows, half))
+        table[:count] = cos
+        table[rows:rows + count] = sin
+        hi, lo = pair(table)
+        back.append(np.concatenate([hi, hi, lo], axis=1))
+    hi, lo = pair(x_table)
+    x_forward = np.concatenate([hi, hi, lo], axis=0)
+    hi, lo = pair(x_table.T.copy())
+    x_back = np.concatenate([hi, hi, lo], axis=0)
+    return (*forward, x_forward, x_back, *back)
 
 
 def params():
     return pltpu.CompilerParams(vmem_limit_bytes=VMEM_LIMIT)
+
+
+def cost(flops, nbytes):
+    return pl.CostEstimate(flops=int(flops), bytes_accessed=int(nbytes), transcendentals=0)
 
 
 def wave_kernel(extent, me_ref, info_ref, plane_ref, coef_ref, out_ref, kc_ref, len_ref, whi_ref, wlo_ref, sc_ref, ss_ref):
@@ -176,6 +199,7 @@
 
     nt = ((1,), (1,))
     own_row, own_col = signed(1), signed(2)
+    own_row = (own_row & 1) * row_blocks()[0] + (own_row >> 1)
     tall = lax.broadcasted_iota(jnp.int32, (LANES, total), 0)
     place = lax.broadcasted_iota(jnp.int32, (LANES, total), 1)
     in_col = tall == own_col
@@ -229,7 +253,7 @@
 
 def plane_kernel(
     planes, first_ref, map_ref, src_ref, dst_ref, row_ref, col_ref, recv_ref,
-    xr_hi, xr_lo, xi_hi, xi_lo, y_hi, y_lo, yb_hi, yb_lo, br_hi, br_lo, bi_hi, bi_lo,
+    y_even, y_odd, x_forward, x_back, back_even, back_odd,
     pot_hbm, out_ref, x_ref, s_ref, gr_ref, gi_ref, pot_ref, sem,
 ):
     devices = recv_ref.shape[0]
@@ -283,36 +307,56 @@
             grids[part][pl.ds(r + at * rows, 8, stride=rows), :] = value
 
     fetch.wait()
-    table_xr = (xr_hi[...], xr_lo[...])
-    table_xi = (xi_hi[...], xi_lo[...])
-    table_y = (y_hi[...], y_lo[...])
-    table_yb = (yb_hi[...], yb_lo[...])
-    table_br = (br_hi[...], br_lo[...])
-    table_bi = (bi_hi[...], bi_lo[...])
-
-    @pl.loop(0, planes // 2, unroll=3)
+    even_rows, odd_rows = row_blocks()
+    folded = extent // 2
+    group = 4 if planes % 4 == 0 else 2
+
+    def dot(x, y):
+        return jnp.dot(x, y, preferred_element_type=F32)
+
+    def stack(x, axis):
+        hi, lo = split(x)
+        return jnp.concatenate([hi, lo, hi], axis=axis)
+
+    def times_wave(both, cut, sign):
+        cos, sin = both[:cut], both[cut:]
+        re = cos[:, :LANES] - sign * sin[:, LANES:]
+        im = cos[:, LANES:] + sign * sin[:, :LANES]
+        return re, im
+
+    @pl.loop(0, planes // group)
     def _(step):
-        base = pl.multiple_of(step * 2 * rows, 8)
-        pick = pl.ds(base, 2 * rows)
-        spectrum = split(jnp.concatenate([gr_ref[pick, :], gi_ref[pick, :]], axis=1))
-        a_re = dot3(spectrum, table_xr)
-        a_im = dot3(spectrum, table_xi)
-        back_re, back_im = [], []
-        for t in range(2):
-            mid = jnp.concatenate(
-                [a_re[t * rows:(t + 1) * rows], a_im[t * rows:(t + 1) * rows]], axis=0
-            )
-            field = dot3(table_y, split(mid))
-            v = pot_ref[2 * step + t]
-            weighted = jnp.concatenate([field[:extent] * v, field[extent:] * v], axis=0)
-            back = dot3(table_yb, split(weighted))
-            back_re.append(back[:rows])
-            back_im.append(back[rows:])
-        b_re = split(jnp.concatenate(back_re, axis=0))
-        b_im = split(jnp.concatenate(back_im, axis=0))
-        back = dot3(b_re, table_br) + dot3(b_im, table_bi)
-        gr_ref[pick, :] = back[:, :LANES]
-        gi_ref[pick, :] = back[:, LANES:]
+        lines = []
+        for t in range(group):
+            base = pl.multiple_of((step * group + t) * rows, 16)
+            even, odd = pl.ds(base, even_rows), pl.ds(base + even_rows, odd_rows)
+            parts = []
+            for pick, table, size in ((even, y_even, even_rows), (odd, y_odd, odd_rows)):
+                spectrum = jnp.concatenate([gr_ref[pick, :], gi_ref[pick, :]], axis=1)
+                parts.append(times_wave(dot(table[...], stack(spectrum, 0)), folded, 1.0))
+            (e_re, e_im), (o_re, o_im) = parts
+            lines.append(jnp.concatenate([e_re + o_re, e_im + o_im], axis=1))
+            lines.append(jnp.concatenate([e_re - o_re, e_im - o_im], axis=1))
+        field = dot(stack(jnp.concatenate(lines, axis=0), 1), x_forward[...])
+        wide = field.shape[1] // 2
+        spare = jnp.zeros((extent, wide - extent), F32)
+        weighted = []
+        for t in range(group):
+            v = jnp.concatenate([pot_ref[step * group + t], spare], axis=1)
+            mine = field[t * extent:(t + 1) * extent]
+            weighted.append(jnp.concatenate([mine[:, :wide] * v, mine[:, wide:] * v], axis=1))
+        back = dot(stack(jnp.concatenate(weighted, axis=0), 1), x_back[...])
+        for t in range(group):
+            base = pl.multiple_of((step * group + t) * rows, 16)
+            even, odd = pl.ds(base, even_rows), pl.ds(base + even_rows, odd_rows)
+            upper = back[t * extent:t * extent + folded]
+            lower = back[t * extent + folded:(t + 1) * extent]
+            for pick, table, size, value in (
+                (even, back_even, even_rows, upper + lower), (odd, back_odd, odd_rows, upper - lower)
+            ):
+                re, im = times_wave(dot(table[...], stack(value, 0)), size, -1.0)
+                gr_ref[pick, :] = re
+                gi_ref[pick, :] = im
 
     @pl.loop(0, rows, unroll=8)
     def _(r):
@@ -434,8 +478,7 @@
     padded_planes = up8(planes)
     if sticks != LANES + LANES // 2 or devices % 2 or planes % 2:
         raise ValueError("sizes")
-    kept = 2 * RADIUS + 1
-    rows = up8(kept)
+    rows = sum(row_blocks())
     volume = 1.0 / (extent * extent * extent)
     me = lax.axis_index("tg").astype(jnp.int32)
     coef = coefficients.reshape(sticks, 2, padded)
@@ -482,13 +525,14 @@
             longer_list,
         ),
         compiler_params=params(),
+        cost_estimate=cost(4e9, 1e5),
         name="stick_map",
     )(info)
 
     weighted = pl.pallas_call(
         functools.partial(plane_kernel, planes),
         out_shape=jax.ShapeDtypeStruct((devices, block + 8, LANES), F32),
-        in_specs=[smem] + [vmem] * 18 + [pl.BlockSpec(memory_space=pl.ANY)],
+        in_specs=[smem] + [vmem] * 12 + [pl.BlockSpec(memory_space=pl.ANY)],
         out_specs=vmem,
         scratch_shapes=[
             pltpu.VMEM((windows, 2 * padded_planes, LANES), F32),
@@ -499,6 +543,7 @@
             pltpu.SemaphoreType.DMA,
         ],
         compiler_params=params(),
+        cost_estimate=cost(2e10, 1e7),
         name="planes",
     )(first, stick_map, source, target, row_w, col_w, received, *[jnp.asarray(t) for t in tables(extent)], potential)
 

time: 83 us -> 75.9 us (0.914)
  waiting for transfers between devices: 9.62 us -> 3.28 us
  starting transfers between devices: 10.8 us -> 13.2 us
  Pallas kernels: 41.4 us -> 39.6 us
  blocking collectives: 15.9 us -> 14.5 us
    all_to_all x1, waiting for transfers between devices: 9.61 us -> 3.26 us  [shards(): lax.all_to_all(sent, 'tg', split_axis=0, concat_axis=0, tiled=True)]
    ppermute x3, starting transfers between devices: 0.51 us -> 2.98 us  [shards(): coefs.append(lax.ppermute(coef, 'band', ring))]
    pallas_call x1, Pallas kernels: 29.5 us -> 27.7 us  [shards(): pl.pallas_call(functools.partial(plane_kernel, planes), out_shape=jax.Sha...]
    all_to_all x1, blocking collectives: 15.9 us -> 14.5 us  [shards(): lax.all_to_all(outgoing, 'tg', split_axis=0, concat_axis=0, tiled=True)]
  transfers between devices with their start and end apart: 7 -> 7, of which waited for: 1 -> 1; matrix products, arithmetic and copies ran while one was open for 0% -> 0% of each run, Pallas kernels for 40% -> 41%
where the time goes in v5:
time: 75.9 us; the launch traced here: 75.3 us
  Pallas kernels  39.6 us (52%)
  blocking collectives  14.5 us (19%)
  starting transfers between devices  13.2 us (17%)
  local copies, waits for them, and re-layouts  3.9 us (5%)
  waiting for transfers between devices  3.28 us (4%)
    pallas_call x1, Pallas kernels, shards(): pl.pallas_call(functools.partial(plane_kernel, planes), out_shape=jax.Sha...  27.7 us
    all_to_all x1, blocking collectives, shards(): lax.all_to_all(outgoing, 'tg', split_axis=0, concat_axis=0, tiled=True)  14.5 us
    all_to_all x1, starting transfers between devices, shards(): lax.all_to_all(sent, 'tg', split_axis=0, concat_axis=0, tiled=True)  7.25 us
    pallas_call x1, Pallas kernels, shards(): pl.pallas_call(functools.partial(map_kernel, extent), out_shape=(jax.Shap...  3.37 us
    pallas_call x1, Pallas kernels, shards(): pl.pallas_call(functools.partial(inner_kernel, bands, volume, norm), out_...  3.26 us
    all_to_all x1, waiting for transfers between devices, shards(): lax.all_to_all(sent, 'tg', split_axis=0, concat_axis=0, tiled=True)  3.26 us
    ppermute x3, starting transfers between devices, shards(): fields.append(lax.ppermute(received, 'band', ring))  2.99 us
    ppermute x3, starting transfers between devices, shards(): coefs.append(lax.ppermute(coef, 'band', ring))  2.98 us
  transfers between devices with their start and end apart: 7, of which 1 were waited for; matrix products, arithmetic and copies ran while one was open for 0% of the time, Pallas kernels for 41%

profile of v5, /device:TPU:0, one launch (start us, length us, event | category | flops | bytes accessed | tf_op | source)
XLA Modules:
  0.0 75.3 jit_solution(17046627982676642976)
XLA Ops:
  0.6 0.8 %stack.14 = s32[1,8,192]{2,1,0:T(8,128)S(1)} reshape(s32[1536]{0:T(1024)} %param.13) | data formatting | bytes 12288 | tf_op jit(solution)/shard_map/stack | solution.py:486
  1.4 0.8 %stack.13 = s32[1,8,192]{2,1,0:T(8,128)S(1)} reshape(s32[1536]{0:T(1024)} %param.14) | data formatting | bytes 12288 | tf_op jit(solution)/shard_map/stack | solution.py:486
  2.2 0.8 %stack.12 = s32[1,8,192]{2,1,0:T(8,128)S(1)} reshape(s32[1536]{0:T(1024)} %param.15) | data formatting | bytes 12288 | tf_op jit(solution)/shard_map/stack | solution.py:486
  2.9 0.6 copy-done.7
  3.6 2.7 %wave_to_planes.1 = (f32[8,72,128]{2,1,0:T(8,128)}, f32[192,256]{1,0:T(8,128)}, f32[192,128]{1,0:T(8,128)}, bf16[384,256]{1,0:T(8,128)(2,1)}, bf16[384,256]{1,0:...) custom-call(s32[1]{0:T(128)} %bitcast.me_ref, s32[3,8,192]{2,1,0:T(8,128)} %copy-done.7, s32[1,192]{1,0:T(1,128)} %bitcast.10, ...), custom_call_target="tpu_custom_call" | custom-call | tf_op jit(solution)/shard_map/wave_to_planes/pallas_call | solution.py:497
  6.3 7.3 %all-to-all-start = ((f32[8,72,128]{2,1,0:T(8,128)}), f32[8,72,128]{2,1,0:T(8,128)S(1)}, u32[]{:S(2)}, u32[]{:S(2)}) async-start(f32[8,72,128]{2,1,0:T(8,128)} %get-tuple-element.19), calls=%async_computation | async-start | bytes 589824 | tf_op jit(solution)/shard_map/all_to_all | solution.py:513
  13.5 0.0 collective-permute-start.2
  13.6 1.6 %collective-permute-start.1 = (f32[192,2,128]{2,1,0:T(2,128)}, f32[192,2,128]{2,1,0:T(2,128)S(1)}, u32[]{:S(2)}, u32[]{:S(2)}) collective-permute-start(f32[192,2,128]{2,1,0:T(2,128)} %bitcast.7), channel_id=1, source_target_pairs={{16,0},{24,8},{0,16},{8,24},{17,1},{25,9},{1,17},{9,25},{18,2},{26... | collective-permute-start | bytes 589832 | tf_op jit(solution)/shard_map/ppermute | solution.py:553
  15.1 1.4 %collective-permute-start = (f32[192,2,128]{2,1,0:T(2,128)}, f32[192,2,128]{2,1,0:T(2,128)S(1)}, u32[]{:S(2)}, u32[]{:S(2)}) collective-permute-start(f32[192,2,128]{2,1,0:T(2,128)} %bitcast.8), channel_id=1, source_target_pairs={{8,0},{16,8},{24,16},{0,24},{9,1},{17,9},{25,17},{1,25},{10,2},{18... | collective-permute-start | bytes 589832 | tf_op jit(solution)/shard_map/ppermute | solution.py:553
  16.5 3.4 %stick_map.1 = (s32[128,128]{1,0:T(8,128)}, s32[8,128]{1,0:T(8,128)}, s32[12,128]{1,0:T(8,128)}, s32[12,128]{1,0:T(8,128)}, s32[13,128]{1,0:T(8,128)}, /*index=5*/s32[13,128]{1,0:T(8,128)}) custom-call(s32[3,8,192]{2,1,0:T(8,128)} %copy-done.7), custom_call_target="tpu_custom_call" | custom-call | flops 4000000000 | bytes 100000 | tf_op jit(solution)/shard_map/stick_map/pallas_call | solution.py:517
  19.9 3.3 %all-to-all-done.recv_ref.refs_5_ = f32[8,72,128]{2,1,0:T(8,128)S(1)} async-done(((f32[8,72,128]{2,1,0:T(8,128)}), f32[8,72,128]{2,1,0:T(8,128)S(1)}, u32[]{:S(2)}, u32[]{:S(2)}) %all-to-all-start) | async-done | bytes 294944 | tf_op jit(solution)/shard_map/all_to_all | solution.py:513
  23.2 0.0 collective-permute-start.5
  23.2 1.5 %collective-permute-start.4 = (f32[8,72,128]{2,1,0:T(8,128)S(1)}, f32[8,72,128]{2,1,0:T(8,128)S(1)}, u32[]{:S(2)}, u32[]{:S(2)}) collective-permute-start(f32[8,72,128]{2,1,0:T(8,128)S(1)} %all-to-all-done.recv_ref.refs_5_), channel_id=1, source_target_pairs={{16,0},{24,8},{0,16},{8,24},{17,1},{25,9},{1,17},{9,25},{18,2},{26... | collective-permute-start | bytes 884744 | tf_op jit(solution)/shard_map/ppermute | solution.py:554
  24.7 0.0 collective-permute-done.2.refs_4_
  24.7 1.4 %collective-permute-start.3 = (f32[8,72,128]{2,1,0:T(8,128)S(1)}, f32[8,72,128]{2,1,0:T(8,128)S(1)}, u32[]{:S(2)}, u32[]{:S(2)}) collective-permute-start(f32[8,72,128]{2,1,0:T(8,128)S(1)} %all-to-all-done.recv_ref.refs_5_), channel_id=1, source_target_pairs={{8,0},{16,8},{24,16},{0,24},{9,1},{17,9},{25,17},{1,25},{10,2},{18... | collective-permute-start | bytes 884744 | tf_op jit(solution)/shard_map/ppermute | solution.py:554
  26.2 0.0 copy-done
  26.2 27.7 %planes.1.refs_9_ = f32[8,80,128]{2,1,0:T(8,128)} custom-call(s32[8,128]{1,0:T(8,128)} %get-tuple-element.20.first_ref, s32[128,128]{1,0:T(8,128)} %get-tuple-element.21.map_ref, s32[12,128]{1,0:T(8,128)} %get-tuple-element.22.src_ref, s32[12,128]{1,0:T(8,128)} %get-tuple-element.23.dst_ref, s32[13,128]{1,0:T(8,128)} %get-tuple-element.24.row_ref, ...), custom_call_target="tpu_custom_call" | custom-call | flops 20000000000 | bytes 10000000 | tf_op jit(solution)/shard_map/planes/pallas_call | solution.py:532
  53.9 0.0 copy-done.4
  53.9 0.0 collective-permute-done.1.refs_3_
  53.9 0.0 collective-permute-done.refs_2_
  53.9 0.0 copy-start.6
  53.9 0.0 collective-permute-done.5.refs_8_
  53.9 0.0 collective-permute-done.4.refs_7_
  54.0 0.0 collective-permute-done.3.refs_6_
  54.0 0.6 copy-done.5
  54.6 0.1 copy-done.6
  54.6 0.1 copy-done.1
  54.7 0.1 copy-done.2
  54.8 0.1 copy-done.3
  54.9 3.3 %inner.1 = f32[8,80,128]{2,1,0:T(8,128)} custom-call(s32[1]{0:T(128)} %bitcast.3.band_ref, f32[192,256]{1,0:T(8,128)} %get-tuple-element.18.refs_0_.kc_ref, f32[192,2,128]{2,1,0:T(2,128)} %bitcast.9, f32[192,2,128]{2,1,0:T(2,128)} %copy-done.6, f32[192,2,128]{2,1,0:T(2,128)} %copy-done.5, f32[192,2,128]{2,1,0:T(2,128)} %copy-done.4, f32[8,72,128]{2,1,0:T(8,128)} %copy-done, ...), custom_call_target="tpu_custom_call" | custom-call | tf_op jit(solution)/shard_map/inner/pallas_call | solution.py:557
  58.2 14.5 %all_to_all.10.ret_ref = f32[8,80,128]{2,1,0:T(8,128)} all-to-all(f32[8,80,128]{2,1,0:T(8,128)} %inner.1), channel_id=1, replica_groups=mesh['band'=4,'tg'=8] {'tg'}, dimensions={0} | all-to-all | bytes 655360 | tf_op jit(solution)/shard_map/all_to_all | solution.py:566
  72.7 2.5 %planes_to_wave.1 = (f32[192,2,128]{2,1,0:T(2,128)}, f32[2,1,4]{2,1,0:T(1,128)}) custom-call(f32[192,128]{1,0:T(8,128)} %get-tuple-element.17.len_ref, f32[8,80,128]{2,1,0:T(8,128)} %all_to_all.10.ret_ref, f32[192,256]{1,0:T(8,128)} %get-tuple-element.18.refs_0_.kc_ref, bf16[384,256]{1,0:T(8,128)(2,1)} %get-tuple-element.26.whi_ref, ...), custom_call_target="tpu_custom_call" | custom-call | tf_op jit(solution)/shard_map/planes_to_wave/pallas_call | solution.py:567
  (10 shorter events, 0.0 us)
Async XLA Ops:
  2.9 0.6 copy-start.7
  6.3 16.9 %all-to-all-start = ((f32[8,72,128]{2,1,0:T(8,128)}), f32[8,72,128]{2,1,0:T(8,128)S(1)}, u32[]{:S(2)}, u32[]{:S(2)}) async-start(f32[8,72,128]{2,1,0:T(8,128)} %get-tuple-element.19), calls=%async_computation | async-start | bytes 589824 | tf_op jit(solution)/shard_map/all_to_all | solution.py:513
  13.5 11.2 %collective-permute-start.2 = (f32[192,2,128]{2,1,0:T(2,128)}, f32[192,2,128]{2,1,0:T(2,128)S(1)}, u32[]{:S(2)}, u32[]{:S(2)}) collective-permute-start(f32[192,2,128]{2,1,0:T(2,128)} %bitcast.6), channel_id=1, source_target_pairs={{24,0},{0,8},{8,16},{16,24},{25,1},{1,9},{9,17},{17,25},{26,2},{2,... | collective-permute-start | bytes 589832 | tf_op jit(solution)/shard_map/ppermute | solution.py:553
  13.6 40.3 %collective-permute-start.1 = (f32[192,2,128]{2,1,0:T(2,128)}, f32[192,2,128]{2,1,0:T(2,128)S(1)}, u32[]{:S(2)}, u32[]{:S(2)}) collective-permute-start(f32[192,2,128]{2,1,0:T(2,128)} %bitcast.7), channel_id=1, source_target_pairs={{16,0},{24,8},{0,16},{8,24},{17,1},{25,9},{1,17},{9,25},{18,2},{26... | collective-permute-start | bytes 589832 | tf_op jit(solution)/shard_map/ppermute | solution.py:553
  15.1 38.8 %collective-permute-start = (f32[192,2,128]{2,1,0:T(2,128)}, f32[192,2,128]{2,1,0:T(2,128)S(1)}, u32[]{:S(2)}, u32[]{:S(2)}) collective-permute-start(f32[192,2,128]{2,1,0:T(2,128)} %bitcast.8), channel_id=1, source_target_pairs={{8,0},{16,8},{24,16},{0,24},{9,1},{17,9},{25,17},{1,25},{10,2},{18... | collective-permute-start | bytes 589832 | tf_op jit(solution)/shard_map/ppermute | solution.py:553
  23.2 3.0 %copy-start = (f32[8,72,128]{2,1,0:T(8,128)}, f32[8,72,128]{2,1,0:T(8,128)S(1)}, u32[]{:S(2)}) copy-start(f32[8,72,128]{2,1,0:T(8,128)S(1)} %all-to-all-done.recv_ref.refs_5_) | copy-start | bytes 884740
  23.2 30.7 %collective-permute-start.5 = (f32[8,72,128]{2,1,0:T(8,128)S(1)}, f32[8,72,128]{2,1,0:T(8,128)S(1)}, u32[]{:S(2)}, u32[]{:S(2)}) collective-permute-start(f32[8,72,128]{2,1,0:T(8,128)S(1)} %all-to-all-done.recv_ref.refs_5_), channel_id=1, source_target_pairs={{24,0},{0,8},{8,16},{16,24},{25,1},{1,9},{9,17},{17,25},{26,2},{2,... | collective-permute-start | bytes 884744 | tf_op jit(solution)/shard_map/ppermute | solution.py:554
  23.2 30.8 %collective-permute-start.4 = (f32[8,72,128]{2,1,0:T(8,128)S(1)}, f32[8,72,128]{2,1,0:T(8,128)S(1)}, u32[]{:S(2)}, u32[]{:S(2)}) collective-permute-start(f32[8,72,128]{2,1,0:T(8,128)S(1)} %all-to-all-done.recv_ref.refs_5_), channel_id=1, source_target_pairs={{16,0},{24,8},{0,16},{8,24},{17,1},{25,9},{1,17},{9,25},{18,2},{26... | collective-permute-start | bytes 884744 | tf_op jit(solution)/shard_map/ppermute | solution.py:554
  24.7 29.1 %copy-start.4 = (f32[192,2,128]{2,1,0:T(2,128)}, f32[192,2,128]{2,1,0:T(2,128)S(1)}, u32[]{:S(2)}) copy-start(f32[192,2,128]{2,1,0:T(2,128)S(1)} %collective-permute-done.2.refs_4_) | copy-start | bytes 589828
  24.7 29.2 %collective-permute-start.3 = (f32[8,72,128]{2,1,0:T(8,128)S(1)}, f32[8,72,128]{2,1,0:T(8,128)S(1)}, u32[]{:S(2)}, u32[]{:S(2)}) collective-permute-start(f32[8,72,128]{2,1,0:T(8,128)S(1)} %all-to-all-done.recv_ref.refs_5_), channel_id=1, source_target_pairs={{8,0},{16,8},{24,16},{0,24},{9,1},{17,9},{25,17},{1,25},{10,2},{18... | collective-permute-start | bytes 884744 | tf_op jit(solution)/shard_map/ppermute | solution.py:554
  53.9 0.7 copy-start.5
  53.9 0.7 copy-start.6
  53.9 0.8 %copy-start.1 = (f32[8,72,128]{2,1,0:T(8,128)}, f32[8,72,128]{2,1,0:T(8,128)S(1)}, u32[]{:S(2)}) copy-start(f32[8,72,128]{2,1,0:T(8,128)S(1)} %collective-permute-done.5.refs_8_) | copy-start | bytes 884740
  53.9 0.9 %copy-start.2 = (f32[8,72,128]{2,1,0:T(8,128)}, f32[8,72,128]{2,1,0:T(8,128)S(1)}, u32[]{:S(2)}) copy-start(f32[8,72,128]{2,1,0:T(8,128)S(1)} %collective-permute-done.4.refs_7_) | copy-start | bytes 884740
  54.0 1.0 %copy-start.3 = (f32[8,72,128]{2,1,0:T(8,128)}, f32[8,72,128]{2,1,0:T(8,128)S(1)}, u32[]{:S(2)}) copy-start(f32[8,72,128]{2,1,0:T(8,128)S(1)} %collective-permute-done.3.refs_6_) | copy-start | bytes 884740

commit v6 on v5

--- a/solution.py
+++ b/solution.py
@@ -111,14 +111,23 @@
     return pl.CostEstimate(flops=int(flops), bytes_accessed=int(nbytes), transcendentals=0)
 
 
-def wave_kernel(extent, me_ref, info_ref, plane_ref, coef_ref, out_ref, kc_ref, len_ref, whi_ref, wlo_ref, sc_ref, ss_ref):
+def wave_kernel(extent, me_ref, length_ref, row_ref, col_ref, plane_ref, coef_ref, out_ref, kc_ref, len_ref, whi_ref, wlo_ref, sc_ref, ss_ref):
     devices = out_ref.shape[0]
     sticks, _, padded = coef_ref.shape
     padded_planes = plane_ref.shape[1] // devices
     me = me_ref[0]
-    length_row = info_ref[0, pl.ds(me, 1), :].astype(F32)
-    at_row = info_ref[1, pl.ds(me, 1), :]
-    at_col = info_ref[2, pl.ds(me, 1), :]
+    half = LANES // 2
+    lead = (me * sticks) // LANES
+    odd = (me * sticks) % LANES != 0
+
+    def own(ref):
+        first, second = ref[pl.ds(lead, 1), :], ref[pl.ds(lead + 1, 1), :]
+        both = jnp.concatenate([first, second], axis=1)
+        return jnp.where(odd, both[:, half:], both[:, :sticks])
+
+    length_row = own(length_ref).astype(F32)
+    at_row = own(row_ref)
+    at_col = own(col_ref)
     at_row = jnp.where(at_row <= RADIUS, at_row, at_row - extent).astype(F32)
     at_col = jnp.where(at_col <= RADIUS, at_col, at_col - extent).astype(F32)
     square_row = at_row * at_row + at_col * at_col
@@ -176,20 +185,21 @@
         )
 
 
-def window_row(values):
-    devices = values.shape[0]
-    parts = [values[d:d + 1, :LANES] for d in range(devices)]
-    parts += [values[d:d + 1, LANES:] for d in range(devices)]
+def window_row(values, sticks):
+    line = jnp.concatenate([values[i:i + 1] for i in range(values.shape[0])], axis=1)
+    starts = range(0, line.shape[1], sticks)
+    parts = [line[:, at:at + LANES] for at in starts]
+    parts += [line[:, at + LANES:at + sticks] for at in starts]
     return jnp.concatenate(parts, axis=1)
 
 
-def map_kernel(extent, info_ref, map_ref, first_ref, src_ref, dst_ref, row_ref, col_ref):
+def map_kernel(extent, sticks, in_row_ref, in_col_ref, map_ref, first_ref, src_ref, dst_ref, row_ref, col_ref):
     windows = src_ref.shape[0]
     total = windows * LANES
 
-    def signed(part):
-        value = info_ref[part]
-        return window_row(jnp.where(value <= RADIUS, value, value - extent) + RADIUS)
+    def signed(ref):
+        value = ref[...]
+        return window_row(jnp.where(value <= RADIUS, value, value - extent) + RADIUS, sticks)
 
     def dot(x, y, dims=((1,), (0,))):
         return lax.dot_general(x, y, (dims, ((), ())), preferred_element_type=F32)
@@ -198,7 +208,7 @@
         return condition.astype(F32).astype(BF16)
 
     nt = ((1,), (1,))
-    own_row, own_col = signed(1), signed(2)
+    own_row, own_col = signed(in_row_ref), signed(in_col_ref)
     own_row = (own_row & 1) * row_blocks()[0] + (own_row >> 1)
     tall = lax.broadcasted_iota(jnp.int32, (LANES, total), 0)
     place = lax.broadcasted_iota(jnp.int32, (LANES, total), 1)
@@ -309,7 +319,7 @@
     fetch.wait()
     even_rows, odd_rows = row_blocks()
     folded = extent // 2
-    group = 4 if planes % 4 == 0 else 2
+    group = 2
 
     def dot(x, y):
         return jnp.dot(x, y, preferred_element_type=F32)
@@ -324,7 +334,7 @@
         im = cos[:, LANES:] + sign * sin[:, :LANES]
         return re, im
 
-    @pl.loop(0, planes // group)
+    @pl.loop(0, planes // group, unroll=3)
     def _(step):
         lines = []
         for t in range(group):
@@ -483,7 +493,7 @@
     me = lax.axis_index("tg").astype(jnp.int32)
     coef = coefficients.reshape(sticks, 2, padded)
 
-    info = jnp.stack([stick_length, stick_row, stick_col]).reshape(3, devices, sticks)
+    length, row, col = (v.reshape(-1, LANES) for v in (stick_length, stick_row, stick_col))
     slots = plane_of_slot.reshape(devices, planes)
     if padded_planes > planes:
         slots = jnp.pad(slots, ((0, 0), (0, padded_planes - planes)), constant_values=-1)
@@ -505,17 +515,17 @@
             jax.ShapeDtypeStruct((total_planes, sticks), F32),
             jax.ShapeDtypeStruct((total_planes, sticks), F32),
         ),
-        in_specs=[smem] + [vmem] * 3,
+        in_specs=[smem] + [vmem] * 5,
         compiler_params=params(),
         name="wave_to_planes",
-    )(me.reshape(1), info, slots, coef)
+    )(me.reshape(1), length, row, col, slots, coef)
 
     received = lax.all_to_all(sent, "tg", split_axis=0, concat_axis=0, tiled=True)
 
     window_list = jax.ShapeDtypeStruct((windows, LANES), jnp.int32)
     longer_list = jax.ShapeDtypeStruct((windows + 1, LANES), jnp.int32)
     stick_map, first, source, target, row_w, col_w = pl.pallas_call(
-        functools.partial(map_kernel, extent),
+        functools.partial(map_kernel, extent, sticks),
         out_shape=(
             jax.ShapeDtypeStruct((LANES, LANES), jnp.int32),
             jax.ShapeDtypeStruct((8, LANES), jnp.int32),
@@ -527,7 +537,7 @@
         compiler_params=params(),
         cost_estimate=cost(4e9, 1e5),
         name="stick_map",
-    )(info)
+    )(row, col)
 
     weighted = pl.pallas_call(
         functools.partial(plane_kernel, planes),

time: 75.9 us -> 74.6 us (0.983)
  local copies, waits for them, and re-layouts: 3.9 us -> 0.97 us
  Pallas kernels: 39.6 us -> 41.5 us
    another operation x4 -> x0, local copies, waits for them, and re-layouts: 2.31 us -> none  [shards(): jnp.stack([stick_length, stick_row, stick_col]).reshape(3, devices, sticks)]
    pallas_call x1, Pallas kernels: 27.7 us -> 29.3 us  [shards(): pl.pallas_call(functools.partial(plane_kernel, planes), out_shape=jax.Sha...]
    unnamed x18 -> x14, local copies, waits for them, and re-layouts: 1.59 us -> 0.97 us
  transfers between devices with their start and end apart: 7 -> 7, of which waited for: 1 -> 1; matrix products, arithmetic and copies ran while one was open for 0% -> 0% of each run, Pallas kernels for 41% -> 44%
where the time goes in v6:
time: 74.6 us; the launch traced here: 74.2 us
  Pallas kernels  41.5 us (56%)
  blocking collectives  14.5 us (19%)
  starting transfers between devices  13.2 us (18%)
  waiting for transfers between devices  3.21 us (4%)
  local copies, waits for them, and re-layouts  0.97 us (1%)
  between operations  0.75 us (1%)
    pallas_call x1, Pallas kernels, shards(): pl.pallas_call(functools.partial(plane_kernel, planes), out_shape=jax.Sha...  29.3 us
    all_to_all x1, blocking collectives, shards(): lax.all_to_all(outgoing, 'tg', split_axis=0, concat_axis=0, tiled=True)  14.5 us
    all_to_all x1, starting transfers between devices, shards(): lax.all_to_all(sent, 'tg', split_axis=0, concat_axis=0, tiled=True)  7.25 us
    pallas_call x1, Pallas kernels, shards(): pl.pallas_call(functools.partial(map_kernel, extent, sticks), out_shape=(...  3.44 us
    pallas_call x1, Pallas kernels, shards(): pl.pallas_call(functools.partial(inner_kernel, bands, volume, norm), out_...  3.27 us
    all_to_all x1, waiting for transfers between devices, shards(): lax.all_to_all(sent, 'tg', split_axis=0, concat_axis=0, tiled=True)  3.19 us
    ppermute x3, starting transfers between devices, shards(): fields.append(lax.ppermute(received, 'band', ring))  2.99 us
    ppermute x3, starting transfers between devices, shards(): coefs.append(lax.ppermute(coef, 'band', ring))  2.98 us
  transfers between devices with their start and end apart: 7, of which 1 were waited for; matrix products, arithmetic and copies ran while one was open for 0% of the time, Pallas kernels for 44%

profile of v6, /device:TPU:0, one launch (start us, length us, event | category | flops | bytes accessed | tf_op | source)
XLA Modules:
  0.0 74.2 jit_solution(6024903459326094116)
XLA Ops:
  0.6 2.9 %wave_to_planes.1 = (f32[8,72,128]{2,1,0:T(8,128)}, f32[192,256]{1,0:T(8,128)}, f32[192,128]{1,0:T(8,128)}, bf16[384,256]{1,0:T(8,128)(2,1)}, bf16[384,256]{1,0:...) custom-call(s32[1]{0:T(128)} %bitcast.me_ref, s32[12,128]{1,0:T(8,128)} %bitcast.13, s32[12,128]{1,0:T(8,128)} %bitcast.14, ...), custom_call_target="tpu_custom_call" | custom-call | tf_op jit(solution)/shard_map/wave_to_planes/pallas_call | solution.py:507
  3.5 7.3 %all-to-all-start = ((f32[8,72,128]{2,1,0:T(8,128)}), f32[8,72,128]{2,1,0:T(8,128)S(1)}, u32[]{:S(2)}, u32[]{:S(2)}) async-start(f32[8,72,128]{2,1,0:T(8,128)} %get-tuple-element.19), calls=%async_computation | async-start | bytes 589824 | tf_op jit(solution)/shard_map/all_to_all | solution.py:523
  10.8 0.0 collective-permute-start.2
  10.8 1.6 %collective-permute-start.1 = (f32[192,2,128]{2,1,0:T(2,128)}, f32[192,2,128]{2,1,0:T(2,128)S(1)}, u32[]{:S(2)}, u32[]{:S(2)}) collective-permute-start(f32[192,2,128]{2,1,0:T(2,128)} %bitcast.10), channel_id=1, source_target_pairs={{16,0},{24,8},{0,16},{8,24},{17,1},{25,9},{1,17},{9,25},{18,2},{26... | collective-permute-start | bytes 589832 | tf_op jit(solution)/shard_map/ppermute | solution.py:563
  12.4 1.4 %collective-permute-start = (f32[192,2,128]{2,1,0:T(2,128)}, f32[192,2,128]{2,1,0:T(2,128)S(1)}, u32[]{:S(2)}, u32[]{:S(2)}) collective-permute-start(f32[192,2,128]{2,1,0:T(2,128)} %bitcast.11), channel_id=1, source_target_pairs={{8,0},{16,8},{24,16},{0,24},{9,1},{17,9},{25,17},{1,25},{10,2},{18... | collective-permute-start | bytes 589832 | tf_op jit(solution)/shard_map/ppermute | solution.py:563
  13.8 3.4 %stick_map.1 = (s32[128,128]{1,0:T(8,128)}, s32[8,128]{1,0:T(8,128)}, s32[12,128]{1,0:T(8,128)}, s32[12,128]{1,0:T(8,128)}, s32[13,128]{1,0:T(8,128)}, /*index=5*/s32[13,128]{1,0:T(8,128)}) custom-call(s32[12,128]{1,0:T(8,128)} %bitcast.15, s32[12,128]{1,0:T(8,128)} %bitcast.17), custom_call_target="tpu_custom_call" | custom-call | flops 4000000000 | bytes 100000 | tf_op jit(solution)/shard_map/stick_map/pallas_call | solution.py:527
  17.2 3.2 %all-to-all-done.recv_ref.refs_5_ = f32[8,72,128]{2,1,0:T(8,128)S(1)} async-done(((f32[8,72,128]{2,1,0:T(8,128)}), f32[8,72,128]{2,1,0:T(8,128)S(1)}, u32[]{:S(2)}, u32[]{:S(2)}) %all-to-all-start) | async-done | bytes 294944 | tf_op jit(solution)/shard_map/all_to_all | solution.py:523
  20.4 0.0 collective-permute-start.5
  20.4 1.5 %collective-permute-start.4 = (f32[8,72,128]{2,1,0:T(8,128)S(1)}, f32[8,72,128]{2,1,0:T(8,128)S(1)}, u32[]{:S(2)}, u32[]{:S(2)}) collective-permute-start(f32[8,72,128]{2,1,0:T(8,128)S(1)} %all-to-all-done.recv_ref.refs_5_), channel_id=1, source_target_pairs={{16,0},{24,8},{0,16},{8,24},{17,1},{25,9},{1,17},{9,25},{18,2},{26... | collective-permute-start | bytes 884744 | tf_op jit(solution)/shard_map/ppermute | solution.py:564
  22.0 0.0 collective-permute-done.2.refs_4_
  22.0 1.4 %collective-permute-start.3 = (f32[8,72,128]{2,1,0:T(8,128)S(1)}, f32[8,72,128]{2,1,0:T(8,128)S(1)}, u32[]{:S(2)}, u32[]{:S(2)}) collective-permute-start(f32[8,72,128]{2,1,0:T(8,128)S(1)} %all-to-all-done.recv_ref.refs_5_), channel_id=1, source_target_pairs={{8,0},{16,8},{24,16},{0,24},{9,1},{17,9},{25,17},{1,25},{10,2},{18... | collective-permute-start | bytes 884744 | tf_op jit(solution)/shard_map/ppermute | solution.py:564
  23.4 0.0 copy-done
  23.4 29.3 %planes.1.refs_9_ = f32[8,80,128]{2,1,0:T(8,128)} custom-call(s32[8,128]{1,0:T(8,128)} %get-tuple-element.20.first_ref, s32[128,128]{1,0:T(8,128)} %get-tuple-element.21.map_ref, s32[12,128]{1,0:T(8,128)} %get-tuple-element.22.src_ref, s32[12,128]{1,0:T(8,128)} %get-tuple-element.23.dst_ref, s32[13,128]{1,0:T(8,128)} %get-tuple-element.24.row_ref, ...), custom_call_target="tpu_custom_call" | custom-call | flops 20000000000 | bytes 10000000 | tf_op jit(solution)/shard_map/planes/pallas_call | solution.py:542
  52.8 0.0 copy-done.4
  52.8 0.0 collective-permute-done.1.refs_3_
  52.8 0.0 copy-start.5
  52.8 0.0 collective-permute-done.refs_2_
  52.8 0.0 copy-start.6
  52.8 0.0 collective-permute-done.5.refs_8_
  52.8 0.0 copy-start.1
  52.8 0.0 collective-permute-done.4.refs_7_
  52.8 0.0 copy-start.2
  52.8 0.0 collective-permute-done.3.refs_6_
  52.9 0.0 copy-start.3
  52.9 0.6 copy-done.5
  53.5 0.1 copy-done.6
  53.5 0.1 copy-done.1
  53.6 0.1 copy-done.2
  53.7 0.1 copy-done.3
  53.8 3.3 %inner.1 = f32[8,80,128]{2,1,0:T(8,128)} custom-call(s32[1]{0:T(128)} %bitcast.6.band_ref, f32[192,256]{1,0:T(8,128)} %get-tuple-element.18.refs_0_.kc_ref, f32[192,2,128]{2,1,0:T(2,128)} %bitcast.12, f32[192,2,128]{2,1,0:T(2,128)} %copy-done.6, f32[192,2,128]{2,1,0:T(2,128)} %copy-done.5, f32[192,2,128]{2,1,0:T(2,128)} %copy-done.4, f32[8,72,128]{2,1,0:T(8,128)} %copy-done, ...), custom_call_target="tpu_custom_call" | custom-call | tf_op jit(solution)/shard_map/inner/pallas_call | solution.py:567
  57.1 14.5 %all_to_all.10.ret_ref = f32[8,80,128]{2,1,0:T(8,128)} all-to-all(f32[8,80,128]{2,1,0:T(8,128)} %inner.1), channel_id=1, replica_groups=mesh['band'=4,'tg'=8] {'tg'}, dimensions={0} | all-to-all | bytes 655360 | tf_op jit(solution)/shard_map/all_to_all | solution.py:576
  71.6 2.5 %planes_to_wave.1 = (f32[192,2,128]{2,1,0:T(2,128)}, f32[2,1,4]{2,1,0:T(1,128)}) custom-call(f32[192,128]{1,0:T(8,128)} %get-tuple-element.17.len_ref, f32[8,80,128]{2,1,0:T(8,128)} %all_to_all.10.ret_ref, f32[192,256]{1,0:T(8,128)} %get-tuple-element.18.refs_0_.kc_ref, bf16[384,256]{1,0:T(8,128)(2,1)} %get-tuple-element.26.whi_ref, ...), custom_call_target="tpu_custom_call" | custom-call | tf_op jit(solution)/shard_map/planes_to_wave/pallas_call | solution.py:577
  (2 shorter events, 0.0 us)
Async XLA Ops:
  3.5 16.9 %all-to-all-start = ((f32[8,72,128]{2,1,0:T(8,128)}), f32[8,72,128]{2,1,0:T(8,128)S(1)}, u32[]{:S(2)}, u32[]{:S(2)}) async-start(f32[8,72,128]{2,1,0:T(8,128)} %get-tuple-element.19), calls=%async_computation | async-start | bytes 589824 | tf_op jit(solution)/shard_map/all_to_all | solution.py:523
  10.8 11.2 %collective-permute-start.2 = (f32[192,2,128]{2,1,0:T(2,128)}, f32[192,2,128]{2,1,0:T(2,128)S(1)}, u32[]{:S(2)}, u32[]{:S(2)}) collective-permute-start(f32[192,2,128]{2,1,0:T(2,128)} %bitcast.9), channel_id=1, source_target_pairs={{24,0},{0,8},{8,16},{16,24},{25,1},{1,9},{9,17},{17,25},{26,2},{2,... | collective-permute-start | bytes 589832 | tf_op jit(solution)/shard_map/ppermute | solution.py:563
  10.8 42.0 %collective-permute-start.1 = (f32[192,2,128]{2,1,0:T(2,128)}, f32[192,2,128]{2,1,0:T(2,128)S(1)}, u32[]{:S(2)}, u32[]{:S(2)}) collective-permute-start(f32[192,2,128]{2,1,0:T(2,128)} %bitcast.10), channel_id=1, source_target_pairs={{16,0},{24,8},{0,16},{8,24},{17,1},{25,9},{1,17},{9,25},{18,2},{26... | collective-permute-start | bytes 589832 | tf_op jit(solution)/shard_map/ppermute | solution.py:563
  12.4 40.4 %collective-permute-start = (f32[192,2,128]{2,1,0:T(2,128)}, f32[192,2,128]{2,1,0:T(2,128)S(1)}, u32[]{:S(2)}, u32[]{:S(2)}) collective-permute-start(f32[192,2,128]{2,1,0:T(2,128)} %bitcast.11), channel_id=1, source_target_pairs={{8,0},{16,8},{24,16},{0,24},{9,1},{17,9},{25,17},{1,25},{10,2},{18... | collective-permute-start | bytes 589832 | tf_op jit(solution)/shard_map/ppermute | solution.py:563
  20.4 3.0 %copy-start = (f32[8,72,128]{2,1,0:T(8,128)}, f32[8,72,128]{2,1,0:T(8,128)S(1)}, u32[]{:S(2)}) copy-start(f32[8,72,128]{2,1,0:T(8,128)S(1)} %all-to-all-done.recv_ref.refs_5_) | copy-start | bytes 884740
  20.4 32.4 %collective-permute-start.5 = (f32[8,72,128]{2,1,0:T(8,128)S(1)}, f32[8,72,128]{2,1,0:T(8,128)S(1)}, u32[]{:S(2)}, u32[]{:S(2)}) collective-permute-start(f32[8,72,128]{2,1,0:T(8,128)S(1)} %all-to-all-done.recv_ref.refs_5_), channel_id=1, source_target_pairs={{24,0},{0,8},{8,16},{16,24},{25,1},{1,9},{9,17},{17,25},{26,2},{2,... | collective-permute-start | bytes 884744 | tf_op jit(solution)/shard_map/ppermute | solution.py:564
  20.4 32.4 %collective-permute-start.4 = (f32[8,72,128]{2,1,0:T(8,128)S(1)}, f32[8,72,128]{2,1,0:T(8,128)S(1)}, u32[]{:S(2)}, u32[]{:S(2)}) collective-permute-start(f32[8,72,128]{2,1,0:T(8,128)S(1)} %all-to-all-done.recv_ref.refs_5_), channel_id=1, source_target_pairs={{16,0},{24,8},{0,16},{8,24},{17,1},{25,9},{1,17},{9,25},{18,2},{26... | collective-permute-start | bytes 884744 | tf_op jit(solution)/shard_map/ppermute | solution.py:564
  22.0 30.8 %copy-start.4 = (f32[192,2,128]{2,1,0:T(2,128)}, f32[192,2,128]{2,1,0:T(2,128)S(1)}, u32[]{:S(2)}) copy-start(f32[192,2,128]{2,1,0:T(2,128)S(1)} %collective-permute-done.2.refs_4_) | copy-start | bytes 589828
  22.0 30.9 %collective-permute-start.3 = (f32[8,72,128]{2,1,0:T(8,128)S(1)}, f32[8,72,128]{2,1,0:T(8,128)S(1)}, u32[]{:S(2)}, u32[]{:S(2)}) collective-permute-start(f32[8,72,128]{2,1,0:T(8,128)S(1)} %all-to-all-done.recv_ref.refs_5_), channel_id=1, source_target_pairs={{8,0},{16,8},{24,16},{0,24},{9,1},{17,9},{25,17},{1,25},{10,2},{18... | collective-permute-start | bytes 884744 | tf_op jit(solution)/shard_map/ppermute | solution.py:564
  52.8 0.7 copy-start.5
  52.8 0.7 copy-start.6
  52.8 0.8 %copy-start.1 = (f32[8,72,128]{2,1,0:T(8,128)}, f32[8,72,128]{2,1,0:T(8,128)S(1)}, u32[]{:S(2)}) copy-start(f32[8,72,128]{2,1,0:T(8,128)S(1)} %collective-permute-done.5.refs_8_) | copy-start | bytes 884740
  52.8 0.9 %copy-start.2 = (f32[8,72,128]{2,1,0:T(8,128)}, f32[8,72,128]{2,1,0:T(8,128)S(1)}, u32[]{:S(2)}) copy-start(f32[8,72,128]{2,1,0:T(8,128)S(1)} %collective-permute-done.4.refs_7_) | copy-start | bytes 884740
  52.9 1.0 %copy-start.3 = (f32[8,72,128]{2,1,0:T(8,128)}, f32[8,72,128]{2,1,0:T(8,128)S(1)}, u32[]{:S(2)}) copy-start(f32[8,72,128]{2,1,0:T(8,128)S(1)} %collective-permute-done.3.refs_6_) | copy-start | bytes 884740

commit v7 on v6

--- a/solution.py
+++ b/solution.py
@@ -319,7 +319,7 @@
     fetch.wait()
     even_rows, odd_rows = row_blocks()
     folded = extent // 2
-    group = 2
+    group = next(g for g in (8, 4, 2) if planes % g == 0)
 
     def dot(x, y):
         return jnp.dot(x, y, preferred_element_type=F32)
@@ -334,7 +334,7 @@
         im = cos[:, LANES:] + sign * sin[:, :LANES]
         return re, im
 
-    @pl.loop(0, planes // group, unroll=3)
+    @pl.loop(0, planes // group)
     def _(step):
         lines = []
         for t in range(group):
@@ -399,17 +399,17 @@
         out_ref[d, 3 * padded_planes:, :] = jnp.zeros((8, LANES), F32)
 
 
-def inner_kernel(bands, volume, norm, band_ref, *refs):
+def inner_kernel(bands, volume, norm, place_ref, *refs):
     kc_ref = refs[0]
     coefs = refs[1:1 + bands]
     fields = refs[1 + bands:1 + 2 * bands]
     in_ref = refs[1 + 2 * bands]
-    out_ref = refs[2 + 2 * bands]
+    out_refs = refs[2 + 2 * bands:]
     devices = in_ref.shape[0]
     padded_planes = (in_ref.shape[1] - 8) // 3
     half = LANES // 2
     padded = coefs[0].shape[2]
-    me = band_ref[0]
+    me, mine = place_ref[0], place_ref[1]
     low = lax.broadcasted_iota(jnp.int32, (padded_planes, LANES), 1) < half
 
     def fold(x):
@@ -444,32 +444,32 @@
             partial = sums[m][part] + volume * local[m][part]
             scalar = jnp.sum(jnp.sum(partial, axis=1, keepdims=True), axis=0, keepdims=True)
             tile = jnp.where((lane == at) & (row == part), sign * norm * scalar, tile)
-    for d in range(devices):
-        out_ref[d, 0:3 * padded_planes, :] = in_ref[d, 0:3 * padded_planes, :]
-        out_ref[d, 3 * padded_planes:, :] = tile
-
-
-def final_kernel(volume, len_ref, ret_ref, kc_ref, whi_ref, wlo_ref, sc_ref, ss_ref, out_ref, sub_ref):
-    devices = ret_ref.shape[0]
-    padded_planes = (ret_ref.shape[1] - 8) // 3
+    for k in range(devices):
+        out_refs[k][0:3 * padded_planes, :] = in_ref[lax.rem(mine + k, devices), 0:3 * padded_planes, :]
+        out_refs[k][3 * padded_planes:, :] = tile
+
+
+def final_kernel(volume, devices, me_ref, len_ref, *refs):
+    ret_refs = refs[:devices]
+    kc_ref, whi_ref, wlo_ref, sc_ref, ss_ref, out_ref, sub_ref, stack_ref = refs[devices:]
+    padded_planes = (ret_refs[0].shape[0] - 8) // 3
     sticks, _, padded = out_ref.shape
     half = LANES // 2
     bands = sub_ref.shape[2]
     total = jnp.zeros((8, LANES), F32)
-    parts = []
-    for d in range(devices):
-        value = ret_ref[d]
+    me = me_ref[0]
+    for k in range(devices):
+        value = ret_refs[k][...]
+        base = pl.multiple_of(lax.rem(me + devices - k, devices) * padded_planes, 8)
         total = total + value[3 * padded_planes:]
         rest = value[2 * padded_planes:3 * padded_planes]
         re = jnp.concatenate([value[:padded_planes], rest[:, :half]], axis=1)
         im = jnp.concatenate([value[padded_planes:2 * padded_planes], rest[:, half:]], axis=1)
-        c = sc_ref[d * padded_planes:(d + 1) * padded_planes, :]
-        s = ss_ref[d * padded_planes:(d + 1) * padded_planes, :]
-        parts.append(re * c - im * s)
-        parts.append(re * s + im * c)
-    stacked = jnp.concatenate(parts, axis=0)
-    spare = jnp.zeros((stacked.shape[0], 2 * LANES - sticks), F32)
-    turned = jnp.transpose(jnp.concatenate([stacked, spare], axis=1))[:sticks]
+        c = sc_ref[pl.ds(base, padded_planes), :]
+        s = ss_ref[pl.ds(base, padded_planes), :]
+        stack_ref[pl.ds(2 * base, padded_planes), :sticks] = re * c - im * s
+        stack_ref[pl.ds(2 * base + padded_planes, padded_planes), :sticks] = re * s + im * c
+    turned = jnp.transpose(stack_ref[...])[:sticks]
     local = dot3(split(turned), (whi_ref[...], wlo_ref[...])) * volume
     position = lax.broadcasted_iota(jnp.int32, (sticks, padded), 1).astype(F32)
     kept = position < len_ref[:, 0:1]
@@ -562,27 +562,32 @@
         ring = [((b + shift) % bands, b) for b in range(bands)]
         coefs.append(lax.ppermute(coef, "band", ring))
         fields.append(lax.ppermute(received, "band", ring))
-    band = lax.axis_index("band").astype(jnp.int32).reshape(1)
+    band = lax.axis_index("band").astype(jnp.int32)
     norm = 1.0 / (total_sticks * padded)
+    places = jnp.stack([band, me])
     outgoing = pl.pallas_call(
         functools.partial(inner_kernel, bands, volume, norm),
-        out_shape=jax.ShapeDtypeStruct((devices, block + 8, LANES), F32),
-        in_specs=[pl.BlockSpec(memory_space=pltpu.SMEM)] + [vmem] * (2 + 2 * bands),
-        out_specs=vmem,
+        out_shape=(jax.ShapeDtypeStruct((block + 8, LANES), F32),) * devices,
+        in_specs=[smem] + [vmem] * (2 + 2 * bands),
         compiler_params=params(),
         name="inner",
-    )(band, kc, *coefs, *fields, weighted)
-
-    returned = lax.all_to_all(outgoing, "tg", split_axis=0, concat_axis=0, tiled=True)
+    )(places, kc, *coefs, *fields, weighted)
+
+    returned = [outgoing[0]]
+    for k in range(1, devices):
+        ring = [(d, (d + k) % devices) for d in range(devices)]
+        returned.append(lax.ppermute(outgoing[k], "tg", ring))
     applied, subspace = pl.pallas_call(
-        functools.partial(final_kernel, volume),
+        functools.partial(final_kernel, volume, devices),
         out_shape=(
             jax.ShapeDtypeStruct((sticks, 2, padded), F32),
             jax.ShapeDtypeStruct((2, 1, bands), F32),
         ),
+        in_specs=[smem] + [vmem] * (6 + devices),
+        scratch_shapes=[pltpu.VMEM((2 * total_planes, 2 * LANES), F32)],
         compiler_params=params(),
         name="planes_to_wave",
-    )(lengths, returned, kc, whi, wlo, shift_cos, shift_sin)
+    )(me.reshape(1), lengths, *returned, kc, whi, wlo, shift_cos, shift_sin)
     return applied.reshape(1, sticks, 2, padded), subspace
 
 

time: 74.6 us -> 71.3 us (0.956)
  blocking collectives: 14.5 us -> 0 us
  starting transfers between devices: 13.2 us -> 23.9 us
  Pallas kernels: 41.5 us -> 38.8 us
  waiting for transfers between devices: 3.21 us -> 5.21 us
    all_to_all x1 -> x0, blocking collectives: 14.5 us -> none  [shards(): lax.all_to_all(outgoing, 'tg', split_axis=0, concat_axis=0, tiled=True)]
    ppermute x0 -> x7, starting transfers between devices: none -> 10.7 us  [shards(): returned.append(lax.ppermute(outgoing[k], 'tg', ring))]
    pallas_call x1, Pallas kernels: 29.3 us -> 26.5 us  [shards(): pl.pallas_call(functools.partial(plane_kernel, planes), out_shape=jax.Sha...]
    ppermute x0 -> x7, waiting for transfers between devices: none -> 2.59 us  [shards(): returned.append(lax.ppermute(outgoing[k], 'tg', ring))]
    unnamed x14 -> x28, local copies, waits for them, and re-layouts: 0.97 us -> 1.57 us
  transfers between devices with their start and end apart: 7 -> 14, of which waited for: 1 -> 4; matrix products, arithmetic and copies ran while one was open for 0% -> 1% of each run, Pallas kernels for 44% -> 42%
where the time goes in v7:
time: 71.3 us; the launch traced here: 70.9 us
  Pallas kernels  38.8 us (54%)
  starting transfers between devices  23.9 us (34%)
  waiting for transfers between devices  5.21 us (7%)
  local copies, waits for them, and re-layouts  1.57 us (2%)
  between operations  0.8 us (1%)
    pallas_call x1, Pallas kernels, shards(): pl.pallas_call(functools.partial(plane_kernel, planes), out_shape=jax.Sha...  26.5 us
    ppermute x7, starting transfers between devices, shards(): returned.append(lax.ppermute(outgoing[k], 'tg', ring))  10.7 us
    all_to_all x1, starting transfers between devices, shards(): lax.all_to_all(sent, 'tg', split_axis=0, concat_axis=0, tiled=True)  7.25 us
    pallas_call x1, Pallas kernels, shards(): pl.pallas_call(functools.partial(map_kernel, extent, sticks), out_shape=(...  3.42 us
    pallas_call x1, Pallas kernels, shards(): pl.pallas_call(functools.partial(inner_kernel, bands, volume, norm), out_...  3.32 us
    ppermute x3, starting transfers between devices, shards(): fields.append(lax.ppermute(received, 'band', ring))  2.98 us
    ppermute x3, starting transfers between devices, shards(): coefs.append(lax.ppermute(coef, 'band', ring))  2.98 us
    pallas_call x1, Pallas kernels, shards(): pl.pallas_call(functools.partial(wave_kernel, extent), out_shape=(jax.Sha...  2.91 us
  transfers between devices with their start and end apart: 14, of which 4 were waited for; matrix products, arithmetic and copies ran while one was open for 1% of the time, Pallas kernels for 42%

profile of v7, /device:TPU:0, one launch (start us, length us, event | category | flops | bytes accessed | tf_op | source)
XLA Modules:
  0.0 70.9 jit_solution(16160886492831602486)
XLA Ops:
  0.6 2.9 %wave_to_planes.1 = (f32[8,72,128]{2,1,0:T(8,128)}, f32[192,256]{1,0:T(8,128)}, f32[192,128]{1,0:T(8,128)}, bf16[384,256]{1,0:T(8,128)(2,1)}, bf16[384,256]{1,0:...) custom-call(s32[1]{0:T(128)} %bitcast.me_ref, s32[12,128]{1,0:T(8,128)} %bitcast.13, s32[12,128]{1,0:T(8,128)} %bitcast.14, ...), custom_call_target="tpu_custom_call" | custom-call | tf_op jit(solution)/shard_map/wave_to_planes/pallas_call | solution.py:507
  3.5 7.3 %all-to-all-start = ((f32[8,72,128]{2,1,0:T(8,128)}), f32[8,72,128]{2,1,0:T(8,128)S(1)}, u32[]{:S(2)}, u32[]{:S(2)}) async-start(f32[8,72,128]{2,1,0:T(8,128)} %get-tuple-element.27), calls=%async_computation | async-start | bytes 589824 | tf_op jit(solution)/shard_map/all_to_all | solution.py:523
  10.8 0.0 collective-permute-start.2
  10.8 1.6 %collective-permute-start.1 = (f32[192,2,128]{2,1,0:T(2,128)}, f32[192,2,128]{2,1,0:T(2,128)S(1)}, u32[]{:S(2)}, u32[]{:S(2)}) collective-permute-start(f32[192,2,128]{2,1,0:T(2,128)} %bitcast.10), channel_id=1, source_target_pairs={{16,0},{24,8},{0,16},{8,24},{17,1},{25,9},{1,17},{9,25},{18,2},{26... | collective-permute-start | bytes 589832 | tf_op jit(solution)/shard_map/ppermute | solution.py:563
  12.4 1.4 %collective-permute-start = (f32[192,2,128]{2,1,0:T(2,128)}, f32[192,2,128]{2,1,0:T(2,128)S(1)}, u32[]{:S(2)}, u32[]{:S(2)}) collective-permute-start(f32[192,2,128]{2,1,0:T(2,128)} %bitcast.11), channel_id=1, source_target_pairs={{8,0},{16,8},{24,16},{0,24},{9,1},{17,9},{25,17},{1,25},{10,2},{18... | collective-permute-start | bytes 589832 | tf_op jit(solution)/shard_map/ppermute | solution.py:563
  13.8 3.4 %stick_map.1 = (s32[128,128]{1,0:T(8,128)}, s32[8,128]{1,0:T(8,128)}, s32[12,128]{1,0:T(8,128)}, s32[12,128]{1,0:T(8,128)}, s32[13,128]{1,0:T(8,128)}, /*index=5*/s32[13,128]{1,0:T(8,128)}) custom-call(s32[12,128]{1,0:T(8,128)} %bitcast.15, s32[12,128]{1,0:T(8,128)} %bitcast.17), custom_call_target="tpu_custom_call" | custom-call | flops 4000000000 | bytes 100000 | tf_op jit(solution)/shard_map/stick_map/pallas_call | solution.py:527
  17.2 0.6 pad_add_fusion.place_ref
  17.8 2.6 %all-to-all-done.recv_ref.refs_5_ = f32[8,72,128]{2,1,0:T(8,128)S(1)} async-done(((f32[8,72,128]{2,1,0:T(8,128)}), f32[8,72,128]{2,1,0:T(8,128)S(1)}, u32[]{:S(2)}, u32[]{:S(2)}) %all-to-all-start) | async-done | bytes 294944 | tf_op jit(solution)/shard_map/all_to_all | solution.py:523
  20.4 1.5 %collective-permute-start.4 = (f32[8,72,128]{2,1,0:T(8,128)S(1)}, f32[8,72,128]{2,1,0:T(8,128)S(1)}, u32[]{:S(2)}, u32[]{:S(2)}) collective-permute-start(f32[8,72,128]{2,1,0:T(8,128)S(1)} %all-to-all-done.recv_ref.refs_5_), channel_id=1, source_target_pairs={{16,0},{24,8},{0,16},{8,24},{17,1},{25,9},{1,17},{9,25},{18,2},{26... | collective-permute-start | bytes 884744 | tf_op jit(solution)/shard_map/ppermute | solution.py:564
  22.0 1.4 %collective-permute-start.3 = (f32[8,72,128]{2,1,0:T(8,128)S(1)}, f32[8,72,128]{2,1,0:T(8,128)S(1)}, u32[]{:S(2)}, u32[]{:S(2)}) collective-permute-start(f32[8,72,128]{2,1,0:T(8,128)S(1)} %all-to-all-done.recv_ref.refs_5_), channel_id=1, source_target_pairs={{8,0},{16,8},{24,16},{0,24},{9,1},{17,9},{25,17},{1,25},{10,2},{18... | collective-permute-start | bytes 884744 | tf_op jit(solution)/shard_map/ppermute | solution.py:564
  23.4 26.5 %planes.1.refs_9_ = f32[8,80,128]{2,1,0:T(8,128)} custom-call(s32[8,128]{1,0:T(8,128)} %get-tuple-element.28.first_ref, s32[128,128]{1,0:T(8,128)} %get-tuple-element.29.map_ref, s32[12,128]{1,0:T(8,128)} %get-tuple-element.30.src_ref, s32[12,128]{1,0:T(8,128)} %get-tuple-element.31.dst_ref, s32[13,128]{1,0:T(8,128)} %get-tuple-element.32.row_ref, ...), custom_call_target="tpu_custom_call" | custom-call | flops 20000000000 | bytes 10000000 | tf_op jit(solution)/shard_map/planes/pallas_call | solution.py:542
  49.9 0.0 collective-permute-done.refs_2_
  49.9 0.0 copy-start.6
  50.0 0.0 collective-permute-done.4.refs_7_
  50.0 0.0 collective-permute-done.3.refs_6_
  50.0 0.6 copy-done.5
  50.6 0.1 copy-done.6
  50.6 0.1 copy-done.1
  50.8 0.1 copy-done.2
  50.9 0.1 copy-done.3
  51.0 3.3 %inner.1 = (f32[80,128]{1,0:T(8,128)}, f32[80,128]{1,0:T(8,128)}, f32[80,128]{1,0:T(8,128)}, f32[80,128]{1,0:T(8,128)}, f32[80,128]{1,0:T(8,128)}, /*index=5*/f3...) custom-call(s32[2]{0:T(128)} %pad_add_fusion.place_ref, f32[192,256]{1,0:T(8,128)} %get-tuple-element.26.refs_0_.refs_8_, ...), custom_call_target="tpu_custom_call" | custom-call | tf_op jit(solution)/shard_map/inner/pallas_call | solution.py:568
  54.3 1.5 %collective-permute-start.6 = (f32[80,128]{1,0:T(8,128)}, f32[80,128]{1,0:T(8,128)S(1)}, u32[]{:S(2)}, u32[]{:S(2)}) collective-permute-start(f32[80,128]{1,0:T(8,128)} %get-tuple-element.35), channel_id=1, source_target_pairs={{0,1},{1,2},{2,3},{3,4},{4,5},{5,6},{6,7},{7,0},{8,9},{9,10},{10,1... | collective-permute-start | bytes 122888 | tf_op jit(solution)/shard_map/ppermute | solution.py:579
  55.8 1.7 %collective-permute-start.8 = (f32[80,128]{1,0:T(8,128)}, f32[80,128]{1,0:T(8,128)S(1)}, u32[]{:S(2)}, u32[]{:S(2)}) collective-permute-start(f32[80,128]{1,0:T(8,128)} %get-tuple-element.37), channel_id=1, source_target_pairs={{0,3},{1,4},{2,5},{3,6},{4,7},{5,0},{6,1},{7,2},{8,11},{9,12},{10,... | collective-permute-start | bytes 122888 | tf_op jit(solution)/shard_map/ppermute | solution.py:579
  57.5 3.1 %collective-permute-start.9 = (f32[80,128]{1,0:T(8,128)}, f32[80,128]{1,0:T(8,128)S(1)}, u32[]{:S(2)}, u32[]{:S(2)}) collective-permute-start(f32[80,128]{1,0:T(8,128)} %get-tuple-element.38), channel_id=1, source_target_pairs={{0,4},{1,5},{2,6},{3,7},{4,0},{5,1},{6,2},{7,3},{8,12},{9,13},{10,... | collective-permute-start | bytes 122888 | tf_op jit(solution)/shard_map/ppermute | solution.py:579
  60.6 1.0 %collective-permute-start.10 = (f32[80,128]{1,0:T(8,128)}, f32[80,128]{1,0:T(8,128)S(1)}, u32[]{:S(2)}, u32[]{:S(2)}) collective-permute-start(f32[80,128]{1,0:T(8,128)} %get-tuple-element.39), channel_id=1, source_target_pairs={{0,5},{1,6},{2,7},{3,0},{4,1},{5,2},{6,3},{7,4},{8,13},{9,14},{10,... | collective-permute-start | bytes 122888 | tf_op jit(solution)/shard_map/ppermute | solution.py:579
  61.6 1.8 %collective-permute-start.11 = (f32[80,128]{1,0:T(8,128)}, f32[80,128]{1,0:T(8,128)S(1)}, u32[]{:S(2)}, u32[]{:S(2)}) collective-permute-start(f32[80,128]{1,0:T(8,128)} %get-tuple-element.40), channel_id=1, source_target_pairs={{0,6},{1,7},{2,0},{3,1},{4,2},{5,3},{6,4},{7,5},{8,14},{9,15},{10,... | collective-permute-start | bytes 122888 | tf_op jit(solution)/shard_map/ppermute | solution.py:579
  63.4 1.6 %collective-permute-start.12 = (f32[80,128]{1,0:T(8,128)}, f32[80,128]{1,0:T(8,128)S(1)}, u32[]{:S(2)}, u32[]{:S(2)}) collective-permute-start(f32[80,128]{1,0:T(8,128)} %get-tuple-element.41), channel_id=1, source_target_pairs={{0,7},{1,0},{2,1},{3,2},{4,3},{5,4},{6,5},{7,6},{8,15},{9,8},{10,9... | collective-permute-start | bytes 122888 | tf_op jit(solution)/shard_map/ppermute | solution.py:579
  65.0 0.7 collective-permute-done.10.refs_5_
  65.7 0.5 collective-permute-done.11.refs_6_
  66.2 1.4 %collective-permute-done.12.refs_7_ = f32[80,128]{1,0:T(8,128)S(1)} collective-permute-done((f32[80,128]{1,0:T(8,128)}, f32[80,128]{1,0:T(8,128)S(1)}, u32[]{:S(2)}, u32[]{:S(2)}) %collective-permute-start.12) | collective-permute-done | bytes 40992 | tf_op jit(solution)/shard_map/ppermute | solution.py:579
  67.7 0.6 copy-done.13
  68.2 2.7 %planes_to_wave.1 = (f32[192,2,128]{2,1,0:T(2,128)}, f32[2,1,4]{2,1,0:T(1,128)}) custom-call(s32[1]{0:T(128)} %bitcast.me_ref, f32[192,128]{1,0:T(8,128)} %get-tuple-element.25.len_ref, f32[80,128]{1,0:T(8,128)} %get-tuple-element.34.refs_0_, f32[80,128]{1,0:T(8,128)} %copy-done.7, f32[80,128]{1,0:T(8,128)} %copy-done.8, f32[80,128]{1,0:T(8,128)} %copy-done.9, ...), custom_call_target="tpu_custom_call" | custom-call | tf_op jit(solution)/shard_map/planes_to_wave/pallas_call | solution.py:580
  (30 shorter events, 0.1 us)
Async XLA Ops:
  3.5 16.9 %all-to-all-start = ((f32[8,72,128]{2,1,0:T(8,128)}), f32[8,72,128]{2,1,0:T(8,128)S(1)}, u32[]{:S(2)}, u32[]{:S(2)}) async-start(f32[8,72,128]{2,1,0:T(8,128)} %get-tuple-element.27), calls=%async_computation | async-start | bytes 589824 | tf_op jit(solution)/shard_map/all_to_all | solution.py:523
  10.8 11.2 %collective-permute-start.2 = (f32[192,2,128]{2,1,0:T(2,128)}, f32[192,2,128]{2,1,0:T(2,128)S(1)}, u32[]{:S(2)}, u32[]{:S(2)}) collective-permute-start(f32[192,2,128]{2,1,0:T(2,128)} %bitcast.9), channel_id=1, source_target_pairs={{24,0},{0,8},{8,16},{16,24},{25,1},{1,9},{9,17},{17,25},{26,2},{2,... | collective-permute-start | bytes 589832 | tf_op jit(solution)/shard_map/ppermute | solution.py:563
  10.8 39.1 %collective-permute-start.1 = (f32[192,2,128]{2,1,0:T(2,128)}, f32[192,2,128]{2,1,0:T(2,128)S(1)}, u32[]{:S(2)}, u32[]{:S(2)}) collective-permute-start(f32[192,2,128]{2,1,0:T(2,128)} %bitcast.10), channel_id=1, source_target_pairs={{16,0},{24,8},{0,16},{8,24},{17,1},{25,9},{1,17},{9,25},{18,2},{26... | collective-permute-start | bytes 589832 | tf_op jit(solution)/shard_map/ppermute | solution.py:563
  12.4 37.5 %collective-permute-start = (f32[192,2,128]{2,1,0:T(2,128)}, f32[192,2,128]{2,1,0:T(2,128)S(1)}, u32[]{:S(2)}, u32[]{:S(2)}) collective-permute-start(f32[192,2,128]{2,1,0:T(2,128)} %bitcast.11), channel_id=1, source_target_pairs={{8,0},{16,8},{24,16},{0,24},{9,1},{17,9},{25,17},{1,25},{10,2},{18... | collective-permute-start | bytes 589832 | tf_op jit(solution)/shard_map/ppermute | solution.py:563
  20.4 3.0 %copy-start = (f32[8,72,128]{2,1,0:T(8,128)}, f32[8,72,128]{2,1,0:T(8,128)S(1)}, u32[]{:S(2)}) copy-start(f32[8,72,128]{2,1,0:T(8,128)S(1)} %all-to-all-done.recv_ref.refs_5_) | copy-start | bytes 884740
  20.4 29.5 %collective-permute-start.5 = (f32[8,72,128]{2,1,0:T(8,128)S(1)}, f32[8,72,128]{2,1,0:T(8,128)S(1)}, u32[]{:S(2)}, u32[]{:S(2)}) collective-permute-start(f32[8,72,128]{2,1,0:T(8,128)S(1)} %all-to-all-done.recv_ref.refs_5_), channel_id=1, source_target_pairs={{24,0},{0,8},{8,16},{16,24},{25,1},{1,9},{9,17},{17,25},{26,2},{2,... | collective-permute-start | bytes 884744 | tf_op jit(solution)/shard_map/ppermute | solution.py:564
  20.4 29.5 %collective-permute-start.4 = (f32[8,72,128]{2,1,0:T(8,128)S(1)}, f32[8,72,128]{2,1,0:T(8,128)S(1)}, u32[]{:S(2)}, u32[]{:S(2)}) collective-permute-start(f32[8,72,128]{2,1,0:T(8,128)S(1)} %all-to-all-done.recv_ref.refs_5_), channel_id=1, source_target_pairs={{16,0},{24,8},{0,16},{8,24},{17,1},{25,9},{1,17},{9,25},{18,2},{26... | collective-permute-start | bytes 884744 | tf_op jit(solution)/shard_map/ppermute | solution.py:564
  22.0 27.9 %copy-start.4 = (f32[192,2,128]{2,1,0:T(2,128)}, f32[192,2,128]{2,1,0:T(2,128)S(1)}, u32[]{:S(2)}) copy-start(f32[192,2,128]{2,1,0:T(2,128)S(1)} %collective-permute-done.2.refs_4_) | copy-start | bytes 589828
  22.0 28.0 %collective-permute-start.3 = (f32[8,72,128]{2,1,0:T(8,128)S(1)}, f32[8,72,128]{2,1,0:T(8,128)S(1)}, u32[]{:S(2)}, u32[]{:S(2)}) collective-permute-start(f32[8,72,128]{2,1,0:T(8,128)S(1)} %all-to-all-done.recv_ref.refs_5_), channel_id=1, source_target_pairs={{8,0},{16,8},{24,16},{0,24},{9,1},{17,9},{25,17},{1,25},{10,2},{18... | collective-permute-start | bytes 884744 | tf_op jit(solution)/shard_map/ppermute | solution.py:564
  49.9 0.7 copy-start.5
  49.9 0.7 %copy-start.6 = (f32[192,2,128]{2,1,0:T(2,128)}, f32[192,2,128]{2,1,0:T(2,128)S(1)}, u32[]{:S(2)}) copy-start(f32[192,2,128]{2,1,0:T(2,128)S(1)} %collective-permute-done.refs_2_) | copy-start | bytes 589828
  50.0 0.8 %copy-start.1 = (f32[8,72,128]{2,1,0:T(8,128)}, f32[8,72,128]{2,1,0:T(8,128)S(1)}, u32[]{:S(2)}) copy-start(f32[8,72,128]{2,1,0:T(8,128)S(1)} %collective-permute-done.5.refs_8_) | copy-start | bytes 884740
  50.0 0.9 %copy-start.2 = (f32[8,72,128]{2,1,0:T(8,128)}, f32[8,72,128]{2,1,0:T(8,128)S(1)}, u32[]{:S(2)}) copy-start(f32[8,72,128]{2,1,0:T(8,128)S(1)} %collective-permute-done.4.refs_7_) | copy-start | bytes 884740
  50.0 1.0 %copy-start.3 = (f32[8,72,128]{2,1,0:T(8,128)}, f32[8,72,128]{2,1,0:T(8,128)S(1)}, u32[]{:S(2)}) copy-start(f32[8,72,128]{2,1,0:T(8,128)S(1)} %collective-permute-done.3.refs_6_) | copy-start | bytes 884740
  54.3 7.3 %collective-permute-start.6 = (f32[80,128]{1,0:T(8,128)}, f32[80,128]{1,0:T(8,128)S(1)}, u32[]{:S(2)}, u32[]{:S(2)}) collective-permute-start(f32[80,128]{1,0:T(8,128)} %get-tuple-element.35), channel_id=1, source_target_pairs={{0,1},{1,2},{2,3},{3,4},{4,5},{5,6},{6,7},{7,0},{8,9},{9,10},{10,1... | collective-permute-start | bytes 122888 | tf_op jit(solution)/shard_map/ppermute | solution.py:579
  55.8 7.7 %collective-permute-start.7 = (f32[80,128]{1,0:T(8,128)}, f32[80,128]{1,0:T(8,128)S(1)}, u32[]{:S(2)}, u32[]{:S(2)}) collective-permute-start(f32[80,128]{1,0:T(8,128)} %get-tuple-element.36), channel_id=1, source_target_pairs={{0,2},{1,3},{2,4},{3,5},{4,6},{5,7},{6,0},{7,1},{8,10},{9,11},{10,... | collective-permute-start | bytes 122888 | tf_op jit(solution)/shard_map/ppermute | solution.py:579
  55.8 9.3 %collective-permute-start.8 = (f32[80,128]{1,0:T(8,128)}, f32[80,128]{1,0:T(8,128)S(1)}, u32[]{:S(2)}, u32[]{:S(2)}) collective-permute-start(f32[80,128]{1,0:T(8,128)} %get-tuple-element.37), channel_id=1, source_target_pairs={{0,3},{1,4},{2,5},{3,6},{4,7},{5,0},{6,1},{7,2},{8,11},{9,12},{10,... | collective-permute-start | bytes 122888 | tf_op jit(solution)/shard_map/ppermute | solution.py:579
  57.5 7.6 %collective-permute-start.9 = (f32[80,128]{1,0:T(8,128)}, f32[80,128]{1,0:T(8,128)S(1)}, u32[]{:S(2)}, u32[]{:S(2)}) collective-permute-start(f32[80,128]{1,0:T(8,128)} %get-tuple-element.38), channel_id=1, source_target_pairs={{0,4},{1,5},{2,6},{3,7},{4,0},{5,1},{6,2},{7,3},{8,12},{9,13},{10,... | collective-permute-start | bytes 122888 | tf_op jit(solution)/shard_map/ppermute | solution.py:579
  60.6 5.1 %collective-permute-start.10 = (f32[80,128]{1,0:T(8,128)}, f32[80,128]{1,0:T(8,128)S(1)}, u32[]{:S(2)}, u32[]{:S(2)}) collective-permute-start(f32[80,128]{1,0:T(8,128)} %get-tuple-element.39), channel_id=1, source_target_pairs={{0,5},{1,6},{2,7},{3,0},{4,1},{5,2},{6,3},{7,4},{8,13},{9,14},{10,... | collective-permute-start | bytes 122888 | tf_op jit(solution)/shard_map/ppermute | solution.py:579
  61.6 6.1 %copy-start.7 = (f32[80,128]{1,0:T(8,128)}, f32[80,128]{1,0:T(8,128)S(1)}, u32[]{:S(2)}) copy-start(f32[80,128]{1,0:T(8,128)S(1)} %collective-permute-done.6.refs_1_) | copy-start | bytes 122884
  61.6 4.7 %collective-permute-start.11 = (f32[80,128]{1,0:T(8,128)}, f32[80,128]{1,0:T(8,128)S(1)}, u32[]{:S(2)}, u32[]{:S(2)}) collective-permute-start(f32[80,128]{1,0:T(8,128)} %get-tuple-element.40), channel_id=1, source_target_pairs={{0,6},{1,7},{2,0},{3,1},{4,2},{5,3},{6,4},{7,5},{8,14},{9,15},{10,... | collective-permute-start | bytes 122888 | tf_op jit(solution)/shard_map/ppermute | solution.py:579
  63.4 4.2 %copy-start.8 = (f32[80,128]{1,0:T(8,128)}, f32[80,128]{1,0:T(8,128)S(1)}, u32[]{:S(2)}) copy-start(f32[80,128]{1,0:T(8,128)S(1)} %collective-permute-done.7.refs_2_) | copy-start | bytes 122884
  63.4 4.2 %collective-permute-start.12 = (f32[80,128]{1,0:T(8,128)}, f32[80,128]{1,0:T(8,128)S(1)}, u32[]{:S(2)}, u32[]{:S(2)}) collective-permute-start(f32[80,128]{1,0:T(8,128)} %get-tuple-element.41), channel_id=1, source_target_pairs={{0,7},{1,0},{2,1},{3,2},{4,3},{5,4},{6,5},{7,6},{8,15},{9,8},{10,9... | collective-permute-start | bytes 122888 | tf_op jit(solution)/shard_map/ppermute | solution.py:579
  65.0 2.6 %copy-start.9 = (f32[80,128]{1,0:T(8,128)}, f32[80,128]{1,0:T(8,128)S(1)}, u32[]{:S(2)}) copy-start(f32[80,128]{1,0:T(8,128)S(1)} %collective-permute-done.8.refs_3_) | copy-start | bytes 122884
  65.0 2.6 %copy-start.10 = (f32[80,128]{1,0:T(8,128)}, f32[80,128]{1,0:T(8,128)S(1)}, u32[]{:S(2)}) copy-start(f32[80,128]{1,0:T(8,128)S(1)} %collective-permute-done.9.refs_4_) | copy-start | bytes 122884
  65.7 1.9 %copy-start.11 = (f32[80,128]{1,0:T(8,128)}, f32[80,128]{1,0:T(8,128)S(1)}, u32[]{:S(2)}) copy-start(f32[80,128]{1,0:T(8,128)S(1)} %collective-permute-done.10.refs_5_) | copy-start | bytes 122884
  66.2 1.4 %copy-start.12 = (f32[80,128]{1,0:T(8,128)}, f32[80,128]{1,0:T(8,128)S(1)}, u32[]{:S(2)}) copy-start(f32[80,128]{1,0:T(8,128)S(1)} %collective-permute-done.11.refs_6_) | copy-start | bytes 122884
  67.6 0.6 copy-start.13

commit v8 on v7

--- a/solution.py
+++ b/solution.py
@@ -14,7 +14,6 @@
 LANES = 128
 F32 = jnp.float32
 BF16 = jnp.bfloat16
-VMEM_LIMIT = 56 * 1024 * 1024
 
 
 def up8(n):
@@ -103,8 +102,8 @@
     return (*forward, x_forward, x_back, *back)
 
 
-def params():
-    return pltpu.CompilerParams(vmem_limit_bytes=VMEM_LIMIT)
+def params(megabytes):
+    return pltpu.CompilerParams(vmem_limit_bytes=int(min(megabytes, 56) * 2**20))
 
 
 def cost(flops, nbytes):
@@ -516,7 +515,7 @@
             jax.ShapeDtypeStruct((total_planes, sticks), F32),
         ),
         in_specs=[smem] + [vmem] * 5,
-        compiler_params=params(),
+        compiler_params=params(8 + 8 * total_planes / 192),
         name="wave_to_planes",
     )(me.reshape(1), length, row, col, slots, coef)
 
@@ -534,7 +533,7 @@
             longer_list,
             longer_list,
         ),
-        compiler_params=params(),
+        compiler_params=params(14 * total_sticks / 1536),
         cost_estimate=cost(4e9, 1e5),
         name="stick_map",
     )(row, col)
@@ -552,7 +551,7 @@
             pltpu.VMEM(potential.shape, F32),
             pltpu.SemaphoreType.DMA,
         ],
-        compiler_params=params(),
+        compiler_params=params(36),
         cost_estimate=cost(2e10, 1e7),
         name="planes",
     )(first, stick_map, source, target, row_w, col_w, received, *[jnp.asarray(t) for t in tables(extent)], potential)
@@ -569,7 +568,7 @@
         functools.partial(inner_kernel, bands, volume, norm),
         out_shape=(jax.ShapeDtypeStruct((block + 8, LANES), F32),) * devices,
         in_specs=[smem] + [vmem] * (2 + 2 * bands),
-        compiler_params=params(),
+        compiler_params=params(6 + 1.5 * bands),
         name="inner",
     )(places, kc, *coefs, *fields, weighted)
 
@@ -585,7 +584,7 @@
         ),
         in_specs=[smem] + [vmem] * (6 + devices),
         scratch_shapes=[pltpu.VMEM((2 * total_planes, 2 * LANES), F32)],
-        compiler_params=params(),
+        compiler_params=params(6 + 6 * total_planes / 192),
         name="planes_to_wave",
     )(me.reshape(1), lengths, *returned, kc, whi, wlo, shift_cos, shift_sin)
     return applied.reshape(1, sticks, 2, padded), subspace

time: 71.3 us -> 77 us (1.080)
  local copies, waits for them, and re-layouts: 1.57 us -> 16.3 us
  Pallas kernels: 38.8 us -> 31.7 us
  waiting for transfers between devices: 5.21 us -> 3.19 us
    unnamed x28 -> x46, local copies, waits for them, and re-layouts: 1.57 us -> 16.3 us
    all_to_all x1, waiting for transfers between devices: 2.6 us -> 0.63 us  [shards(): lax.all_to_all(sent, 'tg', split_axis=0, concat_axis=0, tiled=True)]
    pallas_call x1, Pallas kernels: 3.32 us -> 1.44 us  [shards(): pl.pallas_call(functools.partial(inner_kernel, bands, volume, norm), out_...]
    pallas_call x1, Pallas kernels: 26.5 us -> 25.1 us  [shards(): pl.pallas_call(functools.partial(plane_kernel, planes), out_shape=jax.Sha...]
    pallas_call x1, Pallas kernels: 2.69 us -> 1.28 us  [shards(): pl.pallas_call(functools.partial(final_kernel, volume, devices), out_shap...]
    pallas_call x1, Pallas kernels: 3.42 us -> 2.09 us  [shards(): pl.pallas_call(functools.partial(map_kernel, extent, sticks), out_shape=(...]
    pallas_call x1, Pallas kernels: 2.91 us -> 1.8 us  [shards(): pl.pallas_call(functools.partial(wave_kernel, extent), out_shape=(jax.Sha...]
  transfers between devices with their start and end apart: 14 -> 14, of which waited for: 4 -> 4; matrix products, arithmetic and copies ran while one was open for 1% -> 0% of each run, Pallas kernels for 42% -> 36%
where the time goes in v8:
time: 77 us; the launch traced here: 76.2 us
  Pallas kernels  31.7 us (41%)
  starting transfers between devices  24.2 us (31%)
  local copies, waits for them, and re-layouts  16.3 us (21%)
  waiting for transfers between devices  3.19 us (4%)
    pallas_call x1, Pallas kernels, shards(): pl.pallas_call(functools.partial(plane_kernel, planes), out_shape=jax.Sha...  25.1 us
    unnamed x46, local copies, waits for them, and re-layouts  16.3 us
    ppermute x7, starting transfers between devices, shards(): returned.append(lax.ppermute(outgoing[k], 'tg', ring))  11 us
    all_to_all x1, starting transfers between devices, shards(): lax.all_to_all(sent, 'tg', split_axis=0, concat_axis=0, tiled=True)  7.25 us
    ppermute x3, starting transfers between devices, shards(): fields.append(lax.ppermute(received, 'band', ring))  2.99 us
    ppermute x3, starting transfers between devices, shards(): coefs.append(lax.ppermute(coef, 'band', ring))  2.98 us
    ppermute x7, waiting for transfers between devices, shards(): returned.append(lax.ppermute(outgoing[k], 'tg', ring))  2.54 us
    pallas_call x1, Pallas kernels, shards(): pl.pallas_call(functools.partial(map_kernel, extent, sticks), out_shape=(...  2.09 us
  transfers between devices with their start and end apart: 14, of which 4 were waited for; matrix products, arithmetic and copies ran while one was open for 0% of the time, Pallas kernels for 36%

profile of v8, /device:TPU:0, one launch (start us, length us, event | category | flops | bytes accessed | tf_op | source)
XLA Modules:
  0.0 76.2 jit_solution(5907499064795875731)
XLA Ops:
  0.6 0.9 %copy-done = f32[1,192,2,128]{3,2,1,0:T(2,128)S(1)} copy-done((f32[1,192,2,128]{3,2,1,0:T(2,128)S(1)}, f32[1,192,2,128]{3,2,1,0:T(2,128)}, u32[]{:S(2)}) %copy-start) | copy-done | bytes 196632
  1.6 0.7 copy-done.2
  2.3 0.7 copy-done.3
  3.0 0.7 copy-done.5
  4.3 1.8 %wave_to_planes.1 = (f32[8,72,128]{2,1,0:T(8,128)}, f32[192,256]{1,0:T(8,128)S(1)}, f32[192,128]{1,0:T(8,128)S(1)}, bf16[384,256]{1,0:T(8,128)(2,1)S(1)}, bf16[3...) custom-call(s32[1]{0:T(128)} %bitcast.me_ref, s32[12,128]{1,0:T(8,128)S(1)} %bitcast.13, ...), custom_call_target="tpu_custom_call" | custom-call | tf_op jit(solution)/shard_map/wave_to_planes/pallas_call | solution.py:506
  6.1 7.3 %all-to-all-start = ((f32[8,72,128]{2,1,0:T(8,128)}), f32[8,72,128]{2,1,0:T(8,128)S(1)}, u32[]{:S(2)}, u32[]{:S(2)}) async-start(f32[8,72,128]{2,1,0:T(8,128)} %get-tuple-element.27), calls=%async_computation | async-start | bytes 589824 | tf_op jit(solution)/shard_map/all_to_all | solution.py:522
  13.4 1.6 %collective-permute-start.1 = (f32[192,2,128]{2,1,0:T(2,128)}, f32[192,2,128]{2,1,0:T(2,128)S(1)}, u32[]{:S(2)}, u32[]{:S(2)}) collective-permute-start(f32[192,2,128]{2,1,0:T(2,128)} %bitcast.9), channel_id=1, source_target_pairs={{16,0},{24,8},{0,16},{8,24},{17,1},{25,9},{1,17},{9,25},{18,2},{26... | collective-permute-start | bytes 589832 | tf_op jit(solution)/shard_map/ppermute | solution.py:562
  15.0 1.4 %collective-permute-start = (f32[192,2,128]{2,1,0:T(2,128)}, f32[192,2,128]{2,1,0:T(2,128)S(1)}, u32[]{:S(2)}, u32[]{:S(2)}) collective-permute-start(f32[192,2,128]{2,1,0:T(2,128)} %bitcast.10), channel_id=1, source_target_pairs={{8,0},{16,8},{24,16},{0,24},{9,1},{17,9},{25,17},{1,25},{10,2},{18... | collective-permute-start | bytes 589832 | tf_op jit(solution)/shard_map/ppermute | solution.py:562
  16.4 0.7 copy-done.4
  17.1 0.7 copy-done.6
  17.8 2.1 %stick_map.1 = (s32[128,128]{1,0:T(8,128)S(1)}, s32[8,128]{1,0:T(8,128)S(1)}, s32[12,128]{1,0:T(8,128)S(1)}, s32[12,128]{1,0:T(8,128)S(1)}, s32[13,128]{1,0:T(8,128)S(1)}, /*index=5*/s32[13,128]{1,0:T(8,128)S(1)}) custom-call(s32[12,128]{1,0:T(8,128)S(1)} %bitcast.15, s32[12,128]{1,0:T(8,128)S(1)} %bitcast.17), custom_call_target="tpu_custom_call" | custom-call | flops 4000000000 | bytes 100000 | tf_op jit(solution)/shard_map/stick_map/pallas_call | solution.py:526
  23.0 1.6 %collective-permute-start.4 = (f32[8,72,128]{2,1,0:T(8,128)S(1)}, f32[8,72,128]{2,1,0:T(8,128)S(1)}, u32[]{:S(2)}, u32[]{:S(2)}) collective-permute-start(f32[8,72,128]{2,1,0:T(8,128)S(1)} %all-to-all-done.recv_ref.refs_5_), channel_id=1, source_target_pairs={{16,0},{24,8},{0,16},{8,24},{17,1},{25,9},{1,17},{9,25},{18,2},{26... | collective-permute-start | bytes 884744 | tf_op jit(solution)/shard_map/ppermute | solution.py:563
  24.6 1.4 %collective-permute-start.3 = (f32[8,72,128]{2,1,0:T(8,128)S(1)}, f32[8,72,128]{2,1,0:T(8,128)S(1)}, u32[]{:S(2)}, u32[]{:S(2)}) collective-permute-start(f32[8,72,128]{2,1,0:T(8,128)S(1)} %all-to-all-done.recv_ref.refs_5_), channel_id=1, source_target_pairs={{8,0},{16,8},{24,16},{0,24},{9,1},{17,9},{25,17},{1,25},{10,2},{18... | collective-permute-start | bytes 884744 | tf_op jit(solution)/shard_map/ppermute | solution.py:563
  26.0 2.3 %copy-done.8 = f32[24,192,192]{2,1,0:T(8,128)S(1)} copy-done((f32[24,192,192]{2,1,0:T(8,128)S(1)}, f32[24,192,192]{2,1,0:T(8,128)}, u32[]{:S(2)}) %copy-start.8) | copy-done | bytes 3538968
  28.3 0.9 %copy-done.11 = bf16[128,288]{1,0:T(8,128)(2,1)S(1)} copy-done((bf16[128,288]{1,0:T(8,128)(2,1)S(1)}, bf16[128,288]{1,0:T(8,128)(2,1)}, u32[]{:S(2)}) %copy-start.11) | copy-done | bytes 73752
  29.2 0.9 %copy-done.12 = bf16[192,144]{1,0:T(8,128)(2,1)S(1)} copy-done((bf16[192,144]{1,0:T(8,128)(2,1)S(1)}, bf16[192,144]{1,0:T(8,128)(2,1)}, u32[]{:S(2)}) %copy-start.12) | copy-done | bytes 55320
  30.1 0.9 %copy-done.13 = bf16[192,192]{1,0:T(8,128)(2,1)S(1)} copy-done((bf16[192,192]{1,0:T(8,128)(2,1)S(1)}, bf16[192,192]{1,0:T(8,128)(2,1)}, u32[]{:S(2)}) %copy-start.13) | copy-done | bytes 73752
  31.0 0.9 %copy-done.14 = bf16[96,288]{1,0:T(8,128)(2,1)S(1)} copy-done((bf16[96,288]{1,0:T(8,128)(2,1)S(1)}, bf16[96,288]{1,0:T(8,128)(2,1)}, u32[]{:S(2)}) %copy-start.14) | copy-done | bytes 55320
  31.9 0.8 %copy-done.16 = s32[128,128]{1,0:T(8,128)S(1)} copy-done((s32[128,128]{1,0:T(8,128)S(1)}, s32[128,128]{1,0:T(8,128)}, u32[]{:S(2)}) %copy-start.16) | copy-done | bytes 65560
  33.5 0.7 copy-done.20
  34.1 0.7 copy-done.22
  34.8 25.1 %planes.1.refs_9_ = f32[8,80,128]{2,1,0:T(8,128)S(1)} custom-call(s32[8,128]{1,0:T(8,128)S(1)} %get-tuple-element.28.first_ref, s32[128,128]{1,0:T(8,128)S(1)} %copy-done.16, s32[12,128]{1,0:T(8,128)S(1)} %get-tuple-element.30.src_ref, s32[12,128]{1,0:T(8,128)S(1)} %copy-done.18, s32[13,128]{1,0:T(8,128)S(1)} %copy-done.20, s32[13,128]{1,0:T(8,128)S(1)} %copy-done.22, ...), custom_call_target="tpu_custom_call" | custom-call | flops 20000000000 | bytes 10000000 | tf_op jit(solution)/shard_map/planes/pallas_call | solution.py:541
  60.0 1.4 %inner.1 = (f32[80,128]{1,0:T(8,128)S(1)}, f32[80,128]{1,0:T(8,128)S(1)}, f32[80,128]{1,0:T(8,128)S(1)}, f32[80,128]{1,0:T(8,128)S(1)}, f32[80,128]{1,0:T(8,128)...) custom-call(s32[2]{0:T(128)S(1)} %pad_add_fusion.place_ref, ...), custom_call_target="tpu_custom_call" | custom-call | tf_op jit(solution)/shard_map/inner/pallas_call | solution.py:567
  61.4 1.5 %collective-permute-start.6 = (f32[80,128]{1,0:T(8,128)S(1)}, f32[80,128]{1,0:T(8,128)S(1)}, u32[]{:S(2)}, u32[]{:S(2)}) collective-permute-start(f32[80,128]{1,0:T(8,128)S(1)} %get-tuple-element.35), channel_id=1, source_target_pairs={{0,1},{1,2},{2,3},{3,4},{4,5},{5,6},{6,7},{7,0},{8,9},{9,10},{10,1... | collective-permute-start | bytes 122888 | tf_op jit(solution)/shard_map/ppermute | solution.py:578
  63.3 2.4 %collective-permute-start.8 = (f32[80,128]{1,0:T(8,128)S(1)}, f32[80,128]{1,0:T(8,128)S(1)}, u32[]{:S(2)}, u32[]{:S(2)}) collective-permute-start(f32[80,128]{1,0:T(8,128)S(1)} %get-tuple-element.37), channel_id=1, source_target_pairs={{0,3},{1,4},{2,5},{3,6},{4,7},{5,0},{6,1},{7,2},{8,11},{9,12},{10,... | collective-permute-start | bytes 122888 | tf_op jit(solution)/shard_map/ppermute | solution.py:578
  65.7 2.1 %collective-permute-start.9 = (f32[80,128]{1,0:T(8,128)S(1)}, f32[80,128]{1,0:T(8,128)S(1)}, u32[]{:S(2)}, u32[]{:S(2)}) collective-permute-start(f32[80,128]{1,0:T(8,128)S(1)} %get-tuple-element.38), channel_id=1, source_target_pairs={{0,4},{1,5},{2,6},{3,7},{4,0},{5,1},{6,2},{7,3},{8,12},{9,13},{10,... | collective-permute-start | bytes 122888 | tf_op jit(solution)/shard_map/ppermute | solution.py:578
  67.8 1.7 %collective-permute-start.10 = (f32[80,128]{1,0:T(8,128)S(1)}, f32[80,128]{1,0:T(8,128)S(1)}, u32[]{:S(2)}, u32[]{:S(2)}) collective-permute-start(f32[80,128]{1,0:T(8,128)S(1)} %get-tuple-element.39), channel_id=1, source_target_pairs={{0,5},{1,6},{2,7},{3,0},{4,1},{5,2},{6,3},{7,4},{8,13},{9,14},{10,... | collective-permute-start | bytes 122888 | tf_op jit(solution)/shard_map/ppermute | solution.py:578
  69.5 1.4 %collective-permute-start.11 = (f32[80,128]{1,0:T(8,128)S(1)}, f32[80,128]{1,0:T(8,128)S(1)}, u32[]{:S(2)}, u32[]{:S(2)}) collective-permute-start(f32[80,128]{1,0:T(8,128)S(1)} %get-tuple-element.40), channel_id=1, source_target_pairs={{0,6},{1,7},{2,0},{3,1},{4,2},{5,3},{6,4},{7,5},{8,14},{9,15},{10,... | collective-permute-start | bytes 122888 | tf_op jit(solution)/shard_map/ppermute | solution.py:578
  70.9 1.5 %collective-permute-start.12 = (f32[80,128]{1,0:T(8,128)S(1)}, f32[80,128]{1,0:T(8,128)S(1)}, u32[]{:S(2)}, u32[]{:S(2)}) collective-permute-start(f32[80,128]{1,0:T(8,128)S(1)} %get-tuple-element.41), channel_id=1, source_target_pairs={{0,7},{1,0},{2,1},{3,2},{4,3},{5,4},{6,5},{7,6},{8,15},{9,8},{10,9... | collective-permute-start | bytes 122888 | tf_op jit(solution)/shard_map/ppermute | solution.py:578
  72.7 0.9 %collective-permute-done.11.refs_6_ = f32[80,128]{1,0:T(8,128)S(1)} collective-permute-done((f32[80,128]{1,0:T(8,128)S(1)}, f32[80,128]{1,0:T(8,128)S(1)}, u32[]{:S(2)}, u32[]{:S(2)}) %collective-permute-start.11) | collective-permute-done | bytes 40992 | tf_op jit(solution)/shard_map/ppermute | solution.py:578
  73.6 1.3 %collective-permute-done.12.refs_7_ = f32[80,128]{1,0:T(8,128)S(1)} collective-permute-done((f32[80,128]{1,0:T(8,128)S(1)}, f32[80,128]{1,0:T(8,128)S(1)}, u32[]{:S(2)}, u32[]{:S(2)}) %collective-permute-start.12) | collective-permute-done | bytes 40992 | tf_op jit(solution)/shard_map/ppermute | solution.py:578
  74.9 1.3 %planes_to_wave.1 = (f32[192,2,128]{2,1,0:T(2,128)}, f32[2,1,4]{2,1,0:T(1,128)}) custom-call(s32[1]{0:T(128)} %bitcast.me_ref, f32[192,128]{1,0:T(8,128)S(1)} %get-tuple-element.25.len_ref, f32[80,128]{1,0:T(8,128)S(1)} %get-tuple-element.34.refs_0_, f32[80,128]{1,0:T(8,128)S(1)} %collective-permute-done.6.refs_1_, ...), custom_call_target="tpu_custom_call" | custom-call | tf_op jit(solution)/shard_map/planes_to_wave/pallas_call | solution.py:579
  (48 shorter events, 5.2 us)
Async XLA Ops:
  0.6 0.9 %copy-start = (f32[1,192,2,128]{3,2,1,0:T(2,128)S(1)}, f32[1,192,2,128]{3,2,1,0:T(2,128)}, u32[]{:S(2)}) copy-start(f32[1,192,2,128]{3,2,1,0:T(2,128)} %param.12) | copy-start | bytes 589828
  1.6 0.7 copy-start.2
  2.3 0.7 copy-start.3
  3.0 0.7 copy-start.5
  6.1 16.9 %all-to-all-start = ((f32[8,72,128]{2,1,0:T(8,128)}), f32[8,72,128]{2,1,0:T(8,128)S(1)}, u32[]{:S(2)}, u32[]{:S(2)}) async-start(f32[8,72,128]{2,1,0:T(8,128)} %get-tuple-element.27), calls=%async_computation | async-start | bytes 589824 | tf_op jit(solution)/shard_map/all_to_all | solution.py:522
  13.4 11.2 %collective-permute-start.2 = (f32[192,2,128]{2,1,0:T(2,128)}, f32[192,2,128]{2,1,0:T(2,128)S(1)}, u32[]{:S(2)}, u32[]{:S(2)}) collective-permute-start(f32[192,2,128]{2,1,0:T(2,128)} %bitcast.8), channel_id=1, source_target_pairs={{24,0},{0,8},{8,16},{16,24},{25,1},{1,9},{9,17},{17,25},{26,2},{2,... | collective-permute-start | bytes 589832 | tf_op jit(solution)/shard_map/ppermute | solution.py:562
  13.4 46.5 %collective-permute-start.1 = (f32[192,2,128]{2,1,0:T(2,128)}, f32[192,2,128]{2,1,0:T(2,128)S(1)}, u32[]{:S(2)}, u32[]{:S(2)}) collective-permute-start(f32[192,2,128]{2,1,0:T(2,128)} %bitcast.9), channel_id=1, source_target_pairs={{16,0},{24,8},{0,16},{8,24},{17,1},{25,9},{1,17},{9,25},{18,2},{26... | collective-permute-start | bytes 589832 | tf_op jit(solution)/shard_map/ppermute | solution.py:562
  15.0 44.9 %collective-permute-start = (f32[192,2,128]{2,1,0:T(2,128)}, f32[192,2,128]{2,1,0:T(2,128)S(1)}, u32[]{:S(2)}, u32[]{:S(2)}) collective-permute-start(f32[192,2,128]{2,1,0:T(2,128)} %bitcast.10), channel_id=1, source_target_pairs={{8,0},{16,8},{24,16},{0,24},{9,1},{17,9},{25,17},{1,25},{10,2},{18... | collective-permute-start | bytes 589832 | tf_op jit(solution)/shard_map/ppermute | solution.py:562
  16.4 0.7 copy-start.4
  17.1 0.7 copy-start.6
  17.8 8.2 %copy-start.9 = (bf16[1536,256]{1,0:T(8,128)(2,1)S(1)}, bf16[1536,256]{1,0:T(8,128)(2,1)}, u32[]{:S(2)}) copy-start(bf16[1536,256]{1,0:T(8,128)(2,1)} %constant.23.clone.x_back) | copy-start | bytes 2359300
  17.8 8.2 %copy-start.10 = (bf16[768,512]{1,0:T(8,128)(2,1)S(1)}, bf16[768,512]{1,0:T(8,128)(2,1)}, u32[]{:S(2)}) copy-start(bf16[768,512]{1,0:T(8,128)(2,1)} %constant.22.clone.x_forward) | copy-start | bytes 2359300
  23.0 36.9 %collective-permute-start.5 = (f32[8,72,128]{2,1,0:T(8,128)S(1)}, f32[8,72,128]{2,1,0:T(8,128)S(1)}, u32[]{:S(2)}, u32[]{:S(2)}) collective-permute-start(f32[8,72,128]{2,1,0:T(8,128)S(1)} %all-to-all-done.recv_ref.refs_5_), channel_id=1, source_target_pairs={{24,0},{0,8},{8,16},{16,24},{25,1},{1,9},{9,17},{17,25},{26,2},{2,... | collective-permute-start | bytes 884744 | tf_op jit(solution)/shard_map/ppermute | solution.py:563
  23.0 36.9 %collective-permute-start.4 = (f32[8,72,128]{2,1,0:T(8,128)S(1)}, f32[8,72,128]{2,1,0:T(8,128)S(1)}, u32[]{:S(2)}, u32[]{:S(2)}) collective-permute-start(f32[8,72,128]{2,1,0:T(8,128)S(1)} %all-to-all-done.recv_ref.refs_5_), channel_id=1, source_target_pairs={{16,0},{24,8},{0,16},{8,24},{17,1},{25,9},{1,17},{9,25},{18,2},{26... | collective-permute-start | bytes 884744 | tf_op jit(solution)/shard_map/ppermute | solution.py:563
  24.6 35.4 %collective-permute-start.3 = (f32[8,72,128]{2,1,0:T(8,128)S(1)}, f32[8,72,128]{2,1,0:T(8,128)S(1)}, u32[]{:S(2)}, u32[]{:S(2)}) collective-permute-start(f32[8,72,128]{2,1,0:T(8,128)S(1)} %all-to-all-done.recv_ref.refs_5_), channel_id=1, source_target_pairs={{8,0},{16,8},{24,16},{0,24},{9,1},{17,9},{25,17},{1,25},{10,2},{18... | collective-permute-start | bytes 884744 | tf_op jit(solution)/shard_map/ppermute | solution.py:563
  26.0 2.3 %copy-start.8 = (f32[24,192,192]{2,1,0:T(8,128)S(1)}, f32[24,192,192]{2,1,0:T(8,128)}, u32[]{:S(2)}) copy-start(f32[24,192,192]{2,1,0:T(8,128)} %pot_hbm.1) | copy-start | bytes 10616836
  28.3 0.9 %copy-start.11 = (bf16[128,288]{1,0:T(8,128)(2,1)S(1)}, bf16[128,288]{1,0:T(8,128)(2,1)}, u32[]{:S(2)}) copy-start(bf16[128,288]{1,0:T(8,128)(2,1)} %constant.24.clone.back_even) | copy-start | bytes 221188
  29.2 0.9 %copy-start.12 = (bf16[192,144]{1,0:T(8,128)(2,1)S(1)}, bf16[192,144]{1,0:T(8,128)(2,1)}, u32[]{:S(2)}) copy-start(bf16[192,144]{1,0:T(8,128)(2,1)} %constant.21.clone.y_odd) | copy-start | bytes 165892
  30.1 0.9 %copy-start.13 = (bf16[192,192]{1,0:T(8,128)(2,1)S(1)}, bf16[192,192]{1,0:T(8,128)(2,1)}, u32[]{:S(2)}) copy-start(bf16[192,192]{1,0:T(8,128)(2,1)} %constant.20.clone.y_even) | copy-start | bytes 221188
  31.0 0.9 %copy-start.14 = (bf16[96,288]{1,0:T(8,128)(2,1)S(1)}, bf16[96,288]{1,0:T(8,128)(2,1)}, u32[]{:S(2)}) copy-start(bf16[96,288]{1,0:T(8,128)(2,1)} %constant.25.clone.back_odd) | copy-start | bytes 165892
  31.9 0.8 %copy-start.16 = (s32[128,128]{1,0:T(8,128)S(1)}, s32[128,128]{1,0:T(8,128)}, u32[]{:S(2)}) copy-start(s32[128,128]{1,0:T(8,128)} %copy-done.15) | copy-start | bytes 196612
  32.8 0.7 copy-start.18
  33.4 0.7 copy-start.20
  34.1 0.7 copy-start.22
  34.8 25.1 %copy-start.1 = (f32[1,192,2,128]{3,2,1,0:T(2,128)S(1)}, f32[1,192,2,128]{3,2,1,0:T(2,128)}, u32[]{:S(2)}) copy-start(f32[1,192,2,128]{3,2,1,0:T(2,128)} %param.12) | copy-start | bytes 589828
  61.4 8.1 %collective-permute-start.6 = (f32[80,128]{1,0:T(8,128)S(1)}, f32[80,128]{1,0:T(8,128)S(1)}, u32[]{:S(2)}, u32[]{:S(2)}) collective-permute-start(f32[80,128]{1,0:T(8,128)S(1)} %get-tuple-element.35), channel_id=1, source_target_pairs={{0,1},{1,2},{2,3},{3,4},{4,5},{5,6},{6,7},{7,0},{8,9},{9,10},{10,1... | collective-permute-start | bytes 122888 | tf_op jit(solution)/shard_map/ppermute | solution.py:578
  62.9 8.1 %collective-permute-start.7 = (f32[80,128]{1,0:T(8,128)S(1)}, f32[80,128]{1,0:T(8,128)S(1)}, u32[]{:S(2)}, u32[]{:S(2)}) collective-permute-start(f32[80,128]{1,0:T(8,128)S(1)} %get-tuple-element.36), channel_id=1, source_target_pairs={{0,2},{1,3},{2,4},{3,5},{4,6},{5,7},{6,0},{7,1},{8,10},{9,11},{10,... | collective-permute-start | bytes 122888 | tf_op jit(solution)/shard_map/ppermute | solution.py:578
  63.3 9.1 %collective-permute-start.8 = (f32[80,128]{1,0:T(8,128)S(1)}, f32[80,128]{1,0:T(8,128)S(1)}, u32[]{:S(2)}, u32[]{:S(2)}) collective-permute-start(f32[80,128]{1,0:T(8,128)S(1)} %get-tuple-element.37), channel_id=1, source_target_pairs={{0,3},{1,4},{2,5},{3,6},{4,7},{5,0},{6,1},{7,2},{8,11},{9,12},{10,... | collective-permute-start | bytes 122888 | tf_op jit(solution)/shard_map/ppermute | solution.py:578
  65.7 6.7 %collective-permute-start.9 = (f32[80,128]{1,0:T(8,128)S(1)}, f32[80,128]{1,0:T(8,128)S(1)}, u32[]{:S(2)}, u32[]{:S(2)}) collective-permute-start(f32[80,128]{1,0:T(8,128)S(1)} %get-tuple-element.38), channel_id=1, source_target_pairs={{0,4},{1,5},{2,6},{3,7},{4,0},{5,1},{6,2},{7,3},{8,12},{9,13},{10,... | collective-permute-start | bytes 122888 | tf_op jit(solution)/shard_map/ppermute | solution.py:578
  67.8 4.9 %collective-permute-start.10 = (f32[80,128]{1,0:T(8,128)S(1)}, f32[80,128]{1,0:T(8,128)S(1)}, u32[]{:S(2)}, u32[]{:S(2)}) collective-permute-start(f32[80,128]{1,0:T(8,128)S(1)} %get-tuple-element.39), channel_id=1, source_target_pairs={{0,5},{1,6},{2,7},{3,0},{4,1},{5,2},{6,3},{7,4},{8,13},{9,14},{10,... | collective-permute-start | bytes 122888 | tf_op jit(solution)/shard_map/ppermute | solution.py:578
  69.5 4.1 %collective-permute-start.11 = (f32[80,128]{1,0:T(8,128)S(1)}, f32[80,128]{1,0:T(8,128)S(1)}, u32[]{:S(2)}, u32[]{:S(2)}) collective-permute-start(f32[80,128]{1,0:T(8,128)S(1)} %get-tuple-element.40), channel_id=1, source_target_pairs={{0,6},{1,7},{2,0},{3,1},{4,2},{5,3},{6,4},{7,5},{8,14},{9,15},{10,... | collective-permute-start | bytes 122888 | tf_op jit(solution)/shard_map/ppermute | solution.py:578
  70.9 4.0 %collective-permute-start.12 = (f32[80,128]{1,0:T(8,128)S(1)}, f32[80,128]{1,0:T(8,128)S(1)}, u32[]{:S(2)}, u32[]{:S(2)}) collective-permute-start(f32[80,128]{1,0:T(8,128)S(1)} %get-tuple-element.41), channel_id=1, source_target_pairs={{0,7},{1,0},{2,1},{3,2},{4,3},{5,4},{6,5},{7,6},{8,15},{9,8},{10,9... | collective-permute-start | bytes 122888 | tf_op jit(solution)/shard_map/ppermute | solution.py:578
  (5 other events, 3.1 us)

commit v9 on v8

--- a/solution.py
+++ b/solution.py
@@ -99,18 +99,47 @@
     x_forward = np.concatenate([hi, hi, lo], axis=0)
     hi, lo = pair(x_table.T.copy())
     x_back = np.concatenate([hi, hi, lo], axis=0)
-    return (*forward, x_forward, x_back, *back)
+    depth = x_back.shape[0] // 2
+    rows = [x_forward, np.concatenate([x_back[:depth], x_back[depth:]], axis=1)]
+    y_rows = np.zeros((2 * half, 2 * wide), hi.dtype)
+    y_rows[:, :forward[0].shape[1]] = forward[0]
+    y_rows[:, wide:wide + forward[1].shape[1]] = forward[1]
+    rows.append(y_rows)
+    for table in back:
+        rows.append(np.pad(table, ((0, 0), (0, 2 * wide - table.shape[1]))))
+    return np.concatenate(rows, axis=0)
 
 
 def params(megabytes):
     return pltpu.CompilerParams(vmem_limit_bytes=int(min(megabytes, 56) * 2**20))
 
 
+def fetch_all(sources, targets, sems):
+    copies = [
+        pltpu.make_async_copy(source, target, sems.at[i])
+        for i, (source, target) in enumerate(zip(sources, targets))
+    ]
+    for copy in copies:
+        copy.start()
+    return copies
+
+
 def cost(flops, nbytes):
     return pl.CostEstimate(flops=int(flops), bytes_accessed=int(nbytes), transcendentals=0)
 
 
-def wave_kernel(extent, me_ref, length_ref, row_ref, col_ref, plane_ref, coef_ref, out_ref, kc_ref, len_ref, whi_ref, wlo_ref, sc_ref, ss_ref):
+def wave_kernel(
+    extent, me_ref, length_hbm, row_hbm, col_hbm, plane_hbm, coef_hbm,
+    out_ref, kc_ref, len_ref, whi_ref, wlo_ref, sc_ref, ss_ref,
+    length_ref, row_ref, col_ref, plane_ref, coef_ref, sems,
+):
+    copies = fetch_all(
+        (length_hbm, row_hbm, col_hbm, plane_hbm, coef_hbm),
+        (length_ref, row_ref, col_ref, plane_ref, coef_ref),
+        sems,
+    )
+    for copy in copies:
+        copy.wait()
     devices = out_ref.shape[0]
     sticks, _, padded = coef_ref.shape
     padded_planes = plane_ref.shape[1] // devices
@@ -192,7 +221,12 @@
     return jnp.concatenate(parts, axis=1)
 
 
-def map_kernel(extent, sticks, in_row_ref, in_col_ref, map_ref, first_ref, src_ref, dst_ref, row_ref, col_ref):
+def map_kernel(
+    extent, sticks, in_row_hbm, in_col_hbm, map_ref, first_ref, src_ref, dst_ref, row_ref, col_ref,
+    in_row_ref, in_col_ref, sems,
+):
+    for copy in fetch_all((in_row_hbm, in_col_hbm), (in_row_ref, in_col_ref), sems):
+        copy.wait()
     windows = src_ref.shape[0]
     total = windows * LANES
 
@@ -262,17 +296,16 @@
 
 def plane_kernel(
     planes, first_ref, map_ref, src_ref, dst_ref, row_ref, col_ref, recv_ref,
-    y_even, y_odd, x_forward, x_back, back_even, back_odd,
-    pot_hbm, out_ref, x_ref, s_ref, gr_ref, gi_ref, pot_ref, sem,
+    *refs,
 ):
+    table_hbm, pot_hbm, out_ref, x_ref, s_ref, gr_ref, gi_ref, table_ref, pot_ref, sems = refs
     devices = recv_ref.shape[0]
     padded_planes = recv_ref.shape[1] // 3
     windows = x_ref.shape[0]
     rows = gr_ref.shape[0] // padded_planes
     extent = pot_ref.shape[1]
     half = LANES // 2
-    fetch = pltpu.make_async_copy(pot_hbm, pot_ref, sem)
-    fetch.start()
+    copies = fetch_all((table_hbm, pot_hbm), (table_ref, pot_ref), sems)
 
     low = lax.broadcasted_iota(jnp.int32, (padded_planes, LANES), 1) < half
     for d in range(devices):
@@ -315,10 +348,25 @@
             part, at = j // blocks, 8 * (j % blocks)
             grids[part][pl.ds(r + at * rows, 8, stride=rows), :] = value
 
-    fetch.wait()
+    for copy in copies:
+        copy.wait()
     even_rows, odd_rows = row_blocks()
     folded = extent // 2
     group = next(g for g in (8, 4, 2) if planes % g == 0)
+
+    wide = table_ref.shape[1] // 2
+    deep = 6 * LANES
+    at_y = deep + 3 * wide
+    at_even = at_y + extent
+    at_odd = at_even + 2 * even_rows
+    x_forward = table_ref[0:deep, :]
+    x_back = jnp.concatenate(
+        [table_ref[deep:at_y, :wide], table_ref[deep:at_y, wide:]], axis=0
+    )
+    y_even = table_ref[at_y:at_even, :3 * even_rows]
+    y_odd = table_ref[at_y:at_even, wide:wide + 3 * odd_rows]
+    back_even = table_ref[at_even:at_odd, :3 * folded]
+    back_odd = table_ref[at_odd:at_odd + 2 * odd_rows, :3 * folded]
 
     def dot(x, y):
         return jnp.dot(x, y, preferred_element_type=F32)
@@ -342,19 +390,18 @@
             parts = []
             for pick, table, size in ((even, y_even, even_rows), (odd, y_odd, odd_rows)):
                 spectrum = jnp.concatenate([gr_ref[pick, :], gi_ref[pick, :]], axis=1)
-                parts.append(times_wave(dot(table[...], stack(spectrum, 0)), folded, 1.0))
+                parts.append(times_wave(dot(table, stack(spectrum, 0)), folded, 1.0))
             (e_re, e_im), (o_re, o_im) = parts
             lines.append(jnp.concatenate([e_re + o_re, e_im + o_im], axis=1))
             lines.append(jnp.concatenate([e_re - o_re, e_im - o_im], axis=1))
-        field = dot(stack(jnp.concatenate(lines, axis=0), 1), x_forward[...])
-        wide = field.shape[1] // 2
+        field = dot(stack(jnp.concatenate(lines, axis=0), 1), x_forward)
         spare = jnp.zeros((extent, wide - extent), F32)
         weighted = []
         for t in range(group):
             v = jnp.concatenate([pot_ref[step * group + t], spare], axis=1)
             mine = field[t * extent:(t + 1) * extent]
             weighted.append(jnp.concatenate([mine[:, :wide] * v, mine[:, wide:] * v], axis=1))
-        back = dot(stack(jnp.concatenate(weighted, axis=0), 1), x_back[...])
+        back = dot(stack(jnp.concatenate(weighted, axis=0), 1), x_back)
         for t in range(group):
             base = pl.multiple_of((step * group + t) * rows, 16)
             even, odd = pl.ds(base, even_rows), pl.ds(base + even_rows, odd_rows)
@@ -363,7 +410,7 @@
             for pick, table, size, value in (
                 (even, back_even, even_rows, upper + lower), (odd, back_odd, odd_rows, upper - lower)
             ):
-                re, im = times_wave(dot(table[...], stack(value, 0)), size, -1.0)
+                re, im = times_wave(dot(table, stack(value, 0)), size, -1.0)
                 gr_ref[pick, :] = re
                 gi_ref[pick, :] = im
 
@@ -500,6 +547,7 @@
     windows = total_sticks // LANES
     smem = pl.BlockSpec(memory_space=pltpu.SMEM)
     vmem = pl.BlockSpec(memory_space=pltpu.VMEM)
+    hbm = pl.BlockSpec(memory_space=pltpu.HBM)
 
     block = 3 * padded_planes
     total_planes = devices * padded_planes
@@ -514,8 +562,16 @@
             jax.ShapeDtypeStruct((total_planes, sticks), F32),
             jax.ShapeDtypeStruct((total_planes, sticks), F32),
         ),
-        in_specs=[smem] + [vmem] * 5,
-        compiler_params=params(8 + 8 * total_planes / 192),
+        in_specs=[smem] + [hbm] * 5,
+        scratch_shapes=[
+            pltpu.VMEM(length.shape, jnp.int32),
+            pltpu.VMEM(row.shape, jnp.int32),
+            pltpu.VMEM(col.shape, jnp.int32),
+            pltpu.VMEM(slots.shape, jnp.int32),
+            pltpu.VMEM(coef.shape, F32),
+            pltpu.SemaphoreType.DMA((5,)),
+        ],
+        compiler_params=params(56),
         name="wave_to_planes",
     )(me.reshape(1), length, row, col, slots, coef)
 
@@ -533,28 +589,36 @@
             longer_list,
             longer_list,
         ),
+        in_specs=[hbm] * 2,
+        scratch_shapes=[
+            pltpu.VMEM(row.shape, jnp.int32),
+            pltpu.VMEM(col.shape, jnp.int32),
+            pltpu.SemaphoreType.DMA((2,)),
+        ],
         compiler_params=params(14 * total_sticks / 1536),
         cost_estimate=cost(4e9, 1e5),
         name="stick_map",
     )(row, col)
 
+    constants = jnp.asarray(tables(extent))
     weighted = pl.pallas_call(
         functools.partial(plane_kernel, planes),
         out_shape=jax.ShapeDtypeStruct((devices, block + 8, LANES), F32),
-        in_specs=[smem] + [vmem] * 12 + [pl.BlockSpec(memory_space=pl.ANY)],
+        in_specs=[smem] + [vmem] * 6 + [hbm] * 2,
         out_specs=vmem,
         scratch_shapes=[
             pltpu.VMEM((windows, 2 * padded_planes, LANES), F32),
             pltpu.VMEM((windows + 1, 2 * padded_planes, LANES), F32),
             pltpu.VMEM((padded_planes * rows, LANES), F32),
             pltpu.VMEM((padded_planes * rows, LANES), F32),
+            pltpu.VMEM(constants.shape, BF16),
             pltpu.VMEM(potential.shape, F32),
-            pltpu.SemaphoreType.DMA,
+            pltpu.SemaphoreType.DMA((2,)),
         ],
-        compiler_params=params(36),
+        compiler_params=params(52),
         cost_estimate=cost(2e10, 1e7),
         name="planes",
-    )(first, stick_map, source, target, row_w, col_w, received, *[jnp.asarray(t) for t in tables(extent)], potential)
+    )(first, stick_map, source, target, row_w, col_w, received, constants, potential)
 
     coefs, fields = [coef], [received]
     for shift in range(1, bands):

time: 77 us -> 64.4 us (0.84)
  local copies, waits for them, and re-layouts: 16.3 us -> 1.42 us
  waiting for transfers between devices: 3.19 us -> 5.41 us
    unnamed x46 -> x18, local copies, waits for them, and re-layouts: 16.3 us -> 1.42 us
    all_to_all x1, waiting for transfers between devices: 0.63 us -> 3.02 us  [shards(): lax.all_to_all(sent, 'tg', split_axis=0, concat_axis=0, tiled=True)]
    pallas_call x1, Pallas kernels: 1.8 us -> 2.91 us  [shards(): pl.pallas_call(functools.partial(wave_kernel, extent), out_shape=(jax.Sha...]
  transfers between devices with their start and end apart: 14 -> 14, of which waited for: 4 -> 4; matrix products, arithmetic and copies ran while one was open for 0% -> 0% of each run, Pallas kernels for 36% -> 42%
where the time goes in v9:
time: 64.4 us; the launch traced here: 64.1 us
  Pallas kernels  32.4 us (50%)
  starting transfers between devices  24 us (37%)
  waiting for transfers between devices  5.41 us (8%)
  local copies, waits for them, and re-layouts  1.42 us (2%)
  between operations  0.79 us (1%)
    pallas_call x1, Pallas kernels, shards(): pl.pallas_call(functools.partial(plane_kernel, planes), out_shape=jax.Sha...  24.7 us
    ppermute x7, starting transfers between devices, shards(): returned.append(lax.ppermute(outgoing[k], 'tg', ring))  10.7 us
    all_to_all x1, starting transfers between devices, shards(): lax.all_to_all(sent, 'tg', split_axis=0, concat_axis=0, tiled=True)  7.27 us
    all_to_all x1, waiting for transfers between devices, shards(): lax.all_to_all(sent, 'tg', split_axis=0, concat_axis=0, tiled=True)  3.02 us
    ppermute x3, starting transfers between devices, shards(): fields.append(lax.ppermute(received, 'band', ring))  2.99 us
    ppermute x3, starting transfers between devices, shards(): coefs.append(lax.ppermute(coef, 'band', ring))  2.98 us
    pallas_call x1, Pallas kernels, shards(): pl.pallas_call(functools.partial(wave_kernel, extent), out_shape=(jax.Sha...  2.91 us
    ppermute x7, waiting for transfers between devices, shards(): returned.append(lax.ppermute(outgoing[k], 'tg', ring))  2.37 us
  transfers between devices with their start and end apart: 14, of which 4 were waited for; matrix products, arithmetic and copies ran while one was open for 0% of the time, Pallas kernels for 42%

profile of v9, /device:TPU:0, one launch (start us, length us, event | category | flops | bytes accessed | tf_op | source)
XLA Modules:
  0.0 64.1 jit_solution(1387861755464928860)
XLA Ops:
  0.6 2.9 %wave_to_planes.1 = (f32[8,72,128]{2,1,0:T(8,128)}, f32[192,256]{1,0:T(8,128)}, f32[192,128]{1,0:T(8,128)}, bf16[384,256]{1,0:T(8,128)(2,1)}, bf16[384,256]{1,0:...) custom-call(s32[1]{0:T(128)} %bitcast.me_ref, s32[12,128]{1,0:T(8,128)} %bitcast.17, s32[12,128]{1,0:T(8,128)} %bitcast.13, ...), custom_call_target="tpu_custom_call" | custom-call | tf_op jit(solution)/shard_map/wave_to_planes/pallas_call | solution.py:554
  3.6 7.3 %all-to-all-start = ((f32[8,72,128]{2,1,0:T(8,128)}), f32[8,72,128]{2,1,0:T(8,128)S(1)}, u32[]{:S(2)}, u32[]{:S(2)}) async-start(f32[8,72,128]{2,1,0:T(8,128)} %get-tuple-element.27), calls=%async_computation | async-start | bytes 589824 | tf_op jit(solution)/shard_map/all_to_all | solution.py:578
  10.8 0.0 collective-permute-start.2
  10.8 1.6 %collective-permute-start.1 = (f32[192,2,128]{2,1,0:T(2,128)}, f32[192,2,128]{2,1,0:T(2,128)S(1)}, u32[]{:S(2)}, u32[]{:S(2)}) collective-permute-start(f32[192,2,128]{2,1,0:T(2,128)} %bitcast.10), channel_id=1, source_target_pairs={{16,0},{24,8},{0,16},{8,24},{17,1},{25,9},{1,17},{9,25},{18,2},{26... | collective-permute-start | bytes 589832 | tf_op jit(solution)/shard_map/ppermute | solution.py:626
  12.4 1.4 %collective-permute-start = (f32[192,2,128]{2,1,0:T(2,128)}, f32[192,2,128]{2,1,0:T(2,128)S(1)}, u32[]{:S(2)}, u32[]{:S(2)}) collective-permute-start(f32[192,2,128]{2,1,0:T(2,128)} %bitcast.11), channel_id=1, source_target_pairs={{8,0},{16,8},{24,16},{0,24},{9,1},{17,9},{25,17},{1,25},{10,2},{18... | collective-permute-start | bytes 589832 | tf_op jit(solution)/shard_map/ppermute | solution.py:626
  13.8 0.7 %copy-done.7 = s32[1536]{0:T(1024)S(1)} copy-done((s32[1536]{0:T(1024)S(1)}, s32[1536]{0:T(1024)}, u32[]{:S(2)}) %copy-start.7) | copy-done | bytes 6168
  14.5 0.7 %copy-done.8 = s32[1536]{0:T(1024)S(1)} copy-done((s32[1536]{0:T(1024)S(1)}, s32[1536]{0:T(1024)}, u32[]{:S(2)}) %copy-start.8) | copy-done | bytes 6168
  15.2 2.1 %stick_map.1 = (s32[128,128]{1,0:T(8,128)S(1)}, s32[8,128]{1,0:T(8,128)S(1)}, s32[12,128]{1,0:T(8,128)S(1)}, s32[12,128]{1,0:T(8,128)S(1)}, s32[13,128]{1,0:T(8,128)S(1)}, /*index=5*/s32[13,128]{1,0:T(8,128)S(1)}) custom-call(s32[12,128]{1,0:T(8,128)S(1)} %bitcast.14, s32[12,128]{1,0:T(8,128)S(1)} %bitcast.16), custom_call_target="tpu_custom_call" | custom-call | flops 4000000000 | bytes 100000 | tf_op jit(solution)/shard_map/stick_map/pallas_call | solution.py:582
  17.3 0.1 pad_add_fusion.place_ref
  17.4 3.0 %all-to-all-done.recv_ref.refs_5_ = f32[8,72,128]{2,1,0:T(8,128)S(1)} async-done(((f32[8,72,128]{2,1,0:T(8,128)}), f32[8,72,128]{2,1,0:T(8,128)S(1)}, u32[]{:S(2)}, u32[]{:S(2)}) %all-to-all-start) | async-done | bytes 294944 | tf_op jit(solution)/shard_map/all_to_all | solution.py:578
  20.4 0.0 collective-permute-start.5
  20.4 1.6 %collective-permute-start.4 = (f32[8,72,128]{2,1,0:T(8,128)S(1)}, f32[8,72,128]{2,1,0:T(8,128)S(1)}, u32[]{:S(2)}, u32[]{:S(2)}) collective-permute-start(f32[8,72,128]{2,1,0:T(8,128)S(1)} %all-to-all-done.recv_ref.refs_5_), channel_id=1, source_target_pairs={{16,0},{24,8},{0,16},{8,24},{17,1},{25,9},{1,17},{9,25},{18,2},{26... | collective-permute-start | bytes 884744 | tf_op jit(solution)/shard_map/ppermute | solution.py:627
  22.0 0.0 collective-permute-done.2.refs_4_
  22.0 1.4 %collective-permute-start.3 = (f32[8,72,128]{2,1,0:T(8,128)S(1)}, f32[8,72,128]{2,1,0:T(8,128)S(1)}, u32[]{:S(2)}, u32[]{:S(2)}) collective-permute-start(f32[8,72,128]{2,1,0:T(8,128)S(1)} %all-to-all-done.recv_ref.refs_5_), channel_id=1, source_target_pairs={{8,0},{16,8},{24,16},{0,24},{9,1},{17,9},{25,17},{1,25},{10,2},{18... | collective-permute-start | bytes 884744 | tf_op jit(solution)/shard_map/ppermute | solution.py:627
  23.5 24.7 %planes.1.refs_9_ = f32[8,80,128]{2,1,0:T(8,128)S(1)} custom-call(s32[8,128]{1,0:T(8,128)S(1)} %get-tuple-element.28.first_ref, s32[128,128]{1,0:T(8,128)S(1)} %get-tuple-element.29.map_ref, s32[12,128]{1,0:T(8,128)S(1)} %get-tuple-element.30.src_ref, s32[12,128]{1,0:T(8,128)S(1)} %get-tuple-element.31.dst_ref, s32[13,128]{1,0:T(8,128)S(1)} %get-tuple-element.32.row_ref, ...), custom_call_target="tpu_custom_call" | custom-call | flops 20000000000 | bytes 10000000 | tf_op jit(solution)/shard_map/planes/pallas_call | solution.py:604
  48.2 0.0 collective-permute-done.1.refs_3_
  48.2 0.0 collective-permute-done.5.refs_8_
  48.2 0.0 collective-permute-done.4.refs_7_
  48.2 1.4 %inner.1 = (f32[80,128]{1,0:T(8,128)S(1)}, f32[80,128]{1,0:T(8,128)S(1)}, f32[80,128]{1,0:T(8,128)S(1)}, f32[80,128]{1,0:T(8,128)S(1)}, f32[80,128]{1,0:T(8,128)...) custom-call(s32[2]{0:T(128)S(1)} %pad_add_fusion.place_ref, f32[192,256]{1,0:T(8,128)S(1)} %copy-done, ...), custom_call_target="tpu_custom_call" | custom-call | tf_op jit(solution)/shard_map/inner/pallas_call | solution.py:631
  49.7 1.4 %collective-permute-start.6 = (f32[80,128]{1,0:T(8,128)S(1)}, f32[80,128]{1,0:T(8,128)S(1)}, u32[]{:S(2)}, u32[]{:S(2)}) collective-permute-start(f32[80,128]{1,0:T(8,128)S(1)} %get-tuple-element.35), channel_id=1, source_target_pairs={{0,1},{1,2},{2,3},{3,4},{4,5},{5,6},{6,7},{7,0},{8,9},{9,10},{10,1... | collective-permute-start | bytes 122888 | tf_op jit(solution)/shard_map/ppermute | solution.py:642
  51.1 0.0 collective-permute-start.7
  51.1 1.8 %collective-permute-start.8 = (f32[80,128]{1,0:T(8,128)S(1)}, f32[80,128]{1,0:T(8,128)S(1)}, u32[]{:S(2)}, u32[]{:S(2)}) collective-permute-start(f32[80,128]{1,0:T(8,128)S(1)} %get-tuple-element.37), channel_id=1, source_target_pairs={{0,3},{1,4},{2,5},{3,6},{4,7},{5,0},{6,1},{7,2},{8,11},{9,12},{10,... | collective-permute-start | bytes 122888 | tf_op jit(solution)/shard_map/ppermute | solution.py:642
  52.9 3.1 %collective-permute-start.9 = (f32[80,128]{1,0:T(8,128)S(1)}, f32[80,128]{1,0:T(8,128)S(1)}, u32[]{:S(2)}, u32[]{:S(2)}) collective-permute-start(f32[80,128]{1,0:T(8,128)S(1)} %get-tuple-element.38), channel_id=1, source_target_pairs={{0,4},{1,5},{2,6},{3,7},{4,0},{5,1},{6,2},{7,3},{8,12},{9,13},{10,... | collective-permute-start | bytes 122888 | tf_op jit(solution)/shard_map/ppermute | solution.py:642
  56.0 1.0 %collective-permute-start.10 = (f32[80,128]{1,0:T(8,128)S(1)}, f32[80,128]{1,0:T(8,128)S(1)}, u32[]{:S(2)}, u32[]{:S(2)}) collective-permute-start(f32[80,128]{1,0:T(8,128)S(1)} %get-tuple-element.39), channel_id=1, source_target_pairs={{0,5},{1,6},{2,7},{3,0},{4,1},{5,2},{6,3},{7,4},{8,13},{9,14},{10,... | collective-permute-start | bytes 122888 | tf_op jit(solution)/shard_map/ppermute | solution.py:642
  57.0 0.0 collective-permute-done.6.refs_1_
  57.0 1.8 %collective-permute-start.11 = (f32[80,128]{1,0:T(8,128)S(1)}, f32[80,128]{1,0:T(8,128)S(1)}, u32[]{:S(2)}, u32[]{:S(2)}) collective-permute-start(f32[80,128]{1,0:T(8,128)S(1)} %get-tuple-element.40), channel_id=1, source_target_pairs={{0,6},{1,7},{2,0},{3,1},{4,2},{5,3},{6,4},{7,5},{8,14},{9,15},{10,... | collective-permute-start | bytes 122888 | tf_op jit(solution)/shard_map/ppermute | solution.py:642
  58.8 1.6 %collective-permute-start.12 = (f32[80,128]{1,0:T(8,128)S(1)}, f32[80,128]{1,0:T(8,128)S(1)}, u32[]{:S(2)}, u32[]{:S(2)}) collective-permute-start(f32[80,128]{1,0:T(8,128)S(1)} %get-tuple-element.41), channel_id=1, source_target_pairs={{0,7},{1,0},{2,1},{3,2},{4,3},{5,4},{6,5},{7,6},{8,15},{9,8},{10,9... | collective-permute-start | bytes 122888 | tf_op jit(solution)/shard_map/ppermute | solution.py:642
  60.4 0.0 collective-permute-done.8.refs_3_
  60.4 0.5 collective-permute-done.10.refs_5_
  60.9 0.5 collective-permute-done.11.refs_6_
  61.4 1.4 %collective-permute-done.12.refs_7_ = f32[80,128]{1,0:T(8,128)S(1)} collective-permute-done((f32[80,128]{1,0:T(8,128)S(1)}, f32[80,128]{1,0:T(8,128)S(1)}, u32[]{:S(2)}, u32[]{:S(2)}) %collective-permute-start.12) | collective-permute-done | bytes 40992 | tf_op jit(solution)/shard_map/ppermute | solution.py:642
  62.8 1.3 %planes_to_wave.1 = (f32[192,2,128]{2,1,0:T(2,128)}, f32[2,1,4]{2,1,0:T(1,128)}) custom-call(s32[1]{0:T(128)} %bitcast.me_ref, f32[192,128]{1,0:T(8,128)S(1)} %copy-done.6, f32[80,128]{1,0:T(8,128)S(1)} %get-tuple-element.34.refs_0_, f32[80,128]{1,0:T(8,128)S(1)} %collective-permute-done.6.refs_1_, f32[80,128]{1,0:T(8,128)S(1)} %collective-permute-done.7.refs_2_, ...), custom_call_target="tpu_custom_call" | custom-call | tf_op jit(solution)/shard_map/planes_to_wave/pallas_call | solution.py:643
  (20 shorter events, 0.0 us)
Async XLA Ops:
  3.6 16.9 %all-to-all-start = ((f32[8,72,128]{2,1,0:T(8,128)}), f32[8,72,128]{2,1,0:T(8,128)S(1)}, u32[]{:S(2)}, u32[]{:S(2)}) async-start(f32[8,72,128]{2,1,0:T(8,128)} %get-tuple-element.27), calls=%async_computation | async-start | bytes 589824 | tf_op jit(solution)/shard_map/all_to_all | solution.py:578
  10.8 11.2 %collective-permute-start.2 = (f32[192,2,128]{2,1,0:T(2,128)}, f32[192,2,128]{2,1,0:T(2,128)S(1)}, u32[]{:S(2)}, u32[]{:S(2)}) collective-permute-start(f32[192,2,128]{2,1,0:T(2,128)} %bitcast.9), channel_id=1, source_target_pairs={{24,0},{0,8},{8,16},{16,24},{25,1},{1,9},{9,17},{17,25},{26,2},{2,... | collective-permute-start | bytes 589832 | tf_op jit(solution)/shard_map/ppermute | solution.py:626
  10.8 37.3 %collective-permute-start.1 = (f32[192,2,128]{2,1,0:T(2,128)}, f32[192,2,128]{2,1,0:T(2,128)S(1)}, u32[]{:S(2)}, u32[]{:S(2)}) collective-permute-start(f32[192,2,128]{2,1,0:T(2,128)} %bitcast.10), channel_id=1, source_target_pairs={{16,0},{24,8},{0,16},{8,24},{17,1},{25,9},{1,17},{9,25},{18,2},{26... | collective-permute-start | bytes 589832 | tf_op jit(solution)/shard_map/ppermute | solution.py:626
  12.4 35.8 %collective-permute-start = (f32[192,2,128]{2,1,0:T(2,128)}, f32[192,2,128]{2,1,0:T(2,128)S(1)}, u32[]{:S(2)}, u32[]{:S(2)}) collective-permute-start(f32[192,2,128]{2,1,0:T(2,128)} %bitcast.11), channel_id=1, source_target_pairs={{8,0},{16,8},{24,16},{0,24},{9,1},{17,9},{25,17},{1,25},{10,2},{18... | collective-permute-start | bytes 589832 | tf_op jit(solution)/shard_map/ppermute | solution.py:626
  13.8 0.7 %copy-start.7 = (s32[1536]{0:T(1024)S(1)}, s32[1536]{0:T(1024)}, u32[]{:S(2)}) copy-start(s32[1536]{0:T(1024)} %param.9) | copy-start | bytes 18436
  14.5 0.7 %copy-start.8 = (s32[1536]{0:T(1024)S(1)}, s32[1536]{0:T(1024)}, u32[]{:S(2)}) copy-start(s32[1536]{0:T(1024)} %param.8) | copy-start | bytes 18436
  20.4 27.8 %collective-permute-start.5 = (f32[8,72,128]{2,1,0:T(8,128)S(1)}, f32[8,72,128]{2,1,0:T(8,128)S(1)}, u32[]{:S(2)}, u32[]{:S(2)}) collective-permute-start(f32[8,72,128]{2,1,0:T(8,128)S(1)} %all-to-all-done.recv_ref.refs_5_), channel_id=1, source_target_pairs={{24,0},{0,8},{8,16},{16,24},{25,1},{1,9},{9,17},{17,25},{26,2},{2,... | collective-permute-start | bytes 884744 | tf_op jit(solution)/shard_map/ppermute | solution.py:627
  20.4 27.8 %collective-permute-start.4 = (f32[8,72,128]{2,1,0:T(8,128)S(1)}, f32[8,72,128]{2,1,0:T(8,128)S(1)}, u32[]{:S(2)}, u32[]{:S(2)}) collective-permute-start(f32[8,72,128]{2,1,0:T(8,128)S(1)} %all-to-all-done.recv_ref.refs_5_), channel_id=1, source_target_pairs={{16,0},{24,8},{0,16},{8,24},{17,1},{25,9},{1,17},{9,25},{18,2},{26... | collective-permute-start | bytes 884744 | tf_op jit(solution)/shard_map/ppermute | solution.py:627
  22.0 26.2 %collective-permute-start.3 = (f32[8,72,128]{2,1,0:T(8,128)S(1)}, f32[8,72,128]{2,1,0:T(8,128)S(1)}, u32[]{:S(2)}, u32[]{:S(2)}) collective-permute-start(f32[8,72,128]{2,1,0:T(8,128)S(1)} %all-to-all-done.recv_ref.refs_5_), channel_id=1, source_target_pairs={{8,0},{16,8},{24,16},{0,24},{9,1},{17,9},{25,17},{1,25},{10,2},{18... | collective-permute-start | bytes 884744 | tf_op jit(solution)/shard_map/ppermute | solution.py:627
  23.4 24.8 %copy-start = (f32[192,256]{1,0:T(8,128)S(1)}, f32[192,256]{1,0:T(8,128)}, u32[]{:S(2)}) copy-start(f32[192,256]{1,0:T(8,128)} %get-tuple-element.26.refs_0_.refs_8_) | copy-start | bytes 589828
  23.4 24.8 %copy-start.1 = (f32[1,192,2,128]{3,2,1,0:T(2,128)S(1)}, f32[1,192,2,128]{3,2,1,0:T(2,128)}, u32[]{:S(2)}) copy-start(f32[1,192,2,128]{3,2,1,0:T(2,128)} %param.7) | copy-start | bytes 589828
  23.4 39.3 %copy-start.2 = (bf16[384,256]{1,0:T(8,128)(2,1)S(1)}, bf16[384,256]{1,0:T(8,128)(2,1)}, u32[]{:S(2)}) copy-start(bf16[384,256]{1,0:T(8,128)(2,1)} %get-tuple-element.42.refs_9_) | copy-start | bytes 589828
  23.4 39.3 %copy-start.3 = (bf16[384,256]{1,0:T(8,128)(2,1)S(1)}, bf16[384,256]{1,0:T(8,128)(2,1)}, u32[]{:S(2)}) copy-start(bf16[384,256]{1,0:T(8,128)(2,1)} %get-tuple-element.43.refs_10_) | copy-start | bytes 589828
  23.4 39.3 %copy-start.4 = (f32[192,192]{1,0:T(8,128)S(1)}, f32[192,192]{1,0:T(8,128)}, u32[]{:S(2)}) copy-start(f32[192,192]{1,0:T(8,128)} %get-tuple-element.44.refs_11_) | copy-start | bytes 442372
  23.5 39.3 %copy-start.5 = (f32[192,192]{1,0:T(8,128)S(1)}, f32[192,192]{1,0:T(8,128)}, u32[]{:S(2)}) copy-start(f32[192,192]{1,0:T(8,128)} %get-tuple-element.45.refs_12_) | copy-start | bytes 442372
  23.5 39.3 %copy-start.6 = (f32[192,128]{1,0:T(8,128)S(1)}, f32[192,128]{1,0:T(8,128)}, u32[]{:S(2)}) copy-start(f32[192,128]{1,0:T(8,128)} %get-tuple-element.25.len_ref) | copy-start | bytes 294916
  49.7 7.3 %collective-permute-start.6 = (f32[80,128]{1,0:T(8,128)S(1)}, f32[80,128]{1,0:T(8,128)S(1)}, u32[]{:S(2)}, u32[]{:S(2)}) collective-permute-start(f32[80,128]{1,0:T(8,128)S(1)} %get-tuple-element.35), channel_id=1, source_target_pairs={{0,1},{1,2},{2,3},{3,4},{4,5},{5,6},{6,7},{7,0},{8,9},{9,10},{10,1... | collective-permute-start | bytes 122888 | tf_op jit(solution)/shard_map/ppermute | solution.py:642
  51.1 7.7 %collective-permute-start.7 = (f32[80,128]{1,0:T(8,128)S(1)}, f32[80,128]{1,0:T(8,128)S(1)}, u32[]{:S(2)}, u32[]{:S(2)}) collective-permute-start(f32[80,128]{1,0:T(8,128)S(1)} %get-tuple-element.36), channel_id=1, source_target_pairs={{0,2},{1,3},{2,4},{3,5},{4,6},{5,7},{6,0},{7,1},{8,10},{9,11},{10,... | collective-permute-start | bytes 122888 | tf_op jit(solution)/shard_map/ppermute | solution.py:642
  51.1 9.3 %collective-permute-start.8 = (f32[80,128]{1,0:T(8,128)S(1)}, f32[80,128]{1,0:T(8,128)S(1)}, u32[]{:S(2)}, u32[]{:S(2)}) collective-permute-start(f32[80,128]{1,0:T(8,128)S(1)} %get-tuple-element.37), channel_id=1, source_target_pairs={{0,3},{1,4},{2,5},{3,6},{4,7},{5,0},{6,1},{7,2},{8,11},{9,12},{10,... | collective-permute-start | bytes 122888 | tf_op jit(solution)/shard_map/ppermute | solution.py:642
  52.9 7.5 %collective-permute-start.9 = (f32[80,128]{1,0:T(8,128)S(1)}, f32[80,128]{1,0:T(8,128)S(1)}, u32[]{:S(2)}, u32[]{:S(2)}) collective-permute-start(f32[80,128]{1,0:T(8,128)S(1)} %get-tuple-element.38), channel_id=1, source_target_pairs={{0,4},{1,5},{2,6},{3,7},{4,0},{5,1},{6,2},{7,3},{8,12},{9,13},{10,... | collective-permute-start | bytes 122888 | tf_op jit(solution)/shard_map/ppermute | solution.py:642
  56.0 4.9 %collective-permute-start.10 = (f32[80,128]{1,0:T(8,128)S(1)}, f32[80,128]{1,0:T(8,128)S(1)}, u32[]{:S(2)}, u32[]{:S(2)}) collective-permute-start(f32[80,128]{1,0:T(8,128)S(1)} %get-tuple-element.39), channel_id=1, source_target_pairs={{0,5},{1,6},{2,7},{3,0},{4,1},{5,2},{6,3},{7,4},{8,13},{9,14},{10,... | collective-permute-start | bytes 122888 | tf_op jit(solution)/shard_map/ppermute | solution.py:642
  57.0 4.4 %collective-permute-start.11 = (f32[80,128]{1,0:T(8,128)S(1)}, f32[80,128]{1,0:T(8,128)S(1)}, u32[]{:S(2)}, u32[]{:S(2)}) collective-permute-start(f32[80,128]{1,0:T(8,128)S(1)} %get-tuple-element.40), channel_id=1, source_target_pairs={{0,6},{1,7},{2,0},{3,1},{4,2},{5,3},{6,4},{7,5},{8,14},{9,15},{10,... | collective-permute-start | bytes 122888 | tf_op jit(solution)/shard_map/ppermute | solution.py:642
  58.8 4.0 %collective-permute-start.12 = (f32[80,128]{1,0:T(8,128)S(1)}, f32[80,128]{1,0:T(8,128)S(1)}, u32[]{:S(2)}, u32[]{:S(2)}) collective-permute-start(f32[80,128]{1,0:T(8,128)S(1)} %get-tuple-element.41), channel_id=1, source_target_pairs={{0,7},{1,0},{2,1},{3,2},{4,3},{5,4},{6,5},{7,6},{8,15},{9,8},{10,9... | collective-permute-start | bytes 122888 | tf_op jit(solution)/shard_map/ppermute | solution.py:642

commit v10 on v9

--- a/solution.py
+++ b/solution.py
@@ -65,47 +65,46 @@
 
 @functools.cache
 def tables(extent):
-    kept = 2 * RADIUS + 1
     half = extent // 2
     grid = np.arange(extent)
-    freq = np.arange(kept) - RADIUS
+    freq = np.arange(2 * RADIUS + 1) - RADIUS
 
     def angles(f, g):
         a = 2.0 * np.pi * ((f[:, None] * g[None, :]) % extent) / extent
         return np.cos(a), np.sin(a)
 
-    cos, sin = angles(freq, grid)
     wide = 2 * LANES
-    x_table = np.zeros((wide, 2 * wide))
-    x_table[:kept, :extent] = cos
-    x_table[LANES:LANES + kept, :extent] = -sin
-    x_table[:kept, wide:wide + extent] = sin
-    x_table[LANES:LANES + kept, wide:wide + extent] = cos
-    forward, back = [], []
+    x_forward, x_back, forward, back = [], [], [], []
     for offset, rows in zip((0, 1), row_blocks()):
         cos, sin = angles(freq[offset::2], grid[:half])
         count = cos.shape[0]
-        table = np.zeros((2 * half, rows))
-        table[:half, :count] = cos.T
-        table[half:, :count] = sin.T
+        table = np.zeros((LANES, wide))
+        table[:count, :half] = cos
+        table[LANES // 2:LANES // 2 + count, :half] = -sin
+        table[:count, LANES:LANES + half] = sin
+        table[LANES // 2:LANES // 2 + count, LANES:LANES + half] = cos
         hi, lo = pair(table)
-        forward.append(np.concatenate([hi, hi, lo], axis=1))
+        x_forward.append(np.concatenate([hi, hi, lo], axis=0))
+        hi, lo = pair(table.T.copy())
+        x_back.append(
+            np.concatenate(
+                [np.concatenate([hi, lo], axis=1), np.concatenate([hi, np.zeros_like(lo)], axis=1)], axis=0
+            )
+        )
+        parts = []
+        for wave in (cos, sin):
+            table = np.zeros((half, rows))
+            table[:, :count] = wave.T
+            hi, lo = pair(table)
+            parts += [hi, hi, lo]
+        forward.append(np.concatenate(parts, axis=1))
         table = np.zeros((2 * rows, half))
         table[:count] = cos
         table[rows:rows + count] = sin
         hi, lo = pair(table)
         back.append(np.concatenate([hi, hi, lo], axis=1))
-    hi, lo = pair(x_table)
-    x_forward = np.concatenate([hi, hi, lo], axis=0)
-    hi, lo = pair(x_table.T.copy())
-    x_back = np.concatenate([hi, hi, lo], axis=0)
-    depth = x_back.shape[0] // 2
-    rows = [x_forward, np.concatenate([x_back[:depth], x_back[depth:]], axis=1)]
-    y_rows = np.zeros((2 * half, 2 * wide), hi.dtype)
-    y_rows[:, :forward[0].shape[1]] = forward[0]
-    y_rows[:, wide:wide + forward[1].shape[1]] = forward[1]
-    rows.append(y_rows)
-    for table in back:
+    rows = [np.concatenate(x_forward, axis=1), np.concatenate(x_back, axis=1)]
+    for table in forward + back:
         rows.append(np.pad(table, ((0, 0), (0, 2 * wide - table.shape[1]))))
     return np.concatenate(rows, axis=0)
 
@@ -222,7 +221,8 @@
 
 
 def map_kernel(
-    extent, sticks, in_row_hbm, in_col_hbm, map_ref, first_ref, src_ref, dst_ref, row_ref, col_ref,
+    extent, sticks, in_row_hbm, in_col_hbm,
+    even_ref, odd_ref, first_ref, src_ref, dst_ref, row_ref, col_ref,
     in_row_ref, in_col_ref, sems,
 ):
     for copy in fetch_all((in_row_hbm, in_col_hbm), (in_row_ref, in_col_ref), sems):
@@ -242,7 +242,9 @@
 
     nt = ((1,), (1,))
     own_row, own_col = signed(in_row_ref), signed(in_col_ref)
+    half = LANES // 2
     own_row = (own_row & 1) * row_blocks()[0] + (own_row >> 1)
+    own_col = (own_col & 1) * half + (own_col >> 1)
     tall = lax.broadcasted_iota(jnp.int32, (LANES, total), 0)
     place = lax.broadcasted_iota(jnp.int32, (LANES, total), 1)
     in_col = tall == own_col
@@ -259,11 +261,25 @@
     start = dot(dot(after, taken_b).astype(BF16), ones)
     end = start + dot(taken_b, ones)
     start_t = dot(ones, dot(taken_tb, before).astype(BF16))
-    limit = windows - 1.0
-    first = jnp.minimum(jnp.floor(start * (1.0 / LANES)), limit)
-    code = jnp.where(taken > 0.5, dot(taken_b, before) + start - LANES * first, -1.0)
-    map_ref[...] = code.astype(jnp.int32)
-    first_ref[...] = jnp.minimum(jnp.floor(start_t[0:8] * (1.0 / LANES)), limit).astype(jnp.int32)
+    left = across < half
+    standing = dot(taken_b, before) + start
+    low_ones = bits(down < half)
+    high_start = start + dot(taken_b, low_ones)
+    ones_t = bits(across < half)
+    high_start_t = start_t + dot(ones_t, taken_tb)
+    limit = 2.0 * windows - 1.0
+
+    def first_window(value):
+        return jnp.minimum(jnp.floor(value * (1.0 / half)), limit)
+
+    for ref, begin in ((even_ref, start), (odd_ref, high_start)):
+        code = jnp.where(taken > 0.5, standing - half * first_window(begin), -1.0)
+        turned = pltpu.roll(code, half, 1)
+        both = jnp.where(left, code, turned) if ref is even_ref else jnp.where(left, turned, code)
+        ref[...] = both.astype(jnp.int32)
+    first_ref[...] = jnp.concatenate(
+        [first_window(start_t[0:8]), first_window(high_start_t[0:8])], axis=0
+    ).astype(jnp.int32)
 
     spot = place.astype(F32)
     in_range = (spot >= start[:, 0:1]) & (spot < end[:, 0:1])
@@ -282,12 +298,23 @@
     place_lo = place_t - 64.0 * place_hi
     placed = dot(place_hi.astype(BF16), row_hot) * 64.0 + dot(place_lo.astype(BF16), row_hot)
     target = jnp.sum(jnp.where(in_col, placed, 0.0), axis=0, keepdims=True)
-    for values, ref in ((source, src_ref), (target, dst_ref), (sorted_row, row_ref), (sorted_col, col_ref)):
+    for values, ref in ((source, src_ref), (target, dst_ref)):
         values = values.astype(jnp.int32)
         for w in range(windows):
             ref[w:w + 1, :] = values[:, w * LANES:(w + 1) * LANES]
-    row_ref[windows:windows + 1, :] = jnp.full((1, LANES), -1, jnp.int32)
-    col_ref[windows:windows + 1, :] = jnp.zeros((1, LANES), jnp.int32)
+    is_left = left[0:8]
+    shift = jnp.where(is_left, 0, half)
+    sorted_col = sorted_col.astype(jnp.int32)
+    sorted_key = sorted_row.astype(jnp.int32) * 2 + (sorted_col >> 6)
+    sorted_col = sorted_col & (half - 1)
+    for values, ref, add in ((sorted_key, row_ref, 0), (sorted_col, col_ref, shift)):
+        for w in range(windows):
+            line = jnp.broadcast_to(values[:, w * LANES:(w + 1) * LANES], (8, LANES))
+            turned = pltpu.roll(line, half, 1)
+            ref[2 * w:2 * w + 1, :] = (jnp.where(is_left, line, turned) + add)[0:1]
+            ref[2 * w + 1:2 * w + 2, :] = (jnp.where(is_left, turned, line) + add)[0:1]
+    row_ref[2 * windows:2 * windows + 1, :] = jnp.full((1, LANES), -1, jnp.int32)
+    col_ref[2 * windows:2 * windows + 1, :] = jnp.zeros((1, LANES), jnp.int32)
 
 
 def lane_take(x, index):
@@ -295,14 +322,14 @@
 
 
 def plane_kernel(
-    planes, first_ref, map_ref, src_ref, dst_ref, row_ref, col_ref, recv_ref,
+    planes, first_ref, even_ref, odd_ref, src_ref, dst_ref, row_ref, col_ref, recv_ref,
     *refs,
 ):
-    table_hbm, pot_hbm, out_ref, x_ref, s_ref, gr_ref, gi_ref, table_ref, pot_ref, sems = refs
+    table_hbm, pot_hbm, out_ref, x_ref, s_ref, t_ref, ge_ref, go_ref, table_ref, pot_ref, sems = refs
     devices = recv_ref.shape[0]
     padded_planes = recv_ref.shape[1] // 3
     windows = x_ref.shape[0]
-    rows = gr_ref.shape[0] // padded_planes
+    rows = ge_ref.shape[0] // padded_planes
     extent = pot_ref.shape[1]
     half = LANES // 2
     copies = fetch_all((table_hbm, pot_hbm), (table_ref, pot_ref), sems)
@@ -319,7 +346,6 @@
         )
 
     blocks = padded_planes // 8
-    grids = (gr_ref, gi_ref)
 
     def reorder(order_ref, from_ref, to_ref):
         @pl.loop(0, windows, unroll=4)
@@ -334,37 +360,42 @@
                 to_ref[v, 8 * j:8 * j + 8, :] = value
 
     reorder(src_ref, x_ref, s_ref)
+    for w in range(windows):
+        re, im = s_ref[w, 0:padded_planes, :], s_ref[w, padded_planes:2 * padded_planes, :]
+        t_ref[2 * w] = jnp.where(low, re, pltpu.roll(im, half, 1))
+        t_ref[2 * w + 1] = jnp.where(low, pltpu.roll(re, half, 1), im)
+
+    left = low[0:8]
+    upper_lanes = jnp.where(left, 0, half)
+    sides = ((0, even_ref, ge_ref), (1, odd_ref, go_ref))
 
     @pl.loop(0, rows, unroll=8)
     def _(r):
-        first = first_ref[0, r]
-        code = jnp.broadcast_to(map_ref[pl.ds(r, 1), :], (8, LANES))
-        index = code & (LANES - 1)
-        window = code >> 7
-        for j in range(2 * blocks):
-            lead = lane_take(s_ref[first, 8 * j:8 * j + 8, :], index)
-            trail = lane_take(s_ref[first + 1, 8 * j:8 * j + 8, :], index)
-            value = jnp.where(window == 0, lead, jnp.where(window == 1, trail, 0.0))
-            part, at = j // blocks, 8 * (j % blocks)
-            grids[part][pl.ds(r + at * rows, 8, stride=rows), :] = value
+        for side, code_ref, grid_ref in sides:
+            first = first_ref[8 * side, r]
+            code = jnp.broadcast_to(code_ref[pl.ds(r, 1), :], (8, LANES))
+            index = (code & (half - 1)) + upper_lanes
+            window = code >> 6
+            for j in range(blocks):
+                lead = lane_take(t_ref[first, 8 * j:8 * j + 8, :], index)
+                trail = lane_take(t_ref[first + 1, 8 * j:8 * j + 8, :], index)
+                value = jnp.where(window == 0, lead, jnp.where(window == 1, trail, 0.0))
+                grid_ref[pl.ds(r + 8 * j * rows, 8, stride=rows), :] = value
 
     for copy in copies:
         copy.wait()
     even_rows, odd_rows = row_blocks()
     folded = extent // 2
     group = next(g for g in (8, 4, 2) if planes % g == 0)
-
-    wide = table_ref.shape[1] // 2
-    deep = 6 * LANES
-    at_y = deep + 3 * wide
-    at_even = at_y + extent
+    wide = 2 * LANES
+    at_back = 3 * LANES
+    at_y = at_back + 2 * wide
+    at_even = at_y + 2 * folded
     at_odd = at_even + 2 * even_rows
-    x_forward = table_ref[0:deep, :]
-    x_back = jnp.concatenate(
-        [table_ref[deep:at_y, :wide], table_ref[deep:at_y, wide:]], axis=0
-    )
-    y_even = table_ref[at_y:at_even, :3 * even_rows]
-    y_odd = table_ref[at_y:at_even, wide:wide + 3 * odd_rows]
+    x_forward = (table_ref[0:at_back, :wide], table_ref[0:at_back, wide:])
+    x_back = (table_ref[at_back:at_y, :wide], table_ref[at_back:at_y, wide:])
+    y_even = table_ref[at_y:at_y + folded, :6 * even_rows]
+    y_odd = table_ref[at_y + folded:at_even, :6 * odd_rows]
     back_even = table_ref[at_even:at_odd, :3 * folded]
     back_odd = table_ref[at_odd:at_odd + 2 * odd_rows, :3 * folded]
 
@@ -375,60 +406,77 @@
         hi, lo = split(x)
         return jnp.concatenate([hi, lo, hi], axis=axis)
 
-    def times_wave(both, cut, sign):
-        cos, sin = both[:cut], both[cut:]
-        re = cos[:, :LANES] - sign * sin[:, LANES:]
-        im = cos[:, LANES:] + sign * sin[:, :LANES]
-        return re, im
+    def turn(x):
+        lane = lax.broadcasted_iota(jnp.int32, (x.shape[0], LANES), 1) < half
+        parts = []
+        for at in range(0, x.shape[1], LANES):
+            rolled = pltpu.roll(x[:, at:at + LANES], half, 1)
+            parts.append(jnp.where(lane, -rolled, rolled))
+        return jnp.concatenate(parts, axis=1)
 
     @pl.loop(0, planes // group)
     def _(step):
         lines = []
         for t in range(group):
             base = pl.multiple_of((step * group + t) * rows, 16)
-            even, odd = pl.ds(base, even_rows), pl.ds(base + even_rows, odd_rows)
             parts = []
-            for pick, table, size in ((even, y_even, even_rows), (odd, y_odd, odd_rows)):
-                spectrum = jnp.concatenate([gr_ref[pick, :], gi_ref[pick, :]], axis=1)
-                parts.append(times_wave(dot(table, stack(spectrum, 0)), folded, 1.0))
-            (e_re, e_im), (o_re, o_im) = parts
-            lines.append(jnp.concatenate([e_re + o_re, e_im + o_im], axis=1))
-            lines.append(jnp.concatenate([e_re - o_re, e_im - o_im], axis=1))
-        field = dot(stack(jnp.concatenate(lines, axis=0), 1), x_forward)
-        spare = jnp.zeros((extent, wide - extent), F32)
-        weighted = []
+            for at, size, table in ((0, even_rows, y_even), (even_rows, odd_rows, y_odd)):
+                pick = pl.ds(base + at, size)
+                spectrum = jnp.concatenate([ge_ref[pick, :], go_ref[pick, :]], axis=1)
+                both = jnp.concatenate([stack(spectrum, 0), stack(turn(spectrum), 0)], axis=0)
+                parts.append(dot(table, both))
+            lines.append(parts[0] + parts[1])
+            lines.append(parts[0] - parts[1])
+        lines = jnp.concatenate(lines, axis=0)
+        field_even = dot(stack(lines[:, :LANES], 1), x_forward[0])
+        field_odd = dot(stack(lines[:, LANES:], 1), x_forward[1])
+        spare = jnp.zeros((extent, LANES - folded), F32)
+        sums, differences = [], []
         for t in range(group):
-            v = jnp.concatenate([pot_ref[step * group + t], spare], axis=1)
-            mine = field[t * extent:(t + 1) * extent]
-            weighted.append(jnp.concatenate([mine[:, :wide] * v, mine[:, wide:] * v], axis=1))
-        back = dot(stack(jnp.concatenate(weighted, axis=0), 1), x_back)
+            v = pot_ref[step * group + t]
+            v_near = jnp.concatenate([v[:, :folded], spare], axis=1)
+            v_far = jnp.concatenate([v[:, folded:], spare], axis=1)
+            even = field_even[t * extent:(t + 1) * extent]
+            odd = field_odd[t * extent:(t + 1) * extent]
+            near = (even + odd) * jnp.concatenate([v_near, v_near], axis=1)
+            far = (even - odd) * jnp.concatenate([v_far, v_far], axis=1)
+            sums.append(near + far)
+            differences.append(near - far)
+        back = []
+        for weighted, table in ((sums, x_back[0]), (differences, x_back[1])):
+            both = dot(jnp.concatenate(split(jnp.concatenate(weighted, axis=0)), axis=1), table)
+            back.append(both[:, :LANES] + both[:, LANES:])
+        back = jnp.concatenate(back, axis=1)
         for t in range(group):
             base = pl.multiple_of((step * group + t) * rows, 16)
-            even, odd = pl.ds(base, even_rows), pl.ds(base + even_rows, odd_rows)
             upper = back[t * extent:t * extent + folded]
             lower = back[t * extent + folded:(t + 1) * extent]
-            for pick, table, size, value in (
-                (even, back_even, even_rows, upper + lower), (odd, back_odd, odd_rows, upper - lower)
+            for at, size, table, value in (
+                (0, even_rows, back_even, upper + lower), (even_rows, odd_rows, back_odd, upper - lower)
             ):
-                re, im = times_wave(dot(table, stack(value, 0)), size, -1.0)
-                gr_ref[pick, :] = re
-                gi_ref[pick, :] = im
+                both = dot(table, stack(value, 0))
+                value = both[:size] - turn(both[size:])
+                pick = pl.ds(base + at, size)
+                ge_ref[pick, :] = value[:, :LANES]
+                go_ref[pick, :] = value[:, LANES:]
 
     @pl.loop(0, rows, unroll=8)
     def _(r):
-        first = first_ref[0, r]
-        values = []
-        for j in range(2 * blocks):
-            part, at = j // blocks, 8 * (j % blocks)
-            values.append(grids[part][pl.ds(r + at * rows, 8, stride=rows), :])
-        for t in range(2):
-            index = jnp.broadcast_to(col_ref[pl.ds(first + t, 1), :], (8, LANES))
-            hit = jnp.broadcast_to(row_ref[pl.ds(first + t, 1), :], (8, LANES)) == r
-            for j in range(2 * blocks):
-                pltpu.store(
-                    s_ref.at[first + t, 8 * j:8 * j + 8, :], lane_take(values[j], index), mask=hit
-                )
-
+        for side, _, grid_ref in sides:
+            first = first_ref[8 * side, r]
+            values = [grid_ref[pl.ds(r + 8 * j * rows, 8, stride=rows), :] for j in range(blocks)]
+            for t in range(2):
+                index = jnp.broadcast_to(col_ref[pl.ds(first + t, 1), :], (8, LANES))
+                hit = jnp.broadcast_to(row_ref[pl.ds(first + t, 1), :], (8, LANES)) == 2 * r + side
+                for j in range(blocks):
+                    pltpu.store(
+                        t_ref.at[first + t, 8 * j:8 * j + 8, :], lane_take(values[j], index), mask=hit
+                    )
+
+    for w in range(windows):
+        first, second = t_ref[2 * w], t_ref[2 * w + 1]
+        s_ref[w, 0:padded_planes, :] = jnp.where(low, first, pltpu.roll(second, half, 1))
+        s_ref[w, padded_planes:2 * padded_planes, :] = jnp.where(low, pltpu.roll(first, half, 1), second)
     reorder(dst_ref, s_ref, x_ref)
     for w in range(devices):
         out_ref[w, 0:2 * padded_planes, :] = x_ref[w]
@@ -578,12 +626,14 @@
     received = lax.all_to_all(sent, "tg", split_axis=0, concat_axis=0, tiled=True)
 
     window_list = jax.ShapeDtypeStruct((windows, LANES), jnp.int32)
-    longer_list = jax.ShapeDtypeStruct((windows + 1, LANES), jnp.int32)
-    stick_map, first, source, target, row_w, col_w = pl.pallas_call(
+    longer_list = jax.ShapeDtypeStruct((2 * windows + 1, LANES), jnp.int32)
+    square = jax.ShapeDtypeStruct((LANES, LANES), jnp.int32)
+    even_map, odd_map, first, source, target, row_w, col_w = pl.pallas_call(
         functools.partial(map_kernel, extent, sticks),
         out_shape=(
-            jax.ShapeDtypeStruct((LANES, LANES), jnp.int32),
-            jax.ShapeDtypeStruct((8, LANES), jnp.int32),
+            square,
+            square,
+            jax.ShapeDtypeStruct((16, LANES), jnp.int32),
             window_list,
             window_list,
             longer_list,
@@ -604,11 +654,12 @@
     weighted = pl.pallas_call(
         functools.partial(plane_kernel, planes),
         out_shape=jax.ShapeDtypeStruct((devices, block + 8, LANES), F32),
-        in_specs=[smem] + [vmem] * 6 + [hbm] * 2,
+        in_specs=[smem] + [vmem] * 7 + [hbm] * 2,
         out_specs=vmem,
         scratch_shapes=[
             pltpu.VMEM((windows, 2 * padded_planes, LANES), F32),
-            pltpu.VMEM((windows + 1, 2 * padded_planes, LANES), F32),
+            pltpu.VMEM((windows, 2 * padded_planes, LANES), F32),
+            pltpu.VMEM((2 * windows + 1, padded_planes, LANES), F32),
             pltpu.VMEM((padded_planes * rows, LANES), F32),
             pltpu.VMEM((padded_planes * rows, LANES), F32),
             pltpu.VMEM(constants.shape, BF16),
@@ -618,7 +669,7 @@
         compiler_params=params(52),
         cost_estimate=cost(2e10, 1e7),
         name="planes",
-    )(first, stick_map, source, target, row_w, col_w, received, constants, potential)
+    )(first, even_map, odd_map, source, target, row_w, col_w, received, constants, potential)
 
     coefs, fields = [coef], [received]
     for shift in range(1, bands):

time: 64.4 us -> 60.4 us (0.938)
  Pallas kernels: 32.4 us -> 28.6 us
    pallas_call x1, Pallas kernels: 24.7 us -> 20.7 us  [shards(): pl.pallas_call(functools.partial(plane_kernel, planes), out_shape=jax.Sha...]
  transfers between devices with their start and end apart: 14 -> 14, of which waited for: 4 -> 4; matrix products, arithmetic and copies ran while one was open for 0% -> 0% of each run, Pallas kernels for 42% -> 38%
where the time goes in v10:
time: 60.4 us; the launch traced here: 60.1 us
  Pallas kernels  28.6 us (47%)
  starting transfers between devices  24 us (40%)
  waiting for transfers between devices  5.25 us (9%)
  local copies, waits for them, and re-layouts  1.42 us (2%)
  between operations  0.79 us (1%)
    pallas_call x1, Pallas kernels, shards(): pl.pallas_call(functools.partial(plane_kernel, planes), out_shape=jax.Sha...  20.7 us
    ppermute x7, starting transfers between devices, shards(): returned.append(lax.ppermute(outgoing[k], 'tg', ring))  10.7 us
    all_to_all x1, starting transfers between devices, shards(): lax.all_to_all(sent, 'tg', split_axis=0, concat_axis=0, tiled=True)  7.27 us
    ppermute x3, starting transfers between devices, shards(): fields.append(lax.ppermute(received, 'band', ring))  2.99 us
    ppermute x3, starting transfers between devices, shards(): coefs.append(lax.ppermute(coef, 'band', ring))  2.98 us
    pallas_call x1, Pallas kernels, shards(): pl.pallas_call(functools.partial(wave_kernel, extent), out_shape=(jax.Sha...  2.91 us
    all_to_all x1, waiting for transfers between devices, shards(): lax.all_to_all(sent, 'tg', split_axis=0, concat_axis=0, tiled=True)  2.85 us
    ppermute x7, waiting for transfers between devices, shards(): returned.append(lax.ppermute(outgoing[k], 'tg', ring))  2.38 us
  transfers between devices with their start and end apart: 14, of which 4 were waited for; matrix products, arithmetic and copies ran while one was open for 0% of the time, Pallas kernels for 38%

profile of v10, /device:TPU:0, one launch (start us, length us, event | category | flops | bytes accessed | tf_op | source)
XLA Modules:
  0.0 60.1 jit_solution(11144614607666154191)
XLA Ops:
  0.6 2.9 %wave_to_planes.1 = (f32[8,72,128]{2,1,0:T(8,128)}, f32[192,256]{1,0:T(8,128)}, f32[192,128]{1,0:T(8,128)}, bf16[384,256]{1,0:T(8,128)(2,1)}, bf16[384,256]{1,0:...) custom-call(s32[1]{0:T(128)} %bitcast.me_ref, s32[12,128]{1,0:T(8,128)} %bitcast.17, s32[12,128]{1,0:T(8,128)} %bitcast.13, ...), custom_call_target="tpu_custom_call" | custom-call | tf_op jit(solution)/shard_map/wave_to_planes/pallas_call | solution.py:602
  3.6 7.3 %all-to-all-start = ((f32[8,72,128]{2,1,0:T(8,128)}), f32[8,72,128]{2,1,0:T(8,128)S(1)}, u32[]{:S(2)}, u32[]{:S(2)}) async-start(f32[8,72,128]{2,1,0:T(8,128)} %get-tuple-element.28), calls=%async_computation | async-start | bytes 589824 | tf_op jit(solution)/shard_map/all_to_all | solution.py:626
  10.8 0.0 collective-permute-start.2
  10.8 1.6 %collective-permute-start.1 = (f32[192,2,128]{2,1,0:T(2,128)}, f32[192,2,128]{2,1,0:T(2,128)S(1)}, u32[]{:S(2)}, u32[]{:S(2)}) collective-permute-start(f32[192,2,128]{2,1,0:T(2,128)} %bitcast.10), channel_id=1, source_target_pairs={{16,0},{24,8},{0,16},{8,24},{17,1},{25,9},{1,17},{9,25},{18,2},{26... | collective-permute-start | bytes 589832 | tf_op jit(solution)/shard_map/ppermute | solution.py:677
  12.4 1.4 %collective-permute-start = (f32[192,2,128]{2,1,0:T(2,128)}, f32[192,2,128]{2,1,0:T(2,128)S(1)}, u32[]{:S(2)}, u32[]{:S(2)}) collective-permute-start(f32[192,2,128]{2,1,0:T(2,128)} %bitcast.11), channel_id=1, source_target_pairs={{8,0},{16,8},{24,16},{0,24},{9,1},{17,9},{25,17},{1,25},{10,2},{18... | collective-permute-start | bytes 589832 | tf_op jit(solution)/shard_map/ppermute | solution.py:677
  13.8 0.7 %copy-done.7 = s32[1536]{0:T(1024)S(1)} copy-done((s32[1536]{0:T(1024)S(1)}, s32[1536]{0:T(1024)}, u32[]{:S(2)}) %copy-start.7) | copy-done | bytes 6168
  14.5 0.7 %copy-done.8 = s32[1536]{0:T(1024)S(1)} copy-done((s32[1536]{0:T(1024)S(1)}, s32[1536]{0:T(1024)}, u32[]{:S(2)}) %copy-start.8) | copy-done | bytes 6168
  15.2 2.3 %stick_map.1 = (s32[128,128]{1,0:T(8,128)S(1)}, s32[128,128]{1,0:T(8,128)S(1)}, s32[16,128]{1,0:T(8,128)S(1)}, s32[12,128]{1,0:T(8,128)S(1)}, s32[12,128]{1,0:T(...) custom-call(s32[12,128]{1,0:T(8,128)S(1)} %bitcast.14, s32[12,128]{1,0:T(8,128)S(1)} %bitcast.16), custom_call_target="tpu_custom_call" | custom-call | flops 4000000000 | bytes 100000 | tf_op jit(solution)/shard_map/stick_map/pallas_call | solution.py:631
  17.5 0.1 pad_add_fusion.place_ref
  17.6 2.9 %all-to-all-done.recv_ref.refs_5_ = f32[8,72,128]{2,1,0:T(8,128)S(1)} async-done(((f32[8,72,128]{2,1,0:T(8,128)}), f32[8,72,128]{2,1,0:T(8,128)S(1)}, u32[]{:S(2)}, u32[]{:S(2)}) %all-to-all-start) | async-done | bytes 294944 | tf_op jit(solution)/shard_map/all_to_all | solution.py:626
  20.4 0.0 collective-permute-start.5
  20.4 1.6 %collective-permute-start.4 = (f32[8,72,128]{2,1,0:T(8,128)S(1)}, f32[8,72,128]{2,1,0:T(8,128)S(1)}, u32[]{:S(2)}, u32[]{:S(2)}) collective-permute-start(f32[8,72,128]{2,1,0:T(8,128)S(1)} %all-to-all-done.recv_ref.refs_5_), channel_id=1, source_target_pairs={{16,0},{24,8},{0,16},{8,24},{17,1},{25,9},{1,17},{9,25},{18,2},{26... | collective-permute-start | bytes 884744 | tf_op jit(solution)/shard_map/ppermute | solution.py:678
  22.0 1.4 %collective-permute-start.3 = (f32[8,72,128]{2,1,0:T(8,128)S(1)}, f32[8,72,128]{2,1,0:T(8,128)S(1)}, u32[]{:S(2)}, u32[]{:S(2)}) collective-permute-start(f32[8,72,128]{2,1,0:T(8,128)S(1)} %all-to-all-done.recv_ref.refs_5_), channel_id=1, source_target_pairs={{8,0},{16,8},{24,16},{0,24},{9,1},{17,9},{25,17},{1,25},{10,2},{18... | collective-permute-start | bytes 884744 | tf_op jit(solution)/shard_map/ppermute | solution.py:678
  23.5 20.7 %planes.1.refs_9_ = f32[8,80,128]{2,1,0:T(8,128)S(1)} custom-call(s32[16,128]{1,0:T(8,128)S(1)} %get-tuple-element.29.first_ref, s32[128,128]{1,0:T(8,128)S(1)} %get-tuple-element.30.even_ref, s32[128,128]{1,0:T(8,128)S(1)} %get-tuple-element.31.odd_ref, s32[12,128]{1,0:T(8,128)S(1)} %get-tuple-element.32.src_ref, s32[12,128]{1,0:T(8,128)S(1)} %get-tuple-element.33.dst_ref, ...), custom_call_target="tpu_custom_call" | custom-call | flops 20000000000 | bytes 10000000 | tf_op jit(solution)/shard_map/planes/pallas_call | solution.py:654
  44.1 0.0 collective-permute-done.1.refs_3_
  44.2 0.0 collective-permute-done.refs_2_
  44.2 0.0 collective-permute-done.4.refs_7_
  44.2 0.0 collective-permute-done.3.refs_6_
  44.2 1.4 %inner.1 = (f32[80,128]{1,0:T(8,128)S(1)}, f32[80,128]{1,0:T(8,128)S(1)}, f32[80,128]{1,0:T(8,128)S(1)}, f32[80,128]{1,0:T(8,128)S(1)}, f32[80,128]{1,0:T(8,128)...) custom-call(s32[2]{0:T(128)S(1)} %pad_add_fusion.place_ref, f32[192,256]{1,0:T(8,128)S(1)} %copy-done, ...), custom_call_target="tpu_custom_call" | custom-call | tf_op jit(solution)/shard_map/inner/pallas_call | solution.py:682
  45.6 1.4 %collective-permute-start.6 = (f32[80,128]{1,0:T(8,128)S(1)}, f32[80,128]{1,0:T(8,128)S(1)}, u32[]{:S(2)}, u32[]{:S(2)}) collective-permute-start(f32[80,128]{1,0:T(8,128)S(1)} %get-tuple-element.37), channel_id=1, source_target_pairs={{0,1},{1,2},{2,3},{3,4},{4,5},{5,6},{6,7},{7,0},{8,9},{9,10},{10,1... | collective-permute-start | bytes 122888 | tf_op jit(solution)/shard_map/ppermute | solution.py:693
  47.1 0.0 collective-permute-start.7
  47.1 1.7 %collective-permute-start.8 = (f32[80,128]{1,0:T(8,128)S(1)}, f32[80,128]{1,0:T(8,128)S(1)}, u32[]{:S(2)}, u32[]{:S(2)}) collective-permute-start(f32[80,128]{1,0:T(8,128)S(1)} %get-tuple-element.39), channel_id=1, source_target_pairs={{0,3},{1,4},{2,5},{3,6},{4,7},{5,0},{6,1},{7,2},{8,11},{9,12},{10,... | collective-permute-start | bytes 122888 | tf_op jit(solution)/shard_map/ppermute | solution.py:693
  48.8 3.1 %collective-permute-start.9 = (f32[80,128]{1,0:T(8,128)S(1)}, f32[80,128]{1,0:T(8,128)S(1)}, u32[]{:S(2)}, u32[]{:S(2)}) collective-permute-start(f32[80,128]{1,0:T(8,128)S(1)} %get-tuple-element.40), channel_id=1, source_target_pairs={{0,4},{1,5},{2,6},{3,7},{4,0},{5,1},{6,2},{7,3},{8,12},{9,13},{10,... | collective-permute-start | bytes 122888 | tf_op jit(solution)/shard_map/ppermute | solution.py:693
  52.0 1.0 %collective-permute-start.10 = (f32[80,128]{1,0:T(8,128)S(1)}, f32[80,128]{1,0:T(8,128)S(1)}, u32[]{:S(2)}, u32[]{:S(2)}) collective-permute-start(f32[80,128]{1,0:T(8,128)S(1)} %get-tuple-element.41), channel_id=1, source_target_pairs={{0,5},{1,6},{2,7},{3,0},{4,1},{5,2},{6,3},{7,4},{8,13},{9,14},{10,... | collective-permute-start | bytes 122888 | tf_op jit(solution)/shard_map/ppermute | solution.py:693
  52.9 0.0 collective-permute-done.6.refs_1_
  52.9 1.8 %collective-permute-start.11 = (f32[80,128]{1,0:T(8,128)S(1)}, f32[80,128]{1,0:T(8,128)S(1)}, u32[]{:S(2)}, u32[]{:S(2)}) collective-permute-start(f32[80,128]{1,0:T(8,128)S(1)} %get-tuple-element.42), channel_id=1, source_target_pairs={{0,6},{1,7},{2,0},{3,1},{4,2},{5,3},{6,4},{7,5},{8,14},{9,15},{10,... | collective-permute-start | bytes 122888 | tf_op jit(solution)/shard_map/ppermute | solution.py:693
  54.7 0.0 collective-permute-done.7.refs_2_
  54.7 1.6 %collective-permute-start.12 = (f32[80,128]{1,0:T(8,128)S(1)}, f32[80,128]{1,0:T(8,128)S(1)}, u32[]{:S(2)}, u32[]{:S(2)}) collective-permute-start(f32[80,128]{1,0:T(8,128)S(1)} %get-tuple-element.43), channel_id=1, source_target_pairs={{0,7},{1,0},{2,1},{3,2},{4,3},{5,4},{6,5},{7,6},{8,15},{9,8},{10,9... | collective-permute-start | bytes 122888 | tf_op jit(solution)/shard_map/ppermute | solution.py:693
  56.4 0.5 collective-permute-done.10.refs_5_
  56.9 0.5 collective-permute-done.11.refs_6_
  57.4 1.4 %collective-permute-done.12.refs_7_ = f32[80,128]{1,0:T(8,128)S(1)} collective-permute-done((f32[80,128]{1,0:T(8,128)S(1)}, f32[80,128]{1,0:T(8,128)S(1)}, u32[]{:S(2)}, u32[]{:S(2)}) %collective-permute-start.12) | collective-permute-done | bytes 40992 | tf_op jit(solution)/shard_map/ppermute | solution.py:693
  58.8 1.3 %planes_to_wave.1 = (f32[192,2,128]{2,1,0:T(2,128)}, f32[2,1,4]{2,1,0:T(1,128)}) custom-call(s32[1]{0:T(128)} %bitcast.me_ref, f32[192,128]{1,0:T(8,128)S(1)} %copy-done.6, f32[80,128]{1,0:T(8,128)S(1)} %get-tuple-element.36.refs_0_, f32[80,128]{1,0:T(8,128)S(1)} %collective-permute-done.6.refs_1_, f32[80,128]{1,0:T(8,128)S(1)} %collective-permute-done.7.refs_2_, ...), custom_call_target="tpu_custom_call" | custom-call | tf_op jit(solution)/shard_map/planes_to_wave/pallas_call | solution.py:694
  (20 shorter events, 0.0 us)
Async XLA Ops:
  3.6 16.9 %all-to-all-start = ((f32[8,72,128]{2,1,0:T(8,128)}), f32[8,72,128]{2,1,0:T(8,128)S(1)}, u32[]{:S(2)}, u32[]{:S(2)}) async-start(f32[8,72,128]{2,1,0:T(8,128)} %get-tuple-element.28), calls=%async_computation | async-start | bytes 589824 | tf_op jit(solution)/shard_map/all_to_all | solution.py:626
  10.8 11.2 %collective-permute-start.2 = (f32[192,2,128]{2,1,0:T(2,128)}, f32[192,2,128]{2,1,0:T(2,128)S(1)}, u32[]{:S(2)}, u32[]{:S(2)}) collective-permute-start(f32[192,2,128]{2,1,0:T(2,128)} %bitcast.9), channel_id=1, source_target_pairs={{24,0},{0,8},{8,16},{16,24},{25,1},{1,9},{9,17},{17,25},{26,2},{2,... | collective-permute-start | bytes 589832 | tf_op jit(solution)/shard_map/ppermute | solution.py:677
  10.8 33.3 %collective-permute-start.1 = (f32[192,2,128]{2,1,0:T(2,128)}, f32[192,2,128]{2,1,0:T(2,128)S(1)}, u32[]{:S(2)}, u32[]{:S(2)}) collective-permute-start(f32[192,2,128]{2,1,0:T(2,128)} %bitcast.10), channel_id=1, source_target_pairs={{16,0},{24,8},{0,16},{8,24},{17,1},{25,9},{1,17},{9,25},{18,2},{26... | collective-permute-start | bytes 589832 | tf_op jit(solution)/shard_map/ppermute | solution.py:677
  12.4 31.7 %collective-permute-start = (f32[192,2,128]{2,1,0:T(2,128)}, f32[192,2,128]{2,1,0:T(2,128)S(1)}, u32[]{:S(2)}, u32[]{:S(2)}) collective-permute-start(f32[192,2,128]{2,1,0:T(2,128)} %bitcast.11), channel_id=1, source_target_pairs={{8,0},{16,8},{24,16},{0,24},{9,1},{17,9},{25,17},{1,25},{10,2},{18... | collective-permute-start | bytes 589832 | tf_op jit(solution)/shard_map/ppermute | solution.py:677
  13.8 0.7 %copy-start.7 = (s32[1536]{0:T(1024)S(1)}, s32[1536]{0:T(1024)}, u32[]{:S(2)}) copy-start(s32[1536]{0:T(1024)} %param.9) | copy-start | bytes 18436
  14.5 0.7 %copy-start.8 = (s32[1536]{0:T(1024)S(1)}, s32[1536]{0:T(1024)}, u32[]{:S(2)}) copy-start(s32[1536]{0:T(1024)} %param.8) | copy-start | bytes 18436
  20.4 23.7 %collective-permute-start.5 = (f32[8,72,128]{2,1,0:T(8,128)S(1)}, f32[8,72,128]{2,1,0:T(8,128)S(1)}, u32[]{:S(2)}, u32[]{:S(2)}) collective-permute-start(f32[8,72,128]{2,1,0:T(8,128)S(1)} %all-to-all-done.recv_ref.refs_5_), channel_id=1, source_target_pairs={{24,0},{0,8},{8,16},{16,24},{25,1},{1,9},{9,17},{17,25},{26,2},{2,... | collective-permute-start | bytes 884744 | tf_op jit(solution)/shard_map/ppermute | solution.py:678
  20.4 23.7 %collective-permute-start.4 = (f32[8,72,128]{2,1,0:T(8,128)S(1)}, f32[8,72,128]{2,1,0:T(8,128)S(1)}, u32[]{:S(2)}, u32[]{:S(2)}) collective-permute-start(f32[8,72,128]{2,1,0:T(8,128)S(1)} %all-to-all-done.recv_ref.refs_5_), channel_id=1, source_target_pairs={{16,0},{24,8},{0,16},{8,24},{17,1},{25,9},{1,17},{9,25},{18,2},{26... | collective-permute-start | bytes 884744 | tf_op jit(solution)/shard_map/ppermute | solution.py:678
  22.0 22.2 %collective-permute-start.3 = (f32[8,72,128]{2,1,0:T(8,128)S(1)}, f32[8,72,128]{2,1,0:T(8,128)S(1)}, u32[]{:S(2)}, u32[]{:S(2)}) collective-permute-start(f32[8,72,128]{2,1,0:T(8,128)S(1)} %all-to-all-done.recv_ref.refs_5_), channel_id=1, source_target_pairs={{8,0},{16,8},{24,16},{0,24},{9,1},{17,9},{25,17},{1,25},{10,2},{18... | collective-permute-start | bytes 884744 | tf_op jit(solution)/shard_map/ppermute | solution.py:678
  23.4 20.8 %copy-start = (f32[192,256]{1,0:T(8,128)S(1)}, f32[192,256]{1,0:T(8,128)}, u32[]{:S(2)}) copy-start(f32[192,256]{1,0:T(8,128)} %get-tuple-element.27.refs_0_.refs_8_) | copy-start | bytes 589828
  23.4 20.8 %copy-start.1 = (f32[1,192,2,128]{3,2,1,0:T(2,128)S(1)}, f32[1,192,2,128]{3,2,1,0:T(2,128)}, u32[]{:S(2)}) copy-start(f32[1,192,2,128]{3,2,1,0:T(2,128)} %param.7) | copy-start | bytes 589828
  23.4 35.3 %copy-start.2 = (bf16[384,256]{1,0:T(8,128)(2,1)S(1)}, bf16[384,256]{1,0:T(8,128)(2,1)}, u32[]{:S(2)}) copy-start(bf16[384,256]{1,0:T(8,128)(2,1)} %get-tuple-element.44.refs_9_) | copy-start | bytes 589828
  23.4 35.3 %copy-start.3 = (bf16[384,256]{1,0:T(8,128)(2,1)S(1)}, bf16[384,256]{1,0:T(8,128)(2,1)}, u32[]{:S(2)}) copy-start(bf16[384,256]{1,0:T(8,128)(2,1)} %get-tuple-element.45.refs_10_) | copy-start | bytes 589828
  23.4 35.3 %copy-start.4 = (f32[192,192]{1,0:T(8,128)S(1)}, f32[192,192]{1,0:T(8,128)}, u32[]{:S(2)}) copy-start(f32[192,192]{1,0:T(8,128)} %get-tuple-element.46.refs_11_) | copy-start | bytes 442372
  23.5 35.3 %copy-start.5 = (f32[192,192]{1,0:T(8,128)S(1)}, f32[192,192]{1,0:T(8,128)}, u32[]{:S(2)}) copy-start(f32[192,192]{1,0:T(8,128)} %get-tuple-element.47.refs_12_) | copy-start | bytes 442372
  23.5 35.3 %copy-start.6 = (f32[192,128]{1,0:T(8,128)S(1)}, f32[192,128]{1,0:T(8,128)}, u32[]{:S(2)}) copy-start(f32[192,128]{1,0:T(8,128)} %get-tuple-element.26.len_ref) | copy-start | bytes 294916
  45.6 7.3 %collective-permute-start.6 = (f32[80,128]{1,0:T(8,128)S(1)}, f32[80,128]{1,0:T(8,128)S(1)}, u32[]{:S(2)}, u32[]{:S(2)}) collective-permute-start(f32[80,128]{1,0:T(8,128)S(1)} %get-tuple-element.37), channel_id=1, source_target_pairs={{0,1},{1,2},{2,3},{3,4},{4,5},{5,6},{6,7},{7,0},{8,9},{9,10},{10,1... | collective-permute-start | bytes 122888 | tf_op jit(solution)/shard_map/ppermute | solution.py:693
  47.1 7.7 %collective-permute-start.7 = (f32[80,128]{1,0:T(8,128)S(1)}, f32[80,128]{1,0:T(8,128)S(1)}, u32[]{:S(2)}, u32[]{:S(2)}) collective-permute-start(f32[80,128]{1,0:T(8,128)S(1)} %get-tuple-element.38), channel_id=1, source_target_pairs={{0,2},{1,3},{2,4},{3,5},{4,6},{5,7},{6,0},{7,1},{8,10},{9,11},{10,... | collective-permute-start | bytes 122888 | tf_op jit(solution)/shard_map/ppermute | solution.py:693
  47.1 9.3 %collective-permute-start.8 = (f32[80,128]{1,0:T(8,128)S(1)}, f32[80,128]{1,0:T(8,128)S(1)}, u32[]{:S(2)}, u32[]{:S(2)}) collective-permute-start(f32[80,128]{1,0:T(8,128)S(1)} %get-tuple-element.39), channel_id=1, source_target_pairs={{0,3},{1,4},{2,5},{3,6},{4,7},{5,0},{6,1},{7,2},{8,11},{9,12},{10,... | collective-permute-start | bytes 122888 | tf_op jit(solution)/shard_map/ppermute | solution.py:693
  48.8 7.5 %collective-permute-start.9 = (f32[80,128]{1,0:T(8,128)S(1)}, f32[80,128]{1,0:T(8,128)S(1)}, u32[]{:S(2)}, u32[]{:S(2)}) collective-permute-start(f32[80,128]{1,0:T(8,128)S(1)} %get-tuple-element.40), channel_id=1, source_target_pairs={{0,4},{1,5},{2,6},{3,7},{4,0},{5,1},{6,2},{7,3},{8,12},{9,13},{10,... | collective-permute-start | bytes 122888 | tf_op jit(solution)/shard_map/ppermute | solution.py:693
  52.0 4.9 %collective-permute-start.10 = (f32[80,128]{1,0:T(8,128)S(1)}, f32[80,128]{1,0:T(8,128)S(1)}, u32[]{:S(2)}, u32[]{:S(2)}) collective-permute-start(f32[80,128]{1,0:T(8,128)S(1)} %get-tuple-element.41), channel_id=1, source_target_pairs={{0,5},{1,6},{2,7},{3,0},{4,1},{5,2},{6,3},{7,4},{8,13},{9,14},{10,... | collective-permute-start | bytes 122888 | tf_op jit(solution)/shard_map/ppermute | solution.py:693
  52.9 4.4 %collective-permute-start.11 = (f32[80,128]{1,0:T(8,128)S(1)}, f32[80,128]{1,0:T(8,128)S(1)}, u32[]{:S(2)}, u32[]{:S(2)}) collective-permute-start(f32[80,128]{1,0:T(8,128)S(1)} %get-tuple-element.42), channel_id=1, source_target_pairs={{0,6},{1,7},{2,0},{3,1},{4,2},{5,3},{6,4},{7,5},{8,14},{9,15},{10,... | collective-permute-start | bytes 122888 | tf_op jit(solution)/shard_map/ppermute | solution.py:693
  54.7 4.0 %collective-permute-start.12 = (f32[80,128]{1,0:T(8,128)S(1)}, f32[80,128]{1,0:T(8,128)S(1)}, u32[]{:S(2)}, u32[]{:S(2)}) collective-permute-start(f32[80,128]{1,0:T(8,128)S(1)} %get-tuple-element.43), channel_id=1, source_target_pairs={{0,7},{1,0},{2,1},{3,2},{4,3},{5,4},{6,5},{7,6},{8,15},{9,8},{10,9... | collective-permute-start | bytes 122888 | tf_op jit(solution)/shard_map/ppermute | solution.py:693

commit v11 on v10

--- a/solution.py
+++ b/solution.py
@@ -533,13 +533,13 @@
     row = lax.broadcasted_iota(jnp.int32, (8, LANES), 0)
     tile = jnp.zeros((8, LANES), F32)
     for m in range(bands):
-        at = lax.rem(me + m, bands)
+        at = me ^ m
         for part, sign in ((0, 1.0), (1, -1.0)):
             partial = sums[m][part] + volume * local[m][part]
             scalar = jnp.sum(jnp.sum(partial, axis=1, keepdims=True), axis=0, keepdims=True)
             tile = jnp.where((lane == at) & (row == part), sign * norm * scalar, tile)
     for k in range(devices):
-        out_refs[k][0:3 * padded_planes, :] = in_ref[lax.rem(mine + k, devices), 0:3 * padded_planes, :]
+        out_refs[k][0:3 * padded_planes, :] = in_ref[mine ^ k, 0:3 * padded_planes, :]
         out_refs[k][3 * padded_planes:, :] = tile
 
 
@@ -554,7 +554,7 @@
     me = me_ref[0]
     for k in range(devices):
         value = ret_refs[k][...]
-        base = pl.multiple_of(lax.rem(me + devices - k, devices) * padded_planes, 8)
+        base = pl.multiple_of((me ^ k) * padded_planes, 8)
         total = total + value[3 * padded_planes:]
         rest = value[2 * padded_planes:3 * padded_planes]
         re = jnp.concatenate([value[:padded_planes], rest[:, :half]], axis=1)
@@ -573,6 +573,10 @@
     sub_ref[:, 0, :] = total[0:2, :bands]
 
 
+def pairs(count, k):
+    return [(d, d ^ k) for d in range(count)]
+
+
 def shards(bands, devices, coefficients, stick_col, stick_row, stick_length, plane_of_slot, potential):
     extent = plane_of_slot.shape[0]
     sticks = coefficients.shape[1]
@@ -580,7 +584,8 @@
     total_sticks = stick_col.shape[0]
     planes = potential.shape[0]
     padded_planes = up8(planes)
-    if sticks != LANES + LANES // 2 or devices % 2 or planes % 2:
+    powers = devices & (devices - 1) == 0 and bands & (bands - 1) == 0
+    if sticks != LANES + LANES // 2 or not powers or planes % 2:
         raise ValueError("sizes")
     rows = sum(row_blocks())
     volume = 1.0 / (extent * extent * extent)
@@ -672,10 +677,9 @@
     )(first, even_map, odd_map, source, target, row_w, col_w, received, constants, potential)
 
     coefs, fields = [coef], [received]
-    for shift in range(1, bands):
-        ring = [((b + shift) % bands, b) for b in range(bands)]
-        coefs.append(lax.ppermute(coef, "band", ring))
-        fields.append(lax.ppermute(received, "band", ring))
+    for m in range(1, bands):
+        coefs.append(lax.ppermute(coef, "band", pairs(bands, m)))
+        fields.append(lax.ppermute(received, "band", pairs(bands, m)))
     band = lax.axis_index("band").astype(jnp.int32)
     norm = 1.0 / (total_sticks * padded)
     places = jnp.stack([band, me])
@@ -689,8 +693,7 @@
 
     returned = [outgoing[0]]
     for k in range(1, devices):
-        ring = [(d, (d + k) % devices) for d in range(devices)]
-        returned.append(lax.ppermute(outgoing[k], "tg", ring))
+        returned.append(lax.ppermute(outgoing[k], "tg", pairs(devices, k)))
     applied, subspace = pl.pallas_call(
         functools.partial(final_kernel, volume, devices),
         out_shape=(

time: 60.4 us -> 61.7 us (1.022)
  waiting for transfers between devices: 5.25 us -> 8.28 us
  starting transfers between devices: 24 us -> 22.2 us
    ppermute x13, waiting for transfers between devices: 2.39 us -> 4.31 us  [the longest x7 4.29 us: shards(): returned.append(lax.ppermute(outgoing[k], 'tg', pairs(devices, k)))]
    ppermute x13, starting transfers between devices: 16.7 us -> 14.9 us  [the longest x7 11.2 us: shards(): returned.append(lax.ppermute(outgoing[k], 'tg', pairs(devices, k)))]
    all_to_all x1, waiting for transfers between devices: 2.85 us -> 3.97 us  [shards(): lax.all_to_all(sent, 'tg', split_axis=0, concat_axis=0, tiled=True)]
  transfers between devices with their start and end apart: 14 -> 14, of which waited for: 4 -> 4; matrix products, arithmetic and copies ran while one was open for 0% -> 0% of each run, Pallas kernels for 38% -> 37%
where the time goes in v11:
time: 61.7 us; the launch traced here: 61.3 us
  Pallas kernels  28.6 us (46%)
  starting transfers between devices  22.2 us (36%)
  waiting for transfers between devices  8.28 us (13%)
  local copies, waits for them, and re-layouts  1.42 us (2%)
  between operations  0.78 us (1%)
    pallas_call x1, Pallas kernels, shards(): pl.pallas_call(functools.partial(plane_kernel, planes), out_shape=jax.Sha...  20.7 us
    ppermute x7, starting transfers between devices, shards(): returned.append(lax.ppermute(outgoing[k], 'tg', pairs(devices, k)))  11.2 us
    all_to_all x1, starting transfers between devices, shards(): lax.all_to_all(sent, 'tg', split_axis=0, concat_axis=0, tiled=True)  7.27 us
    ppermute x7, waiting for transfers between devices, shards(): returned.append(lax.ppermute(outgoing[k], 'tg', pairs(devices, k)))  4.29 us
    all_to_all x1, waiting for transfers between devices, shards(): lax.all_to_all(sent, 'tg', split_axis=0, concat_axis=0, tiled=True)  3.97 us
    pallas_call x1, Pallas kernels, shards(): pl.pallas_call(functools.partial(wave_kernel, extent), out_shape=(jax.Sha...  2.91 us
    pallas_call x1, Pallas kernels, shards(): pl.pallas_call(functools.partial(map_kernel, extent, sticks), out_shape=(...  2.3 us
    ppermute x3, starting transfers between devices, shards(): fields.append(lax.ppermute(received, 'band', pairs(bands, m)))  1.86 us
  transfers between devices with their start and end apart: 14, of which 4 were waited for; matrix products, arithmetic and copies ran while one was open for 0% of the time, Pallas kernels for 37%

profile of v11, /device:TPU:0, one launch (start us, length us, event | category | flops | bytes accessed | tf_op | source)
XLA Modules:
  0.0 61.3 jit_solution(12921653846750404539)
XLA Ops:
  0.6 2.9 %wave_to_planes.1 = (f32[8,72,128]{2,1,0:T(8,128)}, f32[192,256]{1,0:T(8,128)}, f32[192,128]{1,0:T(8,128)}, bf16[384,256]{1,0:T(8,128)(2,1)}, bf16[384,256]{1,0:...) custom-call(s32[1]{0:T(128)} %bitcast.me_ref, s32[12,128]{1,0:T(8,128)} %bitcast.17, s32[12,128]{1,0:T(8,128)} %bitcast.13, ...), custom_call_target="tpu_custom_call" | custom-call | tf_op jit(solution)/shard_map/wave_to_planes/pallas_call | solution.py:607
  3.6 7.3 %all-to-all-start = ((f32[8,72,128]{2,1,0:T(8,128)}), f32[8,72,128]{2,1,0:T(8,128)S(1)}, u32[]{:S(2)}, u32[]{:S(2)}) async-start(f32[8,72,128]{2,1,0:T(8,128)} %get-tuple-element.28), calls=%async_computation | async-start | bytes 589824 | tf_op jit(solution)/shard_map/all_to_all | solution.py:631
  10.8 0.7 %collective-permute-start.2 = (f32[192,2,128]{2,1,0:T(2,128)}, f32[192,2,128]{2,1,0:T(2,128)S(1)}, u32[]{:S(2)}, u32[]{:S(2)}) collective-permute-start(f32[192,2,128]{2,1,0:T(2,128)} %bitcast.9), channel_id=1, source_target_pairs={{0,24},{8,16},{16,8},{24,0},{1,25},{9,17},{17,9},{25,1},{2,26},{10... | collective-permute-start | bytes 589832 | tf_op jit(solution)/shard_map/ppermute | solution.py:681
  11.5 0.9 %collective-permute-start.1 = (f32[192,2,128]{2,1,0:T(2,128)}, f32[192,2,128]{2,1,0:T(2,128)S(1)}, u32[]{:S(2)}, u32[]{:S(2)}) collective-permute-start(f32[192,2,128]{2,1,0:T(2,128)} %bitcast.10), channel_id=1, source_target_pairs={{0,16},{8,24},{16,0},{24,8},{1,17},{9,25},{17,1},{25,9},{2,18},{10... | collective-permute-start | bytes 589832 | tf_op jit(solution)/shard_map/ppermute | solution.py:681
  12.4 0.3 collective-permute-start
  12.7 0.7 %copy-done.7 = s32[1536]{0:T(1024)S(1)} copy-done((s32[1536]{0:T(1024)S(1)}, s32[1536]{0:T(1024)}, u32[]{:S(2)}) %copy-start.7) | copy-done | bytes 6168
  13.4 0.7 %copy-done.8 = s32[1536]{0:T(1024)S(1)} copy-done((s32[1536]{0:T(1024)S(1)}, s32[1536]{0:T(1024)}, u32[]{:S(2)}) %copy-start.8) | copy-done | bytes 6168
  14.1 2.3 %stick_map.1 = (s32[128,128]{1,0:T(8,128)S(1)}, s32[128,128]{1,0:T(8,128)S(1)}, s32[16,128]{1,0:T(8,128)S(1)}, s32[12,128]{1,0:T(8,128)S(1)}, s32[12,128]{1,0:T(...) custom-call(s32[12,128]{1,0:T(8,128)S(1)} %bitcast.14, s32[12,128]{1,0:T(8,128)S(1)} %bitcast.16), custom_call_target="tpu_custom_call" | custom-call | flops 4000000000 | bytes 100000 | tf_op jit(solution)/shard_map/stick_map/pallas_call | solution.py:636
  16.4 0.1 pad_add_fusion.place_ref
  16.5 4.0 %all-to-all-done.recv_ref.refs_5_ = f32[8,72,128]{2,1,0:T(8,128)S(1)} async-done(((f32[8,72,128]{2,1,0:T(8,128)}), f32[8,72,128]{2,1,0:T(8,128)S(1)}, u32[]{:S(2)}, u32[]{:S(2)}) %all-to-all-start) | async-done | bytes 294944 | tf_op jit(solution)/shard_map/all_to_all | solution.py:631
  20.4 0.0 collective-permute-start.5
  20.4 1.6 %collective-permute-start.4 = (f32[8,72,128]{2,1,0:T(8,128)S(1)}, f32[8,72,128]{2,1,0:T(8,128)S(1)}, u32[]{:S(2)}, u32[]{:S(2)}) collective-permute-start(f32[8,72,128]{2,1,0:T(8,128)S(1)} %all-to-all-done.recv_ref.refs_5_), channel_id=1, source_target_pairs={{0,16},{8,24},{16,0},{24,8},{1,17},{9,25},{17,1},{25,9},{2,18},{10... | collective-permute-start | bytes 884744 | tf_op jit(solution)/shard_map/ppermute | solution.py:682
  22.0 0.0 collective-permute-done.2.refs_4_
  22.0 0.3 collective-permute-start.3
  22.3 20.7 %planes.1.refs_9_ = f32[8,80,128]{2,1,0:T(8,128)S(1)} custom-call(s32[16,128]{1,0:T(8,128)S(1)} %get-tuple-element.29.first_ref, s32[128,128]{1,0:T(8,128)S(1)} %get-tuple-element.30.even_ref, s32[128,128]{1,0:T(8,128)S(1)} %get-tuple-element.31.odd_ref, s32[12,128]{1,0:T(8,128)S(1)} %get-tuple-element.32.src_ref, s32[12,128]{1,0:T(8,128)S(1)} %get-tuple-element.33.dst_ref, ...), custom_call_target="tpu_custom_call" | custom-call | flops 20000000000 | bytes 10000000 | tf_op jit(solution)/shard_map/planes/pallas_call | solution.py:659
  43.0 0.0 collective-permute-done.1.refs_3_
  43.0 0.0 collective-permute-done.refs_2_
  43.1 0.0 collective-permute-done.4.refs_7_
  43.1 0.0 collective-permute-done.3.refs_6_
  43.1 1.4 %inner.1 = (f32[80,128]{1,0:T(8,128)S(1)}, f32[80,128]{1,0:T(8,128)S(1)}, f32[80,128]{1,0:T(8,128)S(1)}, f32[80,128]{1,0:T(8,128)S(1)}, f32[80,128]{1,0:T(8,128)...) custom-call(s32[2]{0:T(128)S(1)} %pad_add_fusion.place_ref, f32[192,256]{1,0:T(8,128)S(1)} %copy-done, ...), custom_call_target="tpu_custom_call" | custom-call | tf_op jit(solution)/shard_map/inner/pallas_call | solution.py:686
  44.5 1.5 %collective-permute-start.6 = (f32[80,128]{1,0:T(8,128)S(1)}, f32[80,128]{1,0:T(8,128)S(1)}, u32[]{:S(2)}, u32[]{:S(2)}) collective-permute-start(f32[80,128]{1,0:T(8,128)S(1)} %get-tuple-element.37), channel_id=1, source_target_pairs={{0,1},{1,0},{2,3},{3,2},{4,5},{5,4},{6,7},{7,6},{8,9},{9,8},{10,11... | collective-permute-start | bytes 122888 | tf_op jit(solution)/shard_map/ppermute | solution.py:696
  46.0 2.1 %collective-permute-start.8 = (f32[80,128]{1,0:T(8,128)S(1)}, f32[80,128]{1,0:T(8,128)S(1)}, u32[]{:S(2)}, u32[]{:S(2)}) collective-permute-start(f32[80,128]{1,0:T(8,128)S(1)} %get-tuple-element.39), channel_id=1, source_target_pairs={{0,3},{1,2},{2,1},{3,0},{4,7},{5,6},{6,5},{7,4},{8,11},{9,10},{10,... | collective-permute-start | bytes 122888 | tf_op jit(solution)/shard_map/ppermute | solution.py:696
  48.1 1.0 %collective-permute-start.9 = (f32[80,128]{1,0:T(8,128)S(1)}, f32[80,128]{1,0:T(8,128)S(1)}, u32[]{:S(2)}, u32[]{:S(2)}) collective-permute-start(f32[80,128]{1,0:T(8,128)S(1)} %get-tuple-element.40), channel_id=1, source_target_pairs={{0,4},{1,5},{2,6},{3,7},{4,0},{5,1},{6,2},{7,3},{8,12},{9,13},{10,... | collective-permute-start | bytes 122888 | tf_op jit(solution)/shard_map/ppermute | solution.py:696
  49.1 2.8 %collective-permute-start.10 = (f32[80,128]{1,0:T(8,128)S(1)}, f32[80,128]{1,0:T(8,128)S(1)}, u32[]{:S(2)}, u32[]{:S(2)}) collective-permute-start(f32[80,128]{1,0:T(8,128)S(1)} %get-tuple-element.41), channel_id=1, source_target_pairs={{0,5},{1,4},{2,7},{3,6},{4,1},{5,0},{6,3},{7,2},{8,13},{9,12},{10,... | collective-permute-start | bytes 122888 | tf_op jit(solution)/shard_map/ppermute | solution.py:696
  51.8 1.5 %collective-permute-start.11 = (f32[80,128]{1,0:T(8,128)S(1)}, f32[80,128]{1,0:T(8,128)S(1)}, u32[]{:S(2)}, u32[]{:S(2)}) collective-permute-start(f32[80,128]{1,0:T(8,128)S(1)} %get-tuple-element.42), channel_id=1, source_target_pairs={{0,6},{1,7},{2,4},{3,5},{4,2},{5,3},{6,0},{7,1},{8,14},{9,15},{10,... | collective-permute-start | bytes 122888 | tf_op jit(solution)/shard_map/ppermute | solution.py:696
  53.3 2.4 %collective-permute-start.12 = (f32[80,128]{1,0:T(8,128)S(1)}, f32[80,128]{1,0:T(8,128)S(1)}, u32[]{:S(2)}, u32[]{:S(2)}) collective-permute-start(f32[80,128]{1,0:T(8,128)S(1)} %get-tuple-element.43), channel_id=1, source_target_pairs={{0,7},{1,6},{2,5},{3,4},{4,3},{5,2},{6,1},{7,0},{8,15},{9,14},{10,... | collective-permute-start | bytes 122888 | tf_op jit(solution)/shard_map/ppermute | solution.py:696
  55.7 0.0 collective-permute-done.8.refs_3_
  55.7 0.0 collective-permute-done.9.refs_4_
  55.7 0.6 %collective-permute-done.10.refs_5_ = f32[80,128]{1,0:T(8,128)S(1)} collective-permute-done((f32[80,128]{1,0:T(8,128)S(1)}, f32[80,128]{1,0:T(8,128)S(1)}, u32[]{:S(2)}, u32[]{:S(2)}) %collective-permute-start.10) | collective-permute-done | bytes 40992 | tf_op jit(solution)/shard_map/ppermute | solution.py:696
  56.3 1.4 %collective-permute-done.11.refs_6_ = f32[80,128]{1,0:T(8,128)S(1)} collective-permute-done((f32[80,128]{1,0:T(8,128)S(1)}, f32[80,128]{1,0:T(8,128)S(1)}, u32[]{:S(2)}, u32[]{:S(2)}) %collective-permute-start.11) | collective-permute-done | bytes 40992 | tf_op jit(solution)/shard_map/ppermute | solution.py:696
  57.7 2.3 %collective-permute-done.12.refs_7_ = f32[80,128]{1,0:T(8,128)S(1)} collective-permute-done((f32[80,128]{1,0:T(8,128)S(1)}, f32[80,128]{1,0:T(8,128)S(1)}, u32[]{:S(2)}, u32[]{:S(2)}) %collective-permute-start.12) | collective-permute-done | bytes 40992 | tf_op jit(solution)/shard_map/ppermute | solution.py:696
  60.0 1.3 %planes_to_wave.1 = (f32[192,2,128]{2,1,0:T(2,128)}, f32[2,1,4]{2,1,0:T(1,128)}) custom-call(s32[1]{0:T(128)} %bitcast.me_ref, f32[192,128]{1,0:T(8,128)S(1)} %copy-done.6, f32[80,128]{1,0:T(8,128)S(1)} %get-tuple-element.36.refs_0_, f32[80,128]{1,0:T(8,128)S(1)} %collective-permute-done.6.refs_1_, f32[80,128]{1,0:T(8,128)S(1)} %collective-permute-done.7.refs_2_, ...), custom_call_target="tpu_custom_call" | custom-call | tf_op jit(solution)/shard_map/planes_to_wave/pallas_call | solution.py:697
  (20 shorter events, 0.0 us)
Async XLA Ops:
  3.6 16.9 %all-to-all-start = ((f32[8,72,128]{2,1,0:T(8,128)}), f32[8,72,128]{2,1,0:T(8,128)S(1)}, u32[]{:S(2)}, u32[]{:S(2)}) async-start(f32[8,72,128]{2,1,0:T(8,128)} %get-tuple-element.28), calls=%async_computation | async-start | bytes 589824 | tf_op jit(solution)/shard_map/all_to_all | solution.py:631
  10.8 11.2 %collective-permute-start.2 = (f32[192,2,128]{2,1,0:T(2,128)}, f32[192,2,128]{2,1,0:T(2,128)S(1)}, u32[]{:S(2)}, u32[]{:S(2)}) collective-permute-start(f32[192,2,128]{2,1,0:T(2,128)} %bitcast.9), channel_id=1, source_target_pairs={{0,24},{8,16},{16,8},{24,0},{1,25},{9,17},{17,9},{25,1},{2,26},{10... | collective-permute-start | bytes 589832 | tf_op jit(solution)/shard_map/ppermute | solution.py:681
  11.5 31.5 %collective-permute-start.1 = (f32[192,2,128]{2,1,0:T(2,128)}, f32[192,2,128]{2,1,0:T(2,128)S(1)}, u32[]{:S(2)}, u32[]{:S(2)}) collective-permute-start(f32[192,2,128]{2,1,0:T(2,128)} %bitcast.10), channel_id=1, source_target_pairs={{0,16},{8,24},{16,0},{24,8},{1,17},{9,25},{17,1},{25,9},{2,18},{10... | collective-permute-start | bytes 589832 | tf_op jit(solution)/shard_map/ppermute | solution.py:681
  12.4 30.6 %collective-permute-start = (f32[192,2,128]{2,1,0:T(2,128)}, f32[192,2,128]{2,1,0:T(2,128)S(1)}, u32[]{:S(2)}, u32[]{:S(2)}) collective-permute-start(f32[192,2,128]{2,1,0:T(2,128)} %bitcast.11), channel_id=1, source_target_pairs={{0,8},{8,0},{16,24},{24,16},{1,9},{9,1},{17,25},{25,17},{2,10},{10... | collective-permute-start | bytes 589832 | tf_op jit(solution)/shard_map/ppermute | solution.py:681
  12.7 0.7 %copy-start.7 = (s32[1536]{0:T(1024)S(1)}, s32[1536]{0:T(1024)}, u32[]{:S(2)}) copy-start(s32[1536]{0:T(1024)} %param.9) | copy-start | bytes 18436
  13.4 0.7 %copy-start.8 = (s32[1536]{0:T(1024)S(1)}, s32[1536]{0:T(1024)}, u32[]{:S(2)}) copy-start(s32[1536]{0:T(1024)} %param.8) | copy-start | bytes 18436
  20.4 22.6 %collective-permute-start.5 = (f32[8,72,128]{2,1,0:T(8,128)S(1)}, f32[8,72,128]{2,1,0:T(8,128)S(1)}, u32[]{:S(2)}, u32[]{:S(2)}) collective-permute-start(f32[8,72,128]{2,1,0:T(8,128)S(1)} %all-to-all-done.recv_ref.refs_5_), channel_id=1, source_target_pairs={{0,24},{8,16},{16,8},{24,0},{1,25},{9,17},{17,9},{25,1},{2,26},{10... | collective-permute-start | bytes 884744 | tf_op jit(solution)/shard_map/ppermute | solution.py:682
  20.4 22.6 %collective-permute-start.4 = (f32[8,72,128]{2,1,0:T(8,128)S(1)}, f32[8,72,128]{2,1,0:T(8,128)S(1)}, u32[]{:S(2)}, u32[]{:S(2)}) collective-permute-start(f32[8,72,128]{2,1,0:T(8,128)S(1)} %all-to-all-done.recv_ref.refs_5_), channel_id=1, source_target_pairs={{0,16},{8,24},{16,0},{24,8},{1,17},{9,25},{17,1},{25,9},{2,18},{10... | collective-permute-start | bytes 884744 | tf_op jit(solution)/shard_map/ppermute | solution.py:682
  22.0 21.1 %collective-permute-start.3 = (f32[8,72,128]{2,1,0:T(8,128)S(1)}, f32[8,72,128]{2,1,0:T(8,128)S(1)}, u32[]{:S(2)}, u32[]{:S(2)}) collective-permute-start(f32[8,72,128]{2,1,0:T(8,128)S(1)} %all-to-all-done.recv_ref.refs_5_), channel_id=1, source_target_pairs={{0,8},{8,0},{16,24},{24,16},{1,9},{9,1},{17,25},{25,17},{2,10},{10... | collective-permute-start | bytes 884744 | tf_op jit(solution)/shard_map/ppermute | solution.py:682
  22.3 20.8 %copy-start = (f32[192,256]{1,0:T(8,128)S(1)}, f32[192,256]{1,0:T(8,128)}, u32[]{:S(2)}) copy-start(f32[192,256]{1,0:T(8,128)} %get-tuple-element.27.refs_0_.refs_8_) | copy-start | bytes 589828
  22.3 20.8 %copy-start.1 = (f32[1,192,2,128]{3,2,1,0:T(2,128)S(1)}, f32[1,192,2,128]{3,2,1,0:T(2,128)}, u32[]{:S(2)}) copy-start(f32[1,192,2,128]{3,2,1,0:T(2,128)} %param.7) | copy-start | bytes 589828
  22.3 37.7 %copy-start.2 = (bf16[384,256]{1,0:T(8,128)(2,1)S(1)}, bf16[384,256]{1,0:T(8,128)(2,1)}, u32[]{:S(2)}) copy-start(bf16[384,256]{1,0:T(8,128)(2,1)} %get-tuple-element.44.refs_9_) | copy-start | bytes 589828
  22.3 37.7 %copy-start.3 = (bf16[384,256]{1,0:T(8,128)(2,1)S(1)}, bf16[384,256]{1,0:T(8,128)(2,1)}, u32[]{:S(2)}) copy-start(bf16[384,256]{1,0:T(8,128)(2,1)} %get-tuple-element.45.refs_10_) | copy-start | bytes 589828
  22.3 37.7 %copy-start.4 = (f32[192,192]{1,0:T(8,128)S(1)}, f32[192,192]{1,0:T(8,128)}, u32[]{:S(2)}) copy-start(f32[192,192]{1,0:T(8,128)} %get-tuple-element.46.refs_11_) | copy-start | bytes 442372
  22.3 37.7 %copy-start.5 = (f32[192,192]{1,0:T(8,128)S(1)}, f32[192,192]{1,0:T(8,128)}, u32[]{:S(2)}) copy-start(f32[192,192]{1,0:T(8,128)} %get-tuple-element.47.refs_12_) | copy-start | bytes 442372
  22.3 37.7 %copy-start.6 = (f32[192,128]{1,0:T(8,128)S(1)}, f32[192,128]{1,0:T(8,128)}, u32[]{:S(2)}) copy-start(f32[192,128]{1,0:T(8,128)} %get-tuple-element.26.len_ref) | copy-start | bytes 294916
  44.5 7.3 %collective-permute-start.6 = (f32[80,128]{1,0:T(8,128)S(1)}, f32[80,128]{1,0:T(8,128)S(1)}, u32[]{:S(2)}, u32[]{:S(2)}) collective-permute-start(f32[80,128]{1,0:T(8,128)S(1)} %get-tuple-element.37), channel_id=1, source_target_pairs={{0,1},{1,0},{2,3},{3,2},{4,5},{5,4},{6,7},{7,6},{8,9},{9,8},{10,11... | collective-permute-start | bytes 122888 | tf_op jit(solution)/shard_map/ppermute | solution.py:696
  46.0 7.3 %collective-permute-start.7 = (f32[80,128]{1,0:T(8,128)S(1)}, f32[80,128]{1,0:T(8,128)S(1)}, u32[]{:S(2)}, u32[]{:S(2)}) collective-permute-start(f32[80,128]{1,0:T(8,128)S(1)} %get-tuple-element.38), channel_id=1, source_target_pairs={{0,2},{1,3},{2,0},{3,1},{4,6},{5,7},{6,4},{7,5},{8,10},{9,11},{10,... | collective-permute-start | bytes 122888 | tf_op jit(solution)/shard_map/ppermute | solution.py:696
  46.0 9.7 %collective-permute-start.8 = (f32[80,128]{1,0:T(8,128)S(1)}, f32[80,128]{1,0:T(8,128)S(1)}, u32[]{:S(2)}, u32[]{:S(2)}) collective-permute-start(f32[80,128]{1,0:T(8,128)S(1)} %get-tuple-element.39), channel_id=1, source_target_pairs={{0,3},{1,2},{2,1},{3,0},{4,7},{5,6},{6,5},{7,4},{8,11},{9,10},{10,... | collective-permute-start | bytes 122888 | tf_op jit(solution)/shard_map/ppermute | solution.py:696
  48.1 7.7 %collective-permute-start.9 = (f32[80,128]{1,0:T(8,128)S(1)}, f32[80,128]{1,0:T(8,128)S(1)}, u32[]{:S(2)}, u32[]{:S(2)}) collective-permute-start(f32[80,128]{1,0:T(8,128)S(1)} %get-tuple-element.40), channel_id=1, source_target_pairs={{0,4},{1,5},{2,6},{3,7},{4,0},{5,1},{6,2},{7,3},{8,12},{9,13},{10,... | collective-permute-start | bytes 122888 | tf_op jit(solution)/shard_map/ppermute | solution.py:696
  49.1 7.3 %collective-permute-start.10 = (f32[80,128]{1,0:T(8,128)S(1)}, f32[80,128]{1,0:T(8,128)S(1)}, u32[]{:S(2)}, u32[]{:S(2)}) collective-permute-start(f32[80,128]{1,0:T(8,128)S(1)} %get-tuple-element.41), channel_id=1, source_target_pairs={{0,5},{1,4},{2,7},{3,6},{4,1},{5,0},{6,3},{7,2},{8,13},{9,12},{10,... | collective-permute-start | bytes 122888 | tf_op jit(solution)/shard_map/ppermute | solution.py:696
  51.8 5.9 %collective-permute-start.11 = (f32[80,128]{1,0:T(8,128)S(1)}, f32[80,128]{1,0:T(8,128)S(1)}, u32[]{:S(2)}, u32[]{:S(2)}) collective-permute-start(f32[80,128]{1,0:T(8,128)S(1)} %get-tuple-element.42), channel_id=1, source_target_pairs={{0,6},{1,7},{2,4},{3,5},{4,2},{5,3},{6,0},{7,1},{8,14},{9,15},{10,... | collective-permute-start | bytes 122888 | tf_op jit(solution)/shard_map/ppermute | solution.py:696
  53.3 6.7 %collective-permute-start.12 = (f32[80,128]{1,0:T(8,128)S(1)}, f32[80,128]{1,0:T(8,128)S(1)}, u32[]{:S(2)}, u32[]{:S(2)}) collective-permute-start(f32[80,128]{1,0:T(8,128)S(1)} %get-tuple-element.43), channel_id=1, source_target_pairs={{0,7},{1,6},{2,5},{3,4},{4,3},{5,2},{6,1},{7,0},{8,15},{9,14},{10,... | collective-permute-start | bytes 122888 | tf_op jit(solution)/shard_map/ppermute | solution.py:696

commit v12 on v11

--- a/solution.py
+++ b/solution.py
@@ -128,10 +128,11 @@
 
 
 def wave_kernel(
-    extent, me_ref, length_hbm, row_hbm, col_hbm, plane_hbm, coef_hbm,
-    out_ref, kc_ref, len_ref, whi_ref, wlo_ref, sc_ref, ss_ref,
-    length_ref, row_ref, col_ref, plane_ref, coef_ref, sems,
+    extent, devices, me_ref, length_hbm, row_hbm, col_hbm, plane_hbm, coef_hbm, *refs,
 ):
+    out_refs, refs = refs[:devices], refs[devices:]
+    kc_ref, len_ref, whi_ref, wlo_ref, sc_ref, ss_ref = refs[:6]
+    length_ref, row_ref, col_ref, plane_ref, coef_ref, out_ref, sems = refs[6:]
     copies = fetch_all(
         (length_hbm, row_hbm, col_hbm, plane_hbm, coef_hbm),
         (length_ref, row_ref, col_ref, plane_ref, coef_ref),
@@ -139,7 +140,6 @@
     )
     for copy in copies:
         copy.wait()
-    devices = out_ref.shape[0]
     sticks, _, padded = coef_ref.shape
     padded_planes = plane_ref.shape[1] // devices
     me = me_ref[0]
@@ -210,6 +210,14 @@
         out_ref[d, 2 * padded_planes:3 * padded_planes, :] = jnp.concatenate(
             [along_re[:, LANES:], along_im[:, LANES:]], axis=1
         )
+    for k in range(devices):
+        out_refs[k][...] = out_ref[lax.rem(me + k, devices)]
+
+
+def merge_kernel(devices, me_ref, *refs):
+    me = me_ref[0]
+    for k in range(devices):
+        refs[devices][lax.rem(me + devices - k, devices)] = refs[k][...]
 
 
 def window_row(values, sticks):
@@ -539,7 +547,7 @@
             scalar = jnp.sum(jnp.sum(partial, axis=1, keepdims=True), axis=0, keepdims=True)
             tile = jnp.where((lane == at) & (row == part), sign * norm * scalar, tile)
     for k in range(devices):
-        out_refs[k][0:3 * padded_planes, :] = in_ref[mine ^ k, 0:3 * padded_planes, :]
+        out_refs[k][0:3 * padded_planes, :] = in_ref[lax.rem(mine + k, devices), 0:3 * padded_planes, :]
         out_refs[k][3 * padded_planes:, :] = tile
 
 
@@ -554,7 +562,7 @@
     me = me_ref[0]
     for k in range(devices):
         value = ret_refs[k][...]
-        base = pl.multiple_of((me ^ k) * padded_planes, 8)
+        base = pl.multiple_of(lax.rem(me + devices - k, devices) * padded_planes, 8)
         total = total + value[3 * padded_planes:]
         rest = value[2 * padded_planes:3 * padded_planes]
         re = jnp.concatenate([value[:padded_planes], rest[:, :half]], axis=1)
@@ -573,6 +581,10 @@
     sub_ref[:, 0, :] = total[0:2, :bands]
 
 
+def ring(count, k):
+    return [(d, (d + k) % count) for d in range(count)]
+
+
 def pairs(count, k):
     return [(d, d ^ k) for d in range(count)]
 
@@ -604,10 +616,10 @@
 
     block = 3 * padded_planes
     total_planes = devices * padded_planes
-    sent, kc, lengths, whi, wlo, shift_cos, shift_sin = pl.pallas_call(
-        functools.partial(wave_kernel, extent),
+    *sent, kc, lengths, whi, wlo, shift_cos, shift_sin = pl.pallas_call(
+        functools.partial(wave_kernel, extent, devices),
         out_shape=(
-            jax.ShapeDtypeStruct((devices, block, LANES), F32),
+            *[jax.ShapeDtypeStruct((block, LANES), F32)] * devices,
             jax.ShapeDtypeStruct((sticks, 2 * padded), F32),
             jax.ShapeDtypeStruct((sticks, LANES), F32),
             jax.ShapeDtypeStruct((2 * total_planes, 2 * padded), BF16),
@@ -622,13 +634,23 @@
             pltpu.VMEM(col.shape, jnp.int32),
             pltpu.VMEM(slots.shape, jnp.int32),
             pltpu.VMEM(coef.shape, F32),
+            pltpu.VMEM((devices, block, LANES), F32),
             pltpu.SemaphoreType.DMA((5,)),
         ],
         compiler_params=params(56),
         name="wave_to_planes",
     )(me.reshape(1), length, row, col, slots, coef)
 
-    received = lax.all_to_all(sent, "tg", split_axis=0, concat_axis=0, tiled=True)
+    arrived = [sent[0]]
+    for k in range(1, devices):
+        arrived.append(lax.ppermute(sent[k], "tg", ring(devices, k)))
+    received = pl.pallas_call(
+        functools.partial(merge_kernel, devices),
+        out_shape=jax.ShapeDtypeStruct((devices, block, LANES), F32),
+        in_specs=[smem] + [vmem] * devices,
+        compiler_params=params(4),
+        name="merge",
+    )(me.reshape(1), *arrived)
 
     window_list = jax.ShapeDtypeStruct((windows, LANES), jnp.int32)
     longer_list = jax.ShapeDtypeStruct((2 * windows + 1, LANES), jnp.int32)
@@ -693,7 +715,7 @@
 
     returned = [outgoing[0]]
     for k in range(1, devices):
-        returned.append(lax.ppermute(outgoing[k], "tg", pairs(devices, k)))
+        returned.append(lax.ppermute(outgoing[k], "tg", ring(devices, k)))
     applied, subspace = pl.pallas_call(
         functools.partial(final_kernel, volume, devices),
         out_shape=(

time: 61.7 us -> 63.9 us (1.036)
  starting transfers between devices: 22.2 us -> 28 us
  waiting for transfers between devices: 8.28 us -> 4.52 us
    ppermute x7 -> x14, starting transfers between devices: 11.2 us -> 23 us  [the longest x7 12.4 us: shards(): arrived.append(lax.ppermute(sent[k], 'tg', ring(devices, k)))]
    all_to_all x1 -> x0, starting transfers between devices: 7.27 us -> none  [shards(): lax.all_to_all(sent, 'tg', split_axis=0, concat_axis=0, tiled=True)]
    all_to_all x1 -> x0, waiting for transfers between devices: 3.97 us -> none  [shards(): lax.all_to_all(sent, 'tg', split_axis=0, concat_axis=0, tiled=True)]
    ppermute x3, starting transfers between devices: 1.86 us -> 3.07 us  [shards(): coefs.append(lax.ppermute(coef, 'band', pairs(bands, m)))]
    ppermute x7 -> x14, waiting for transfers between devices: 4.29 us -> 4.51 us  [the longest x7 2.66 us: shards(): returned.append(lax.ppermute(outgoing[k], 'tg', ring(devices, k)))]
    pallas_call x1 -> x2, Pallas kernels: 2.91 us -> 3 us  [the longest x1 2.97 us: shards(): pl.pallas_call(functools.partial(wave_kernel, extent, devices), out_shape...]
    unnamed x18 -> x26, local copies, waits for them, and re-layouts: 1.42 us -> 1.43 us
  transfers between devices with their start and end apart: 14 -> 20, of which waited for: 4 -> 5; matrix products, arithmetic and copies ran while one was open for 0% -> 0% of each run, Pallas kernels for 37% -> 41%
where the time goes in v12:
time: 63.9 us; the launch traced here: 63.5 us
  Pallas kernels  28.7 us (45%)
  starting transfers between devices  28 us (44%)
  waiting for transfers between devices  4.52 us (7%)
  local copies, waits for them, and re-layouts  1.43 us (2%)
  between operations  0.8 us (1%)
    pallas_call x1, Pallas kernels, shards(): pl.pallas_call(functools.partial(plane_kernel, planes), out_shape=jax.Sha...  20.7 us
    ppermute x7, starting transfers between devices, shards(): arrived.append(lax.ppermute(sent[k], 'tg', ring(devices, k)))  12.4 us
    ppermute x7, starting transfers between devices, shards(): returned.append(lax.ppermute(outgoing[k], 'tg', ring(devices, k)))  10.6 us
    ppermute x3, starting transfers between devices, shards(): coefs.append(lax.ppermute(coef, 'band', pairs(bands, m)))  3.07 us
    pallas_call x1, Pallas kernels, shards(): pl.pallas_call(functools.partial(wave_kernel, extent, devices), out_shape...  2.97 us
    ppermute x7, waiting for transfers between devices, shards(): returned.append(lax.ppermute(outgoing[k], 'tg', ring(devices, k)))  2.66 us
    pallas_call x1, Pallas kernels, shards(): pl.pallas_call(functools.partial(map_kernel, extent, sticks), out_shape=(...  2.3 us
    ppermute x3, starting transfers between devices, shards(): fields.append(lax.ppermute(received, 'band', pairs(bands, m)))  1.92 us
  transfers between devices with their start and end apart: 20, of which 5 were waited for; matrix products, arithmetic and copies ran while one was open for 0% of the time, Pallas kernels for 41%

profile of v12, /device:TPU:0, one launch (start us, length us, event | category | flops | bytes accessed | tf_op | source)
XLA Modules:
  0.0 63.5 jit_solution(11314140484075523529)
XLA Ops:
  0.6 2.5 %collective-permute-start.2 = (f32[192,2,128]{2,1,0:T(2,128)}, f32[192,2,128]{2,1,0:T(2,128)S(1)}, u32[]{:S(2)}, u32[]{:S(2)}) collective-permute-start(f32[192,2,128]{2,1,0:T(2,128)} %bitcast.8), channel_id=1, source_target_pairs={{0,24},{8,16},{16,8},{24,0},{1,25},{9,17},{17,9},{25,1},{2,26},{10... | collective-permute-start | bytes 589832 | tf_op jit(solution)/shard_map/ppermute | solution.py:703
  3.1 3.0 %wave_to_planes.1 = (f32[72,128]{1,0:T(8,128)}, f32[72,128]{1,0:T(8,128)}, f32[72,128]{1,0:T(8,128)}, f32[72,128]{1,0:T(8,128)}, f32[72,128]{1,0:T(8,128)}, /*in...) custom-call(s32[1]{0:T(128)} %bitcast.me_ref, ...), custom_call_target="tpu_custom_call" | custom-call | tf_op jit(solution)/shard_map/wave_to_planes/pallas_call | solution.py:619
  6.1 1.5 %collective-permute-start.3 = (f32[72,128]{1,0:T(8,128)}, f32[72,128]{1,0:T(8,128)S(1)}, u32[]{:S(2)}, u32[]{:S(2)}) collective-permute-start(f32[72,128]{1,0:T(8,128)} %get-tuple-element.36), channel_id=1, source_target_pairs={{0,1},{1,2},{2,3},{3,4},{4,5},{5,6},{6,7},{7,0},{8,9},{9,10},{10,1... | collective-permute-start | bytes 110600 | tf_op jit(solution)/shard_map/ppermute | solution.py:646
  7.6 1.6 %collective-permute-start.4 = (f32[72,128]{1,0:T(8,128)}, f32[72,128]{1,0:T(8,128)S(1)}, u32[]{:S(2)}, u32[]{:S(2)}) collective-permute-start(f32[72,128]{1,0:T(8,128)} %get-tuple-element.37), channel_id=1, source_target_pairs={{0,2},{1,3},{2,4},{3,5},{4,6},{5,7},{6,0},{7,1},{8,10},{9,11},{10,... | collective-permute-start | bytes 110600 | tf_op jit(solution)/shard_map/ppermute | solution.py:646
  9.2 2.5 %collective-permute-start.5 = (f32[72,128]{1,0:T(8,128)}, f32[72,128]{1,0:T(8,128)S(1)}, u32[]{:S(2)}, u32[]{:S(2)}) collective-permute-start(f32[72,128]{1,0:T(8,128)} %get-tuple-element.38), channel_id=1, source_target_pairs={{0,3},{1,4},{2,5},{3,6},{4,7},{5,0},{6,1},{7,2},{8,11},{9,12},{10,... | collective-permute-start | bytes 110600 | tf_op jit(solution)/shard_map/ppermute | solution.py:646
  11.8 1.2 %collective-permute-start.6 = (f32[72,128]{1,0:T(8,128)}, f32[72,128]{1,0:T(8,128)S(1)}, u32[]{:S(2)}, u32[]{:S(2)}) collective-permute-start(f32[72,128]{1,0:T(8,128)} %get-tuple-element.39), channel_id=1, source_target_pairs={{0,4},{1,5},{2,6},{3,7},{4,0},{5,1},{6,2},{7,3},{8,12},{9,13},{10,... | collective-permute-start | bytes 110600 | tf_op jit(solution)/shard_map/ppermute | solution.py:646
  13.0 0.7 %copy-done.8 = s32[1536]{0:T(1024)S(1)} copy-done((s32[1536]{0:T(1024)S(1)}, s32[1536]{0:T(1024)}, u32[]{:S(2)}) %copy-start.8) | copy-done | bytes 6168
  13.7 0.7 %copy-done.9 = s32[1536]{0:T(1024)S(1)} copy-done((s32[1536]{0:T(1024)S(1)}, s32[1536]{0:T(1024)}, u32[]{:S(2)}) %copy-start.9) | copy-done | bytes 6168
  14.4 2.3 %stick_map.1 = (s32[128,128]{1,0:T(8,128)S(1)}, s32[128,128]{1,0:T(8,128)S(1)}, s32[16,128]{1,0:T(8,128)S(1)}, s32[12,128]{1,0:T(8,128)S(1)}, s32[12,128]{1,0:T(...) custom-call(s32[12,128]{1,0:T(8,128)S(1)} %bitcast.14, s32[12,128]{1,0:T(8,128)S(1)} %bitcast.16), custom_call_target="tpu_custom_call" | custom-call | flops 4000000000 | bytes 100000 | tf_op jit(solution)/shard_map/stick_map/pallas_call | solution.py:658
  16.7 2.7 %collective-permute-start.7 = (f32[72,128]{1,0:T(8,128)S(1)}, f32[72,128]{1,0:T(8,128)S(1)}, u32[]{:S(2)}, u32[]{:S(2)}) collective-permute-start(f32[72,128]{1,0:T(8,128)S(1)} %copy-done.12), channel_id=1, source_target_pairs={{0,5},{1,6},{2,7},{3,0},{4,1},{5,2},{6,3},{7,4},{8,13},{9,14},{10,... | collective-permute-start | bytes 110600 | tf_op jit(solution)/shard_map/ppermute | solution.py:646
  19.4 1.4 %collective-permute-start.8 = (f32[72,128]{1,0:T(8,128)S(1)}, f32[72,128]{1,0:T(8,128)S(1)}, u32[]{:S(2)}, u32[]{:S(2)}) collective-permute-start(f32[72,128]{1,0:T(8,128)S(1)} %copy-done.11), channel_id=1, source_target_pairs={{0,6},{1,7},{2,0},{3,1},{4,2},{5,3},{6,4},{7,5},{8,14},{9,15},{10,... | collective-permute-start | bytes 110600 | tf_op jit(solution)/shard_map/ppermute | solution.py:646
  20.8 1.4 %collective-permute-start.9 = (f32[72,128]{1,0:T(8,128)S(1)}, f32[72,128]{1,0:T(8,128)S(1)}, u32[]{:S(2)}, u32[]{:S(2)}) collective-permute-start(f32[72,128]{1,0:T(8,128)S(1)} %copy-done.10), channel_id=1, source_target_pairs={{0,7},{1,0},{2,1},{3,2},{4,3},{5,4},{6,5},{7,6},{8,15},{9,8},{10,9... | collective-permute-start | bytes 110600 | tf_op jit(solution)/shard_map/ppermute | solution.py:646
  22.2 0.1 pad_add_fusion.place_ref
  22.3 0.6 collective-permute-start.1
  22.9 0.5 collective-permute-done.8.refs_6_
  23.4 1.4 %collective-permute-done.9.refs_7_ = f32[72,128]{1,0:T(8,128)S(1)} collective-permute-done((f32[72,128]{1,0:T(8,128)S(1)}, f32[72,128]{1,0:T(8,128)S(1)}, u32[]{:S(2)}, u32[]{:S(2)}) %collective-permute-start.9) | collective-permute-done | bytes 36896 | tf_op jit(solution)/shard_map/ppermute | solution.py:646
  24.8 0.1 collective-permute-start.12
  24.8 0.7 %collective-permute-start.11 = (f32[8,72,128]{2,1,0:T(8,128)S(1)}, f32[8,72,128]{2,1,0:T(8,128)S(1)}, u32[]{:S(2)}, u32[]{:S(2)}) collective-permute-start(f32[8,72,128]{2,1,0:T(8,128)S(1)} %merge.1.recv_ref.refs_5_), channel_id=1, source_target_pairs={{0,16},{8,24},{16,0},{24,8},{1,17},{9,25},{17,1},{25,9},{2,18},{10... | collective-permute-start | bytes 884744 | tf_op jit(solution)/shard_map/ppermute | solution.py:704
  25.5 1.2 %collective-permute-start.10 = (f32[8,72,128]{2,1,0:T(8,128)S(1)}, f32[8,72,128]{2,1,0:T(8,128)S(1)}, u32[]{:S(2)}, u32[]{:S(2)}) collective-permute-start(f32[8,72,128]{2,1,0:T(8,128)S(1)} %merge.1.recv_ref.refs_5_), channel_id=1, source_target_pairs={{0,8},{8,0},{16,24},{24,16},{1,9},{9,1},{17,25},{25,17},{2,10},{10... | collective-permute-start | bytes 884744 | tf_op jit(solution)/shard_map/ppermute | solution.py:704
  26.7 20.7 %planes.1.refs_9_ = f32[8,80,128]{2,1,0:T(8,128)S(1)} custom-call(s32[16,128]{1,0:T(8,128)S(1)} %get-tuple-element.43.first_ref, s32[128,128]{1,0:T(8,128)S(1)} %get-tuple-element.44.even_ref, s32[128,128]{1,0:T(8,128)S(1)} %get-tuple-element.45.odd_ref, s32[12,128]{1,0:T(8,128)S(1)} %get-tuple-element.46.src_ref, s32[12,128]{1,0:T(8,128)S(1)} %get-tuple-element.47.dst_ref, ...), custom_call_target="tpu_custom_call" | custom-call | flops 20000000000 | bytes 10000000 | tf_op jit(solution)/shard_map/planes/pallas_call | solution.py:681
  47.5 1.5 %inner.1 = (f32[80,128]{1,0:T(8,128)S(1)}, f32[80,128]{1,0:T(8,128)S(1)}, f32[80,128]{1,0:T(8,128)S(1)}, f32[80,128]{1,0:T(8,128)S(1)}, f32[80,128]{1,0:T(8,128)...) custom-call(s32[2]{0:T(128)S(1)} %pad_add_fusion.place_ref, f32[192,256]{1,0:T(8,128)S(1)} %copy-done, ...), custom_call_target="tpu_custom_call" | custom-call | tf_op jit(solution)/shard_map/inner/pallas_call | solution.py:708
  48.9 1.6 %collective-permute-start.13 = (f32[80,128]{1,0:T(8,128)S(1)}, f32[80,128]{1,0:T(8,128)S(1)}, u32[]{:S(2)}, u32[]{:S(2)}) collective-permute-start(f32[80,128]{1,0:T(8,128)S(1)} %get-tuple-element.51), channel_id=1, source_target_pairs={{0,1},{1,2},{2,3},{3,4},{4,5},{5,6},{6,7},{7,0},{8,9},{9,10},{10,1... | collective-permute-start | bytes 122888 | tf_op jit(solution)/shard_map/ppermute | solution.py:718
  50.5 0.2 collective-permute-start.14
  50.8 2.0 %collective-permute-start.15 = (f32[80,128]{1,0:T(8,128)S(1)}, f32[80,128]{1,0:T(8,128)S(1)}, u32[]{:S(2)}, u32[]{:S(2)}) collective-permute-start(f32[80,128]{1,0:T(8,128)S(1)} %get-tuple-element.53), channel_id=1, source_target_pairs={{0,3},{1,4},{2,5},{3,6},{4,7},{5,0},{6,1},{7,2},{8,11},{9,12},{10,... | collective-permute-start | bytes 122888 | tf_op jit(solution)/shard_map/ppermute | solution.py:718
  52.8 2.1 %collective-permute-start.16 = (f32[80,128]{1,0:T(8,128)S(1)}, f32[80,128]{1,0:T(8,128)S(1)}, u32[]{:S(2)}, u32[]{:S(2)}) collective-permute-start(f32[80,128]{1,0:T(8,128)S(1)} %get-tuple-element.54), channel_id=1, source_target_pairs={{0,4},{1,5},{2,6},{3,7},{4,0},{5,1},{6,2},{7,3},{8,12},{9,13},{10,... | collective-permute-start | bytes 122888 | tf_op jit(solution)/shard_map/ppermute | solution.py:718
  54.9 3.1 %collective-permute-start.17 = (f32[80,128]{1,0:T(8,128)S(1)}, f32[80,128]{1,0:T(8,128)S(1)}, u32[]{:S(2)}, u32[]{:S(2)}) collective-permute-start(f32[80,128]{1,0:T(8,128)S(1)} %get-tuple-element.55), channel_id=1, source_target_pairs={{0,5},{1,6},{2,7},{3,0},{4,1},{5,2},{6,3},{7,4},{8,13},{9,14},{10,... | collective-permute-start | bytes 122888 | tf_op jit(solution)/shard_map/ppermute | solution.py:718
  58.1 0.1 collective-permute-start.18
  58.2 1.3 %collective-permute-start.19 = (f32[80,128]{1,0:T(8,128)S(1)}, f32[80,128]{1,0:T(8,128)S(1)}, u32[]{:S(2)}, u32[]{:S(2)}) collective-permute-start(f32[80,128]{1,0:T(8,128)S(1)} %get-tuple-element.57), channel_id=1, source_target_pairs={{0,7},{1,0},{2,1},{3,2},{4,3},{5,4},{6,5},{7,6},{8,15},{9,8},{10,9... | collective-permute-start | bytes 122888 | tf_op jit(solution)/shard_map/ppermute | solution.py:718
  59.5 1.1 %collective-permute-done.17.refs_5_ = f32[80,128]{1,0:T(8,128)S(1)} collective-permute-done((f32[80,128]{1,0:T(8,128)S(1)}, f32[80,128]{1,0:T(8,128)S(1)}, u32[]{:S(2)}, u32[]{:S(2)}) %collective-permute-start.17) | collective-permute-done | bytes 40992 | tf_op jit(solution)/shard_map/ppermute | solution.py:718
  60.6 1.4 %collective-permute-done.18.refs_6_ = f32[80,128]{1,0:T(8,128)S(1)} collective-permute-done((f32[80,128]{1,0:T(8,128)S(1)}, f32[80,128]{1,0:T(8,128)S(1)}, u32[]{:S(2)}, u32[]{:S(2)}) %collective-permute-start.18) | collective-permute-done | bytes 40992 | tf_op jit(solution)/shard_map/ppermute | solution.py:718
  62.1 0.1 collective-permute-done.19.refs_7_
  62.2 1.3 %planes_to_wave.1 = (f32[192,2,128]{2,1,0:T(2,128)}, f32[2,1,4]{2,1,0:T(1,128)}) custom-call(s32[1]{0:T(128)} %bitcast.me_ref, f32[192,128]{1,0:T(8,128)S(1)} %copy-done.6, f32[80,128]{1,0:T(8,128)S(1)} %get-tuple-element.50.refs_0_, f32[80,128]{1,0:T(8,128)S(1)} %collective-permute-done.13.refs_1_, f32[80,128]{1,0:T(8,128)S(1)} %collective-permute-done.14.refs_2_, ...), custom_call_target="tpu_custom_call" | custom-call | tf_op jit(solution)/shard_map/planes_to_wave/pallas_call | solution.py:719
  (41 shorter events, 0.1 us)
Async XLA Ops:
  0.6 24.9 %collective-permute-start.2 = (f32[192,2,128]{2,1,0:T(2,128)}, f32[192,2,128]{2,1,0:T(2,128)S(1)}, u32[]{:S(2)}, u32[]{:S(2)}) collective-permute-start(f32[192,2,128]{2,1,0:T(2,128)} %bitcast.8), channel_id=1, source_target_pairs={{0,24},{8,16},{16,8},{24,0},{1,25},{9,17},{17,9},{25,1},{2,26},{10... | collective-permute-start | bytes 589832 | tf_op jit(solution)/shard_map/ppermute | solution.py:703
  6.1 10.6 %collective-permute-start.3 = (f32[72,128]{1,0:T(8,128)}, f32[72,128]{1,0:T(8,128)S(1)}, u32[]{:S(2)}, u32[]{:S(2)}) collective-permute-start(f32[72,128]{1,0:T(8,128)} %get-tuple-element.36), channel_id=1, source_target_pairs={{0,1},{1,2},{2,3},{3,4},{4,5},{5,6},{6,7},{7,0},{8,9},{9,10},{10,1... | collective-permute-start | bytes 110600 | tf_op jit(solution)/shard_map/ppermute | solution.py:646
  7.6 11.8 %collective-permute-start.4 = (f32[72,128]{1,0:T(8,128)}, f32[72,128]{1,0:T(8,128)S(1)}, u32[]{:S(2)}, u32[]{:S(2)}) collective-permute-start(f32[72,128]{1,0:T(8,128)} %get-tuple-element.37), channel_id=1, source_target_pairs={{0,2},{1,3},{2,4},{3,5},{4,6},{5,7},{6,0},{7,1},{8,10},{9,11},{10,... | collective-permute-start | bytes 110600 | tf_op jit(solution)/shard_map/ppermute | solution.py:646
  9.2 11.5 %collective-permute-start.5 = (f32[72,128]{1,0:T(8,128)}, f32[72,128]{1,0:T(8,128)S(1)}, u32[]{:S(2)}, u32[]{:S(2)}) collective-permute-start(f32[72,128]{1,0:T(8,128)} %get-tuple-element.38), channel_id=1, source_target_pairs={{0,3},{1,4},{2,5},{3,6},{4,7},{5,0},{6,1},{7,2},{8,11},{9,12},{10,... | collective-permute-start | bytes 110600 | tf_op jit(solution)/shard_map/ppermute | solution.py:646
  11.8 10.5 %copy-start.1 = (f32[1,192,2,128]{3,2,1,0:T(2,128)S(1)}, f32[1,192,2,128]{3,2,1,0:T(2,128)}, u32[]{:S(2)}) copy-start(f32[1,192,2,128]{3,2,1,0:T(2,128)} %param.7) | copy-start | bytes 589828
  11.8 13.0 %copy-start.7 = (f32[72,128]{1,0:T(8,128)S(1)}, f32[72,128]{1,0:T(8,128)}, u32[]{:S(2)}) copy-start(f32[72,128]{1,0:T(8,128)} %get-tuple-element.35.refs_0_) | copy-start | bytes 110596
  11.8 10.5 %collective-permute-start.6 = (f32[72,128]{1,0:T(8,128)}, f32[72,128]{1,0:T(8,128)S(1)}, u32[]{:S(2)}, u32[]{:S(2)}) collective-permute-start(f32[72,128]{1,0:T(8,128)} %get-tuple-element.39), channel_id=1, source_target_pairs={{0,4},{1,5},{2,6},{3,7},{4,0},{5,1},{6,2},{7,3},{8,12},{9,13},{10,... | collective-permute-start | bytes 110600 | tf_op jit(solution)/shard_map/ppermute | solution.py:646
  13.0 0.7 %copy-start.8 = (s32[1536]{0:T(1024)S(1)}, s32[1536]{0:T(1024)}, u32[]{:S(2)}) copy-start(s32[1536]{0:T(1024)} %param.9) | copy-start | bytes 18436
  14.4 2.3 %copy-start.12 = (f32[72,128]{1,0:T(8,128)S(1)}, f32[72,128]{1,0:T(8,128)}, u32[]{:S(2)}) copy-start(f32[72,128]{1,0:T(8,128)} %get-tuple-element.40) | copy-start | bytes 110596
  14.4 5.0 %copy-start.11 = (f32[72,128]{1,0:T(8,128)S(1)}, f32[72,128]{1,0:T(8,128)}, u32[]{:S(2)}) copy-start(f32[72,128]{1,0:T(8,128)} %get-tuple-element.41) | copy-start | bytes 110596
  14.4 6.4 %copy-start.10 = (f32[72,128]{1,0:T(8,128)S(1)}, f32[72,128]{1,0:T(8,128)}, u32[]{:S(2)}) copy-start(f32[72,128]{1,0:T(8,128)} %get-tuple-element.42) | copy-start | bytes 110596
  16.7 6.1 %collective-permute-start.7 = (f32[72,128]{1,0:T(8,128)S(1)}, f32[72,128]{1,0:T(8,128)S(1)}, u32[]{:S(2)}, u32[]{:S(2)}) collective-permute-start(f32[72,128]{1,0:T(8,128)S(1)} %copy-done.12), channel_id=1, source_target_pairs={{0,5},{1,6},{2,7},{3,0},{4,1},{5,2},{6,3},{7,4},{8,13},{9,14},{10,... | collective-permute-start | bytes 110600 | tf_op jit(solution)/shard_map/ppermute | solution.py:646
  19.4 4.0 %collective-permute-start.8 = (f32[72,128]{1,0:T(8,128)S(1)}, f32[72,128]{1,0:T(8,128)S(1)}, u32[]{:S(2)}, u32[]{:S(2)}) collective-permute-start(f32[72,128]{1,0:T(8,128)S(1)} %copy-done.11), channel_id=1, source_target_pairs={{0,6},{1,7},{2,0},{3,1},{4,2},{5,3},{6,4},{7,5},{8,14},{9,15},{10,... | collective-permute-start | bytes 110600 | tf_op jit(solution)/shard_map/ppermute | solution.py:646
  20.8 4.0 %collective-permute-start.9 = (f32[72,128]{1,0:T(8,128)S(1)}, f32[72,128]{1,0:T(8,128)S(1)}, u32[]{:S(2)}, u32[]{:S(2)}) collective-permute-start(f32[72,128]{1,0:T(8,128)S(1)} %copy-done.10), channel_id=1, source_target_pairs={{0,7},{1,0},{2,1},{3,2},{4,3},{5,4},{6,5},{7,6},{8,15},{9,8},{10,9... | collective-permute-start | bytes 110600 | tf_op jit(solution)/shard_map/ppermute | solution.py:646
  22.3 25.1 %collective-permute-start.1 = (f32[192,2,128]{2,1,0:T(2,128)S(1)}, f32[192,2,128]{2,1,0:T(2,128)S(1)}, u32[]{:S(2)}, u32[]{:S(2)}) collective-permute-start(f32[192,2,128]{2,1,0:T(2,128)S(1)} %bitcast.10), channel_id=1, source_target_pairs={{0,16},{8,24},{16,0},{24,8},{1,17},{9,25},{17,1},{25,9},{2,18},{10... | collective-permute-start | bytes 589832 | tf_op jit(solution)/shard_map/ppermute | solution.py:703
  22.9 24.5 %collective-permute-start = (f32[192,2,128]{2,1,0:T(2,128)S(1)}, f32[192,2,128]{2,1,0:T(2,128)S(1)}, u32[]{:S(2)}, u32[]{:S(2)}) collective-permute-start(f32[192,2,128]{2,1,0:T(2,128)S(1)} %bitcast.11), channel_id=1, source_target_pairs={{0,8},{8,0},{16,24},{24,16},{1,9},{9,1},{17,25},{25,17},{2,10},{10... | collective-permute-start | bytes 589832 | tf_op jit(solution)/shard_map/ppermute | solution.py:703
  24.8 22.7 %collective-permute-start.12 = (f32[8,72,128]{2,1,0:T(8,128)S(1)}, f32[8,72,128]{2,1,0:T(8,128)S(1)}, u32[]{:S(2)}, u32[]{:S(2)}) collective-permute-start(f32[8,72,128]{2,1,0:T(8,128)S(1)} %merge.1.recv_ref.refs_5_), channel_id=1, source_target_pairs={{0,24},{8,16},{16,8},{24,0},{1,25},{9,17},{17,9},{25,1},{2,26},{10... | collective-permute-start | bytes 884744 | tf_op jit(solution)/shard_map/ppermute | solution.py:704
  24.8 22.6 %collective-permute-start.11 = (f32[8,72,128]{2,1,0:T(8,128)S(1)}, f32[8,72,128]{2,1,0:T(8,128)S(1)}, u32[]{:S(2)}, u32[]{:S(2)}) collective-permute-start(f32[8,72,128]{2,1,0:T(8,128)S(1)} %merge.1.recv_ref.refs_5_), channel_id=1, source_target_pairs={{0,16},{8,24},{16,0},{24,8},{1,17},{9,25},{17,1},{25,9},{2,18},{10... | collective-permute-start | bytes 884744 | tf_op jit(solution)/shard_map/ppermute | solution.py:704
  25.5 21.9 %collective-permute-start.10 = (f32[8,72,128]{2,1,0:T(8,128)S(1)}, f32[8,72,128]{2,1,0:T(8,128)S(1)}, u32[]{:S(2)}, u32[]{:S(2)}) collective-permute-start(f32[8,72,128]{2,1,0:T(8,128)S(1)} %merge.1.recv_ref.refs_5_), channel_id=1, source_target_pairs={{0,8},{8,0},{16,24},{24,16},{1,9},{9,1},{17,25},{25,17},{2,10},{10... | collective-permute-start | bytes 884744 | tf_op jit(solution)/shard_map/ppermute | solution.py:704
  26.7 20.8 %copy-start = (f32[192,256]{1,0:T(8,128)S(1)}, f32[192,256]{1,0:T(8,128)}, u32[]{:S(2)}) copy-start(f32[192,256]{1,0:T(8,128)} %get-tuple-element.34.refs_0_.refs_8_) | copy-start | bytes 589828
  26.7 35.5 %copy-start.2 = (bf16[384,256]{1,0:T(8,128)(2,1)S(1)}, bf16[384,256]{1,0:T(8,128)(2,1)}, u32[]{:S(2)}) copy-start(bf16[384,256]{1,0:T(8,128)(2,1)} %get-tuple-element.58.refs_9_) | copy-start | bytes 589828
  26.7 35.5 %copy-start.3 = (bf16[384,256]{1,0:T(8,128)(2,1)S(1)}, bf16[384,256]{1,0:T(8,128)(2,1)}, u32[]{:S(2)}) copy-start(bf16[384,256]{1,0:T(8,128)(2,1)} %get-tuple-element.59.refs_10_) | copy-start | bytes 589828
  26.7 35.5 %copy-start.4 = (f32[192,192]{1,0:T(8,128)S(1)}, f32[192,192]{1,0:T(8,128)}, u32[]{:S(2)}) copy-start(f32[192,192]{1,0:T(8,128)} %get-tuple-element.60.refs_11_) | copy-start | bytes 442372
  26.7 35.5 %copy-start.5 = (f32[192,192]{1,0:T(8,128)S(1)}, f32[192,192]{1,0:T(8,128)}, u32[]{:S(2)}) copy-start(f32[192,192]{1,0:T(8,128)} %get-tuple-element.61.refs_12_) | copy-start | bytes 442372
  26.7 35.5 %copy-start.6 = (f32[192,128]{1,0:T(8,128)S(1)}, f32[192,128]{1,0:T(8,128)}, u32[]{:S(2)}) copy-start(f32[192,128]{1,0:T(8,128)} %get-tuple-element.33.len_ref) | copy-start | bytes 294916
  48.9 9.1 %collective-permute-start.13 = (f32[80,128]{1,0:T(8,128)S(1)}, f32[80,128]{1,0:T(8,128)S(1)}, u32[]{:S(2)}, u32[]{:S(2)}) collective-permute-start(f32[80,128]{1,0:T(8,128)S(1)} %get-tuple-element.51), channel_id=1, source_target_pairs={{0,1},{1,2},{2,3},{3,4},{4,5},{5,6},{6,7},{7,0},{8,9},{9,10},{10,1... | collective-permute-start | bytes 122888 | tf_op jit(solution)/shard_map/ppermute | solution.py:718
  50.5 7.7 %collective-permute-start.14 = (f32[80,128]{1,0:T(8,128)S(1)}, f32[80,128]{1,0:T(8,128)S(1)}, u32[]{:S(2)}, u32[]{:S(2)}) collective-permute-start(f32[80,128]{1,0:T(8,128)S(1)} %get-tuple-element.52), channel_id=1, source_target_pairs={{0,2},{1,3},{2,4},{3,5},{4,6},{5,7},{6,0},{7,1},{8,10},{9,11},{10,... | collective-permute-start | bytes 122888 | tf_op jit(solution)/shard_map/ppermute | solution.py:718
  50.8 8.8 %collective-permute-start.15 = (f32[80,128]{1,0:T(8,128)S(1)}, f32[80,128]{1,0:T(8,128)S(1)}, u32[]{:S(2)}, u32[]{:S(2)}) collective-permute-start(f32[80,128]{1,0:T(8,128)S(1)} %get-tuple-element.53), channel_id=1, source_target_pairs={{0,3},{1,4},{2,5},{3,6},{4,7},{5,0},{6,1},{7,2},{8,11},{9,12},{10,... | collective-permute-start | bytes 122888 | tf_op jit(solution)/shard_map/ppermute | solution.py:718
  52.8 6.8 %collective-permute-start.16 = (f32[80,128]{1,0:T(8,128)S(1)}, f32[80,128]{1,0:T(8,128)S(1)}, u32[]{:S(2)}, u32[]{:S(2)}) collective-permute-start(f32[80,128]{1,0:T(8,128)S(1)} %get-tuple-element.54), channel_id=1, source_target_pairs={{0,4},{1,5},{2,6},{3,7},{4,0},{5,1},{6,2},{7,3},{8,12},{9,13},{10,... | collective-permute-start | bytes 122888 | tf_op jit(solution)/shard_map/ppermute | solution.py:718
  54.9 5.7 %collective-permute-start.17 = (f32[80,128]{1,0:T(8,128)S(1)}, f32[80,128]{1,0:T(8,128)S(1)}, u32[]{:S(2)}, u32[]{:S(2)}) collective-permute-start(f32[80,128]{1,0:T(8,128)S(1)} %get-tuple-element.55), channel_id=1, source_target_pairs={{0,5},{1,6},{2,7},{3,0},{4,1},{5,2},{6,3},{7,4},{8,13},{9,14},{10,... | collective-permute-start | bytes 122888 | tf_op jit(solution)/shard_map/ppermute | solution.py:718
  58.1 4.0 %collective-permute-start.18 = (f32[80,128]{1,0:T(8,128)S(1)}, f32[80,128]{1,0:T(8,128)S(1)}, u32[]{:S(2)}, u32[]{:S(2)}) collective-permute-start(f32[80,128]{1,0:T(8,128)S(1)} %get-tuple-element.56), channel_id=1, source_target_pairs={{0,6},{1,7},{2,0},{3,1},{4,2},{5,3},{6,4},{7,5},{8,14},{9,15},{10,... | collective-permute-start | bytes 122888 | tf_op jit(solution)/shard_map/ppermute | solution.py:718
  58.2 4.0 %collective-permute-start.19 = (f32[80,128]{1,0:T(8,128)S(1)}, f32[80,128]{1,0:T(8,128)S(1)}, u32[]{:S(2)}, u32[]{:S(2)}) collective-permute-start(f32[80,128]{1,0:T(8,128)S(1)} %get-tuple-element.57), channel_id=1, source_target_pairs={{0,7},{1,0},{2,1},{3,2},{4,3},{5,4},{6,5},{7,6},{8,15},{9,8},{10,9... | collective-permute-start | bytes 122888 | tf_op jit(solution)/shard_map/ppermute | solution.py:718
  (1 other events, 0.7 us)

commit v13 on v11

--- a/solution.py
+++ b/solution.py
@@ -137,7 +137,7 @@
         (length_ref, row_ref, col_ref, plane_ref, coef_ref),
         sems,
     )
-    for copy in copies:
+    for copy in copies[:4]:
         copy.wait()
     devices = out_ref.shape[0]
     sticks, _, padded = coef_ref.shape
@@ -172,11 +172,6 @@
     square = aux_col[:, LANES // 2:LANES // 2 + 1]
     middle = (length - 1.0) * 0.5
     position = lax.broadcasted_iota(jnp.int32, (sticks, padded), 1).astype(F32)
-    kept = (position < length).astype(F32)
-    kinetic = (square + (position - middle) * (position - middle)) * (1.0 / (RADIUS * RADIUS))
-    wave = jnp.concatenate([coef_ref[:, 0, :] * kept, coef_ref[:, 1, :] * kept], axis=1)
-    kc_ref[...] = wave * jnp.concatenate([kinetic, kinetic], axis=1)
-
     total = plane_ref.shape[1]
     plane_row = jnp.broadcast_to(plane_ref[...].astype(F32), (LANES, total))
     plane_col = jnp.transpose(plane_row)[:, 0:1]
@@ -197,6 +192,11 @@
     shift_cos, shift_sin = trig(plane_col * ((length_row - 1.0) * 0.5), extent)
     sc_ref[...] = shift_cos
     ss_ref[...] = shift_sin
+    copies[4].wait()
+    kept = (position < length).astype(F32)
+    kinetic = (square + (position - middle) * (position - middle)) * (1.0 / (RADIUS * RADIUS))
+    wave = jnp.concatenate([coef_ref[:, 0, :] * kept, coef_ref[:, 1, :] * kept], axis=1)
+    kc_ref[...] = wave * jnp.concatenate([kinetic, kinetic], axis=1)
     raw = dot3(table, split(wave), ((1,), (1,)))
     for d in range(devices):
         at = 2 * d * padded_planes
@@ -386,7 +386,7 @@
         copy.wait()
     even_rows, odd_rows = row_blocks()
     folded = extent // 2
-    group = next(g for g in (8, 4, 2) if planes % g == 0)
+    group = next(g for g in (12, 8, 6, 4, 2) if planes % g == 0)
     wide = 2 * LANES
     at_back = 3 * LANES
     at_y = at_back + 2 * wide
@@ -539,7 +539,7 @@
             scalar = jnp.sum(jnp.sum(partial, axis=1, keepdims=True), axis=0, keepdims=True)
             tile = jnp.where((lane == at) & (row == part), sign * norm * scalar, tile)
     for k in range(devices):
-        out_refs[k][0:3 * padded_planes, :] = in_ref[mine ^ k, 0:3 * padded_planes, :]
+        out_refs[k][0:3 * padded_planes, :] = in_ref[lax.rem(mine + k, devices), 0:3 * padded_planes, :]
         out_refs[k][3 * padded_planes:, :] = tile
 
 
@@ -554,7 +554,7 @@
     me = me_ref[0]
     for k in range(devices):
         value = ret_refs[k][...]
-        base = pl.multiple_of((me ^ k) * padded_planes, 8)
+        base = pl.multiple_of(lax.rem(me + devices - k, devices) * padded_planes, 8)
         total = total + value[3 * padded_planes:]
         rest = value[2 * padded_planes:3 * padded_planes]
         re = jnp.concatenate([value[:padded_planes], rest[:, :half]], axis=1)
@@ -584,8 +584,7 @@
     total_sticks = stick_col.shape[0]
     planes = potential.shape[0]
     padded_planes = up8(planes)
-    powers = devices & (devices - 1) == 0 and bands & (bands - 1) == 0
-    if sticks != LANES + LANES // 2 or not powers or planes % 2:
+    if sticks != LANES + LANES // 2 or devices % 2 or planes % 2 or bands & (bands - 1):
         raise ValueError("sizes")
     rows = sum(row_blocks())
     volume = 1.0 / (extent * extent * extent)
@@ -693,7 +692,8 @@
 
     returned = [outgoing[0]]
     for k in range(1, devices):
-        returned.append(lax.ppermute(outgoing[k], "tg", pairs(devices, k)))
+        ring = [(d, (d + k) % devices) for d in range(devices)]
+        returned.append(lax.ppermute(outgoing[k], "tg", ring))
     applied, subspace = pl.pallas_call(
         functools.partial(final_kernel, volume, devices),
         out_shape=(

time: 61.7 us -> 58.8 us (0.953)
  waiting for transfers between devices: 8.28 us -> 6.37 us
    ppermute x7, waiting for transfers between devices: 4.29 us -> 2.38 us  [shards(): returned.append(lax.ppermute(outgoing[k], 'tg', ring))]
  transfers between devices with their start and end apart: 14 -> 14, of which waited for: 4 -> 4; matrix products, arithmetic and copies ran while one was open for 0% -> 0% of each run, Pallas kernels for 37% -> 39%
where the time goes in v13:
time: 58.8 us; the launch traced here: 58.5 us
  Pallas kernels  28.1 us (48%)
  starting transfers between devices  21.7 us (37%)
  waiting for transfers between devices  6.37 us (11%)
  local copies, waits for them, and re-layouts  1.42 us (2%)
  between operations  0.78 us (1%)
    pallas_call x1, Pallas kernels, shards(): pl.pallas_call(functools.partial(plane_kernel, planes), out_shape=jax.Sha...  20.3 us
    ppermute x7, starting transfers between devices, shards(): returned.append(lax.ppermute(outgoing[k], 'tg', ring))  10.7 us
    all_to_all x1, starting transfers between devices, shards(): lax.all_to_all(sent, 'tg', split_axis=0, concat_axis=0, tiled=True)  7.27 us
    all_to_all x1, waiting for transfers between devices, shards(): lax.all_to_all(sent, 'tg', split_axis=0, concat_axis=0, tiled=True)  3.97 us
    pallas_call x1, Pallas kernels, shards(): pl.pallas_call(functools.partial(wave_kernel, extent), out_shape=(jax.Sha...  2.75 us
    ppermute x7, waiting for transfers between devices, shards(): returned.append(lax.ppermute(outgoing[k], 'tg', ring))  2.38 us
    pallas_call x1, Pallas kernels, shards(): pl.pallas_call(functools.partial(map_kernel, extent, sticks), out_shape=(...  2.3 us
    ppermute x3, starting transfers between devices, shards(): fields.append(lax.ppermute(received, 'band', pairs(bands, m)))  1.86 us
  transfers between devices with their start and end apart: 14, of which 4 were waited for; matrix products, arithmetic and copies ran while one was open for 0% of the time, Pallas kernels for 39%

profile of v13, /device:TPU:0, one launch (start us, length us, event | category | flops | bytes accessed | tf_op | source)
XLA Modules:
  0.0 58.5 jit_solution(10606337579148903912)
XLA Ops:
  0.6 2.8 %wave_to_planes.1 = (f32[8,72,128]{2,1,0:T(8,128)}, f32[192,256]{1,0:T(8,128)}, f32[192,128]{1,0:T(8,128)}, bf16[384,256]{1,0:T(8,128)(2,1)}, bf16[384,256]{1,0:...) custom-call(s32[1]{0:T(128)} %bitcast.me_ref, s32[12,128]{1,0:T(8,128)} %bitcast.17, s32[12,128]{1,0:T(8,128)} %bitcast.13, ...), custom_call_target="tpu_custom_call" | custom-call | tf_op jit(solution)/shard_map/wave_to_planes/pallas_call | solution.py:606
  3.4 7.3 %all-to-all-start = ((f32[8,72,128]{2,1,0:T(8,128)}), f32[8,72,128]{2,1,0:T(8,128)S(1)}, u32[]{:S(2)}, u32[]{:S(2)}) async-start(f32[8,72,128]{2,1,0:T(8,128)} %get-tuple-element.28), calls=%async_computation | async-start | bytes 589824 | tf_op jit(solution)/shard_map/all_to_all | solution.py:630
  10.7 0.7 %collective-permute-start.2 = (f32[192,2,128]{2,1,0:T(2,128)}, f32[192,2,128]{2,1,0:T(2,128)S(1)}, u32[]{:S(2)}, u32[]{:S(2)}) collective-permute-start(f32[192,2,128]{2,1,0:T(2,128)} %bitcast.9), channel_id=1, source_target_pairs={{0,24},{8,16},{16,8},{24,0},{1,25},{9,17},{17,9},{25,1},{2,26},{10... | collective-permute-start | bytes 589832 | tf_op jit(solution)/shard_map/ppermute | solution.py:680
  11.3 0.9 %collective-permute-start.1 = (f32[192,2,128]{2,1,0:T(2,128)}, f32[192,2,128]{2,1,0:T(2,128)S(1)}, u32[]{:S(2)}, u32[]{:S(2)}) collective-permute-start(f32[192,2,128]{2,1,0:T(2,128)} %bitcast.10), channel_id=1, source_target_pairs={{0,16},{8,24},{16,0},{24,8},{1,17},{9,25},{17,1},{25,9},{2,18},{10... | collective-permute-start | bytes 589832 | tf_op jit(solution)/shard_map/ppermute | solution.py:680
  12.3 0.3 collective-permute-start
  12.5 0.7 %copy-done.7 = s32[1536]{0:T(1024)S(1)} copy-done((s32[1536]{0:T(1024)S(1)}, s32[1536]{0:T(1024)}, u32[]{:S(2)}) %copy-start.7) | copy-done | bytes 6168
  13.2 0.7 %copy-done.8 = s32[1536]{0:T(1024)S(1)} copy-done((s32[1536]{0:T(1024)S(1)}, s32[1536]{0:T(1024)}, u32[]{:S(2)}) %copy-start.8) | copy-done | bytes 6168
  13.9 2.3 %stick_map.1 = (s32[128,128]{1,0:T(8,128)S(1)}, s32[128,128]{1,0:T(8,128)S(1)}, s32[16,128]{1,0:T(8,128)S(1)}, s32[12,128]{1,0:T(8,128)S(1)}, s32[12,128]{1,0:T(...) custom-call(s32[12,128]{1,0:T(8,128)S(1)} %bitcast.14, s32[12,128]{1,0:T(8,128)S(1)} %bitcast.16), custom_call_target="tpu_custom_call" | custom-call | flops 4000000000 | bytes 100000 | tf_op jit(solution)/shard_map/stick_map/pallas_call | solution.py:635
  16.2 0.1 pad_add_fusion.place_ref
  16.3 4.0 %all-to-all-done.recv_ref.refs_5_ = f32[8,72,128]{2,1,0:T(8,128)S(1)} async-done(((f32[8,72,128]{2,1,0:T(8,128)}), f32[8,72,128]{2,1,0:T(8,128)S(1)}, u32[]{:S(2)}, u32[]{:S(2)}) %all-to-all-start) | async-done | bytes 294944 | tf_op jit(solution)/shard_map/all_to_all | solution.py:630
  20.3 0.0 collective-permute-start.5
  20.3 1.6 %collective-permute-start.4 = (f32[8,72,128]{2,1,0:T(8,128)S(1)}, f32[8,72,128]{2,1,0:T(8,128)S(1)}, u32[]{:S(2)}, u32[]{:S(2)}) collective-permute-start(f32[8,72,128]{2,1,0:T(8,128)S(1)} %all-to-all-done.recv_ref.refs_5_), channel_id=1, source_target_pairs={{0,16},{8,24},{16,0},{24,8},{1,17},{9,25},{17,1},{25,9},{2,18},{10... | collective-permute-start | bytes 884744 | tf_op jit(solution)/shard_map/ppermute | solution.py:681
  21.8 0.0 collective-permute-done.2.refs_4_
  21.8 0.3 collective-permute-start.3
  22.2 20.3 %planes.1.refs_9_ = f32[8,80,128]{2,1,0:T(8,128)S(1)} custom-call(s32[16,128]{1,0:T(8,128)S(1)} %get-tuple-element.29.first_ref, s32[128,128]{1,0:T(8,128)S(1)} %get-tuple-element.30.even_ref, s32[128,128]{1,0:T(8,128)S(1)} %get-tuple-element.31.odd_ref, s32[12,128]{1,0:T(8,128)S(1)} %get-tuple-element.32.src_ref, s32[12,128]{1,0:T(8,128)S(1)} %get-tuple-element.33.dst_ref, ...), custom_call_target="tpu_custom_call" | custom-call | flops 20000000000 | bytes 10000000 | tf_op jit(solution)/shard_map/planes/pallas_call | solution.py:658
  42.5 0.0 collective-permute-done.1.refs_3_
  42.5 0.0 collective-permute-done.refs_2_
  42.5 0.0 collective-permute-done.5.refs_8_
  42.6 0.0 collective-permute-done.4.refs_7_
  42.6 0.0 collective-permute-done.3.refs_6_
  42.6 1.4 %inner.1 = (f32[80,128]{1,0:T(8,128)S(1)}, f32[80,128]{1,0:T(8,128)S(1)}, f32[80,128]{1,0:T(8,128)S(1)}, f32[80,128]{1,0:T(8,128)S(1)}, f32[80,128]{1,0:T(8,128)...) custom-call(s32[2]{0:T(128)S(1)} %pad_add_fusion.place_ref, f32[192,256]{1,0:T(8,128)S(1)} %copy-done, ...), custom_call_target="tpu_custom_call" | custom-call | tf_op jit(solution)/shard_map/inner/pallas_call | solution.py:685
  44.0 1.4 %collective-permute-start.6 = (f32[80,128]{1,0:T(8,128)S(1)}, f32[80,128]{1,0:T(8,128)S(1)}, u32[]{:S(2)}, u32[]{:S(2)}) collective-permute-start(f32[80,128]{1,0:T(8,128)S(1)} %get-tuple-element.37), channel_id=1, source_target_pairs={{0,1},{1,2},{2,3},{3,4},{4,5},{5,6},{6,7},{7,0},{8,9},{9,10},{10,1... | collective-permute-start | bytes 122888 | tf_op jit(solution)/shard_map/ppermute | solution.py:696
  45.5 1.7 %collective-permute-start.8 = (f32[80,128]{1,0:T(8,128)S(1)}, f32[80,128]{1,0:T(8,128)S(1)}, u32[]{:S(2)}, u32[]{:S(2)}) collective-permute-start(f32[80,128]{1,0:T(8,128)S(1)} %get-tuple-element.39), channel_id=1, source_target_pairs={{0,3},{1,4},{2,5},{3,6},{4,7},{5,0},{6,1},{7,2},{8,11},{9,12},{10,... | collective-permute-start | bytes 122888 | tf_op jit(solution)/shard_map/ppermute | solution.py:696
  47.2 3.2 %collective-permute-start.9 = (f32[80,128]{1,0:T(8,128)S(1)}, f32[80,128]{1,0:T(8,128)S(1)}, u32[]{:S(2)}, u32[]{:S(2)}) collective-permute-start(f32[80,128]{1,0:T(8,128)S(1)} %get-tuple-element.40), channel_id=1, source_target_pairs={{0,4},{1,5},{2,6},{3,7},{4,0},{5,1},{6,2},{7,3},{8,12},{9,13},{10,... | collective-permute-start | bytes 122888 | tf_op jit(solution)/shard_map/ppermute | solution.py:696
  50.4 0.9 %collective-permute-start.10 = (f32[80,128]{1,0:T(8,128)S(1)}, f32[80,128]{1,0:T(8,128)S(1)}, u32[]{:S(2)}, u32[]{:S(2)}) collective-permute-start(f32[80,128]{1,0:T(8,128)S(1)} %get-tuple-element.41), channel_id=1, source_target_pairs={{0,5},{1,6},{2,7},{3,0},{4,1},{5,2},{6,3},{7,4},{8,13},{9,14},{10,... | collective-permute-start | bytes 122888 | tf_op jit(solution)/shard_map/ppermute | solution.py:696
  51.3 1.8 %collective-permute-start.11 = (f32[80,128]{1,0:T(8,128)S(1)}, f32[80,128]{1,0:T(8,128)S(1)}, u32[]{:S(2)}, u32[]{:S(2)}) collective-permute-start(f32[80,128]{1,0:T(8,128)S(1)} %get-tuple-element.42), channel_id=1, source_target_pairs={{0,6},{1,7},{2,0},{3,1},{4,2},{5,3},{6,4},{7,5},{8,14},{9,15},{10,... | collective-permute-start | bytes 122888 | tf_op jit(solution)/shard_map/ppermute | solution.py:696
  53.1 0.0 collective-permute-done.7.refs_2_
  53.1 1.6 %collective-permute-start.12 = (f32[80,128]{1,0:T(8,128)S(1)}, f32[80,128]{1,0:T(8,128)S(1)}, u32[]{:S(2)}, u32[]{:S(2)}) collective-permute-start(f32[80,128]{1,0:T(8,128)S(1)} %get-tuple-element.43), channel_id=1, source_target_pairs={{0,7},{1,0},{2,1},{3,2},{4,3},{5,4},{6,5},{7,6},{8,15},{9,8},{10,9... | collective-permute-start | bytes 122888 | tf_op jit(solution)/shard_map/ppermute | solution.py:696
  54.8 0.7 %collective-permute-done.10.refs_5_ = f32[80,128]{1,0:T(8,128)S(1)} collective-permute-done((f32[80,128]{1,0:T(8,128)S(1)}, f32[80,128]{1,0:T(8,128)S(1)}, u32[]{:S(2)}, u32[]{:S(2)}) %collective-permute-start.10) | collective-permute-done | bytes 40992 | tf_op jit(solution)/shard_map/ppermute | solution.py:696
  55.5 0.5 collective-permute-done.11.refs_6_
  56.0 1.2 %collective-permute-done.12.refs_7_ = f32[80,128]{1,0:T(8,128)S(1)} collective-permute-done((f32[80,128]{1,0:T(8,128)S(1)}, f32[80,128]{1,0:T(8,128)S(1)}, u32[]{:S(2)}, u32[]{:S(2)}) %collective-permute-start.12) | collective-permute-done | bytes 40992 | tf_op jit(solution)/shard_map/ppermute | solution.py:696
  57.2 1.3 %planes_to_wave.1 = (f32[192,2,128]{2,1,0:T(2,128)}, f32[2,1,4]{2,1,0:T(1,128)}) custom-call(s32[1]{0:T(128)} %bitcast.me_ref, f32[192,128]{1,0:T(8,128)S(1)} %copy-done.6, f32[80,128]{1,0:T(8,128)S(1)} %get-tuple-element.36.refs_0_, f32[80,128]{1,0:T(8,128)S(1)} %collective-permute-done.6.refs_1_, f32[80,128]{1,0:T(8,128)S(1)} %collective-permute-done.7.refs_2_, ...), custom_call_target="tpu_custom_call" | custom-call | tf_op jit(solution)/shard_map/planes_to_wave/pallas_call | solution.py:697
  (20 shorter events, 0.0 us)
Async XLA Ops:
  3.4 16.9 %all-to-all-start = ((f32[8,72,128]{2,1,0:T(8,128)}), f32[8,72,128]{2,1,0:T(8,128)S(1)}, u32[]{:S(2)}, u32[]{:S(2)}) async-start(f32[8,72,128]{2,1,0:T(8,128)} %get-tuple-element.28), calls=%async_computation | async-start | bytes 589824 | tf_op jit(solution)/shard_map/all_to_all | solution.py:630
  10.7 11.2 %collective-permute-start.2 = (f32[192,2,128]{2,1,0:T(2,128)}, f32[192,2,128]{2,1,0:T(2,128)S(1)}, u32[]{:S(2)}, u32[]{:S(2)}) collective-permute-start(f32[192,2,128]{2,1,0:T(2,128)} %bitcast.9), channel_id=1, source_target_pairs={{0,24},{8,16},{16,8},{24,0},{1,25},{9,17},{17,9},{25,1},{2,26},{10... | collective-permute-start | bytes 589832 | tf_op jit(solution)/shard_map/ppermute | solution.py:680
  11.3 31.2 %collective-permute-start.1 = (f32[192,2,128]{2,1,0:T(2,128)}, f32[192,2,128]{2,1,0:T(2,128)S(1)}, u32[]{:S(2)}, u32[]{:S(2)}) collective-permute-start(f32[192,2,128]{2,1,0:T(2,128)} %bitcast.10), channel_id=1, source_target_pairs={{0,16},{8,24},{16,0},{24,8},{1,17},{9,25},{17,1},{25,9},{2,18},{10... | collective-permute-start | bytes 589832 | tf_op jit(solution)/shard_map/ppermute | solution.py:680
  12.3 30.3 %collective-permute-start = (f32[192,2,128]{2,1,0:T(2,128)}, f32[192,2,128]{2,1,0:T(2,128)S(1)}, u32[]{:S(2)}, u32[]{:S(2)}) collective-permute-start(f32[192,2,128]{2,1,0:T(2,128)} %bitcast.11), channel_id=1, source_target_pairs={{0,8},{8,0},{16,24},{24,16},{1,9},{9,1},{17,25},{25,17},{2,10},{10... | collective-permute-start | bytes 589832 | tf_op jit(solution)/shard_map/ppermute | solution.py:680
  12.5 0.7 %copy-start.7 = (s32[1536]{0:T(1024)S(1)}, s32[1536]{0:T(1024)}, u32[]{:S(2)}) copy-start(s32[1536]{0:T(1024)} %param.9) | copy-start | bytes 18436
  13.2 0.7 %copy-start.8 = (s32[1536]{0:T(1024)S(1)}, s32[1536]{0:T(1024)}, u32[]{:S(2)}) copy-start(s32[1536]{0:T(1024)} %param.8) | copy-start | bytes 18436
  20.3 22.3 %collective-permute-start.5 = (f32[8,72,128]{2,1,0:T(8,128)S(1)}, f32[8,72,128]{2,1,0:T(8,128)S(1)}, u32[]{:S(2)}, u32[]{:S(2)}) collective-permute-start(f32[8,72,128]{2,1,0:T(8,128)S(1)} %all-to-all-done.recv_ref.refs_5_), channel_id=1, source_target_pairs={{0,24},{8,16},{16,8},{24,0},{1,25},{9,17},{17,9},{25,1},{2,26},{10... | collective-permute-start | bytes 884744 | tf_op jit(solution)/shard_map/ppermute | solution.py:681
  20.3 22.3 %collective-permute-start.4 = (f32[8,72,128]{2,1,0:T(8,128)S(1)}, f32[8,72,128]{2,1,0:T(8,128)S(1)}, u32[]{:S(2)}, u32[]{:S(2)}) collective-permute-start(f32[8,72,128]{2,1,0:T(8,128)S(1)} %all-to-all-done.recv_ref.refs_5_), channel_id=1, source_target_pairs={{0,16},{8,24},{16,0},{24,8},{1,17},{9,25},{17,1},{25,9},{2,18},{10... | collective-permute-start | bytes 884744 | tf_op jit(solution)/shard_map/ppermute | solution.py:681
  21.8 20.7 %collective-permute-start.3 = (f32[8,72,128]{2,1,0:T(8,128)S(1)}, f32[8,72,128]{2,1,0:T(8,128)S(1)}, u32[]{:S(2)}, u32[]{:S(2)}) collective-permute-start(f32[8,72,128]{2,1,0:T(8,128)S(1)} %all-to-all-done.recv_ref.refs_5_), channel_id=1, source_target_pairs={{0,8},{8,0},{16,24},{24,16},{1,9},{9,1},{17,25},{25,17},{2,10},{10... | collective-permute-start | bytes 884744 | tf_op jit(solution)/shard_map/ppermute | solution.py:681
  22.1 20.4 %copy-start = (f32[192,256]{1,0:T(8,128)S(1)}, f32[192,256]{1,0:T(8,128)}, u32[]{:S(2)}) copy-start(f32[192,256]{1,0:T(8,128)} %get-tuple-element.27.refs_0_.refs_8_) | copy-start | bytes 589828
  22.1 20.4 %copy-start.1 = (f32[1,192,2,128]{3,2,1,0:T(2,128)S(1)}, f32[1,192,2,128]{3,2,1,0:T(2,128)}, u32[]{:S(2)}) copy-start(f32[1,192,2,128]{3,2,1,0:T(2,128)} %param.7) | copy-start | bytes 589828
  22.1 35.0 %copy-start.2 = (bf16[384,256]{1,0:T(8,128)(2,1)S(1)}, bf16[384,256]{1,0:T(8,128)(2,1)}, u32[]{:S(2)}) copy-start(bf16[384,256]{1,0:T(8,128)(2,1)} %get-tuple-element.44.refs_9_) | copy-start | bytes 589828
  22.2 35.0 %copy-start.3 = (bf16[384,256]{1,0:T(8,128)(2,1)S(1)}, bf16[384,256]{1,0:T(8,128)(2,1)}, u32[]{:S(2)}) copy-start(bf16[384,256]{1,0:T(8,128)(2,1)} %get-tuple-element.45.refs_10_) | copy-start | bytes 589828
  22.2 35.0 %copy-start.4 = (f32[192,192]{1,0:T(8,128)S(1)}, f32[192,192]{1,0:T(8,128)}, u32[]{:S(2)}) copy-start(f32[192,192]{1,0:T(8,128)} %get-tuple-element.46.refs_11_) | copy-start | bytes 442372
  22.2 35.0 %copy-start.5 = (f32[192,192]{1,0:T(8,128)S(1)}, f32[192,192]{1,0:T(8,128)}, u32[]{:S(2)}) copy-start(f32[192,192]{1,0:T(8,128)} %get-tuple-element.47.refs_12_) | copy-start | bytes 442372
  22.2 35.0 %copy-start.6 = (f32[192,128]{1,0:T(8,128)S(1)}, f32[192,128]{1,0:T(8,128)}, u32[]{:S(2)}) copy-start(f32[192,128]{1,0:T(8,128)} %get-tuple-element.26.len_ref) | copy-start | bytes 294916
  44.0 7.3 %collective-permute-start.6 = (f32[80,128]{1,0:T(8,128)S(1)}, f32[80,128]{1,0:T(8,128)S(1)}, u32[]{:S(2)}, u32[]{:S(2)}) collective-permute-start(f32[80,128]{1,0:T(8,128)S(1)} %get-tuple-element.37), channel_id=1, source_target_pairs={{0,1},{1,2},{2,3},{3,4},{4,5},{5,6},{6,7},{7,0},{8,9},{9,10},{10,1... | collective-permute-start | bytes 122888 | tf_op jit(solution)/shard_map/ppermute | solution.py:696
  45.5 7.7 %collective-permute-start.7 = (f32[80,128]{1,0:T(8,128)S(1)}, f32[80,128]{1,0:T(8,128)S(1)}, u32[]{:S(2)}, u32[]{:S(2)}) collective-permute-start(f32[80,128]{1,0:T(8,128)S(1)} %get-tuple-element.38), channel_id=1, source_target_pairs={{0,2},{1,3},{2,4},{3,5},{4,6},{5,7},{6,0},{7,1},{8,10},{9,11},{10,... | collective-permute-start | bytes 122888 | tf_op jit(solution)/shard_map/ppermute | solution.py:696
  45.5 9.3 %collective-permute-start.8 = (f32[80,128]{1,0:T(8,128)S(1)}, f32[80,128]{1,0:T(8,128)S(1)}, u32[]{:S(2)}, u32[]{:S(2)}) collective-permute-start(f32[80,128]{1,0:T(8,128)S(1)} %get-tuple-element.39), channel_id=1, source_target_pairs={{0,3},{1,4},{2,5},{3,6},{4,7},{5,0},{6,1},{7,2},{8,11},{9,12},{10,... | collective-permute-start | bytes 122888 | tf_op jit(solution)/shard_map/ppermute | solution.py:696
  47.2 7.5 %collective-permute-start.9 = (f32[80,128]{1,0:T(8,128)S(1)}, f32[80,128]{1,0:T(8,128)S(1)}, u32[]{:S(2)}, u32[]{:S(2)}) collective-permute-start(f32[80,128]{1,0:T(8,128)S(1)} %get-tuple-element.40), channel_id=1, source_target_pairs={{0,4},{1,5},{2,6},{3,7},{4,0},{5,1},{6,2},{7,3},{8,12},{9,13},{10,... | collective-permute-start | bytes 122888 | tf_op jit(solution)/shard_map/ppermute | solution.py:696
  50.4 5.1 %collective-permute-start.10 = (f32[80,128]{1,0:T(8,128)S(1)}, f32[80,128]{1,0:T(8,128)S(1)}, u32[]{:S(2)}, u32[]{:S(2)}) collective-permute-start(f32[80,128]{1,0:T(8,128)S(1)} %get-tuple-element.41), channel_id=1, source_target_pairs={{0,5},{1,6},{2,7},{3,0},{4,1},{5,2},{6,3},{7,4},{8,13},{9,14},{10,... | collective-permute-start | bytes 122888 | tf_op jit(solution)/shard_map/ppermute | solution.py:696
  51.3 4.7 %collective-permute-start.11 = (f32[80,128]{1,0:T(8,128)S(1)}, f32[80,128]{1,0:T(8,128)S(1)}, u32[]{:S(2)}, u32[]{:S(2)}) collective-permute-start(f32[80,128]{1,0:T(8,128)S(1)} %get-tuple-element.42), channel_id=1, source_target_pairs={{0,6},{1,7},{2,0},{3,1},{4,2},{5,3},{6,4},{7,5},{8,14},{9,15},{10,... | collective-permute-start | bytes 122888 | tf_op jit(solution)/shard_map/ppermute | solution.py:696
  53.1 4.0 %collective-permute-start.12 = (f32[80,128]{1,0:T(8,128)S(1)}, f32[80,128]{1,0:T(8,128)S(1)}, u32[]{:S(2)}, u32[]{:S(2)}) collective-permute-start(f32[80,128]{1,0:T(8,128)S(1)} %get-tuple-element.43), channel_id=1, source_target_pairs={{0,7},{1,0},{2,1},{3,2},{4,3},{5,4},{6,5},{7,6},{8,15},{9,8},{10,9... | collective-permute-start | bytes 122888 | tf_op jit(solution)/shard_map/ppermute | solution.py:696

commit v14 on v13

--- a/solution.py
+++ b/solution.py
@@ -129,7 +129,7 @@
 
 def wave_kernel(
     extent, me_ref, length_hbm, row_hbm, col_hbm, plane_hbm, coef_hbm,
-    out_ref, kc_ref, len_ref, whi_ref, wlo_ref, sc_ref, ss_ref,
+    out_ref, kc_ref, wave_ref, len_ref, whi_ref, wlo_ref, sc_ref, ss_ref,
     length_ref, row_ref, col_ref, plane_ref, coef_ref, sems,
 ):
     copies = fetch_all(
@@ -197,6 +197,8 @@
     kinetic = (square + (position - middle) * (position - middle)) * (1.0 / (RADIUS * RADIUS))
     wave = jnp.concatenate([coef_ref[:, 0, :] * kept, coef_ref[:, 1, :] * kept], axis=1)
     kc_ref[...] = wave * jnp.concatenate([kinetic, kinetic], axis=1)
+    wave_ref[:sticks, :] = wave[:, :padded]
+    wave_ref[sticks:, :] = wave[:, padded:]
     raw = dot3(table, split(wave), ((1,), (1,)))
     for d in range(devices):
         at = 2 * d * padded_planes
@@ -315,6 +317,13 @@
             ref[2 * w + 1:2 * w + 2, :] = (jnp.where(is_left, turned, line) + add)[0:1]
     row_ref[2 * windows:2 * windows + 1, :] = jnp.full((1, LANES), -1, jnp.int32)
     col_ref[2 * windows:2 * windows + 1, :] = jnp.zeros((1, LANES), jnp.int32)
+
+
+def join_kernel(recv_ref, wave_ref, out_ref):
+    devices, block, _ = recv_ref.shape
+    for d in range(devices):
+        out_ref[d * block:(d + 1) * block, :] = recv_ref[d]
+    out_ref[devices * block:, :] = wave_ref[...]
 
 
 def lane_take(x, index):
@@ -495,14 +504,15 @@
 
 def inner_kernel(bands, volume, norm, place_ref, *refs):
     kc_ref = refs[0]
-    coefs = refs[1:1 + bands]
-    fields = refs[1 + bands:1 + 2 * bands]
-    in_ref = refs[1 + 2 * bands]
-    out_refs = refs[2 + 2 * bands:]
+    joint = refs[1:1 + bands]
+    in_ref = refs[1 + bands]
+    out_refs = refs[2 + bands:]
     devices = in_ref.shape[0]
     padded_planes = (in_ref.shape[1] - 8) // 3
     half = LANES // 2
-    padded = coefs[0].shape[2]
+    sticks, padded = kc_ref.shape[0], kc_ref.shape[1] // 2
+    block = 3 * padded_planes
+    at = devices * block
     me, mine = place_ref[0], place_ref[1]
     low = lax.broadcasted_iota(jnp.int32, (padded_planes, LANES), 1) < half
 
@@ -517,7 +527,7 @@
     kc_re, kc_im = kc[:, :padded], kc[:, padded:]
     sums = []
     for m in range(bands):
-        c_re, c_im = coefs[m][:, 0, :], coefs[m][:, 1, :]
+        c_re, c_im = joint[m][at:at + sticks, :], joint[m][at + sticks:, :]
         sums.append([fold(c_re * kc_re + c_im * kc_im), fold(c_re * kc_im - c_im * kc_re)])
     local = [[jnp.zeros((8, LANES), F32), jnp.zeros((8, LANES), F32)] for _ in range(bands)]
     for d in range(devices):
@@ -526,18 +536,18 @@
         turned = pltpu.roll(rest, half, 1)
         other = jnp.concatenate([im, -re, jnp.where(low, turned, -turned)], axis=0)
         for m in range(bands):
-            col = fields[m][d, 0:3 * padded_planes, :]
+            col = joint[m][d * block:(d + 1) * block, :]
             local[m][0] = local[m][0] + fold(col * value)
             local[m][1] = local[m][1] + fold(col * other)
     lane = lax.broadcasted_iota(jnp.int32, (8, LANES), 1)
     row = lax.broadcasted_iota(jnp.int32, (8, LANES), 0)
     tile = jnp.zeros((8, LANES), F32)
     for m in range(bands):
-        at = me ^ m
+        spot = me ^ m
         for part, sign in ((0, 1.0), (1, -1.0)):
             partial = sums[m][part] + volume * local[m][part]
             scalar = jnp.sum(jnp.sum(partial, axis=1, keepdims=True), axis=0, keepdims=True)
-            tile = jnp.where((lane == at) & (row == part), sign * norm * scalar, tile)
+            tile = jnp.where((lane == spot) & (row == part), sign * norm * scalar, tile)
     for k in range(devices):
         out_refs[k][0:3 * padded_planes, :] = in_ref[lax.rem(mine + k, devices), 0:3 * padded_planes, :]
         out_refs[k][3 * padded_planes:, :] = tile
@@ -603,11 +613,12 @@
 
     block = 3 * padded_planes
     total_planes = devices * padded_planes
-    sent, kc, lengths, whi, wlo, shift_cos, shift_sin = pl.pallas_call(
+    sent, kc, wave, lengths, whi, wlo, shift_cos, shift_sin = pl.pallas_call(
         functools.partial(wave_kernel, extent),
         out_shape=(
             jax.ShapeDtypeStruct((devices, block, LANES), F32),
             jax.ShapeDtypeStruct((sticks, 2 * padded), F32),
+            jax.ShapeDtypeStruct((2 * sticks, padded), F32),
             jax.ShapeDtypeStruct((sticks, LANES), F32),
             jax.ShapeDtypeStruct((2 * total_planes, 2 * padded), BF16),
             jax.ShapeDtypeStruct((2 * total_planes, 2 * padded), BF16),
@@ -675,20 +686,24 @@
         name="planes",
     )(first, even_map, odd_map, source, target, row_w, col_w, received, constants, potential)
 
-    coefs, fields = [coef], [received]
-    for m in range(1, bands):
-        coefs.append(lax.ppermute(coef, "band", pairs(bands, m)))
-        fields.append(lax.ppermute(received, "band", pairs(bands, m)))
+    own = pl.pallas_call(
+        join_kernel,
+        out_shape=jax.ShapeDtypeStruct((devices * block + 2 * sticks, LANES), F32),
+        in_specs=[vmem] * 2,
+        compiler_params=params(4),
+        name="join",
+    )(received, wave)
+    joint = [own] + [lax.ppermute(own, "band", pairs(bands, m)) for m in range(1, bands)]
     band = lax.axis_index("band").astype(jnp.int32)
     norm = 1.0 / (total_sticks * padded)
     places = jnp.stack([band, me])
     outgoing = pl.pallas_call(
         functools.partial(inner_kernel, bands, volume, norm),
         out_shape=(jax.ShapeDtypeStruct((block + 8, LANES), F32),) * devices,
-        in_specs=[smem] + [vmem] * (2 + 2 * bands),
+        in_specs=[smem] + [vmem] * (2 + bands),
         compiler_params=params(6 + 1.5 * bands),
         name="inner",
-    )(places, kc, *coefs, *fields, weighted)
+    )(places, kc, *joint, weighted)
 
     returned = [outgoing[0]]
     for k in range(1, devices):

time: 58.8 us -> 60.3 us (1.026)
  waiting for transfers between devices: 6.37 us -> 10 us
  starting transfers between devices: 21.7 us -> 19.9 us
    all_to_all x1, waiting for transfers between devices: 3.97 us -> 5.84 us  [shards(): lax.all_to_all(sent, 'tg', split_axis=0, concat_axis=0, tiled=True)]
    ppermute x6 -> x3, waiting for transfers between devices: 0.02 us -> 1.83 us  [shards(): lax.ppermute(own, 'band', pairs(bands, m))]
    ppermute x6 -> x3, starting transfers between devices: 3.72 us -> 1.92 us  [shards(): lax.ppermute(own, 'band', pairs(bands, m))]
  transfers between devices with their start and end apart: 14 -> 11, of which waited for: 4 -> 5; matrix products, arithmetic and copies ran while one was open for 0% -> 0% of each run, Pallas kernels for 39% -> 38%
where the time goes in v14:
time: 60.3 us; the launch traced here: 59.9 us
  Pallas kernels  27.7 us (46%)
  starting transfers between devices  19.9 us (33%)
  waiting for transfers between devices  10 us (17%)
  local copies, waits for them, and re-layouts  1.42 us (2%)
  between operations  0.73 us (1%)
    pallas_call x1, Pallas kernels, shards(): pl.pallas_call(functools.partial(plane_kernel, planes), out_shape=jax.Sha...  20.3 us
    ppermute x7, starting transfers between devices, shards(): returned.append(lax.ppermute(outgoing[k], 'tg', ring))  10.7 us
    all_to_all x1, starting transfers between devices, shards(): lax.all_to_all(sent, 'tg', split_axis=0, concat_axis=0, tiled=True)  7.26 us
    all_to_all x1, waiting for transfers between devices, shards(): lax.all_to_all(sent, 'tg', split_axis=0, concat_axis=0, tiled=True)  5.84 us
    pallas_call x1, Pallas kernels, shards(): pl.pallas_call(functools.partial(wave_kernel, extent), out_shape=(jax.Sha...  2.76 us
    ppermute x7, waiting for transfers between devices, shards(): returned.append(lax.ppermute(outgoing[k], 'tg', ring))  2.38 us
    pallas_call x1, Pallas kernels, shards(): pl.pallas_call(functools.partial(map_kernel, extent, sticks), out_shape=(...  2.3 us
    ppermute x3, starting transfers between devices, shards(): lax.ppermute(own, 'band', pairs(bands, m))  1.92 us
  transfers between devices with their start and end apart: 11, of which 5 were waited for; matrix products, arithmetic and copies ran while one was open for 0% of the time, Pallas kernels for 38%

profile of v14, /device:TPU:0, one launch (start us, length us, event | category | flops | bytes accessed | tf_op | source)
XLA Modules:
  0.0 59.9 jit_solution(12434268565554840988)
XLA Ops:
  0.6 2.8 %wave_to_planes.1 = (f32[8,72,128]{2,1,0:T(8,128)}, f32[192,256]{1,0:T(8,128)}, f32[384,128]{1,0:T(8,128)}, f32[192,128]{1,0:T(8,128)}, bf16[384,256]{1,0:T(8,12...) custom-call(s32[1]{0:T(128)} %bitcast.me_ref, s32[12,128]{1,0:T(8,128)} %bitcast.13, ...), custom_call_target="tpu_custom_call" | custom-call | tf_op jit(solution)/shard_map/wave_to_planes/pallas_call | solution.py:616
  3.4 7.3 %all-to-all-start = ((f32[8,72,128]{2,1,0:T(8,128)}), f32[8,72,128]{2,1,0:T(8,128)S(1)}, u32[]{:S(2)}, u32[]{:S(2)}) async-start(f32[8,72,128]{2,1,0:T(8,128)} %get-tuple-element.29), calls=%async_computation | async-start | bytes 589824 | tf_op jit(solution)/shard_map/all_to_all | solution.py:641
  10.7 0.1 pad_add_fusion.place_ref
  10.7 0.7 %copy-done.7 = s32[1536]{0:T(1024)S(1)} copy-done((s32[1536]{0:T(1024)S(1)}, s32[1536]{0:T(1024)}, u32[]{:S(2)}) %copy-start.7) | copy-done | bytes 6168
  11.4 0.7 %copy-done.8 = s32[1536]{0:T(1024)S(1)} copy-done((s32[1536]{0:T(1024)S(1)}, s32[1536]{0:T(1024)}, u32[]{:S(2)}) %copy-start.8) | copy-done | bytes 6168
  12.1 2.3 %stick_map.1 = (s32[128,128]{1,0:T(8,128)S(1)}, s32[128,128]{1,0:T(8,128)S(1)}, s32[16,128]{1,0:T(8,128)S(1)}, s32[12,128]{1,0:T(8,128)S(1)}, s32[12,128]{1,0:T(...) custom-call(s32[12,128]{1,0:T(8,128)S(1)} %bitcast.9, s32[12,128]{1,0:T(8,128)S(1)} %bitcast.11), custom_call_target="tpu_custom_call" | custom-call | flops 4000000000 | bytes 100000 | tf_op jit(solution)/shard_map/stick_map/pallas_call | solution.py:646
  14.4 5.8 %all-to-all-done.recv_ref = f32[8,72,128]{2,1,0:T(8,128)S(1)} async-done(((f32[8,72,128]{2,1,0:T(8,128)}), f32[8,72,128]{2,1,0:T(8,128)S(1)}, u32[]{:S(2)}, u32[]{:S(2)}) %all-to-all-start) | async-done | bytes 294944 | tf_op jit(solution)/shard_map/all_to_all | solution.py:641
  20.3 0.1 collective-permute-start.2
  20.4 1.6 %collective-permute-start.1 = (f32[960,128]{1,0:T(8,128)S(1)}, f32[960,128]{1,0:T(8,128)S(1)}, u32[]{:S(2)}, u32[]{:S(2)}) collective-permute-start(f32[960,128]{1,0:T(8,128)S(1)} %join.1.refs_1_), channel_id=1, source_target_pairs={{0,16},{8,24},{16,0},{24,8},{1,17},{9,25},{17,1},{25,9},{2,18},{10... | collective-permute-start | bytes 1474568 | tf_op jit(solution)/shard_map/ppermute | solution.py:696
  22.0 0.3 collective-permute-start
  22.3 0.0 copy-start.4
  22.3 0.0 copy-start.6
  22.3 20.3 %planes.1.refs_5_ = f32[8,80,128]{2,1,0:T(8,128)S(1)} custom-call(s32[16,128]{1,0:T(8,128)S(1)} %get-tuple-element.31.first_ref, s32[128,128]{1,0:T(8,128)S(1)} %get-tuple-element.32.even_ref, s32[128,128]{1,0:T(8,128)S(1)} %get-tuple-element.33.odd_ref, s32[12,128]{1,0:T(8,128)S(1)} %get-tuple-element.34.src_ref, s32[12,128]{1,0:T(8,128)S(1)} %get-tuple-element.35.dst_ref, ...), custom_call_target="tpu_custom_call" | custom-call | flops 20000000000 | bytes 10000000 | tf_op jit(solution)/shard_map/planes/pallas_call | solution.py:669
  42.6 0.0 collective-permute-done.2.refs_4_
  42.6 1.8 %collective-permute-done.1.refs_3_ = f32[960,128]{1,0:T(8,128)S(1)} collective-permute-done((f32[960,128]{1,0:T(8,128)S(1)}, f32[960,128]{1,0:T(8,128)S(1)}, u32[]{:S(2)}, u32[]{:S(2)}) %collective-permute-start.1) | collective-permute-done | bytes 491552 | tf_op jit(solution)/shard_map/ppermute | solution.py:696
  44.4 0.0 collective-permute-done.refs_2_
  44.5 1.0 %inner.1 = (f32[80,128]{1,0:T(8,128)S(1)}, f32[80,128]{1,0:T(8,128)S(1)}, f32[80,128]{1,0:T(8,128)S(1)}, f32[80,128]{1,0:T(8,128)S(1)}, f32[80,128]{1,0:T(8,128)...) custom-call(s32[2]{0:T(128)S(1)} %pad_add_fusion.place_ref, f32[192,256]{1,0:T(8,128)S(1)} %copy-done, ...), custom_call_target="tpu_custom_call" | custom-call | tf_op jit(solution)/shard_map/inner/pallas_call | solution.py:700
  45.4 1.5 %collective-permute-start.3 = (f32[80,128]{1,0:T(8,128)S(1)}, f32[80,128]{1,0:T(8,128)S(1)}, u32[]{:S(2)}, u32[]{:S(2)}) collective-permute-start(f32[80,128]{1,0:T(8,128)S(1)} %get-tuple-element.39), channel_id=1, source_target_pairs={{0,1},{1,2},{2,3},{3,4},{4,5},{5,6},{6,7},{7,0},{8,9},{9,10},{10,1... | collective-permute-start | bytes 122888 | tf_op jit(solution)/shard_map/ppermute | solution.py:711
  46.9 0.0 collective-permute-start.4
  46.9 1.7 %collective-permute-start.5 = (f32[80,128]{1,0:T(8,128)S(1)}, f32[80,128]{1,0:T(8,128)S(1)}, u32[]{:S(2)}, u32[]{:S(2)}) collective-permute-start(f32[80,128]{1,0:T(8,128)S(1)} %get-tuple-element.41), channel_id=1, source_target_pairs={{0,3},{1,4},{2,5},{3,6},{4,7},{5,0},{6,1},{7,2},{8,11},{9,12},{10,... | collective-permute-start | bytes 122888 | tf_op jit(solution)/shard_map/ppermute | solution.py:711
  48.7 3.1 %collective-permute-start.6 = (f32[80,128]{1,0:T(8,128)S(1)}, f32[80,128]{1,0:T(8,128)S(1)}, u32[]{:S(2)}, u32[]{:S(2)}) collective-permute-start(f32[80,128]{1,0:T(8,128)S(1)} %get-tuple-element.42), channel_id=1, source_target_pairs={{0,4},{1,5},{2,6},{3,7},{4,0},{5,1},{6,2},{7,3},{8,12},{9,13},{10,... | collective-permute-start | bytes 122888 | tf_op jit(solution)/shard_map/ppermute | solution.py:711
  51.8 1.0 %collective-permute-start.7 = (f32[80,128]{1,0:T(8,128)S(1)}, f32[80,128]{1,0:T(8,128)S(1)}, u32[]{:S(2)}, u32[]{:S(2)}) collective-permute-start(f32[80,128]{1,0:T(8,128)S(1)} %get-tuple-element.43), channel_id=1, source_target_pairs={{0,5},{1,6},{2,7},{3,0},{4,1},{5,2},{6,3},{7,4},{8,13},{9,14},{10,... | collective-permute-start | bytes 122888 | tf_op jit(solution)/shard_map/ppermute | solution.py:711
  52.8 0.0 collective-permute-done.3.refs_1_
  52.8 1.8 %collective-permute-start.8 = (f32[80,128]{1,0:T(8,128)S(1)}, f32[80,128]{1,0:T(8,128)S(1)}, u32[]{:S(2)}, u32[]{:S(2)}) collective-permute-start(f32[80,128]{1,0:T(8,128)S(1)} %get-tuple-element.44), channel_id=1, source_target_pairs={{0,6},{1,7},{2,0},{3,1},{4,2},{5,3},{6,4},{7,5},{8,14},{9,15},{10,... | collective-permute-start | bytes 122888 | tf_op jit(solution)/shard_map/ppermute | solution.py:711
  54.6 0.0 collective-permute-done.4.refs_2_
  54.6 1.6 %collective-permute-start.9 = (f32[80,128]{1,0:T(8,128)S(1)}, f32[80,128]{1,0:T(8,128)S(1)}, u32[]{:S(2)}, u32[]{:S(2)}) collective-permute-start(f32[80,128]{1,0:T(8,128)S(1)} %get-tuple-element.45), channel_id=1, source_target_pairs={{0,7},{1,0},{2,1},{3,2},{4,3},{5,4},{6,5},{7,6},{8,15},{9,8},{10,9... | collective-permute-start | bytes 122888 | tf_op jit(solution)/shard_map/ppermute | solution.py:711
  56.2 0.0 collective-permute-done.5.refs_3_
  56.2 0.0 collective-permute-done.6.refs_4_
  56.2 0.6 collective-permute-done.7.refs_5_
  56.8 0.6 %collective-permute-done.8.refs_6_ = f32[80,128]{1,0:T(8,128)S(1)} collective-permute-done((f32[80,128]{1,0:T(8,128)S(1)}, f32[80,128]{1,0:T(8,128)S(1)}, u32[]{:S(2)}, u32[]{:S(2)}) %collective-permute-start.8) | collective-permute-done | bytes 40992 | tf_op jit(solution)/shard_map/ppermute | solution.py:711
  57.4 1.2 %collective-permute-done.9.refs_7_ = f32[80,128]{1,0:T(8,128)S(1)} collective-permute-done((f32[80,128]{1,0:T(8,128)S(1)}, f32[80,128]{1,0:T(8,128)S(1)}, u32[]{:S(2)}, u32[]{:S(2)}) %collective-permute-start.9) | collective-permute-done | bytes 40992 | tf_op jit(solution)/shard_map/ppermute | solution.py:711
  58.6 1.3 %planes_to_wave.1 = (f32[192,2,128]{2,1,0:T(2,128)}, f32[2,1,4]{2,1,0:T(1,128)}) custom-call(s32[1]{0:T(128)} %bitcast.me_ref, f32[192,128]{1,0:T(8,128)S(1)} %copy-done.6, f32[80,128]{1,0:T(8,128)S(1)} %get-tuple-element.38.refs_0_, f32[80,128]{1,0:T(8,128)S(1)} %collective-permute-done.3.refs_1_, f32[80,128]{1,0:T(8,128)S(1)} %collective-permute-done.4.refs_2_, ...), custom_call_target="tpu_custom_call" | custom-call | tf_op jit(solution)/shard_map/planes_to_wave/pallas_call | solution.py:712
  (15 shorter events, 0.1 us)
Async XLA Ops:
  3.4 16.9 %all-to-all-start = ((f32[8,72,128]{2,1,0:T(8,128)}), f32[8,72,128]{2,1,0:T(8,128)S(1)}, u32[]{:S(2)}, u32[]{:S(2)}) async-start(f32[8,72,128]{2,1,0:T(8,128)} %get-tuple-element.29), calls=%async_computation | async-start | bytes 589824 | tf_op jit(solution)/shard_map/all_to_all | solution.py:641
  10.7 0.7 %copy-start.7 = (s32[1536]{0:T(1024)S(1)}, s32[1536]{0:T(1024)}, u32[]{:S(2)}) copy-start(s32[1536]{0:T(1024)} %param.9) | copy-start | bytes 18436
  11.4 0.7 %copy-start.8 = (s32[1536]{0:T(1024)S(1)}, s32[1536]{0:T(1024)}, u32[]{:S(2)}) copy-start(s32[1536]{0:T(1024)} %param.8) | copy-start | bytes 18436
  12.1 8.2 %copy-start.5 = (f32[384,128]{1,0:T(8,128)S(1)}, f32[384,128]{1,0:T(8,128)}, u32[]{:S(2)}) copy-start(f32[384,128]{1,0:T(8,128)} %get-tuple-element.30.wave_ref) | copy-start | bytes 589828
  20.3 22.3 %collective-permute-start.2 = (f32[960,128]{1,0:T(8,128)S(1)}, f32[960,128]{1,0:T(8,128)S(1)}, u32[]{:S(2)}, u32[]{:S(2)}) collective-permute-start(f32[960,128]{1,0:T(8,128)S(1)} %join.1.refs_1_), channel_id=1, source_target_pairs={{0,24},{8,16},{16,8},{24,0},{1,25},{9,17},{17,9},{25,1},{2,26},{10... | collective-permute-start | bytes 1474568 | tf_op jit(solution)/shard_map/ppermute | solution.py:696
  20.4 24.0 %collective-permute-start.1 = (f32[960,128]{1,0:T(8,128)S(1)}, f32[960,128]{1,0:T(8,128)S(1)}, u32[]{:S(2)}, u32[]{:S(2)}) collective-permute-start(f32[960,128]{1,0:T(8,128)S(1)} %join.1.refs_1_), channel_id=1, source_target_pairs={{0,16},{8,24},{16,0},{24,8},{1,17},{9,25},{17,1},{25,9},{2,18},{10... | collective-permute-start | bytes 1474568 | tf_op jit(solution)/shard_map/ppermute | solution.py:696
  22.0 22.5 %collective-permute-start = (f32[960,128]{1,0:T(8,128)S(1)}, f32[960,128]{1,0:T(8,128)S(1)}, u32[]{:S(2)}, u32[]{:S(2)}) collective-permute-start(f32[960,128]{1,0:T(8,128)S(1)} %join.1.refs_1_), channel_id=1, source_target_pairs={{0,8},{8,0},{16,24},{24,16},{1,9},{9,1},{17,25},{25,17},{2,10},{10... | collective-permute-start | bytes 1474568 | tf_op jit(solution)/shard_map/ppermute | solution.py:696
  22.3 22.2 %copy-start = (f32[192,256]{1,0:T(8,128)S(1)}, f32[192,256]{1,0:T(8,128)}, u32[]{:S(2)}) copy-start(f32[192,256]{1,0:T(8,128)} %get-tuple-element.28.refs_0_.refs_8_) | copy-start | bytes 589828
  22.3 36.3 %copy-start.1 = (bf16[384,256]{1,0:T(8,128)(2,1)S(1)}, bf16[384,256]{1,0:T(8,128)(2,1)}, u32[]{:S(2)}) copy-start(bf16[384,256]{1,0:T(8,128)(2,1)} %get-tuple-element.46.refs_9_) | copy-start | bytes 589828
  22.3 36.3 %copy-start.2 = (bf16[384,256]{1,0:T(8,128)(2,1)S(1)}, bf16[384,256]{1,0:T(8,128)(2,1)}, u32[]{:S(2)}) copy-start(bf16[384,256]{1,0:T(8,128)(2,1)} %get-tuple-element.47.refs_10_) | copy-start | bytes 589828
  22.3 36.3 %copy-start.3 = (f32[192,192]{1,0:T(8,128)S(1)}, f32[192,192]{1,0:T(8,128)}, u32[]{:S(2)}) copy-start(f32[192,192]{1,0:T(8,128)} %get-tuple-element.48.refs_11_) | copy-start | bytes 442372
  22.3 36.3 %copy-start.4 = (f32[192,192]{1,0:T(8,128)S(1)}, f32[192,192]{1,0:T(8,128)}, u32[]{:S(2)}) copy-start(f32[192,192]{1,0:T(8,128)} %get-tuple-element.49.refs_12_) | copy-start | bytes 442372
  22.3 36.3 %copy-start.6 = (f32[192,128]{1,0:T(8,128)S(1)}, f32[192,128]{1,0:T(8,128)}, u32[]{:S(2)}) copy-start(f32[192,128]{1,0:T(8,128)} %get-tuple-element.27.len_ref) | copy-start | bytes 294916
  45.4 7.3 %collective-permute-start.3 = (f32[80,128]{1,0:T(8,128)S(1)}, f32[80,128]{1,0:T(8,128)S(1)}, u32[]{:S(2)}, u32[]{:S(2)}) collective-permute-start(f32[80,128]{1,0:T(8,128)S(1)} %get-tuple-element.39), channel_id=1, source_target_pairs={{0,1},{1,2},{2,3},{3,4},{4,5},{5,6},{6,7},{7,0},{8,9},{9,10},{10,1... | collective-permute-start | bytes 122888 | tf_op jit(solution)/shard_map/ppermute | solution.py:711
  46.9 7.7 %collective-permute-start.4 = (f32[80,128]{1,0:T(8,128)S(1)}, f32[80,128]{1,0:T(8,128)S(1)}, u32[]{:S(2)}, u32[]{:S(2)}) collective-permute-start(f32[80,128]{1,0:T(8,128)S(1)} %get-tuple-element.40), channel_id=1, source_target_pairs={{0,2},{1,3},{2,4},{3,5},{4,6},{5,7},{6,0},{7,1},{8,10},{9,11},{10,... | collective-permute-start | bytes 122888 | tf_op jit(solution)/shard_map/ppermute | solution.py:711
  46.9 9.3 %collective-permute-start.5 = (f32[80,128]{1,0:T(8,128)S(1)}, f32[80,128]{1,0:T(8,128)S(1)}, u32[]{:S(2)}, u32[]{:S(2)}) collective-permute-start(f32[80,128]{1,0:T(8,128)S(1)} %get-tuple-element.41), channel_id=1, source_target_pairs={{0,3},{1,4},{2,5},{3,6},{4,7},{5,0},{6,1},{7,2},{8,11},{9,12},{10,... | collective-permute-start | bytes 122888 | tf_op jit(solution)/shard_map/ppermute | solution.py:711
  48.7 7.5 %collective-permute-start.6 = (f32[80,128]{1,0:T(8,128)S(1)}, f32[80,128]{1,0:T(8,128)S(1)}, u32[]{:S(2)}, u32[]{:S(2)}) collective-permute-start(f32[80,128]{1,0:T(8,128)S(1)} %get-tuple-element.42), channel_id=1, source_target_pairs={{0,4},{1,5},{2,6},{3,7},{4,0},{5,1},{6,2},{7,3},{8,12},{9,13},{10,... | collective-permute-start | bytes 122888 | tf_op jit(solution)/shard_map/ppermute | solution.py:711
  51.8 5.0 %collective-permute-start.7 = (f32[80,128]{1,0:T(8,128)S(1)}, f32[80,128]{1,0:T(8,128)S(1)}, u32[]{:S(2)}, u32[]{:S(2)}) collective-permute-start(f32[80,128]{1,0:T(8,128)S(1)} %get-tuple-element.43), channel_id=1, source_target_pairs={{0,5},{1,6},{2,7},{3,0},{4,1},{5,2},{6,3},{7,4},{8,13},{9,14},{10,... | collective-permute-start | bytes 122888 | tf_op jit(solution)/shard_map/ppermute | solution.py:711
  52.8 4.7 %collective-permute-start.8 = (f32[80,128]{1,0:T(8,128)S(1)}, f32[80,128]{1,0:T(8,128)S(1)}, u32[]{:S(2)}, u32[]{:S(2)}) collective-permute-start(f32[80,128]{1,0:T(8,128)S(1)} %get-tuple-element.44), channel_id=1, source_target_pairs={{0,6},{1,7},{2,0},{3,1},{4,2},{5,3},{6,4},{7,5},{8,14},{9,15},{10,... | collective-permute-start | bytes 122888 | tf_op jit(solution)/shard_map/ppermute | solution.py:711
  54.6 4.0 %collective-permute-start.9 = (f32[80,128]{1,0:T(8,128)S(1)}, f32[80,128]{1,0:T(8,128)S(1)}, u32[]{:S(2)}, u32[]{:S(2)}) collective-permute-start(f32[80,128]{1,0:T(8,128)S(1)} %get-tuple-element.45), channel_id=1, source_target_pairs={{0,7},{1,0},{2,1},{3,2},{4,3},{5,4},{6,5},{7,6},{8,15},{9,8},{10,9... | collective-permute-start | bytes 122888 | tf_op jit(solution)/shard_map/ppermute | solution.py:711

commit v15 on v13

--- a/solution.py
+++ b/solution.py
@@ -129,7 +129,7 @@
 
 def wave_kernel(
     extent, me_ref, length_hbm, row_hbm, col_hbm, plane_hbm, coef_hbm,
-    out_ref, kc_ref, len_ref, whi_ref, wlo_ref, sc_ref, ss_ref,
+    out_ref, kc_ref, wave_ref, len_ref, whi_ref, wlo_ref, sc_ref, ss_ref,
     length_ref, row_ref, col_ref, plane_ref, coef_ref, sems,
 ):
     copies = fetch_all(
@@ -197,6 +197,8 @@
     kinetic = (square + (position - middle) * (position - middle)) * (1.0 / (RADIUS * RADIUS))
     wave = jnp.concatenate([coef_ref[:, 0, :] * kept, coef_ref[:, 1, :] * kept], axis=1)
     kc_ref[...] = wave * jnp.concatenate([kinetic, kinetic], axis=1)
+    wave_ref[:sticks, :] = wave[:, :padded]
+    wave_ref[sticks:, :] = wave[:, padded:]
     raw = dot3(table, split(wave), ((1,), (1,)))
     for d in range(devices):
         at = 2 * d * padded_planes
@@ -368,8 +370,18 @@
     left = low[0:8]
     upper_lanes = jnp.where(left, 0, half)
     sides = ((0, even_ref, ge_ref), (1, odd_ref, go_ref))
-
-    @pl.loop(0, rows, unroll=8)
+    even_rows, odd_rows = row_blocks()
+    used = up8(RADIUS + 1)
+    for p in range(planes):
+        for at in range(p * rows + used, p * rows + even_rows, 8):
+            ge_ref[at:at + 8, :] = jnp.zeros((8, LANES), F32)
+            go_ref[at:at + 8, :] = jnp.zeros((8, LANES), F32)
+
+    def each_row(body):
+        pl.loop(0, used, unroll=8)(body)
+        pl.loop(even_rows, rows, unroll=8)(body)
+
+    @each_row
     def _(r):
         for side, code_ref, grid_ref in sides:
             first = first_ref[8 * side, r]
@@ -384,7 +396,6 @@
 
     for copy in copies:
         copy.wait()
-    even_rows, odd_rows = row_blocks()
     folded = extent // 2
     group = next(g for g in (12, 8, 6, 4, 2) if planes % g == 0)
     wide = 2 * LANES
@@ -460,7 +471,7 @@
                 ge_ref[pick, :] = value[:, :LANES]
                 go_ref[pick, :] = value[:, LANES:]
 
-    @pl.loop(0, rows, unroll=8)
+    @each_row
     def _(r):
         for side, _, grid_ref in sides:
             first = first_ref[8 * side, r]
@@ -495,14 +506,14 @@
 
 def inner_kernel(bands, volume, norm, place_ref, *refs):
     kc_ref = refs[0]
-    coefs = refs[1:1 + bands]
+    waves = refs[1:1 + bands]
     fields = refs[1 + bands:1 + 2 * bands]
     in_ref = refs[1 + 2 * bands]
     out_refs = refs[2 + 2 * bands:]
     devices = in_ref.shape[0]
     padded_planes = (in_ref.shape[1] - 8) // 3
     half = LANES // 2
-    padded = coefs[0].shape[2]
+    sticks, padded = kc_ref.shape[0], kc_ref.shape[1] // 2
     me, mine = place_ref[0], place_ref[1]
     low = lax.broadcasted_iota(jnp.int32, (padded_planes, LANES), 1) < half
 
@@ -517,7 +528,7 @@
     kc_re, kc_im = kc[:, :padded], kc[:, padded:]
     sums = []
     for m in range(bands):
-        c_re, c_im = coefs[m][:, 0, :], coefs[m][:, 1, :]
+        c_re, c_im = waves[m][:sticks, :], waves[m][sticks:, :]
         sums.append([fold(c_re * kc_re + c_im * kc_im), fold(c_re * kc_im - c_im * kc_re)])
     local = [[jnp.zeros((8, LANES), F32), jnp.zeros((8, LANES), F32)] for _ in range(bands)]
     for d in range(devices):
@@ -533,11 +544,11 @@
     row = lax.broadcasted_iota(jnp.int32, (8, LANES), 0)
     tile = jnp.zeros((8, LANES), F32)
     for m in range(bands):
-        at = me ^ m
+        spot = me ^ m
         for part, sign in ((0, 1.0), (1, -1.0)):
             partial = sums[m][part] + volume * local[m][part]
             scalar = jnp.sum(jnp.sum(partial, axis=1, keepdims=True), axis=0, keepdims=True)
-            tile = jnp.where((lane == at) & (row == part), sign * norm * scalar, tile)
+            tile = jnp.where((lane == spot) & (row == part), sign * norm * scalar, tile)
     for k in range(devices):
         out_refs[k][0:3 * padded_planes, :] = in_ref[lax.rem(mine + k, devices), 0:3 * padded_planes, :]
         out_refs[k][3 * padded_planes:, :] = tile
@@ -603,11 +614,12 @@
 
     block = 3 * padded_planes
     total_planes = devices * padded_planes
-    sent, kc, lengths, whi, wlo, shift_cos, shift_sin = pl.pallas_call(
+    sent, kc, wave, lengths, whi, wlo, shift_cos, shift_sin = pl.pallas_call(
         functools.partial(wave_kernel, extent),
         out_shape=(
             jax.ShapeDtypeStruct((devices, block, LANES), F32),
             jax.ShapeDtypeStruct((sticks, 2 * padded), F32),
+            jax.ShapeDtypeStruct((2 * sticks, padded), F32),
             jax.ShapeDtypeStruct((sticks, LANES), F32),
             jax.ShapeDtypeStruct((2 * total_planes, 2 * padded), BF16),
             jax.ShapeDtypeStruct((2 * total_planes, 2 * padded), BF16),
@@ -675,9 +687,9 @@
         name="planes",
     )(first, even_map, odd_map, source, target, row_w, col_w, received, constants, potential)
 
-    coefs, fields = [coef], [received]
+    waves, fields = [wave], [received]
     for m in range(1, bands):
-        coefs.append(lax.ppermute(coef, "band", pairs(bands, m)))
+        waves.append(lax.ppermute(wave, "band", pairs(bands, m)))
         fields.append(lax.ppermute(received, "band", pairs(bands, m)))
     band = lax.axis_index("band").astype(jnp.int32)
     norm = 1.0 / (total_sticks * padded)
@@ -688,7 +700,7 @@
         in_specs=[smem] + [vmem] * (2 + 2 * bands),
         compiler_params=params(6 + 1.5 * bands),
         name="inner",
-    )(places, kc, *coefs, *fields, weighted)
+    )(places, kc, *waves, *fields, weighted)
 
     returned = [outgoing[0]]
     for k in range(1, devices):

time: 58.8 us -> 57.9 us (0.985)
  Pallas kernels: 28.1 us -> 27.2 us
where the time goes in v15:
time: 57.9 us; the launch traced here: 57.5 us
  Pallas kernels  27.2 us (47%)
  starting transfers between devices  21.7 us (37%)
  waiting for transfers between devices  6.38 us (11%)
  local copies, waits for them, and re-layouts  1.42 us (2%)
  between operations  0.78 us (1%)
    pallas_call x1, Pallas kernels, shards(): pl.pallas_call(functools.partial(plane_kernel, planes), out_shape=jax.Sha...  19.8 us
    ppermute x7, starting transfers between devices, shards(): returned.append(lax.ppermute(outgoing[k], 'tg', ring))  10.7 us
    all_to_all x1, starting transfers between devices, shards(): lax.all_to_all(sent, 'tg', split_axis=0, concat_axis=0, tiled=True)  7.26 us
    all_to_all x1, waiting for transfers between devices, shards(): lax.all_to_all(sent, 'tg', split_axis=0, concat_axis=0, tiled=True)  3.98 us
    pallas_call x1, Pallas kernels, shards(): pl.pallas_call(functools.partial(wave_kernel, extent), out_shape=(jax.Sha...  2.76 us
    ppermute x7, waiting for transfers between devices, shards(): returned.append(lax.ppermute(outgoing[k], 'tg', ring))  2.38 us
    pallas_call x1, Pallas kernels, shards(): pl.pallas_call(functools.partial(map_kernel, extent, sticks), out_shape=(...  2.29 us
    ppermute x3, starting transfers between devices, shards(): fields.append(lax.ppermute(received, 'band', pairs(bands, m)))  1.86 us
  transfers between devices with their start and end apart: 14, of which 4 were waited for; matrix products, arithmetic and copies ran while one was open for 0% of the time, Pallas kernels for 39%

profile of v15, /device:TPU:0, one launch (start us, length us, event | category | flops | bytes accessed | tf_op | source)
XLA Modules:
  0.0 57.5 jit_solution(4946210265503680431)
XLA Ops:
  0.6 2.8 %wave_to_planes.1 = (f32[8,72,128]{2,1,0:T(8,128)}, f32[192,256]{1,0:T(8,128)}, f32[384,128]{1,0:T(8,128)}, f32[192,128]{1,0:T(8,128)}, bf16[384,256]{1,0:T(8,12...) custom-call(s32[1]{0:T(128)} %bitcast.me_ref, s32[12,128]{1,0:T(8,128)} %bitcast.13, ...), custom_call_target="tpu_custom_call" | custom-call | tf_op jit(solution)/shard_map/wave_to_planes/pallas_call | solution.py:617
  3.4 7.3 %all-to-all-start = ((f32[8,72,128]{2,1,0:T(8,128)}), f32[8,72,128]{2,1,0:T(8,128)S(1)}, u32[]{:S(2)}, u32[]{:S(2)}) async-start(f32[8,72,128]{2,1,0:T(8,128)} %get-tuple-element.30), calls=%async_computation | async-start | bytes 589824 | tf_op jit(solution)/shard_map/all_to_all | solution.py:642
  10.7 0.7 %collective-permute-start.2 = (f32[384,128]{1,0:T(8,128)}, f32[384,128]{1,0:T(8,128)S(1)}, u32[]{:S(2)}, u32[]{:S(2)}) collective-permute-start(f32[384,128]{1,0:T(8,128)} %get-tuple-element.29.refs_1_), channel_id=1, source_target_pairs={{0,24},{8,16},{16,8},{24,0},{1,25},{9,17},{17,9},{25,1},{2,26},{10... | collective-permute-start | bytes 589832 | tf_op jit(solution)/shard_map/ppermute | solution.py:692
  11.3 0.9 %collective-permute-start.1 = (f32[384,128]{1,0:T(8,128)}, f32[384,128]{1,0:T(8,128)S(1)}, u32[]{:S(2)}, u32[]{:S(2)}) collective-permute-start(f32[384,128]{1,0:T(8,128)} %get-tuple-element.29.refs_1_), channel_id=1, source_target_pairs={{0,16},{8,24},{16,0},{24,8},{1,17},{9,25},{17,1},{25,9},{2,18},{10... | collective-permute-start | bytes 589832 | tf_op jit(solution)/shard_map/ppermute | solution.py:692
  12.3 0.3 collective-permute-start
  12.5 0.7 %copy-done.7 = s32[1536]{0:T(1024)S(1)} copy-done((s32[1536]{0:T(1024)S(1)}, s32[1536]{0:T(1024)}, u32[]{:S(2)}) %copy-start.7) | copy-done | bytes 6168
  13.2 0.7 %copy-done.8 = s32[1536]{0:T(1024)S(1)} copy-done((s32[1536]{0:T(1024)S(1)}, s32[1536]{0:T(1024)}, u32[]{:S(2)}) %copy-start.8) | copy-done | bytes 6168
  13.9 2.3 %stick_map.1 = (s32[128,128]{1,0:T(8,128)S(1)}, s32[128,128]{1,0:T(8,128)S(1)}, s32[16,128]{1,0:T(8,128)S(1)}, s32[12,128]{1,0:T(8,128)S(1)}, s32[12,128]{1,0:T(...) custom-call(s32[12,128]{1,0:T(8,128)S(1)} %bitcast.9, s32[12,128]{1,0:T(8,128)S(1)} %bitcast.11), custom_call_target="tpu_custom_call" | custom-call | flops 4000000000 | bytes 100000 | tf_op jit(solution)/shard_map/stick_map/pallas_call | solution.py:647
  16.2 0.1 pad_add_fusion.place_ref
  16.3 4.0 %all-to-all-done.recv_ref.refs_5_ = f32[8,72,128]{2,1,0:T(8,128)S(1)} async-done(((f32[8,72,128]{2,1,0:T(8,128)}), f32[8,72,128]{2,1,0:T(8,128)S(1)}, u32[]{:S(2)}, u32[]{:S(2)}) %all-to-all-start) | async-done | bytes 294944 | tf_op jit(solution)/shard_map/all_to_all | solution.py:642
  20.3 0.0 collective-permute-start.5
  20.3 1.6 %collective-permute-start.4 = (f32[8,72,128]{2,1,0:T(8,128)S(1)}, f32[8,72,128]{2,1,0:T(8,128)S(1)}, u32[]{:S(2)}, u32[]{:S(2)}) collective-permute-start(f32[8,72,128]{2,1,0:T(8,128)S(1)} %all-to-all-done.recv_ref.refs_5_), channel_id=1, source_target_pairs={{0,16},{8,24},{16,0},{24,8},{1,17},{9,25},{17,1},{25,9},{2,18},{10... | collective-permute-start | bytes 884744 | tf_op jit(solution)/shard_map/ppermute | solution.py:693
  21.8 0.0 collective-permute-done.2.refs_4_
  21.8 0.3 collective-permute-start.3
  22.2 19.8 %planes.1.refs_9_ = f32[8,80,128]{2,1,0:T(8,128)S(1)} custom-call(s32[16,128]{1,0:T(8,128)S(1)} %get-tuple-element.31.first_ref, s32[128,128]{1,0:T(8,128)S(1)} %get-tuple-element.32.even_ref, s32[128,128]{1,0:T(8,128)S(1)} %get-tuple-element.33.odd_ref, s32[12,128]{1,0:T(8,128)S(1)} %get-tuple-element.34.src_ref, s32[12,128]{1,0:T(8,128)S(1)} %get-tuple-element.35.dst_ref, ...), custom_call_target="tpu_custom_call" | custom-call | flops 20000000000 | bytes 10000000 | tf_op jit(solution)/shard_map/planes/pallas_call | solution.py:670
  42.0 0.0 collective-permute-done.1.refs_3_
  42.1 0.0 collective-permute-done.refs_2_
  42.1 0.0 collective-permute-done.5.refs_8_
  42.1 0.0 collective-permute-done.4.refs_7_
  42.1 0.0 collective-permute-done.3.refs_6_
  42.1 1.0 %inner.1 = (f32[80,128]{1,0:T(8,128)S(1)}, f32[80,128]{1,0:T(8,128)S(1)}, f32[80,128]{1,0:T(8,128)S(1)}, f32[80,128]{1,0:T(8,128)S(1)}, f32[80,128]{1,0:T(8,128)...) custom-call(s32[2]{0:T(128)S(1)} %pad_add_fusion.place_ref, f32[192,256]{1,0:T(8,128)S(1)} %copy-done, ...), custom_call_target="tpu_custom_call" | custom-call | tf_op jit(solution)/shard_map/inner/pallas_call | solution.py:697
  43.1 1.5 %collective-permute-start.6 = (f32[80,128]{1,0:T(8,128)S(1)}, f32[80,128]{1,0:T(8,128)S(1)}, u32[]{:S(2)}, u32[]{:S(2)}) collective-permute-start(f32[80,128]{1,0:T(8,128)S(1)} %get-tuple-element.39), channel_id=1, source_target_pairs={{0,1},{1,2},{2,3},{3,4},{4,5},{5,6},{6,7},{7,0},{8,9},{9,10},{10,1... | collective-permute-start | bytes 122888 | tf_op jit(solution)/shard_map/ppermute | solution.py:708
  44.6 1.7 %collective-permute-start.8 = (f32[80,128]{1,0:T(8,128)S(1)}, f32[80,128]{1,0:T(8,128)S(1)}, u32[]{:S(2)}, u32[]{:S(2)}) collective-permute-start(f32[80,128]{1,0:T(8,128)S(1)} %get-tuple-element.41), channel_id=1, source_target_pairs={{0,3},{1,4},{2,5},{3,6},{4,7},{5,0},{6,1},{7,2},{8,11},{9,12},{10,... | collective-permute-start | bytes 122888 | tf_op jit(solution)/shard_map/ppermute | solution.py:708
  46.3 3.1 %collective-permute-start.9 = (f32[80,128]{1,0:T(8,128)S(1)}, f32[80,128]{1,0:T(8,128)S(1)}, u32[]{:S(2)}, u32[]{:S(2)}) collective-permute-start(f32[80,128]{1,0:T(8,128)S(1)} %get-tuple-element.42), channel_id=1, source_target_pairs={{0,4},{1,5},{2,6},{3,7},{4,0},{5,1},{6,2},{7,3},{8,12},{9,13},{10,... | collective-permute-start | bytes 122888 | tf_op jit(solution)/shard_map/ppermute | solution.py:708
  49.5 1.0 %collective-permute-start.10 = (f32[80,128]{1,0:T(8,128)S(1)}, f32[80,128]{1,0:T(8,128)S(1)}, u32[]{:S(2)}, u32[]{:S(2)}) collective-permute-start(f32[80,128]{1,0:T(8,128)S(1)} %get-tuple-element.43), channel_id=1, source_target_pairs={{0,5},{1,6},{2,7},{3,0},{4,1},{5,2},{6,3},{7,4},{8,13},{9,14},{10,... | collective-permute-start | bytes 122888 | tf_op jit(solution)/shard_map/ppermute | solution.py:708
  50.4 1.8 %collective-permute-start.11 = (f32[80,128]{1,0:T(8,128)S(1)}, f32[80,128]{1,0:T(8,128)S(1)}, u32[]{:S(2)}, u32[]{:S(2)}) collective-permute-start(f32[80,128]{1,0:T(8,128)S(1)} %get-tuple-element.44), channel_id=1, source_target_pairs={{0,6},{1,7},{2,0},{3,1},{4,2},{5,3},{6,4},{7,5},{8,14},{9,15},{10,... | collective-permute-start | bytes 122888 | tf_op jit(solution)/shard_map/ppermute | solution.py:708
  52.2 0.0 collective-permute-done.7.refs_2_
  52.2 1.6 %collective-permute-start.12 = (f32[80,128]{1,0:T(8,128)S(1)}, f32[80,128]{1,0:T(8,128)S(1)}, u32[]{:S(2)}, u32[]{:S(2)}) collective-permute-start(f32[80,128]{1,0:T(8,128)S(1)} %get-tuple-element.45), channel_id=1, source_target_pairs={{0,7},{1,0},{2,1},{3,2},{4,3},{5,4},{6,5},{7,6},{8,15},{9,8},{10,9... | collective-permute-start | bytes 122888 | tf_op jit(solution)/shard_map/ppermute | solution.py:708
  53.8 0.7 %collective-permute-done.10.refs_5_ = f32[80,128]{1,0:T(8,128)S(1)} collective-permute-done((f32[80,128]{1,0:T(8,128)S(1)}, f32[80,128]{1,0:T(8,128)S(1)}, u32[]{:S(2)}, u32[]{:S(2)}) %collective-permute-start.10) | collective-permute-done | bytes 40992 | tf_op jit(solution)/shard_map/ppermute | solution.py:708
  54.6 0.5 collective-permute-done.11.refs_6_
  55.1 1.2 %collective-permute-done.12.refs_7_ = f32[80,128]{1,0:T(8,128)S(1)} collective-permute-done((f32[80,128]{1,0:T(8,128)S(1)}, f32[80,128]{1,0:T(8,128)S(1)}, u32[]{:S(2)}, u32[]{:S(2)}) %collective-permute-start.12) | collective-permute-done | bytes 40992 | tf_op jit(solution)/shard_map/ppermute | solution.py:708
  56.2 1.3 %planes_to_wave.1 = (f32[192,2,128]{2,1,0:T(2,128)}, f32[2,1,4]{2,1,0:T(1,128)}) custom-call(s32[1]{0:T(128)} %bitcast.me_ref, f32[192,128]{1,0:T(8,128)S(1)} %copy-done.6, f32[80,128]{1,0:T(8,128)S(1)} %get-tuple-element.38.refs_0_, f32[80,128]{1,0:T(8,128)S(1)} %collective-permute-done.6.refs_1_, f32[80,128]{1,0:T(8,128)S(1)} %collective-permute-done.7.refs_2_, ...), custom_call_target="tpu_custom_call" | custom-call | tf_op jit(solution)/shard_map/planes_to_wave/pallas_call | solution.py:709
  (20 shorter events, 0.0 us)
Async XLA Ops:
  3.4 16.9 %all-to-all-start = ((f32[8,72,128]{2,1,0:T(8,128)}), f32[8,72,128]{2,1,0:T(8,128)S(1)}, u32[]{:S(2)}, u32[]{:S(2)}) async-start(f32[8,72,128]{2,1,0:T(8,128)} %get-tuple-element.30), calls=%async_computation | async-start | bytes 589824 | tf_op jit(solution)/shard_map/all_to_all | solution.py:642
  10.7 11.2 %collective-permute-start.2 = (f32[384,128]{1,0:T(8,128)}, f32[384,128]{1,0:T(8,128)S(1)}, u32[]{:S(2)}, u32[]{:S(2)}) collective-permute-start(f32[384,128]{1,0:T(8,128)} %get-tuple-element.29.refs_1_), channel_id=1, source_target_pairs={{0,24},{8,16},{16,8},{24,0},{1,25},{9,17},{17,9},{25,1},{2,26},{10... | collective-permute-start | bytes 589832 | tf_op jit(solution)/shard_map/ppermute | solution.py:692
  11.3 30.7 %collective-permute-start.1 = (f32[384,128]{1,0:T(8,128)}, f32[384,128]{1,0:T(8,128)S(1)}, u32[]{:S(2)}, u32[]{:S(2)}) collective-permute-start(f32[384,128]{1,0:T(8,128)} %get-tuple-element.29.refs_1_), channel_id=1, source_target_pairs={{0,16},{8,24},{16,0},{24,8},{1,17},{9,25},{17,1},{25,9},{2,18},{10... | collective-permute-start | bytes 589832 | tf_op jit(solution)/shard_map/ppermute | solution.py:692
  12.3 29.8 %collective-permute-start = (f32[384,128]{1,0:T(8,128)}, f32[384,128]{1,0:T(8,128)S(1)}, u32[]{:S(2)}, u32[]{:S(2)}) collective-permute-start(f32[384,128]{1,0:T(8,128)} %get-tuple-element.29.refs_1_), channel_id=1, source_target_pairs={{0,8},{8,0},{16,24},{24,16},{1,9},{9,1},{17,25},{25,17},{2,10},{10... | collective-permute-start | bytes 589832 | tf_op jit(solution)/shard_map/ppermute | solution.py:692
  12.5 0.7 %copy-start.7 = (s32[1536]{0:T(1024)S(1)}, s32[1536]{0:T(1024)}, u32[]{:S(2)}) copy-start(s32[1536]{0:T(1024)} %param.9) | copy-start | bytes 18436
  13.2 0.7 %copy-start.8 = (s32[1536]{0:T(1024)S(1)}, s32[1536]{0:T(1024)}, u32[]{:S(2)}) copy-start(s32[1536]{0:T(1024)} %param.8) | copy-start | bytes 18436
  20.3 21.8 %collective-permute-start.5 = (f32[8,72,128]{2,1,0:T(8,128)S(1)}, f32[8,72,128]{2,1,0:T(8,128)S(1)}, u32[]{:S(2)}, u32[]{:S(2)}) collective-permute-start(f32[8,72,128]{2,1,0:T(8,128)S(1)} %all-to-all-done.recv_ref.refs_5_), channel_id=1, source_target_pairs={{0,24},{8,16},{16,8},{24,0},{1,25},{9,17},{17,9},{25,1},{2,26},{10... | collective-permute-start | bytes 884744 | tf_op jit(solution)/shard_map/ppermute | solution.py:693
  20.3 21.8 %collective-permute-start.4 = (f32[8,72,128]{2,1,0:T(8,128)S(1)}, f32[8,72,128]{2,1,0:T(8,128)S(1)}, u32[]{:S(2)}, u32[]{:S(2)}) collective-permute-start(f32[8,72,128]{2,1,0:T(8,128)S(1)} %all-to-all-done.recv_ref.refs_5_), channel_id=1, source_target_pairs={{0,16},{8,24},{16,0},{24,8},{1,17},{9,25},{17,1},{25,9},{2,18},{10... | collective-permute-start | bytes 884744 | tf_op jit(solution)/shard_map/ppermute | solution.py:693
  21.8 20.3 %collective-permute-start.3 = (f32[8,72,128]{2,1,0:T(8,128)S(1)}, f32[8,72,128]{2,1,0:T(8,128)S(1)}, u32[]{:S(2)}, u32[]{:S(2)}) collective-permute-start(f32[8,72,128]{2,1,0:T(8,128)S(1)} %all-to-all-done.recv_ref.refs_5_), channel_id=1, source_target_pairs={{0,8},{8,0},{16,24},{24,16},{1,9},{9,1},{17,25},{25,17},{2,10},{10... | collective-permute-start | bytes 884744 | tf_op jit(solution)/shard_map/ppermute | solution.py:693
  22.2 20.0 %copy-start = (f32[192,256]{1,0:T(8,128)S(1)}, f32[192,256]{1,0:T(8,128)}, u32[]{:S(2)}) copy-start(f32[192,256]{1,0:T(8,128)} %get-tuple-element.28.refs_0_.refs_8_) | copy-start | bytes 589828
  22.2 20.0 %copy-start.5 = (f32[384,128]{1,0:T(8,128)S(1)}, f32[384,128]{1,0:T(8,128)}, u32[]{:S(2)}) copy-start(f32[384,128]{1,0:T(8,128)} %get-tuple-element.29.refs_1_) | copy-start | bytes 589828
  22.2 34.1 %copy-start.1 = (bf16[384,256]{1,0:T(8,128)(2,1)S(1)}, bf16[384,256]{1,0:T(8,128)(2,1)}, u32[]{:S(2)}) copy-start(bf16[384,256]{1,0:T(8,128)(2,1)} %get-tuple-element.46.refs_9_) | copy-start | bytes 589828
  22.2 34.1 %copy-start.2 = (bf16[384,256]{1,0:T(8,128)(2,1)S(1)}, bf16[384,256]{1,0:T(8,128)(2,1)}, u32[]{:S(2)}) copy-start(bf16[384,256]{1,0:T(8,128)(2,1)} %get-tuple-element.47.refs_10_) | copy-start | bytes 589828
  22.2 34.1 %copy-start.3 = (f32[192,192]{1,0:T(8,128)S(1)}, f32[192,192]{1,0:T(8,128)}, u32[]{:S(2)}) copy-start(f32[192,192]{1,0:T(8,128)} %get-tuple-element.48.refs_11_) | copy-start | bytes 442372
  22.2 34.1 %copy-start.4 = (f32[192,192]{1,0:T(8,128)S(1)}, f32[192,192]{1,0:T(8,128)}, u32[]{:S(2)}) copy-start(f32[192,192]{1,0:T(8,128)} %get-tuple-element.49.refs_12_) | copy-start | bytes 442372
  22.2 34.1 %copy-start.6 = (f32[192,128]{1,0:T(8,128)S(1)}, f32[192,128]{1,0:T(8,128)}, u32[]{:S(2)}) copy-start(f32[192,128]{1,0:T(8,128)} %get-tuple-element.27.len_ref) | copy-start | bytes 294916
  43.1 7.3 %collective-permute-start.6 = (f32[80,128]{1,0:T(8,128)S(1)}, f32[80,128]{1,0:T(8,128)S(1)}, u32[]{:S(2)}, u32[]{:S(2)}) collective-permute-start(f32[80,128]{1,0:T(8,128)S(1)} %get-tuple-element.39), channel_id=1, source_target_pairs={{0,1},{1,2},{2,3},{3,4},{4,5},{5,6},{6,7},{7,0},{8,9},{9,10},{10,1... | collective-permute-start | bytes 122888 | tf_op jit(solution)/shard_map/ppermute | solution.py:708
  44.6 7.7 %collective-permute-start.7 = (f32[80,128]{1,0:T(8,128)S(1)}, f32[80,128]{1,0:T(8,128)S(1)}, u32[]{:S(2)}, u32[]{:S(2)}) collective-permute-start(f32[80,128]{1,0:T(8,128)S(1)} %get-tuple-element.40), channel_id=1, source_target_pairs={{0,2},{1,3},{2,4},{3,5},{4,6},{5,7},{6,0},{7,1},{8,10},{9,11},{10,... | collective-permute-start | bytes 122888 | tf_op jit(solution)/shard_map/ppermute | solution.py:708
  44.6 9.3 %collective-permute-start.8 = (f32[80,128]{1,0:T(8,128)S(1)}, f32[80,128]{1,0:T(8,128)S(1)}, u32[]{:S(2)}, u32[]{:S(2)}) collective-permute-start(f32[80,128]{1,0:T(8,128)S(1)} %get-tuple-element.41), channel_id=1, source_target_pairs={{0,3},{1,4},{2,5},{3,6},{4,7},{5,0},{6,1},{7,2},{8,11},{9,12},{10,... | collective-permute-start | bytes 122888 | tf_op jit(solution)/shard_map/ppermute | solution.py:708
  46.3 7.5 %collective-permute-start.9 = (f32[80,128]{1,0:T(8,128)S(1)}, f32[80,128]{1,0:T(8,128)S(1)}, u32[]{:S(2)}, u32[]{:S(2)}) collective-permute-start(f32[80,128]{1,0:T(8,128)S(1)} %get-tuple-element.42), channel_id=1, source_target_pairs={{0,4},{1,5},{2,6},{3,7},{4,0},{5,1},{6,2},{7,3},{8,12},{9,13},{10,... | collective-permute-start | bytes 122888 | tf_op jit(solution)/shard_map/ppermute | solution.py:708
  49.5 5.1 %collective-permute-start.10 = (f32[80,128]{1,0:T(8,128)S(1)}, f32[80,128]{1,0:T(8,128)S(1)}, u32[]{:S(2)}, u32[]{:S(2)}) collective-permute-start(f32[80,128]{1,0:T(8,128)S(1)} %get-tuple-element.43), channel_id=1, source_target_pairs={{0,5},{1,6},{2,7},{3,0},{4,1},{5,2},{6,3},{7,4},{8,13},{9,14},{10,... | collective-permute-start | bytes 122888 | tf_op jit(solution)/shard_map/ppermute | solution.py:708
  50.4 4.6 %collective-permute-start.11 = (f32[80,128]{1,0:T(8,128)S(1)}, f32[80,128]{1,0:T(8,128)S(1)}, u32[]{:S(2)}, u32[]{:S(2)}) collective-permute-start(f32[80,128]{1,0:T(8,128)S(1)} %get-tuple-element.44), channel_id=1, source_target_pairs={{0,6},{1,7},{2,0},{3,1},{4,2},{5,3},{6,4},{7,5},{8,14},{9,15},{10,... | collective-permute-start | bytes 122888 | tf_op jit(solution)/shard_map/ppermute | solution.py:708
  52.2 4.0 %collective-permute-start.12 = (f32[80,128]{1,0:T(8,128)S(1)}, f32[80,128]{1,0:T(8,128)S(1)}, u32[]{:S(2)}, u32[]{:S(2)}) collective-permute-start(f32[80,128]{1,0:T(8,128)S(1)} %get-tuple-element.45), channel_id=1, source_target_pairs={{0,7},{1,0},{2,1},{3,2},{4,3},{5,4},{6,5},{7,6},{8,15},{9,8},{10,9... | collective-permute-start | bytes 122888 | tf_op jit(solution)/shard_map/ppermute | solution.py:708

commit v16 on v15

--- a/solution.py
+++ b/solution.py
@@ -397,7 +397,7 @@
     for copy in copies:
         copy.wait()
     folded = extent // 2
-    group = next(g for g in (12, 8, 6, 4, 2) if planes % g == 0)
+    group = next(g for g in (24, 12, 8, 6, 4, 2) if planes % g == 0)
     wide = 2 * LANES
     at_back = 3 * LANES
     at_y = at_back + 2 * wide
@@ -550,7 +550,7 @@
             scalar = jnp.sum(jnp.sum(partial, axis=1, keepdims=True), axis=0, keepdims=True)
             tile = jnp.where((lane == spot) & (row == part), sign * norm * scalar, tile)
     for k in range(devices):
-        out_refs[k][0:3 * padded_planes, :] = in_ref[lax.rem(mine + k, devices), 0:3 * padded_planes, :]
+        out_refs[k][0:3 * padded_planes, :] = in_ref[partner(mine, k, devices, 1), 0:3 * padded_planes, :]
         out_refs[k][3 * padded_planes:, :] = tile
 
 
@@ -565,7 +565,7 @@
     me = me_ref[0]
     for k in range(devices):
         value = ret_refs[k][...]
-        base = pl.multiple_of(lax.rem(me + devices - k, devices) * padded_planes, 8)
+        base = pl.multiple_of(partner(me, k, devices, -1) * padded_planes, 8)
         total = total + value[3 * padded_planes:]
         rest = value[2 * padded_planes:3 * padded_planes]
         re = jnp.concatenate([value[:padded_planes], rest[:, :half]], axis=1)
@@ -582,6 +582,11 @@
     out_ref[:, 0, :] = jnp.where(kept, kc[:, :padded] + local[:, :padded], 0.0)
     out_ref[:, 1, :] = jnp.where(kept, kc[:, padded:] + local[:, padded:], 0.0)
     sub_ref[:, 0, :] = total[0:2, :bands]
+
+
+def partner(device, k, count, sign):
+    half = count // 2
+    return ((device >> 1) + half + sign * (k >> 1)) % half * 2 + ((device & 1) ^ (k & 1))
 
 
 def pairs(count, k):
@@ -704,8 +709,8 @@
 
     returned = [outgoing[0]]
     for k in range(1, devices):
-        ring = [(d, (d + k) % devices) for d in range(devices)]
-        returned.append(lax.ppermute(outgoing[k], "tg", ring))
+        steps = [(d, partner(d, k, devices, 1)) for d in range(devices)]
+        returned.append(lax.ppermute(outgoing[k], "tg", steps))
     applied, subspace = pl.pallas_call(
         functools.partial(final_kernel, volume, devices),
         out_shape=(

time: 57.9 us -> 58.5 us (1.010)
  transfers between devices with their start and end apart: 14 -> 14, of which waited for: 4 -> 3; matrix products, arithmetic and copies ran while one was open for 0% -> 0% of each run, Pallas kernels for 39% -> 38%
where the time goes in v16:
time: 58.5 us; the launch traced here: 58.1 us
  Pallas kernels  26.9 us (46%)
  starting transfers between devices  22.2 us (38%)
  waiting for transfers between devices  6.81 us (12%)
  local copies, waits for them, and re-layouts  1.42 us (2%)
  between operations  0.78 us (1%)
    pallas_call x1, Pallas kernels, shards(): pl.pallas_call(functools.partial(plane_kernel, planes), out_shape=jax.Sha...  19.5 us
    ppermute x7, starting transfers between devices, shards(): returned.append(lax.ppermute(outgoing[k], 'tg', steps))  11.2 us
    all_to_all x1, starting transfers between devices, shards(): lax.all_to_all(sent, 'tg', split_axis=0, concat_axis=0, tiled=True)  7.27 us
    all_to_all x1, waiting for transfers between devices, shards(): lax.all_to_all(sent, 'tg', split_axis=0, concat_axis=0, tiled=True)  3.98 us
    ppermute x7, waiting for transfers between devices, shards(): returned.append(lax.ppermute(outgoing[k], 'tg', steps))  2.82 us
    pallas_call x1, Pallas kernels, shards(): pl.pallas_call(functools.partial(wave_kernel, extent), out_shape=(jax.Sha...  2.76 us
    pallas_call x1, Pallas kernels, shards(): pl.pallas_call(functools.partial(map_kernel, extent, sticks), out_shape=(...  2.3 us
    ppermute x3, starting transfers between devices, shards(): fields.append(lax.ppermute(received, 'band', pairs(bands, m)))  1.86 us
  transfers between devices with their start and end apart: 14, of which 3 were waited for; matrix products, arithmetic and copies ran while one was open for 0% of the time, Pallas kernels for 38%

profile of v16, /device:TPU:0, one launch (start us, length us, event | category | flops | bytes accessed | tf_op | source)
XLA Modules:
  0.0 58.1 jit_solution(1360880804251021242)
XLA Ops:
  0.6 2.8 %wave_to_planes.1 = (f32[8,72,128]{2,1,0:T(8,128)}, f32[192,256]{1,0:T(8,128)}, f32[384,128]{1,0:T(8,128)}, f32[192,128]{1,0:T(8,128)}, bf16[384,256]{1,0:T(8,12...) custom-call(s32[1]{0:T(128)} %bitcast.me_ref, s32[12,128]{1,0:T(8,128)} %bitcast.13, ...), custom_call_target="tpu_custom_call" | custom-call | tf_op jit(solution)/shard_map/wave_to_planes/pallas_call | solution.py:622
  3.4 7.3 %all-to-all-start = ((f32[8,72,128]{2,1,0:T(8,128)}), f32[8,72,128]{2,1,0:T(8,128)S(1)}, u32[]{:S(2)}, u32[]{:S(2)}) async-start(f32[8,72,128]{2,1,0:T(8,128)} %get-tuple-element.30), calls=%async_computation | async-start | bytes 589824 | tf_op jit(solution)/shard_map/all_to_all | solution.py:647
  10.7 0.7 %collective-permute-start.2 = (f32[384,128]{1,0:T(8,128)}, f32[384,128]{1,0:T(8,128)S(1)}, u32[]{:S(2)}, u32[]{:S(2)}) collective-permute-start(f32[384,128]{1,0:T(8,128)} %get-tuple-element.29.refs_1_), channel_id=1, source_target_pairs={{0,24},{8,16},{16,8},{24,0},{1,25},{9,17},{17,9},{25,1},{2,26},{10... | collective-permute-start | bytes 589832 | tf_op jit(solution)/shard_map/ppermute | solution.py:697
  11.3 0.9 %collective-permute-start.1 = (f32[384,128]{1,0:T(8,128)}, f32[384,128]{1,0:T(8,128)S(1)}, u32[]{:S(2)}, u32[]{:S(2)}) collective-permute-start(f32[384,128]{1,0:T(8,128)} %get-tuple-element.29.refs_1_), channel_id=1, source_target_pairs={{0,16},{8,24},{16,0},{24,8},{1,17},{9,25},{17,1},{25,9},{2,18},{10... | collective-permute-start | bytes 589832 | tf_op jit(solution)/shard_map/ppermute | solution.py:697
  12.3 0.3 collective-permute-start
  12.5 0.7 %copy-done.7 = s32[1536]{0:T(1024)S(1)} copy-done((s32[1536]{0:T(1024)S(1)}, s32[1536]{0:T(1024)}, u32[]{:S(2)}) %copy-start.7) | copy-done | bytes 6168
  13.2 0.7 %copy-done.8 = s32[1536]{0:T(1024)S(1)} copy-done((s32[1536]{0:T(1024)S(1)}, s32[1536]{0:T(1024)}, u32[]{:S(2)}) %copy-start.8) | copy-done | bytes 6168
  13.9 2.3 %stick_map.1 = (s32[128,128]{1,0:T(8,128)S(1)}, s32[128,128]{1,0:T(8,128)S(1)}, s32[16,128]{1,0:T(8,128)S(1)}, s32[12,128]{1,0:T(8,128)S(1)}, s32[12,128]{1,0:T(...) custom-call(s32[12,128]{1,0:T(8,128)S(1)} %bitcast.9, s32[12,128]{1,0:T(8,128)S(1)} %bitcast.11), custom_call_target="tpu_custom_call" | custom-call | flops 4000000000 | bytes 100000 | tf_op jit(solution)/shard_map/stick_map/pallas_call | solution.py:652
  16.2 0.1 pad_add_fusion.place_ref
  16.3 4.0 %all-to-all-done.recv_ref.refs_5_ = f32[8,72,128]{2,1,0:T(8,128)S(1)} async-done(((f32[8,72,128]{2,1,0:T(8,128)}), f32[8,72,128]{2,1,0:T(8,128)S(1)}, u32[]{:S(2)}, u32[]{:S(2)}) %all-to-all-start) | async-done | bytes 294944 | tf_op jit(solution)/shard_map/all_to_all | solution.py:647
  20.3 0.0 collective-permute-start.5
  20.3 1.5 %collective-permute-start.4 = (f32[8,72,128]{2,1,0:T(8,128)S(1)}, f32[8,72,128]{2,1,0:T(8,128)S(1)}, u32[]{:S(2)}, u32[]{:S(2)}) collective-permute-start(f32[8,72,128]{2,1,0:T(8,128)S(1)} %all-to-all-done.recv_ref.refs_5_), channel_id=1, source_target_pairs={{0,16},{8,24},{16,0},{24,8},{1,17},{9,25},{17,1},{25,9},{2,18},{10... | collective-permute-start | bytes 884744 | tf_op jit(solution)/shard_map/ppermute | solution.py:698
  21.8 0.0 collective-permute-done.2.refs_4_
  21.8 0.3 collective-permute-start.3
  22.2 19.5 %planes.1.refs_9_ = f32[8,80,128]{2,1,0:T(8,128)S(1)} custom-call(s32[16,128]{1,0:T(8,128)S(1)} %get-tuple-element.31.first_ref, s32[128,128]{1,0:T(8,128)S(1)} %get-tuple-element.32.even_ref, s32[128,128]{1,0:T(8,128)S(1)} %get-tuple-element.33.odd_ref, s32[12,128]{1,0:T(8,128)S(1)} %get-tuple-element.34.src_ref, s32[12,128]{1,0:T(8,128)S(1)} %get-tuple-element.35.dst_ref, ...), custom_call_target="tpu_custom_call" | custom-call | flops 20000000000 | bytes 10000000 | tf_op jit(solution)/shard_map/planes/pallas_call | solution.py:675
  41.7 0.0 collective-permute-done.1.refs_3_
  41.8 0.0 collective-permute-done.refs_2_
  41.8 0.0 collective-permute-done.4.refs_7_
  41.8 0.0 collective-permute-done.3.refs_6_
  41.8 1.0 %inner.1 = (f32[80,128]{1,0:T(8,128)S(1)}, f32[80,128]{1,0:T(8,128)S(1)}, f32[80,128]{1,0:T(8,128)S(1)}, f32[80,128]{1,0:T(8,128)S(1)}, f32[80,128]{1,0:T(8,128)...) custom-call(s32[2]{0:T(128)S(1)} %pad_add_fusion.place_ref, f32[192,256]{1,0:T(8,128)S(1)} %copy-done, ...), custom_call_target="tpu_custom_call" | custom-call | tf_op jit(solution)/shard_map/inner/pallas_call | solution.py:702
  42.8 1.5 %collective-permute-start.6 = (f32[80,128]{1,0:T(8,128)S(1)}, f32[80,128]{1,0:T(8,128)S(1)}, u32[]{:S(2)}, u32[]{:S(2)}) collective-permute-start(f32[80,128]{1,0:T(8,128)S(1)} %get-tuple-element.39), channel_id=1, source_target_pairs={{0,1},{1,0},{2,3},{3,2},{4,5},{5,4},{6,7},{7,6},{8,9},{9,8},{10,11... | collective-permute-start | bytes 122888 | tf_op jit(solution)/shard_map/ppermute | solution.py:713
  44.3 0.0 collective-permute-start.7
  44.3 1.6 %collective-permute-start.8 = (f32[80,128]{1,0:T(8,128)S(1)}, f32[80,128]{1,0:T(8,128)S(1)}, u32[]{:S(2)}, u32[]{:S(2)}) collective-permute-start(f32[80,128]{1,0:T(8,128)S(1)} %get-tuple-element.41), channel_id=1, source_target_pairs={{0,3},{1,2},{2,5},{3,4},{4,7},{5,6},{6,1},{7,0},{8,11},{9,10},{10,... | collective-permute-start | bytes 122888 | tf_op jit(solution)/shard_map/ppermute | solution.py:713
  45.9 2.8 %collective-permute-start.9 = (f32[80,128]{1,0:T(8,128)S(1)}, f32[80,128]{1,0:T(8,128)S(1)}, u32[]{:S(2)}, u32[]{:S(2)}) collective-permute-start(f32[80,128]{1,0:T(8,128)S(1)} %get-tuple-element.42), channel_id=1, source_target_pairs={{0,4},{1,5},{2,6},{3,7},{4,0},{5,1},{6,2},{7,3},{8,12},{9,13},{10,... | collective-permute-start | bytes 122888 | tf_op jit(solution)/shard_map/ppermute | solution.py:713
  48.7 0.8 %collective-permute-start.10 = (f32[80,128]{1,0:T(8,128)S(1)}, f32[80,128]{1,0:T(8,128)S(1)}, u32[]{:S(2)}, u32[]{:S(2)}) collective-permute-start(f32[80,128]{1,0:T(8,128)S(1)} %get-tuple-element.43), channel_id=1, source_target_pairs={{0,5},{1,4},{2,7},{3,6},{4,1},{5,0},{6,3},{7,2},{8,13},{9,12},{10,... | collective-permute-start | bytes 122888 | tf_op jit(solution)/shard_map/ppermute | solution.py:713
  49.5 2.4 %collective-permute-start.11 = (f32[80,128]{1,0:T(8,128)S(1)}, f32[80,128]{1,0:T(8,128)S(1)}, u32[]{:S(2)}, u32[]{:S(2)}) collective-permute-start(f32[80,128]{1,0:T(8,128)S(1)} %get-tuple-element.44), channel_id=1, source_target_pairs={{0,6},{1,7},{2,0},{3,1},{4,2},{5,3},{6,4},{7,5},{8,14},{9,15},{10,... | collective-permute-start | bytes 122888 | tf_op jit(solution)/shard_map/ppermute | solution.py:713
  51.9 0.0 collective-permute-done.7.refs_2_
  51.9 2.1 %collective-permute-start.12 = (f32[80,128]{1,0:T(8,128)S(1)}, f32[80,128]{1,0:T(8,128)S(1)}, u32[]{:S(2)}, u32[]{:S(2)}) collective-permute-start(f32[80,128]{1,0:T(8,128)S(1)} %get-tuple-element.45), channel_id=1, source_target_pairs={{0,7},{1,6},{2,1},{3,0},{4,3},{5,2},{6,5},{7,4},{8,15},{9,14},{10,... | collective-permute-start | bytes 122888 | tf_op jit(solution)/shard_map/ppermute | solution.py:713
  54.0 0.9 %collective-permute-done.10.refs_5_ = f32[80,128]{1,0:T(8,128)S(1)} collective-permute-done((f32[80,128]{1,0:T(8,128)S(1)}, f32[80,128]{1,0:T(8,128)S(1)}, u32[]{:S(2)}, u32[]{:S(2)}) %collective-permute-start.10) | collective-permute-done | bytes 40992 | tf_op jit(solution)/shard_map/ppermute | solution.py:713
  54.9 0.0 collective-permute-done.11.refs_6_
  54.9 1.9 %collective-permute-done.12.refs_7_ = f32[80,128]{1,0:T(8,128)S(1)} collective-permute-done((f32[80,128]{1,0:T(8,128)S(1)}, f32[80,128]{1,0:T(8,128)S(1)}, u32[]{:S(2)}, u32[]{:S(2)}) %collective-permute-start.12) | collective-permute-done | bytes 40992 | tf_op jit(solution)/shard_map/ppermute | solution.py:713
  56.8 1.3 %planes_to_wave.1 = (f32[192,2,128]{2,1,0:T(2,128)}, f32[2,1,4]{2,1,0:T(1,128)}) custom-call(s32[1]{0:T(128)} %bitcast.me_ref, f32[192,128]{1,0:T(8,128)S(1)} %copy-done.6, f32[80,128]{1,0:T(8,128)S(1)} %get-tuple-element.38.refs_0_, f32[80,128]{1,0:T(8,128)S(1)} %collective-permute-done.6.refs_1_, f32[80,128]{1,0:T(8,128)S(1)} %collective-permute-done.7.refs_2_, ...), custom_call_target="tpu_custom_call" | custom-call | tf_op jit(solution)/shard_map/planes_to_wave/pallas_call | solution.py:714
  (20 shorter events, 0.0 us)
Async XLA Ops:
  3.4 16.9 %all-to-all-start = ((f32[8,72,128]{2,1,0:T(8,128)}), f32[8,72,128]{2,1,0:T(8,128)S(1)}, u32[]{:S(2)}, u32[]{:S(2)}) async-start(f32[8,72,128]{2,1,0:T(8,128)} %get-tuple-element.30), calls=%async_computation | async-start | bytes 589824 | tf_op jit(solution)/shard_map/all_to_all | solution.py:647
  10.7 11.2 %collective-permute-start.2 = (f32[384,128]{1,0:T(8,128)}, f32[384,128]{1,0:T(8,128)S(1)}, u32[]{:S(2)}, u32[]{:S(2)}) collective-permute-start(f32[384,128]{1,0:T(8,128)} %get-tuple-element.29.refs_1_), channel_id=1, source_target_pairs={{0,24},{8,16},{16,8},{24,0},{1,25},{9,17},{17,9},{25,1},{2,26},{10... | collective-permute-start | bytes 589832 | tf_op jit(solution)/shard_map/ppermute | solution.py:697
  11.3 30.4 %collective-permute-start.1 = (f32[384,128]{1,0:T(8,128)}, f32[384,128]{1,0:T(8,128)S(1)}, u32[]{:S(2)}, u32[]{:S(2)}) collective-permute-start(f32[384,128]{1,0:T(8,128)} %get-tuple-element.29.refs_1_), channel_id=1, source_target_pairs={{0,16},{8,24},{16,0},{24,8},{1,17},{9,25},{17,1},{25,9},{2,18},{10... | collective-permute-start | bytes 589832 | tf_op jit(solution)/shard_map/ppermute | solution.py:697
  12.3 29.5 %collective-permute-start = (f32[384,128]{1,0:T(8,128)}, f32[384,128]{1,0:T(8,128)S(1)}, u32[]{:S(2)}, u32[]{:S(2)}) collective-permute-start(f32[384,128]{1,0:T(8,128)} %get-tuple-element.29.refs_1_), channel_id=1, source_target_pairs={{0,8},{8,0},{16,24},{24,16},{1,9},{9,1},{17,25},{25,17},{2,10},{10... | collective-permute-start | bytes 589832 | tf_op jit(solution)/shard_map/ppermute | solution.py:697
  12.5 0.7 %copy-start.7 = (s32[1536]{0:T(1024)S(1)}, s32[1536]{0:T(1024)}, u32[]{:S(2)}) copy-start(s32[1536]{0:T(1024)} %param.9) | copy-start | bytes 18436
  13.2 0.7 %copy-start.8 = (s32[1536]{0:T(1024)S(1)}, s32[1536]{0:T(1024)}, u32[]{:S(2)}) copy-start(s32[1536]{0:T(1024)} %param.8) | copy-start | bytes 18436
  20.3 21.5 %collective-permute-start.5 = (f32[8,72,128]{2,1,0:T(8,128)S(1)}, f32[8,72,128]{2,1,0:T(8,128)S(1)}, u32[]{:S(2)}, u32[]{:S(2)}) collective-permute-start(f32[8,72,128]{2,1,0:T(8,128)S(1)} %all-to-all-done.recv_ref.refs_5_), channel_id=1, source_target_pairs={{0,24},{8,16},{16,8},{24,0},{1,25},{9,17},{17,9},{25,1},{2,26},{10... | collective-permute-start | bytes 884744 | tf_op jit(solution)/shard_map/ppermute | solution.py:698
  20.3 21.5 %collective-permute-start.4 = (f32[8,72,128]{2,1,0:T(8,128)S(1)}, f32[8,72,128]{2,1,0:T(8,128)S(1)}, u32[]{:S(2)}, u32[]{:S(2)}) collective-permute-start(f32[8,72,128]{2,1,0:T(8,128)S(1)} %all-to-all-done.recv_ref.refs_5_), channel_id=1, source_target_pairs={{0,16},{8,24},{16,0},{24,8},{1,17},{9,25},{17,1},{25,9},{2,18},{10... | collective-permute-start | bytes 884744 | tf_op jit(solution)/shard_map/ppermute | solution.py:698
  21.8 20.0 %collective-permute-start.3 = (f32[8,72,128]{2,1,0:T(8,128)S(1)}, f32[8,72,128]{2,1,0:T(8,128)S(1)}, u32[]{:S(2)}, u32[]{:S(2)}) collective-permute-start(f32[8,72,128]{2,1,0:T(8,128)S(1)} %all-to-all-done.recv_ref.refs_5_), channel_id=1, source_target_pairs={{0,8},{8,0},{16,24},{24,16},{1,9},{9,1},{17,25},{25,17},{2,10},{10... | collective-permute-start | bytes 884744 | tf_op jit(solution)/shard_map/ppermute | solution.py:698
  22.2 19.7 %copy-start = (f32[192,256]{1,0:T(8,128)S(1)}, f32[192,256]{1,0:T(8,128)}, u32[]{:S(2)}) copy-start(f32[192,256]{1,0:T(8,128)} %get-tuple-element.28.refs_0_.refs_8_) | copy-start | bytes 589828
  22.2 19.7 %copy-start.5 = (f32[384,128]{1,0:T(8,128)S(1)}, f32[384,128]{1,0:T(8,128)}, u32[]{:S(2)}) copy-start(f32[384,128]{1,0:T(8,128)} %get-tuple-element.29.refs_1_) | copy-start | bytes 589828
  22.2 34.7 %copy-start.1 = (bf16[384,256]{1,0:T(8,128)(2,1)S(1)}, bf16[384,256]{1,0:T(8,128)(2,1)}, u32[]{:S(2)}) copy-start(bf16[384,256]{1,0:T(8,128)(2,1)} %get-tuple-element.46.refs_9_) | copy-start | bytes 589828
  22.2 34.7 %copy-start.2 = (bf16[384,256]{1,0:T(8,128)(2,1)S(1)}, bf16[384,256]{1,0:T(8,128)(2,1)}, u32[]{:S(2)}) copy-start(bf16[384,256]{1,0:T(8,128)(2,1)} %get-tuple-element.47.refs_10_) | copy-start | bytes 589828
  22.2 34.7 %copy-start.3 = (f32[192,192]{1,0:T(8,128)S(1)}, f32[192,192]{1,0:T(8,128)}, u32[]{:S(2)}) copy-start(f32[192,192]{1,0:T(8,128)} %get-tuple-element.48.refs_11_) | copy-start | bytes 442372
  22.2 34.7 %copy-start.4 = (f32[192,192]{1,0:T(8,128)S(1)}, f32[192,192]{1,0:T(8,128)}, u32[]{:S(2)}) copy-start(f32[192,192]{1,0:T(8,128)} %get-tuple-element.49.refs_12_) | copy-start | bytes 442372
  22.2 34.7 %copy-start.6 = (f32[192,128]{1,0:T(8,128)S(1)}, f32[192,128]{1,0:T(8,128)}, u32[]{:S(2)}) copy-start(f32[192,128]{1,0:T(8,128)} %get-tuple-element.27.len_ref) | copy-start | bytes 294916
  42.8 6.8 %collective-permute-start.6 = (f32[80,128]{1,0:T(8,128)S(1)}, f32[80,128]{1,0:T(8,128)S(1)}, u32[]{:S(2)}, u32[]{:S(2)}) collective-permute-start(f32[80,128]{1,0:T(8,128)S(1)} %get-tuple-element.39), channel_id=1, source_target_pairs={{0,1},{1,0},{2,3},{3,2},{4,5},{5,4},{6,7},{7,6},{8,9},{9,8},{10,11... | collective-permute-start | bytes 122888 | tf_op jit(solution)/shard_map/ppermute | solution.py:713
  44.3 7.7 %collective-permute-start.7 = (f32[80,128]{1,0:T(8,128)S(1)}, f32[80,128]{1,0:T(8,128)S(1)}, u32[]{:S(2)}, u32[]{:S(2)}) collective-permute-start(f32[80,128]{1,0:T(8,128)S(1)} %get-tuple-element.40), channel_id=1, source_target_pairs={{0,2},{1,3},{2,4},{3,5},{4,6},{5,7},{6,0},{7,1},{8,10},{9,11},{10,... | collective-permute-start | bytes 122888 | tf_op jit(solution)/shard_map/ppermute | solution.py:713
  44.3 9.7 %collective-permute-start.8 = (f32[80,128]{1,0:T(8,128)S(1)}, f32[80,128]{1,0:T(8,128)S(1)}, u32[]{:S(2)}, u32[]{:S(2)}) collective-permute-start(f32[80,128]{1,0:T(8,128)S(1)} %get-tuple-element.41), channel_id=1, source_target_pairs={{0,3},{1,2},{2,5},{3,4},{4,7},{5,6},{6,1},{7,0},{8,11},{9,10},{10,... | collective-permute-start | bytes 122888 | tf_op jit(solution)/shard_map/ppermute | solution.py:713
  45.9 8.1 %collective-permute-start.9 = (f32[80,128]{1,0:T(8,128)S(1)}, f32[80,128]{1,0:T(8,128)S(1)}, u32[]{:S(2)}, u32[]{:S(2)}) collective-permute-start(f32[80,128]{1,0:T(8,128)S(1)} %get-tuple-element.42), channel_id=1, source_target_pairs={{0,4},{1,5},{2,6},{3,7},{4,0},{5,1},{6,2},{7,3},{8,12},{9,13},{10,... | collective-permute-start | bytes 122888 | tf_op jit(solution)/shard_map/ppermute | solution.py:713
  48.7 6.2 %collective-permute-start.10 = (f32[80,128]{1,0:T(8,128)S(1)}, f32[80,128]{1,0:T(8,128)S(1)}, u32[]{:S(2)}, u32[]{:S(2)}) collective-permute-start(f32[80,128]{1,0:T(8,128)S(1)} %get-tuple-element.43), channel_id=1, source_target_pairs={{0,5},{1,4},{2,7},{3,6},{4,1},{5,0},{6,3},{7,2},{8,13},{9,12},{10,... | collective-permute-start | bytes 122888 | tf_op jit(solution)/shard_map/ppermute | solution.py:713
  49.5 5.3 %collective-permute-start.11 = (f32[80,128]{1,0:T(8,128)S(1)}, f32[80,128]{1,0:T(8,128)S(1)}, u32[]{:S(2)}, u32[]{:S(2)}) collective-permute-start(f32[80,128]{1,0:T(8,128)S(1)} %get-tuple-element.44), channel_id=1, source_target_pairs={{0,6},{1,7},{2,0},{3,1},{4,2},{5,3},{6,4},{7,5},{8,14},{9,15},{10,... | collective-permute-start | bytes 122888 | tf_op jit(solution)/shard_map/ppermute | solution.py:713
  51.9 4.9 %collective-permute-start.12 = (f32[80,128]{1,0:T(8,128)S(1)}, f32[80,128]{1,0:T(8,128)S(1)}, u32[]{:S(2)}, u32[]{:S(2)}) collective-permute-start(f32[80,128]{1,0:T(8,128)S(1)} %get-tuple-element.45), channel_id=1, source_target_pairs={{0,7},{1,6},{2,1},{3,0},{4,3},{5,2},{6,5},{7,4},{8,15},{9,14},{10,... | collective-permute-start | bytes 122888 | tf_op jit(solution)/shard_map/ppermute | solution.py:713

commit v17 on v15

--- a/solution.py
+++ b/solution.py
@@ -397,7 +397,7 @@
     for copy in copies:
         copy.wait()
     folded = extent // 2
-    group = next(g for g in (12, 8, 6, 4, 2) if planes % g == 0)
+    group = next(g for g in (24, 12, 8, 6, 4, 2) if planes % g == 0)
     wide = 2 * LANES
     at_back = 3 * LANES
     at_y = at_back + 2 * wide
@@ -702,10 +702,10 @@
         name="inner",
     )(places, kc, *waves, *fields, weighted)
 
-    returned = [outgoing[0]]
-    for k in range(1, devices):
+    returned = list(outgoing)
+    for k in sorted(range(1, devices), key=lambda k: abs(k - devices // 2)):
         ring = [(d, (d + k) % devices) for d in range(devices)]
-        returned.append(lax.ppermute(outgoing[k], "tg", ring))
+        returned[k] = lax.ppermute(outgoing[k], "tg", ring)
     applied, subspace = pl.pallas_call(
         functools.partial(final_kernel, volume, devices),
         out_shape=(

time: 57.9 us -> 57.6 us (level)
  transfers between devices with their start and end apart: 14 -> 14, of which waited for: 4 -> 4; matrix products, arithmetic and copies ran while one was open for 0% -> 0% of each run, Pallas kernels for 39% -> 38%
where the time goes in v17:
time: 57.6 us; the launch traced here: 57.2 us
  Pallas kernels  26.9 us (47%)
  starting transfers between devices  21.7 us (38%)
  waiting for transfers between devices  6.37 us (11%)
  local copies, waits for them, and re-layouts  1.42 us (2%)
  between operations  0.78 us (1%)
    pallas_call x1, Pallas kernels, shards(): pl.pallas_call(functools.partial(plane_kernel, planes), out_shape=jax.Sha...  19.5 us
    ppermute x7, starting transfers between devices, shards(): returned[k] = lax.ppermute(outgoing[k], 'tg', ring)  10.7 us
    all_to_all x1, starting transfers between devices, shards(): lax.all_to_all(sent, 'tg', split_axis=0, concat_axis=0, tiled=True)  7.27 us
    all_to_all x1, waiting for transfers between devices, shards(): lax.all_to_all(sent, 'tg', split_axis=0, concat_axis=0, tiled=True)  3.98 us
    pallas_call x1, Pallas kernels, shards(): pl.pallas_call(functools.partial(wave_kernel, extent), out_shape=(jax.Sha...  2.76 us
    ppermute x7, waiting for transfers between devices, shards(): returned[k] = lax.ppermute(outgoing[k], 'tg', ring)  2.37 us
    pallas_call x1, Pallas kernels, shards(): pl.pallas_call(functools.partial(map_kernel, extent, sticks), out_shape=(...  2.3 us
    ppermute x3, starting transfers between devices, shards(): fields.append(lax.ppermute(received, 'band', pairs(bands, m)))  1.86 us
  transfers between devices with their start and end apart: 14, of which 4 were waited for; matrix products, arithmetic and copies ran while one was open for 0% of the time, Pallas kernels for 38%

profile of v17, /device:TPU:0, one launch (start us, length us, event | category | flops | bytes accessed | tf_op | source)
XLA Modules:
  0.0 57.2 jit_solution(8679358855454581016)
XLA Ops:
  0.6 2.8 %wave_to_planes.1 = (f32[8,72,128]{2,1,0:T(8,128)}, f32[192,256]{1,0:T(8,128)}, f32[384,128]{1,0:T(8,128)}, f32[192,128]{1,0:T(8,128)}, bf16[384,256]{1,0:T(8,12...) custom-call(s32[1]{0:T(128)} %bitcast.me_ref, s32[12,128]{1,0:T(8,128)} %bitcast.13, ...), custom_call_target="tpu_custom_call" | custom-call | tf_op jit(solution)/shard_map/wave_to_planes/pallas_call | solution.py:617
  3.4 7.3 %all-to-all-start = ((f32[8,72,128]{2,1,0:T(8,128)}), f32[8,72,128]{2,1,0:T(8,128)S(1)}, u32[]{:S(2)}, u32[]{:S(2)}) async-start(f32[8,72,128]{2,1,0:T(8,128)} %get-tuple-element.30), calls=%async_computation | async-start | bytes 589824 | tf_op jit(solution)/shard_map/all_to_all | solution.py:642
  10.7 0.7 %collective-permute-start.2 = (f32[384,128]{1,0:T(8,128)}, f32[384,128]{1,0:T(8,128)S(1)}, u32[]{:S(2)}, u32[]{:S(2)}) collective-permute-start(f32[384,128]{1,0:T(8,128)} %get-tuple-element.29.refs_1_), channel_id=1, source_target_pairs={{0,24},{8,16},{16,8},{24,0},{1,25},{9,17},{17,9},{25,1},{2,26},{10... | collective-permute-start | bytes 589832 | tf_op jit(solution)/shard_map/ppermute | solution.py:692
  11.3 0.9 %collective-permute-start.1 = (f32[384,128]{1,0:T(8,128)}, f32[384,128]{1,0:T(8,128)S(1)}, u32[]{:S(2)}, u32[]{:S(2)}) collective-permute-start(f32[384,128]{1,0:T(8,128)} %get-tuple-element.29.refs_1_), channel_id=1, source_target_pairs={{0,16},{8,24},{16,0},{24,8},{1,17},{9,25},{17,1},{25,9},{2,18},{10... | collective-permute-start | bytes 589832 | tf_op jit(solution)/shard_map/ppermute | solution.py:692
  12.3 0.3 collective-permute-start
  12.5 0.7 %copy-done.7 = s32[1536]{0:T(1024)S(1)} copy-done((s32[1536]{0:T(1024)S(1)}, s32[1536]{0:T(1024)}, u32[]{:S(2)}) %copy-start.7) | copy-done | bytes 6168
  13.2 0.7 %copy-done.8 = s32[1536]{0:T(1024)S(1)} copy-done((s32[1536]{0:T(1024)S(1)}, s32[1536]{0:T(1024)}, u32[]{:S(2)}) %copy-start.8) | copy-done | bytes 6168
  13.9 2.3 %stick_map.1 = (s32[128,128]{1,0:T(8,128)S(1)}, s32[128,128]{1,0:T(8,128)S(1)}, s32[16,128]{1,0:T(8,128)S(1)}, s32[12,128]{1,0:T(8,128)S(1)}, s32[12,128]{1,0:T(...) custom-call(s32[12,128]{1,0:T(8,128)S(1)} %bitcast.9, s32[12,128]{1,0:T(8,128)S(1)} %bitcast.11), custom_call_target="tpu_custom_call" | custom-call | flops 4000000000 | bytes 100000 | tf_op jit(solution)/shard_map/stick_map/pallas_call | solution.py:647
  16.2 0.1 pad_add_fusion.place_ref
  16.3 4.0 %all-to-all-done.recv_ref.refs_5_ = f32[8,72,128]{2,1,0:T(8,128)S(1)} async-done(((f32[8,72,128]{2,1,0:T(8,128)}), f32[8,72,128]{2,1,0:T(8,128)S(1)}, u32[]{:S(2)}, u32[]{:S(2)}) %all-to-all-start) | async-done | bytes 294944 | tf_op jit(solution)/shard_map/all_to_all | solution.py:642
  20.3 1.5 %collective-permute-start.4 = (f32[8,72,128]{2,1,0:T(8,128)S(1)}, f32[8,72,128]{2,1,0:T(8,128)S(1)}, u32[]{:S(2)}, u32[]{:S(2)}) collective-permute-start(f32[8,72,128]{2,1,0:T(8,128)S(1)} %all-to-all-done.recv_ref.refs_5_), channel_id=1, source_target_pairs={{0,16},{8,24},{16,0},{24,8},{1,17},{9,25},{17,1},{25,9},{2,18},{10... | collective-permute-start | bytes 884744 | tf_op jit(solution)/shard_map/ppermute | solution.py:693
  21.8 0.0 collective-permute-done.2.refs_4_
  21.8 0.3 collective-permute-start.3
  22.2 19.5 %planes.1.refs_9_ = f32[8,80,128]{2,1,0:T(8,128)S(1)} custom-call(s32[16,128]{1,0:T(8,128)S(1)} %get-tuple-element.31.first_ref, s32[128,128]{1,0:T(8,128)S(1)} %get-tuple-element.32.even_ref, s32[128,128]{1,0:T(8,128)S(1)} %get-tuple-element.33.odd_ref, s32[12,128]{1,0:T(8,128)S(1)} %get-tuple-element.34.src_ref, s32[12,128]{1,0:T(8,128)S(1)} %get-tuple-element.35.dst_ref, ...), custom_call_target="tpu_custom_call" | custom-call | flops 20000000000 | bytes 10000000 | tf_op jit(solution)/shard_map/planes/pallas_call | solution.py:670
  41.7 0.0 collective-permute-done.1.refs_3_
  41.8 0.0 collective-permute-done.refs_2_
  41.8 0.0 collective-permute-done.4.refs_7_
  41.8 0.0 collective-permute-done.3.refs_6_
  41.8 1.0 %inner.1 = (f32[80,128]{1,0:T(8,128)S(1)}, f32[80,128]{1,0:T(8,128)S(1)}, f32[80,128]{1,0:T(8,128)S(1)}, f32[80,128]{1,0:T(8,128)S(1)}, f32[80,128]{1,0:T(8,128)...) custom-call(s32[2]{0:T(128)S(1)} %pad_add_fusion.place_ref, f32[192,256]{1,0:T(8,128)S(1)} %copy-done, ...), custom_call_target="tpu_custom_call" | custom-call | tf_op jit(solution)/shard_map/inner/pallas_call | solution.py:697
  42.8 1.5 %collective-permute-start.6 = (f32[80,128]{1,0:T(8,128)S(1)}, f32[80,128]{1,0:T(8,128)S(1)}, u32[]{:S(2)}, u32[]{:S(2)}) collective-permute-start(f32[80,128]{1,0:T(8,128)S(1)} %get-tuple-element.39), channel_id=1, source_target_pairs={{0,1},{1,2},{2,3},{3,4},{4,5},{5,6},{6,7},{7,0},{8,9},{9,10},{10,1... | collective-permute-start | bytes 122888 | tf_op jit(solution)/shard_map/ppermute | solution.py:708
  44.2 0.0 collective-permute-start.7
  44.2 1.7 %collective-permute-start.8 = (f32[80,128]{1,0:T(8,128)S(1)}, f32[80,128]{1,0:T(8,128)S(1)}, u32[]{:S(2)}, u32[]{:S(2)}) collective-permute-start(f32[80,128]{1,0:T(8,128)S(1)} %get-tuple-element.41), channel_id=1, source_target_pairs={{0,3},{1,4},{2,5},{3,6},{4,7},{5,0},{6,1},{7,2},{8,11},{9,12},{10,... | collective-permute-start | bytes 122888 | tf_op jit(solution)/shard_map/ppermute | solution.py:708
  46.0 3.2 %collective-permute-start.9 = (f32[80,128]{1,0:T(8,128)S(1)}, f32[80,128]{1,0:T(8,128)S(1)}, u32[]{:S(2)}, u32[]{:S(2)}) collective-permute-start(f32[80,128]{1,0:T(8,128)S(1)} %get-tuple-element.42), channel_id=1, source_target_pairs={{0,4},{1,5},{2,6},{3,7},{4,0},{5,1},{6,2},{7,3},{8,12},{9,13},{10,... | collective-permute-start | bytes 122888 | tf_op jit(solution)/shard_map/ppermute | solution.py:708
  49.1 0.9 %collective-permute-start.10 = (f32[80,128]{1,0:T(8,128)S(1)}, f32[80,128]{1,0:T(8,128)S(1)}, u32[]{:S(2)}, u32[]{:S(2)}) collective-permute-start(f32[80,128]{1,0:T(8,128)S(1)} %get-tuple-element.43), channel_id=1, source_target_pairs={{0,5},{1,6},{2,7},{3,0},{4,1},{5,2},{6,3},{7,4},{8,13},{9,14},{10,... | collective-permute-start | bytes 122888 | tf_op jit(solution)/shard_map/ppermute | solution.py:708
  50.1 0.0 collective-permute-done.6.refs_1_
  50.1 1.8 %collective-permute-start.11 = (f32[80,128]{1,0:T(8,128)S(1)}, f32[80,128]{1,0:T(8,128)S(1)}, u32[]{:S(2)}, u32[]{:S(2)}) collective-permute-start(f32[80,128]{1,0:T(8,128)S(1)} %get-tuple-element.44), channel_id=1, source_target_pairs={{0,6},{1,7},{2,0},{3,1},{4,2},{5,3},{6,4},{7,5},{8,14},{9,15},{10,... | collective-permute-start | bytes 122888 | tf_op jit(solution)/shard_map/ppermute | solution.py:708
  51.9 0.0 collective-permute-done.7.refs_2_
  51.9 1.6 %collective-permute-start.12 = (f32[80,128]{1,0:T(8,128)S(1)}, f32[80,128]{1,0:T(8,128)S(1)}, u32[]{:S(2)}, u32[]{:S(2)}) collective-permute-start(f32[80,128]{1,0:T(8,128)S(1)} %get-tuple-element.45), channel_id=1, source_target_pairs={{0,7},{1,0},{2,1},{3,2},{4,3},{5,4},{6,5},{7,6},{8,15},{9,8},{10,9... | collective-permute-start | bytes 122888 | tf_op jit(solution)/shard_map/ppermute | solution.py:708
  53.5 0.7 %collective-permute-done.10.refs_5_ = f32[80,128]{1,0:T(8,128)S(1)} collective-permute-done((f32[80,128]{1,0:T(8,128)S(1)}, f32[80,128]{1,0:T(8,128)S(1)}, u32[]{:S(2)}, u32[]{:S(2)}) %collective-permute-start.10) | collective-permute-done | bytes 40992 | tf_op jit(solution)/shard_map/ppermute | solution.py:708
  54.3 0.5 collective-permute-done.11.refs_6_
  54.8 1.2 %collective-permute-done.12.refs_7_ = f32[80,128]{1,0:T(8,128)S(1)} collective-permute-done((f32[80,128]{1,0:T(8,128)S(1)}, f32[80,128]{1,0:T(8,128)S(1)}, u32[]{:S(2)}, u32[]{:S(2)}) %collective-permute-start.12) | collective-permute-done | bytes 40992 | tf_op jit(solution)/shard_map/ppermute | solution.py:708
  55.9 1.3 %planes_to_wave.1 = (f32[192,2,128]{2,1,0:T(2,128)}, f32[2,1,4]{2,1,0:T(1,128)}) custom-call(s32[1]{0:T(128)} %bitcast.me_ref, f32[192,128]{1,0:T(8,128)S(1)} %copy-done.6, f32[80,128]{1,0:T(8,128)S(1)} %get-tuple-element.38.refs_0_, f32[80,128]{1,0:T(8,128)S(1)} %collective-permute-done.6.refs_1_, f32[80,128]{1,0:T(8,128)S(1)} %collective-permute-done.7.refs_2_, ...), custom_call_target="tpu_custom_call" | custom-call | tf_op jit(solution)/shard_map/planes_to_wave/pallas_call | solution.py:709
  (20 shorter events, 0.0 us)
Async XLA Ops:
  3.4 16.9 %all-to-all-start = ((f32[8,72,128]{2,1,0:T(8,128)}), f32[8,72,128]{2,1,0:T(8,128)S(1)}, u32[]{:S(2)}, u32[]{:S(2)}) async-start(f32[8,72,128]{2,1,0:T(8,128)} %get-tuple-element.30), calls=%async_computation | async-start | bytes 589824 | tf_op jit(solution)/shard_map/all_to_all | solution.py:642
  10.7 11.2 %collective-permute-start.2 = (f32[384,128]{1,0:T(8,128)}, f32[384,128]{1,0:T(8,128)S(1)}, u32[]{:S(2)}, u32[]{:S(2)}) collective-permute-start(f32[384,128]{1,0:T(8,128)} %get-tuple-element.29.refs_1_), channel_id=1, source_target_pairs={{0,24},{8,16},{16,8},{24,0},{1,25},{9,17},{17,9},{25,1},{2,26},{10... | collective-permute-start | bytes 589832 | tf_op jit(solution)/shard_map/ppermute | solution.py:692
  11.3 30.4 %collective-permute-start.1 = (f32[384,128]{1,0:T(8,128)}, f32[384,128]{1,0:T(8,128)S(1)}, u32[]{:S(2)}, u32[]{:S(2)}) collective-permute-start(f32[384,128]{1,0:T(8,128)} %get-tuple-element.29.refs_1_), channel_id=1, source_target_pairs={{0,16},{8,24},{16,0},{24,8},{1,17},{9,25},{17,1},{25,9},{2,18},{10... | collective-permute-start | bytes 589832 | tf_op jit(solution)/shard_map/ppermute | solution.py:692
  12.3 29.5 %collective-permute-start = (f32[384,128]{1,0:T(8,128)}, f32[384,128]{1,0:T(8,128)S(1)}, u32[]{:S(2)}, u32[]{:S(2)}) collective-permute-start(f32[384,128]{1,0:T(8,128)} %get-tuple-element.29.refs_1_), channel_id=1, source_target_pairs={{0,8},{8,0},{16,24},{24,16},{1,9},{9,1},{17,25},{25,17},{2,10},{10... | collective-permute-start | bytes 589832 | tf_op jit(solution)/shard_map/ppermute | solution.py:692
  12.5 0.7 %copy-start.7 = (s32[1536]{0:T(1024)S(1)}, s32[1536]{0:T(1024)}, u32[]{:S(2)}) copy-start(s32[1536]{0:T(1024)} %param.9) | copy-start | bytes 18436
  13.2 0.7 %copy-start.8 = (s32[1536]{0:T(1024)S(1)}, s32[1536]{0:T(1024)}, u32[]{:S(2)}) copy-start(s32[1536]{0:T(1024)} %param.8) | copy-start | bytes 18436
  20.3 21.5 %collective-permute-start.5 = (f32[8,72,128]{2,1,0:T(8,128)S(1)}, f32[8,72,128]{2,1,0:T(8,128)S(1)}, u32[]{:S(2)}, u32[]{:S(2)}) collective-permute-start(f32[8,72,128]{2,1,0:T(8,128)S(1)} %all-to-all-done.recv_ref.refs_5_), channel_id=1, source_target_pairs={{0,24},{8,16},{16,8},{24,0},{1,25},{9,17},{17,9},{25,1},{2,26},{10... | collective-permute-start | bytes 884744 | tf_op jit(solution)/shard_map/ppermute | solution.py:693
  20.3 21.5 %collective-permute-start.4 = (f32[8,72,128]{2,1,0:T(8,128)S(1)}, f32[8,72,128]{2,1,0:T(8,128)S(1)}, u32[]{:S(2)}, u32[]{:S(2)}) collective-permute-start(f32[8,72,128]{2,1,0:T(8,128)S(1)} %all-to-all-done.recv_ref.refs_5_), channel_id=1, source_target_pairs={{0,16},{8,24},{16,0},{24,8},{1,17},{9,25},{17,1},{25,9},{2,18},{10... | collective-permute-start | bytes 884744 | tf_op jit(solution)/shard_map/ppermute | solution.py:693
  21.8 20.0 %collective-permute-start.3 = (f32[8,72,128]{2,1,0:T(8,128)S(1)}, f32[8,72,128]{2,1,0:T(8,128)S(1)}, u32[]{:S(2)}, u32[]{:S(2)}) collective-permute-start(f32[8,72,128]{2,1,0:T(8,128)S(1)} %all-to-all-done.recv_ref.refs_5_), channel_id=1, source_target_pairs={{0,8},{8,0},{16,24},{24,16},{1,9},{9,1},{17,25},{25,17},{2,10},{10... | collective-permute-start | bytes 884744 | tf_op jit(solution)/shard_map/ppermute | solution.py:693
  22.2 19.7 %copy-start = (f32[192,256]{1,0:T(8,128)S(1)}, f32[192,256]{1,0:T(8,128)}, u32[]{:S(2)}) copy-start(f32[192,256]{1,0:T(8,128)} %get-tuple-element.28.refs_0_.refs_8_) | copy-start | bytes 589828
  22.2 19.7 %copy-start.5 = (f32[384,128]{1,0:T(8,128)S(1)}, f32[384,128]{1,0:T(8,128)}, u32[]{:S(2)}) copy-start(f32[384,128]{1,0:T(8,128)} %get-tuple-element.29.refs_1_) | copy-start | bytes 589828
  22.2 33.8 %copy-start.1 = (bf16[384,256]{1,0:T(8,128)(2,1)S(1)}, bf16[384,256]{1,0:T(8,128)(2,1)}, u32[]{:S(2)}) copy-start(bf16[384,256]{1,0:T(8,128)(2,1)} %get-tuple-element.46.refs_9_) | copy-start | bytes 589828
  22.2 33.8 %copy-start.2 = (bf16[384,256]{1,0:T(8,128)(2,1)S(1)}, bf16[384,256]{1,0:T(8,128)(2,1)}, u32[]{:S(2)}) copy-start(bf16[384,256]{1,0:T(8,128)(2,1)} %get-tuple-element.47.refs_10_) | copy-start | bytes 589828
  22.2 33.8 %copy-start.3 = (f32[192,192]{1,0:T(8,128)S(1)}, f32[192,192]{1,0:T(8,128)}, u32[]{:S(2)}) copy-start(f32[192,192]{1,0:T(8,128)} %get-tuple-element.48.refs_11_) | copy-start | bytes 442372
  22.2 33.7 %copy-start.4 = (f32[192,192]{1,0:T(8,128)S(1)}, f32[192,192]{1,0:T(8,128)}, u32[]{:S(2)}) copy-start(f32[192,192]{1,0:T(8,128)} %get-tuple-element.49.refs_12_) | copy-start | bytes 442372
  22.2 33.7 %copy-start.6 = (f32[192,128]{1,0:T(8,128)S(1)}, f32[192,128]{1,0:T(8,128)}, u32[]{:S(2)}) copy-start(f32[192,128]{1,0:T(8,128)} %get-tuple-element.27.len_ref) | copy-start | bytes 294916
  42.8 7.3 %collective-permute-start.6 = (f32[80,128]{1,0:T(8,128)S(1)}, f32[80,128]{1,0:T(8,128)S(1)}, u32[]{:S(2)}, u32[]{:S(2)}) collective-permute-start(f32[80,128]{1,0:T(8,128)S(1)} %get-tuple-element.39), channel_id=1, source_target_pairs={{0,1},{1,2},{2,3},{3,4},{4,5},{5,6},{6,7},{7,0},{8,9},{9,10},{10,1... | collective-permute-start | bytes 122888 | tf_op jit(solution)/shard_map/ppermute | solution.py:708
  44.2 7.7 %collective-permute-start.7 = (f32[80,128]{1,0:T(8,128)S(1)}, f32[80,128]{1,0:T(8,128)S(1)}, u32[]{:S(2)}, u32[]{:S(2)}) collective-permute-start(f32[80,128]{1,0:T(8,128)S(1)} %get-tuple-element.40), channel_id=1, source_target_pairs={{0,2},{1,3},{2,4},{3,5},{4,6},{5,7},{6,0},{7,1},{8,10},{9,11},{10,... | collective-permute-start | bytes 122888 | tf_op jit(solution)/shard_map/ppermute | solution.py:708
  44.2 9.3 %collective-permute-start.8 = (f32[80,128]{1,0:T(8,128)S(1)}, f32[80,128]{1,0:T(8,128)S(1)}, u32[]{:S(2)}, u32[]{:S(2)}) collective-permute-start(f32[80,128]{1,0:T(8,128)S(1)} %get-tuple-element.41), channel_id=1, source_target_pairs={{0,3},{1,4},{2,5},{3,6},{4,7},{5,0},{6,1},{7,2},{8,11},{9,12},{10,... | collective-permute-start | bytes 122888 | tf_op jit(solution)/shard_map/ppermute | solution.py:708
  46.0 7.6 %collective-permute-start.9 = (f32[80,128]{1,0:T(8,128)S(1)}, f32[80,128]{1,0:T(8,128)S(1)}, u32[]{:S(2)}, u32[]{:S(2)}) collective-permute-start(f32[80,128]{1,0:T(8,128)S(1)} %get-tuple-element.42), channel_id=1, source_target_pairs={{0,4},{1,5},{2,6},{3,7},{4,0},{5,1},{6,2},{7,3},{8,12},{9,13},{10,... | collective-permute-start | bytes 122888 | tf_op jit(solution)/shard_map/ppermute | solution.py:708
  49.1 5.1 %collective-permute-start.10 = (f32[80,128]{1,0:T(8,128)S(1)}, f32[80,128]{1,0:T(8,128)S(1)}, u32[]{:S(2)}, u32[]{:S(2)}) collective-permute-start(f32[80,128]{1,0:T(8,128)S(1)} %get-tuple-element.43), channel_id=1, source_target_pairs={{0,5},{1,6},{2,7},{3,0},{4,1},{5,2},{6,3},{7,4},{8,13},{9,14},{10,... | collective-permute-start | bytes 122888 | tf_op jit(solution)/shard_map/ppermute | solution.py:708
  50.1 4.7 %collective-permute-start.11 = (f32[80,128]{1,0:T(8,128)S(1)}, f32[80,128]{1,0:T(8,128)S(1)}, u32[]{:S(2)}, u32[]{:S(2)}) collective-permute-start(f32[80,128]{1,0:T(8,128)S(1)} %get-tuple-element.44), channel_id=1, source_target_pairs={{0,6},{1,7},{2,0},{3,1},{4,2},{5,3},{6,4},{7,5},{8,14},{9,15},{10,... | collective-permute-start | bytes 122888 | tf_op jit(solution)/shard_map/ppermute | solution.py:708
  51.9 4.0 %collective-permute-start.12 = (f32[80,128]{1,0:T(8,128)S(1)}, f32[80,128]{1,0:T(8,128)S(1)}, u32[]{:S(2)}, u32[]{:S(2)}) collective-permute-start(f32[80,128]{1,0:T(8,128)S(1)} %get-tuple-element.45), channel_id=1, source_target_pairs={{0,7},{1,0},{2,1},{3,2},{4,3},{5,4},{6,5},{7,6},{8,15},{9,8},{10,9... | collective-permute-start | bytes 122888 | tf_op jit(solution)/shard_map/ppermute | solution.py:708

commit v18 on v17

--- a/solution.py
+++ b/solution.py
@@ -563,8 +563,8 @@
     bands = sub_ref.shape[2]
     total = jnp.zeros((8, LANES), F32)
     me = me_ref[0]
-    for k in range(devices):
-        value = ret_refs[k][...]
+    for i, k in enumerate(far_first(devices)):
+        value = ret_refs[i][...]
         base = pl.multiple_of(lax.rem(me + devices - k, devices) * padded_planes, 8)
         total = total + value[3 * padded_planes:]
         rest = value[2 * padded_planes:3 * padded_planes]
@@ -582,6 +582,10 @@
     out_ref[:, 0, :] = jnp.where(kept, kc[:, :padded] + local[:, :padded], 0.0)
     out_ref[:, 1, :] = jnp.where(kept, kc[:, padded:] + local[:, padded:], 0.0)
     sub_ref[:, 0, :] = total[0:2, :bands]
+
+
+def far_first(count):
+    return [0] + sorted(range(1, count), key=lambda k: abs(k - count // 2))
 
 
 def pairs(count, k):
@@ -703,7 +707,7 @@
     )(places, kc, *waves, *fields, weighted)
 
     returned = list(outgoing)
-    for k in sorted(range(1, devices), key=lambda k: abs(k - devices // 2)):
+    for k in far_first(devices)[1:]:
         ring = [(d, (d + k) % devices) for d in range(devices)]
         returned[k] = lax.ppermute(outgoing[k], "tg", ring)
     applied, subspace = pl.pallas_call(
@@ -716,7 +720,7 @@
         scratch_shapes=[pltpu.VMEM((2 * total_planes, 2 * LANES), F32)],
         compiler_params=params(6 + 6 * total_planes / 192),
         name="planes_to_wave",
-    )(me.reshape(1), lengths, *returned, kc, whi, wlo, shift_cos, shift_sin)
+    )(me.reshape(1), lengths, *[returned[k] for k in far_first(devices)], kc, whi, wlo, shift_cos, shift_sin)
     return applied.reshape(1, sticks, 2, padded), subspace
 
 

time: 57.6 us -> 59.9 us (1.040)
  starting transfers between devices: 21.7 us -> 24.4 us
    ppermute x7, starting transfers between devices: 10.7 us -> 13.4 us  [shards(): returned[k] = lax.ppermute(outgoing[k], 'tg', ring)]
  transfers between devices with their start and end apart: 14 -> 14, of which waited for: 4 -> 2; matrix products, arithmetic and copies ran while one was open for 0% -> 0% of each run, Pallas kernels for 38% -> 37%
where the time goes in v18:
time: 59.9 us; the launch traced here: 59.5 us
  Pallas kernels  26.9 us (45%)
  starting transfers between devices  24.4 us (41%)
  waiting for transfers between devices  5.97 us (10%)
  local copies, waits for them, and re-layouts  1.42 us (2%)
  between operations  0.79 us (1%)
    pallas_call x1, Pallas kernels, shards(): pl.pallas_call(functools.partial(plane_kernel, planes), out_shape=jax.Sha...  19.5 us
    ppermute x7, starting transfers between devices, shards(): returned[k] = lax.ppermute(outgoing[k], 'tg', ring)  13.4 us
    all_to_all x1, starting transfers between devices, shards(): lax.all_to_all(sent, 'tg', split_axis=0, concat_axis=0, tiled=True)  7.27 us
    all_to_all x1, waiting for transfers between devices, shards(): lax.all_to_all(sent, 'tg', split_axis=0, concat_axis=0, tiled=True)  3.98 us
    pallas_call x1, Pallas kernels, shards(): pl.pallas_call(functools.partial(wave_kernel, extent), out_shape=(jax.Sha...  2.76 us
    pallas_call x1, Pallas kernels, shards(): pl.pallas_call(functools.partial(map_kernel, extent, sticks), out_shape=(...  2.3 us
    ppermute x7, waiting for transfers between devices, shards(): returned[k] = lax.ppermute(outgoing[k], 'tg', ring)  1.98 us
    ppermute x3, starting transfers between devices, shards(): fields.append(lax.ppermute(received, 'band', pairs(bands, m)))  1.86 us
  transfers between devices with their start and end apart: 14, of which 2 were waited for; matrix products, arithmetic and copies ran while one was open for 0% of the time, Pallas kernels for 37%

profile of v18, /device:TPU:0, one launch (start us, length us, event | category | flops | bytes accessed | tf_op | source)
XLA Modules:
  0.0 59.5 jit_solution(6229642785212781014)
XLA Ops:
  0.6 2.8 %wave_to_planes.1 = (f32[8,72,128]{2,1,0:T(8,128)}, f32[192,256]{1,0:T(8,128)}, f32[384,128]{1,0:T(8,128)}, f32[192,128]{1,0:T(8,128)}, bf16[384,256]{1,0:T(8,12...) custom-call(s32[1]{0:T(128)} %bitcast.me_ref, s32[12,128]{1,0:T(8,128)} %bitcast.13, ...), custom_call_target="tpu_custom_call" | custom-call | tf_op jit(solution)/shard_map/wave_to_planes/pallas_call | solution.py:621
  3.4 7.3 %all-to-all-start = ((f32[8,72,128]{2,1,0:T(8,128)}), f32[8,72,128]{2,1,0:T(8,128)S(1)}, u32[]{:S(2)}, u32[]{:S(2)}) async-start(f32[8,72,128]{2,1,0:T(8,128)} %get-tuple-element.30), calls=%async_computation | async-start | bytes 589824 | tf_op jit(solution)/shard_map/all_to_all | solution.py:646
  10.7 0.7 %collective-permute-start.2 = (f32[384,128]{1,0:T(8,128)}, f32[384,128]{1,0:T(8,128)S(1)}, u32[]{:S(2)}, u32[]{:S(2)}) collective-permute-start(f32[384,128]{1,0:T(8,128)} %get-tuple-element.29.refs_1_), channel_id=1, source_target_pairs={{0,24},{8,16},{16,8},{24,0},{1,25},{9,17},{17,9},{25,1},{2,26},{10... | collective-permute-start | bytes 589832 | tf_op jit(solution)/shard_map/ppermute | solution.py:696
  11.3 0.9 %collective-permute-start.1 = (f32[384,128]{1,0:T(8,128)}, f32[384,128]{1,0:T(8,128)S(1)}, u32[]{:S(2)}, u32[]{:S(2)}) collective-permute-start(f32[384,128]{1,0:T(8,128)} %get-tuple-element.29.refs_1_), channel_id=1, source_target_pairs={{0,16},{8,24},{16,0},{24,8},{1,17},{9,25},{17,1},{25,9},{2,18},{10... | collective-permute-start | bytes 589832 | tf_op jit(solution)/shard_map/ppermute | solution.py:696
  12.3 0.3 collective-permute-start
  12.5 0.7 %copy-done.7 = s32[1536]{0:T(1024)S(1)} copy-done((s32[1536]{0:T(1024)S(1)}, s32[1536]{0:T(1024)}, u32[]{:S(2)}) %copy-start.7) | copy-done | bytes 6168
  13.2 0.7 %copy-done.8 = s32[1536]{0:T(1024)S(1)} copy-done((s32[1536]{0:T(1024)S(1)}, s32[1536]{0:T(1024)}, u32[]{:S(2)}) %copy-start.8) | copy-done | bytes 6168
  13.9 2.3 %stick_map.1 = (s32[128,128]{1,0:T(8,128)S(1)}, s32[128,128]{1,0:T(8,128)S(1)}, s32[16,128]{1,0:T(8,128)S(1)}, s32[12,128]{1,0:T(8,128)S(1)}, s32[12,128]{1,0:T(...) custom-call(s32[12,128]{1,0:T(8,128)S(1)} %bitcast.9, s32[12,128]{1,0:T(8,128)S(1)} %bitcast.11), custom_call_target="tpu_custom_call" | custom-call | flops 4000000000 | bytes 100000 | tf_op jit(solution)/shard_map/stick_map/pallas_call | solution.py:651
  16.2 0.1 pad_add_fusion.place_ref
  16.3 4.0 %all-to-all-done.recv_ref.refs_5_ = f32[8,72,128]{2,1,0:T(8,128)S(1)} async-done(((f32[8,72,128]{2,1,0:T(8,128)}), f32[8,72,128]{2,1,0:T(8,128)S(1)}, u32[]{:S(2)}, u32[]{:S(2)}) %all-to-all-start) | async-done | bytes 294944 | tf_op jit(solution)/shard_map/all_to_all | solution.py:646
  20.3 0.0 collective-permute-start.5
  20.3 1.5 %collective-permute-start.4 = (f32[8,72,128]{2,1,0:T(8,128)S(1)}, f32[8,72,128]{2,1,0:T(8,128)S(1)}, u32[]{:S(2)}, u32[]{:S(2)}) collective-permute-start(f32[8,72,128]{2,1,0:T(8,128)S(1)} %all-to-all-done.recv_ref.refs_5_), channel_id=1, source_target_pairs={{0,16},{8,24},{16,0},{24,8},{1,17},{9,25},{17,1},{25,9},{2,18},{10... | collective-permute-start | bytes 884744 | tf_op jit(solution)/shard_map/ppermute | solution.py:697
  21.8 0.0 collective-permute-done.2.refs_4_
  21.8 0.3 collective-permute-start.3
  22.2 19.5 %planes.1.refs_9_ = f32[8,80,128]{2,1,0:T(8,128)S(1)} custom-call(s32[16,128]{1,0:T(8,128)S(1)} %get-tuple-element.31.first_ref, s32[128,128]{1,0:T(8,128)S(1)} %get-tuple-element.32.even_ref, s32[128,128]{1,0:T(8,128)S(1)} %get-tuple-element.33.odd_ref, s32[12,128]{1,0:T(8,128)S(1)} %get-tuple-element.34.src_ref, s32[12,128]{1,0:T(8,128)S(1)} %get-tuple-element.35.dst_ref, ...), custom_call_target="tpu_custom_call" | custom-call | flops 20000000000 | bytes 10000000 | tf_op jit(solution)/shard_map/planes/pallas_call | solution.py:674
  41.7 0.0 collective-permute-done.1.refs_3_
  41.8 0.0 collective-permute-done.refs_2_
  41.8 0.0 collective-permute-done.5.refs_8_
  41.8 0.0 collective-permute-done.4.refs_7_
  41.8 0.0 collective-permute-done.3.refs_6_
  41.8 1.0 %inner.1 = (f32[80,128]{1,0:T(8,128)S(1)}, f32[80,128]{1,0:T(8,128)S(1)}, f32[80,128]{1,0:T(8,128)S(1)}, f32[80,128]{1,0:T(8,128)S(1)}, f32[80,128]{1,0:T(8,128)...) custom-call(s32[2]{0:T(128)S(1)} %pad_add_fusion.place_ref, f32[192,256]{1,0:T(8,128)S(1)} %copy-done, ...), custom_call_target="tpu_custom_call" | custom-call | tf_op jit(solution)/shard_map/inner/pallas_call | solution.py:701
  42.8 1.1 %collective-permute-start.6 = (f32[80,128]{1,0:T(8,128)S(1)}, f32[80,128]{1,0:T(8,128)S(1)}, u32[]{:S(2)}, u32[]{:S(2)}) collective-permute-start(f32[80,128]{1,0:T(8,128)S(1)} %get-tuple-element.39), channel_id=1, source_target_pairs={{0,4},{1,5},{2,6},{3,7},{4,0},{5,1},{6,2},{7,3},{8,12},{9,13},{10,... | collective-permute-start | bytes 122888 | tf_op jit(solution)/shard_map/ppermute | solution.py:712
  43.9 1.9 %collective-permute-start.7 = (f32[80,128]{1,0:T(8,128)S(1)}, f32[80,128]{1,0:T(8,128)S(1)}, u32[]{:S(2)}, u32[]{:S(2)}) collective-permute-start(f32[80,128]{1,0:T(8,128)S(1)} %get-tuple-element.40), channel_id=1, source_target_pairs={{0,3},{1,4},{2,5},{3,6},{4,7},{5,0},{6,1},{7,2},{8,11},{9,12},{10,... | collective-permute-start | bytes 122888 | tf_op jit(solution)/shard_map/ppermute | solution.py:712
  45.7 2.0 %collective-permute-start.8 = (f32[80,128]{1,0:T(8,128)S(1)}, f32[80,128]{1,0:T(8,128)S(1)}, u32[]{:S(2)}, u32[]{:S(2)}) collective-permute-start(f32[80,128]{1,0:T(8,128)S(1)} %get-tuple-element.41), channel_id=1, source_target_pairs={{0,5},{1,6},{2,7},{3,0},{4,1},{5,2},{6,3},{7,4},{8,13},{9,14},{10,... | collective-permute-start | bytes 122888 | tf_op jit(solution)/shard_map/ppermute | solution.py:712
  47.7 0.7 %collective-permute-start.9 = (f32[80,128]{1,0:T(8,128)S(1)}, f32[80,128]{1,0:T(8,128)S(1)}, u32[]{:S(2)}, u32[]{:S(2)}) collective-permute-start(f32[80,128]{1,0:T(8,128)S(1)} %get-tuple-element.42), channel_id=1, source_target_pairs={{0,2},{1,3},{2,4},{3,5},{4,6},{5,7},{6,0},{7,1},{8,10},{9,11},{10,... | collective-permute-start | bytes 122888 | tf_op jit(solution)/shard_map/ppermute | solution.py:712
  48.4 3.2 %collective-permute-start.10 = (f32[80,128]{1,0:T(8,128)S(1)}, f32[80,128]{1,0:T(8,128)S(1)}, u32[]{:S(2)}, u32[]{:S(2)}) collective-permute-start(f32[80,128]{1,0:T(8,128)S(1)} %get-tuple-element.43), channel_id=1, source_target_pairs={{0,6},{1,7},{2,0},{3,1},{4,2},{5,3},{6,4},{7,5},{8,14},{9,15},{10,... | collective-permute-start | bytes 122888 | tf_op jit(solution)/shard_map/ppermute | solution.py:712
  51.5 0.0 collective-permute-done.6.refs_1_
  51.5 1.4 %collective-permute-start.11 = (f32[80,128]{1,0:T(8,128)S(1)}, f32[80,128]{1,0:T(8,128)S(1)}, u32[]{:S(2)}, u32[]{:S(2)}) collective-permute-start(f32[80,128]{1,0:T(8,128)S(1)} %get-tuple-element.44), channel_id=1, source_target_pairs={{0,1},{1,2},{2,3},{3,4},{4,5},{5,6},{6,7},{7,0},{8,9},{9,10},{10,1... | collective-permute-start | bytes 122888 | tf_op jit(solution)/shard_map/ppermute | solution.py:712
  52.9 3.4 %collective-permute-start.12 = (f32[80,128]{1,0:T(8,128)S(1)}, f32[80,128]{1,0:T(8,128)S(1)}, u32[]{:S(2)}, u32[]{:S(2)}) collective-permute-start(f32[80,128]{1,0:T(8,128)S(1)} %get-tuple-element.45), channel_id=1, source_target_pairs={{0,7},{1,0},{2,1},{3,2},{4,3},{5,4},{6,5},{7,6},{8,15},{9,8},{10,9... | collective-permute-start | bytes 122888 | tf_op jit(solution)/shard_map/ppermute | solution.py:712
  56.3 2.0 %collective-permute-done.11.refs_6_ = f32[80,128]{1,0:T(8,128)S(1)} collective-permute-done((f32[80,128]{1,0:T(8,128)S(1)}, f32[80,128]{1,0:T(8,128)S(1)}, u32[]{:S(2)}, u32[]{:S(2)}) %collective-permute-start.11) | collective-permute-done | bytes 40992 | tf_op jit(solution)/shard_map/ppermute | solution.py:712
  58.2 0.0 collective-permute-done.12.refs_7_
  58.3 1.3 %planes_to_wave.1 = (f32[192,2,128]{2,1,0:T(2,128)}, f32[2,1,4]{2,1,0:T(1,128)}) custom-call(s32[1]{0:T(128)} %bitcast.me_ref, f32[192,128]{1,0:T(8,128)S(1)} %copy-done.6, f32[80,128]{1,0:T(8,128)S(1)} %get-tuple-element.38.refs_0_, f32[80,128]{1,0:T(8,128)S(1)} %collective-permute-done.6.refs_1_, f32[80,128]{1,0:T(8,128)S(1)} %collective-permute-done.7.refs_2_, ...), custom_call_target="tpu_custom_call" | custom-call | tf_op jit(solution)/shard_map/planes_to_wave/pallas_call | solution.py:713
  (20 shorter events, 0.0 us)
Async XLA Ops:
  3.4 16.9 %all-to-all-start = ((f32[8,72,128]{2,1,0:T(8,128)}), f32[8,72,128]{2,1,0:T(8,128)S(1)}, u32[]{:S(2)}, u32[]{:S(2)}) async-start(f32[8,72,128]{2,1,0:T(8,128)} %get-tuple-element.30), calls=%async_computation | async-start | bytes 589824 | tf_op jit(solution)/shard_map/all_to_all | solution.py:646
  10.7 11.2 %collective-permute-start.2 = (f32[384,128]{1,0:T(8,128)}, f32[384,128]{1,0:T(8,128)S(1)}, u32[]{:S(2)}, u32[]{:S(2)}) collective-permute-start(f32[384,128]{1,0:T(8,128)} %get-tuple-element.29.refs_1_), channel_id=1, source_target_pairs={{0,24},{8,16},{16,8},{24,0},{1,25},{9,17},{17,9},{25,1},{2,26},{10... | collective-permute-start | bytes 589832 | tf_op jit(solution)/shard_map/ppermute | solution.py:696
  11.3 30.4 %collective-permute-start.1 = (f32[384,128]{1,0:T(8,128)}, f32[384,128]{1,0:T(8,128)S(1)}, u32[]{:S(2)}, u32[]{:S(2)}) collective-permute-start(f32[384,128]{1,0:T(8,128)} %get-tuple-element.29.refs_1_), channel_id=1, source_target_pairs={{0,16},{8,24},{16,0},{24,8},{1,17},{9,25},{17,1},{25,9},{2,18},{10... | collective-permute-start | bytes 589832 | tf_op jit(solution)/shard_map/ppermute | solution.py:696
  12.3 29.5 %collective-permute-start = (f32[384,128]{1,0:T(8,128)}, f32[384,128]{1,0:T(8,128)S(1)}, u32[]{:S(2)}, u32[]{:S(2)}) collective-permute-start(f32[384,128]{1,0:T(8,128)} %get-tuple-element.29.refs_1_), channel_id=1, source_target_pairs={{0,8},{8,0},{16,24},{24,16},{1,9},{9,1},{17,25},{25,17},{2,10},{10... | collective-permute-start | bytes 589832 | tf_op jit(solution)/shard_map/ppermute | solution.py:696
  12.5 0.7 %copy-start.7 = (s32[1536]{0:T(1024)S(1)}, s32[1536]{0:T(1024)}, u32[]{:S(2)}) copy-start(s32[1536]{0:T(1024)} %param.9) | copy-start | bytes 18436
  13.2 0.7 %copy-start.8 = (s32[1536]{0:T(1024)S(1)}, s32[1536]{0:T(1024)}, u32[]{:S(2)}) copy-start(s32[1536]{0:T(1024)} %param.8) | copy-start | bytes 18436
  20.3 21.5 %collective-permute-start.5 = (f32[8,72,128]{2,1,0:T(8,128)S(1)}, f32[8,72,128]{2,1,0:T(8,128)S(1)}, u32[]{:S(2)}, u32[]{:S(2)}) collective-permute-start(f32[8,72,128]{2,1,0:T(8,128)S(1)} %all-to-all-done.recv_ref.refs_5_), channel_id=1, source_target_pairs={{0,24},{8,16},{16,8},{24,0},{1,25},{9,17},{17,9},{25,1},{2,26},{10... | collective-permute-start | bytes 884744 | tf_op jit(solution)/shard_map/ppermute | solution.py:697
  20.3 21.5 %collective-permute-start.4 = (f32[8,72,128]{2,1,0:T(8,128)S(1)}, f32[8,72,128]{2,1,0:T(8,128)S(1)}, u32[]{:S(2)}, u32[]{:S(2)}) collective-permute-start(f32[8,72,128]{2,1,0:T(8,128)S(1)} %all-to-all-done.recv_ref.refs_5_), channel_id=1, source_target_pairs={{0,16},{8,24},{16,0},{24,8},{1,17},{9,25},{17,1},{25,9},{2,18},{10... | collective-permute-start | bytes 884744 | tf_op jit(solution)/shard_map/ppermute | solution.py:697
  21.8 20.0 %collective-permute-start.3 = (f32[8,72,128]{2,1,0:T(8,128)S(1)}, f32[8,72,128]{2,1,0:T(8,128)S(1)}, u32[]{:S(2)}, u32[]{:S(2)}) collective-permute-start(f32[8,72,128]{2,1,0:T(8,128)S(1)} %all-to-all-done.recv_ref.refs_5_), channel_id=1, source_target_pairs={{0,8},{8,0},{16,24},{24,16},{1,9},{9,1},{17,25},{25,17},{2,10},{10... | collective-permute-start | bytes 884744 | tf_op jit(solution)/shard_map/ppermute | solution.py:697
  22.2 19.7 %copy-start = (f32[192,256]{1,0:T(8,128)S(1)}, f32[192,256]{1,0:T(8,128)}, u32[]{:S(2)}) copy-start(f32[192,256]{1,0:T(8,128)} %get-tuple-element.28.refs_0_.refs_8_) | copy-start | bytes 589828
  22.2 19.7 %copy-start.5 = (f32[384,128]{1,0:T(8,128)S(1)}, f32[384,128]{1,0:T(8,128)}, u32[]{:S(2)}) copy-start(f32[384,128]{1,0:T(8,128)} %get-tuple-element.29.refs_1_) | copy-start | bytes 589828
  22.2 36.1 %copy-start.1 = (bf16[384,256]{1,0:T(8,128)(2,1)S(1)}, bf16[384,256]{1,0:T(8,128)(2,1)}, u32[]{:S(2)}) copy-start(bf16[384,256]{1,0:T(8,128)(2,1)} %get-tuple-element.46.refs_9_) | copy-start | bytes 589828
  22.2 36.1 %copy-start.2 = (bf16[384,256]{1,0:T(8,128)(2,1)S(1)}, bf16[384,256]{1,0:T(8,128)(2,1)}, u32[]{:S(2)}) copy-start(bf16[384,256]{1,0:T(8,128)(2,1)} %get-tuple-element.47.refs_10_) | copy-start | bytes 589828
  22.2 36.1 %copy-start.3 = (f32[192,192]{1,0:T(8,128)S(1)}, f32[192,192]{1,0:T(8,128)}, u32[]{:S(2)}) copy-start(f32[192,192]{1,0:T(8,128)} %get-tuple-element.48.refs_11_) | copy-start | bytes 442372
  22.2 36.1 %copy-start.4 = (f32[192,192]{1,0:T(8,128)S(1)}, f32[192,192]{1,0:T(8,128)}, u32[]{:S(2)}) copy-start(f32[192,192]{1,0:T(8,128)} %get-tuple-element.49.refs_12_) | copy-start | bytes 442372
  22.2 36.1 %copy-start.6 = (f32[192,128]{1,0:T(8,128)S(1)}, f32[192,128]{1,0:T(8,128)}, u32[]{:S(2)}) copy-start(f32[192,128]{1,0:T(8,128)} %get-tuple-element.27.len_ref) | copy-start | bytes 294916
  42.8 8.7 %collective-permute-start.6 = (f32[80,128]{1,0:T(8,128)S(1)}, f32[80,128]{1,0:T(8,128)S(1)}, u32[]{:S(2)}, u32[]{:S(2)}) collective-permute-start(f32[80,128]{1,0:T(8,128)S(1)} %get-tuple-element.39), channel_id=1, source_target_pairs={{0,4},{1,5},{2,6},{3,7},{4,0},{5,1},{6,2},{7,3},{8,12},{9,13},{10,... | collective-permute-start | bytes 122888 | tf_op jit(solution)/shard_map/ppermute | solution.py:712
  43.9 9.0 %collective-permute-start.7 = (f32[80,128]{1,0:T(8,128)S(1)}, f32[80,128]{1,0:T(8,128)S(1)}, u32[]{:S(2)}, u32[]{:S(2)}) collective-permute-start(f32[80,128]{1,0:T(8,128)S(1)} %get-tuple-element.40), channel_id=1, source_target_pairs={{0,3},{1,4},{2,5},{3,6},{4,7},{5,0},{6,1},{7,2},{8,11},{9,12},{10,... | collective-permute-start | bytes 122888 | tf_op jit(solution)/shard_map/ppermute | solution.py:712
  45.7 10.5 %collective-permute-start.8 = (f32[80,128]{1,0:T(8,128)S(1)}, f32[80,128]{1,0:T(8,128)S(1)}, u32[]{:S(2)}, u32[]{:S(2)}) collective-permute-start(f32[80,128]{1,0:T(8,128)S(1)} %get-tuple-element.41), channel_id=1, source_target_pairs={{0,5},{1,6},{2,7},{3,0},{4,1},{5,2},{6,3},{7,4},{8,13},{9,14},{10,... | collective-permute-start | bytes 122888 | tf_op jit(solution)/shard_map/ppermute | solution.py:712
  47.7 8.6 %collective-permute-start.9 = (f32[80,128]{1,0:T(8,128)S(1)}, f32[80,128]{1,0:T(8,128)S(1)}, u32[]{:S(2)}, u32[]{:S(2)}) collective-permute-start(f32[80,128]{1,0:T(8,128)S(1)} %get-tuple-element.42), channel_id=1, source_target_pairs={{0,2},{1,3},{2,4},{3,5},{4,6},{5,7},{6,0},{7,1},{8,10},{9,11},{10,... | collective-permute-start | bytes 122888 | tf_op jit(solution)/shard_map/ppermute | solution.py:712
  48.4 7.9 %collective-permute-start.10 = (f32[80,128]{1,0:T(8,128)S(1)}, f32[80,128]{1,0:T(8,128)S(1)}, u32[]{:S(2)}, u32[]{:S(2)}) collective-permute-start(f32[80,128]{1,0:T(8,128)S(1)} %get-tuple-element.43), channel_id=1, source_target_pairs={{0,6},{1,7},{2,0},{3,1},{4,2},{5,3},{6,4},{7,5},{8,14},{9,15},{10,... | collective-permute-start | bytes 122888 | tf_op jit(solution)/shard_map/ppermute | solution.py:712
  51.5 6.7 %collective-permute-start.11 = (f32[80,128]{1,0:T(8,128)S(1)}, f32[80,128]{1,0:T(8,128)S(1)}, u32[]{:S(2)}, u32[]{:S(2)}) collective-permute-start(f32[80,128]{1,0:T(8,128)S(1)} %get-tuple-element.44), channel_id=1, source_target_pairs={{0,1},{1,2},{2,3},{3,4},{4,5},{5,6},{6,7},{7,0},{8,9},{9,10},{10,1... | collective-permute-start | bytes 122888 | tf_op jit(solution)/shard_map/ppermute | solution.py:712
  52.9 5.3 %collective-permute-start.12 = (f32[80,128]{1,0:T(8,128)S(1)}, f32[80,128]{1,0:T(8,128)S(1)}, u32[]{:S(2)}, u32[]{:S(2)}) collective-permute-start(f32[80,128]{1,0:T(8,128)S(1)} %get-tuple-element.45), channel_id=1, source_target_pairs={{0,7},{1,0},{2,1},{3,2},{4,3},{5,4},{6,5},{7,6},{8,15},{9,8},{10,9... | collective-permute-start | bytes 122888 | tf_op jit(solution)/shard_map/ppermute | solution.py:712
